TPU v7x, 32 devices: a whole 2x2x4 slice. The times are simulated.
32 devices in a mesh: row: 4 (over y, core), col: 8 (over z, x).
Axes of the slice: x: 2, y: 2, z: 4, core: 2. Of those that a mesh axis runs over, the one named last changes fastest.
Arguments:
- student_image: bfloat16 [2048, 512], P(('row', 'col')), may hold values from -0.16 to 0.16
- student_text: bfloat16 [2048, 512], P(('row', 'col')), may hold values from -0.16 to 0.16
- teacher_image: bfloat16 [2048, 1280], P(('row', 'col')), may hold values from -32 to 32
- teacher_text: bfloat16 [2048, 1280], P(('row', 'col')), may hold values from -32 to 32
- teacher_scale: float32 [], replicated, may hold values from 20 to 250
- student_scale: float32 [], replicated, may hold values from 10 to 250
Outputs:
- image_grad: float32 [2048, 512], P(('row', 'col'))
- text_grad: float32 [2048, 512], P(('row', 'col'))
All inputs are finite; a program needn't handle non-finite values.
Results may differ from a plain program's by a relative error of at most 0.012.
The roundings to bfloat16 on the way count: a program that leaves them out, or rounds other values in their place, can miss the bound.
Values may be sent and summed in bfloat16 or wider, within the bound.
No kernel may reach another device: no remote copies, remote signals or barrier semaphores. Data moves between devices by JAX's collectives and lax.ppermute only.
A program may use at most 64 MiB of HBM per device.

v0:
```python
import jax
import jax.numpy as jnp
from jax import lax
from jax.sharding import PartitionSpec as P

EPSILON = 1e-12


def unit_rows(raw):
    values = raw.astype(jnp.float32)
    inverse = lax.rsqrt(jnp.sum(values * values, axis=-1, keepdims=True) + EPSILON)
    return (values * inverse, inverse)


def scaled_logits(left, right, scale):
    product = lax.dot_general(
        left, right, (((1,), (1,)), ((), ())), preferred_element_type=jnp.float32
    )
    return scale * product


def block_stats(logits, axis):
    peak = jnp.max(logits, axis=axis)
    total = jnp.sum(jnp.exp(logits - jnp.expand_dims(peak, axis)), axis=axis)
    return (peak, total)


def join_pair(peak_a, total_a, peak_b, total_b):
    top = jnp.maximum(peak_a, peak_b)
    return (top, total_a * jnp.exp(peak_a - top) + total_b * jnp.exp(peak_b - top))


def join_stats(first, second):
    teach_peak, teach_total = join_pair(first[0], first[1], second[0], second[1])
    learn_peak, learn_total = join_pair(first[2], first[3], second[2], second[3])
    return (teach_peak, teach_total, learn_peak, learn_total)


def back_norm(grad, unit, inverse):
    return inverse * (grad - unit * jnp.sum(unit * grad, axis=-1, keepdims=True))


def body(student_image, student_text, teacher_image, teacher_text, teacher_scale, student_scale):
    image_unit, image_inverse = unit_rows(student_image)
    text_unit, text_inverse = unit_rows(student_text)
    pupil_image = image_unit.astype(jnp.bfloat16)
    pupil_text = text_unit.astype(jnp.bfloat16)
    master_image = unit_rows(teacher_image)[0].astype(jnp.bfloat16)
    master_text = unit_rows(teacher_text)[0].astype(jnp.bfloat16)
    tile_images, tile_masters = (
        lax.all_gather(pupil_image, "col", axis=0, tiled=True),
        lax.all_gather(master_image, "col", axis=0, tiled=True),
    )
    tile_texts, tile_master_texts = (
        lax.all_gather(pupil_text, "row", axis=0, tiled=True),
        lax.all_gather(master_text, "row", axis=0, tiled=True),
    )
    rows_total = tile_images.shape[0]
    columns = tile_texts.shape[0]
    width = tile_texts.shape[1]
    rows_block = min(512, rows_total)
    blocks = rows_total // rows_block
    master_blocks = tile_masters.reshape(blocks, rows_block, tile_masters.shape[1])
    pupil_blocks = tile_images.reshape(blocks, rows_block, width)

    def first_pass(carried, pieces):
        master_piece, pupil_piece = pieces
        teach = scaled_logits(master_piece, tile_master_texts, teacher_scale)
        learn = scaled_logits(pupil_piece, tile_texts, student_scale)
        teach_peak, teach_total = block_stats(teach, 0)
        learn_peak, learn_total = block_stats(learn, 0)
        updated = join_stats(carried, (teach_peak, teach_total, learn_peak, learn_total))
        return (updated, block_stats(teach, 1) + block_stats(learn, 1))

    lowest = jnp.full((columns,), -jnp.inf, jnp.float32)
    nothing = jnp.zeros((columns,), jnp.float32)
    column_local, row_blocks = lax.scan(
        first_pass, (lowest, nothing, lowest, nothing), (master_blocks, pupil_blocks)
    )
    row_local = tuple((item.reshape(rows_total) for item in row_blocks))
    row_peaks = lax.pmax((row_local[0], row_local[2]), "col")
    row_totals = lax.psum(
        (
            row_local[1] * jnp.exp(row_local[0] - row_peaks[0]),
            row_local[3] * jnp.exp(row_local[2] - row_peaks[1]),
        ),
        "col",
    )
    row_stats = (row_peaks[0], row_totals[0], row_peaks[1], row_totals[1])
    col_peaks = lax.pmax((column_local[0], column_local[2]), "row")
    col_totals = lax.psum(
        (
            column_local[1] * jnp.exp(column_local[0] - col_peaks[0]),
            column_local[3] * jnp.exp(column_local[2] - col_peaks[1]),
        ),
        "row",
    )
    column_stats = (col_peaks[0], col_totals[0], col_peaks[1], col_totals[1])
    row_split = tuple((item.reshape(blocks, rows_block) for item in row_stats))

    def second_pass(carried, pieces):
        master_piece, pupil_piece, teach_peak, teach_total, learn_peak, learn_total = pieces
        teach = scaled_logits(master_piece, tile_master_texts, teacher_scale)
        learn = scaled_logits(pupil_piece, tile_texts, student_scale)
        rows_part = (
            jnp.exp(learn - learn_peak[:, None]) / learn_total[:, None]
            - jnp.exp(teach - teach_peak[:, None]) / teach_total[:, None]
        )
        cols_part = (
            jnp.exp(learn - column_stats[2][None, :]) / column_stats[3][None, :]
            - jnp.exp(teach - column_stats[0][None, :]) / column_stats[1][None, :]
        )
        weight = (0.5 * (rows_part + cols_part)).astype(jnp.bfloat16)
        image_part = student_scale * jnp.dot(weight, tile_texts, preferred_element_type=jnp.float32)
        text_part = student_scale * lax.dot_general(
            weight, pupil_piece, (((0,), (0,)), ((), ())), preferred_element_type=jnp.float32
        )
        return (carried + text_part, image_part)

    text_partial, image_pieces = lax.scan(
        second_pass,
        jnp.zeros((columns, width), jnp.float32),
        (master_blocks, pupil_blocks) + row_split,
    )
    image_partial = image_pieces.reshape(rows_total, width)
    own_rows = student_image.shape[0]
    image_whole = lax.psum(image_partial, "col")
    text_whole = lax.psum(text_partial, "row")
    image_unit_grad = lax.dynamic_slice_in_dim(
        image_whole, lax.axis_index("col") * own_rows, own_rows, 0
    )
    text_unit_grad = lax.dynamic_slice_in_dim(
        text_whole, lax.axis_index("row") * own_rows, own_rows, 0
    )
    return (
        back_norm(image_unit_grad, image_unit, image_inverse),
        back_norm(text_unit_grad, text_unit, text_inverse),
    )


def solution(mesh):
    placed = (
        P(("row", "col"), None),
        P(("row", "col"), None),
        P(("row", "col"), None),
        P(("row", "col"), None),
        P(),
        P(),
    )
    return jax.shard_map(
        body,
        mesh=mesh,
        in_specs=placed,
        out_specs=(P(("row", "col"), None), P(("row", "col"), None)),
        check_vma=False,
    )
```

profile of v0, /device:TPU:0, one launch (start us, length us, event | category | flops | bytes accessed | tf_op | source)
XLA Modules:
  0.0 239.9 jit_solution(13398785270618385585)
XLA Ops:
  7.2 1.1 fusion
  8.3 1.7 fusion.1
  10.1 1.0 fusion.17
  11.1 0.9 fusion.6
  13.3 7.2 %all_gather.13 = bf16[256,512]{1,0:T(8,128)(2,1)S(1)} all-gather(bf16[64,512]{1,0:T(8,128)(2,1)S(1)} %fusion.6), channel_id=1, replica_groups=mesh['row'=4,'col'=8] {'row'}, dimensions={0}, use_global_device_ids=true | all-gather | bytes 327680 | tf_op jit(solution)/shard_map/all_gather | solution.py:55
  20.5 1.0 fusion.13
  21.7 32.7 %all_gather.12 = bf16[512,512]{1,0:T(8,128)(2,1)S(1)} all-gather(bf16[64,512]{1,0:T(8,128)(2,1)S(1)} %fusion.9), channel_id=1, replica_groups=mesh['row'=4,'col'=8] {'col'}, dimensions={0}, use_global_device_ids=true | all-gather | bytes 589824 | tf_op jit(solution)/shard_map/all_gather | solution.py:51
  54.5 7.9 %all_gather.15 = bf16[256,1280]{1,0:T(8,128)(2,1)S(1)} all-gather(bf16[64,1280]{1,0:T(8,128)(2,1)S(1)} %fusion.3), channel_id=1, replica_groups=mesh['row'=4,'col'=8] {'row'}, dimensions={0}, use_global_device_ids=true | all-gather | bytes 819200 | tf_op jit(solution)/shard_map/all_gather | solution.py:56
  62.4 0.4 fusion.19
  62.8 1.9 fusion.18
  64.8 0.4 exponential_reduce_fusion.2
  65.3 6.1 %all-reduce.3 = (f32[256]{0:T(256)S(1)}, f32[256]{0:T(256)S(1)}) all-reduce(f32[256]{0:T(256)S(1)} %get-tuple-element.67, f32[256]{0:T(256)S(1)} %get-tuple-element.97), channel_id=1, replica_groups=mesh['row'=4,'col'=8] {'row'}, use_global_device_ids=true, to_apply=%region_17.18 | all-reduce | flops 512 | bytes 4096 | tf_op jit(solution)/shard_map/pmax | solution.py:90
  71.5 20.9 %all-reduce.1 = (f32[512]{0:T(512)S(1)}, f32[512]{0:T(512)S(1)}) all-reduce(f32[512]{0:T(512)S(1)} %get-tuple-element.76, f32[512]{0:T(512)S(1)} %get-tuple-element.95), channel_id=1, replica_groups=mesh['row'=4,'col'=8] {'col'}, use_global_device_ids=true, to_apply=%region_9.10 | all-reduce | flops 1024 | bytes 8192 | tf_op jit(solution)/shard_map/pmax | solution.py:81
  92.5 5.7 %all-reduce.2 = (f32[256]{0:T(256)S(1)}, f32[256]{0:T(256)S(1)}) all-reduce(f32[256]{0:T(256)S(1)} %exponential_multiply_fusion.2, f32[256]{0:T(256)S(1)} %exponential_multiply_fusion.3), channel_id=1, replica_groups=mesh['row'=4,'col'=8] {'row'}, use_global_device_ids=true, to_apply=%region_19.20 | all-reduce | flops 512 | bytes 4096 | tf_op jit(solution)/shard_map/psum | solution.py:91
  98.1 17.1 %all-reduce = (f32[512]{0:T(512)S(1)}, f32[512]{0:T(512)S(1)}) all-reduce(f32[512]{0:T(512)S(1)} %exponential_multiply_fusion, f32[512]{0:T(512)S(1)} %exponential_multiply_fusion.1), channel_id=1, replica_groups=mesh['row'=4,'col'=8] {'col'}, use_global_device_ids=true, to_apply=%region_11.12 | all-reduce | flops 1024 | bytes 8192 | tf_op jit(solution)/shard_map/psum | solution.py:82
  115.3 0.4 multiply_convert_fusion
  115.7 1.1 convolution_multiply_fusion.2
  116.9 1.3 convolution_multiply_fusion
  118.3 30.8 %all-reduce.9.cloned.1.call-done = f32[256,512]{1,0:T(8,128)} async-done(((f32[256,512]{1,0:T(8,128)}), f32[256,512]{1,0:T(8,128)}) %all-reduce.9.cloned.1.call-update) | async-done | bytes 524304 | tf_op jit(solution)/shard_map/psum | solution.py:128
  149.1 1.1 fusion.14
  150.2 1.7 fusion.16
  151.9 78.8 %all-reduce.7.cloned.1.call-done = f32[512,512]{1,0:T(8,128)} async-done(((f32[512,512]{1,0:T(8,128)}), f32[512,512]{1,0:T(8,128)}) %all-reduce.7.cloned.1.call-update) | async-done | bytes 1048592 | tf_op jit(solution)/shard_map/psum | solution.py:127
  230.6 1.1 fusion.10
  231.7 1.7 fusion.12
  (26 shorter events, 0.8 us)
Async XLA Ops:
  7.2 14.5 %copy-start.1 = (bf16[64,512]{1,0:T(8,128)(2,1)S(1)}, bf16[64,512]{1,0:T(8,128)(2,1)}, u32[]{:S(2)}) copy-start(bf16[64,512]{1,0:T(8,128)(2,1)} %param.6) | copy-start | bytes 196612
  7.2 14.3 %copy-start.2 = (bf16[64,1280]{1,0:T(8,128)(2,1)S(1)}, bf16[64,1280]{1,0:T(8,128)(2,1)}, u32[]{:S(2)}) copy-start(bf16[64,1280]{1,0:T(8,128)(2,1)} %param.9) | copy-start | bytes 491524
  7.2 55.6 %all-gather.2.cloned.1.call-start = ((), (), s32[]{:S(2)}) async-start(), calls=%async_computation | async-start | bytes 1474560 | tf_op jit(solution)/shard_map/all_gather | solution.py:52
  10.1 139.1 %all-reduce.9.cloned.1.call-start = ((), (), s32[]{:S(2)}) async-start(), calls=%async_computation.2 | async-start | bytes 1048576 | tf_op jit(solution)/shard_map/psum | solution.py:128
  116.9 32.2 %copy-start = (bf16[64,512]{1,0:T(8,128)(2,1)S(1)}, bf16[64,512]{1,0:T(8,128)(2,1)}, u32[]{:S(2)}) copy-start(bf16[64,512]{1,0:T(8,128)(2,1)} %param.7) | copy-start | bytes 196612
  116.9 113.7 %all-reduce.7.cloned.1.call-start = ((), (), s32[]{:S(2)}) async-start(), calls=%async_computation.1 | async-start | bytes 2097152 | tf_op jit(solution)/shard_map/psum | solution.py:127
Sparse Core Ops, SparseCore 0:
  10.2 47.4 all-gather.1
  117.0 32.0 all-reduce.8
  152.6 77.9 all-reduce.6
where the time goes:
time: 240 us
  waiting for transfers between devices  110 us (46%)
  blocking collectives  97.6 us (41%)
  between operations  15.2 us (6%)
  other arithmetic  12.5 us (5%)
  matrix products  4.82 us (2%)
    psum x1, waiting for transfers between devices, body(): image_whole = lax.psum(image_partial, 'col')  78.8 us
    all_gather x1, blocking collectives, body(): lax.all_gather(pupil_image, 'col', axis=0, tiled=True)  32.7 us
    psum x1, waiting for transfers between devices, body(): text_whole = lax.psum(text_partial, 'row')  30.8 us
    pmax x1, blocking collectives, body(): row_peaks = lax.pmax((row_local[0], row_local[2]), 'col')  20.9 us
    psum x1, blocking collectives, body(): lax.psum((row_local[1] * jnp.exp(row_local[0] - row_peaks[0]), row_local[...  17.1 us
    all_gather x1, blocking collectives, body(): lax.all_gather(master_text, 'row', axis=0, tiled=True)  7.88 us
    all_gather x1, blocking collectives, body(): lax.all_gather(pupil_text, 'row', axis=0, tiled=True)  7.22 us
    pmax x1, blocking collectives, body(): col_peaks = lax.pmax((column_local[0], column_local[2]), 'row')  6.14 us
  transfers between devices with their start and end apart: 3, of which 2 were waited for; matrix products, arithmetic and copies ran while one was open for 3% of the time, Pallas kernels for 0%

commit v1 on v0

v1 whole, which is shorter than its diff:
```python
import functools

import jax
import jax.numpy as jnp
from jax import lax
from jax.experimental import pallas as pl
from jax.experimental.pallas import tpu as pltpu
from jax.sharding import Mesh, PartitionSpec as P

EPSILON = 1e-12
SQUARE = ("y", "x")
PLANE = ("core", "y", "x")
LINE = "z"
EVERY = ("y", "core", "z", "x")
F32 = jnp.float32
BF16 = jnp.bfloat16
MANY = 1 << 35


def physical_mesh(mesh):
    rows, cols = mesh.shape["row"], mesh.shape["col"]
    side = rows // 2
    wide = side if cols % side == 0 else 1
    return Mesh(mesh.devices.reshape(side, 2, cols // wide, wide), EVERY)


def unit_rows(raw):
    values = raw.astype(F32)
    inverse = lax.rsqrt(jnp.sum(values * values, axis=-1, keepdims=True) + EPSILON)
    return (values * inverse, inverse)


def put_units(block, pupil_ref, master_ref, at):
    own, width = block.shape[0], pupil_ref.shape[1]
    pupil_ref[pl.ds(at, own), :] = unit_rows(block[:, :width])[0].astype(BF16)
    master_ref[pl.ds(at, own), :] = unit_rows(block[:, width:])[0].astype(BF16)


def image_unit_kernel(core_ref, square_ref, *refs):
    pupil_ref, master_ref = refs[-2:]
    blocks = refs[:-2]
    own = blocks[0].shape[0]
    squares = len(blocks) // 2
    core = core_ref[0]
    for s in range(squares):
        at = jnp.bitwise_xor(square_ref[0], s)
        for ref, half in ((blocks[s], core), (blocks[squares + s], 1 - core)):
            row = pl.multiple_of((half * squares + at) * own, own)
            put_units(ref[...], pupil_ref, master_ref, row)


def text_unit_kernel(z_ref, *refs):
    pupil_ref, master_ref = refs[-2:]
    own = refs[0].shape[0]
    for s, ref in enumerate(refs[:-2]):
        row = pl.multiple_of(jnp.bitwise_xor(z_ref[0], s) * own, own)
        put_units(ref[...], pupil_ref, master_ref, row)


def product(left, right):
    return lax.dot_general(left, right, (((1,), (1,)), ((), ())), preferred_element_type=F32)


def block_lse(logits):
    peak = jnp.max(logits, axis=0, keepdims=True)
    return peak + jnp.log(jnp.sum(jnp.exp(logits - peak), axis=0, keepdims=True))


def join_lse(parts):
    top = functools.reduce(jnp.maximum, parts)
    return top + jnp.log(sum(jnp.exp(p - top) for p in parts))


def logits_kernel(
    teacher_scale_ref, student_scale_ref, pupil_text_ref, master_text_ref, pupil_image_ref,
    master_image_ref, teach_ref, rows_ref, cols_ref,
):
    images = pupil_image_ref.shape[0]
    step = min(512, images)
    for k, (scale_ref, image_ref, text_ref) in enumerate(
        (
            (teacher_scale_ref, master_image_ref, master_text_ref),
            (student_scale_ref, pupil_image_ref, pupil_text_ref),
        )
    ):
        scale = scale_ref[0]
        text = text_ref[...]
        columns = []
        for at in range(0, images, step):
            image = image_ref[at : at + step, :]
            logits = scale * product(image, text)
            if k == 0:
                teach_ref[at : at + step, :] = logits
            columns.append(block_lse(logits))
            row = block_lse(scale * product(text, image))
            for i in range(rows_ref.shape[0]):
                rows_ref[i, k : k + 1, at : at + step] = row
        cols_ref[k : k + 1, :] = join_lse(columns)


def join_kernel(rows_ref, out_ref):
    joined = join_lse([rows_ref[i] for i in range(rows_ref.shape[0])])
    for k in range(0, 8, 2):
        out_ref[k : k + 2, :] = joined


def weight_kernel(depth, z_ref, scale_ref, teach_ref, image_ref, text_ref, rows_ref, *refs):
    col_refs = refs[:depth]
    image_out_ref, own_text_ref = refs[depth : depth + 2]
    text_out_refs = refs[depth + 2 : -1]
    text_part_ref = refs[-1]
    plane, own, _ = image_out_ref.shape
    z = z_ref[0]
    scale = scale_ref[0]
    images = plane * own
    step = min(512, images)
    col = join_lse([ref[...] for ref in col_refs])
    text = text_ref[...]
    for at in range(0, images, step):
        row = jnp.transpose(rows_ref[:, at : at + step])
        image = image_ref[at : at + step, :]
        teach = teach_ref[at : at + step, :]
        learn = scale * product(image, text)
        rows_part = jnp.exp(learn - row[:, 1:2]) - jnp.exp(teach - row[:, 0:1])
        cols_part = jnp.exp(learn - col[1:2, :]) - jnp.exp(teach - col[0:1, :])
        weight = (0.5 * (rows_part + cols_part)).astype(BF16)
        image_part = scale * jnp.dot(weight, text, preferred_element_type=F32)
        for i in range(step // own):
            image_out_ref[at // own + i] = image_part[i * own : (i + 1) * own].astype(BF16)
        text_part = scale * lax.dot_general(
            weight, image, (((0,), (0,)), ((), ())), preferred_element_type=F32
        )
        if at:
            text_part = text_part_ref[...] + text_part
        text_part_ref[...] = text_part
    own_text_ref[...] = text_part_ref[pl.ds(pl.multiple_of(z * own, own), own), :]
    for s in range(1, depth):
        at = pl.multiple_of(jnp.bitwise_xor(z, s) * own, own)
        text_out_refs[s - 1][...] = text_part_ref[pl.ds(at, own), :].astype(BF16)


def back_norm(grad, raw):
    unit, inverse = unit_rows(raw)
    return inverse * (grad - unit * jnp.sum(unit * grad, axis=-1, keepdims=True))


def sum_kernel(parts_ref, out_ref):
    grad = parts_ref[0].astype(F32)
    for i in range(1, parts_ref.shape[0]):
        grad = grad + parts_ref[i].astype(F32)
    out_ref[...] = grad


def back_kernel(image_ref, raw_image_ref, raw_text_ref, *refs):
    image_out_ref, text_out_ref = refs[-2:]
    grad = refs[0][...]
    for ref in refs[1:-2]:
        grad = grad + ref[...].astype(F32)
    text_out_ref[...] = back_norm(grad, raw_text_ref[...])
    image_out_ref[...] = back_norm(image_ref[...], raw_image_ref[...])


def shaped(shape, dtype):
    return jax.ShapeDtypeStruct(shape, dtype)


def call(kernel, outs, ins, specs, out_spec, scratch=(), grant=16, flops=1 << 20):
    return pl.pallas_call(
        kernel,
        out_shape=outs,
        in_specs=specs,
        out_specs=jax.tree.map(lambda _: out_spec, outs),
        scratch_shapes=list(scratch),
        compiler_params=pltpu.CompilerParams(vmem_limit_bytes=grant << 20),
        cost_estimate=pl.CostEstimate(flops=flops, bytes_accessed=1 << 20, transcendentals=0),
    )(*ins)


def make_body(squares, depth):
    plane = 2 * squares
    vmem = pl.BlockSpec(memory_space=pltpu.VMEM)
    smem = pl.BlockSpec(memory_space=pltpu.SMEM)

    def to_line(value, step):
        return lax.ppermute(value, LINE, [(z, z ^ step) for z in range(depth)])

    def to_square(value, step):
        return lax.ppermute(value, SQUARE, [(q, q ^ step) for q in range(squares)])

    def gather_line(value):
        blocks = {0: value}
        for s in sorted(range(1, depth), key=lambda s: bin(s).count("1")):
            near = s & -s
            blocks[s] = to_line(blocks[s ^ near], near)
        return [blocks[s] for s in range(depth)]

    def exchange(value, axes):
        return lax.all_to_all(value, axes, split_axis=0, concat_axis=0, tiled=True)

    def body(student_image, student_text, teacher_image, teacher_text, teacher_scale, student_scale):
        own, width = student_image.shape
        both = width + teacher_image.shape[1]
        images, texts = plane * own, depth * own
        core = lax.axis_index("core").astype(jnp.int32).reshape(1)
        square = lax.axis_index("y") * lax.axis_size("x") + lax.axis_index("x")
        square = square.astype(jnp.int32).reshape(1)
        z = lax.axis_index("z").astype(jnp.int32).reshape(1)
        teacher_scale = teacher_scale.reshape(1)
        student_scale = student_scale.reshape(1)
        grant = 16 if images * texts <= 512 * 256 else 56

        raw_text = jnp.concatenate([student_text, teacher_text], 1)
        raw_texts = gather_line(raw_text)
        raw_image = jnp.concatenate([student_image, teacher_image], 1)
        same = [raw_image] + [to_square(raw_image, s) for s in range(1, squares)]
        other = [lax.ppermute(block, "core", [(0, 1), (1, 0)]) for block in same]

        pupil_text, master_text = call(
            text_unit_kernel,
            (shaped((texts, width), BF16), shaped((texts, both - width), BF16)),
            (z, *raw_texts),
            [smem] + [vmem] * depth,
            vmem,
            grant=grant,
            flops=MANY,
        )
        pupil_image, master_image = call(
            image_unit_kernel,
            (shaped((images, width), BF16), shaped((images, both - width), BF16)),
            (core, square, *same, *other),
            [smem] * 2 + [vmem] * plane,
            vmem,
            grant=grant,
        )
        teach, row_lse, col_lse = call(
            logits_kernel,
            (shaped((images, texts), F32), shaped((plane, 2, images), F32), shaped((2, texts), F32)),
            (teacher_scale, student_scale, pupil_text, master_text, pupil_image, master_image),
            [smem, smem] + [vmem] * 4,
            vmem,
            grant=grant,
        )
        row_lse = call(
            join_kernel, shaped((8, images), F32), (exchange(row_lse, PLANE),), [vmem], vmem, flops=MANY
        )
        col_lses = [col_lse] + [to_line(col_lse, s) for s in range(1, depth)]
        image_parts, own_text_part, *text_parts = call(
            functools.partial(weight_kernel, depth),
            (shaped((plane, own, width), BF16), shaped((own, width), F32))
            + (shaped((own, width), BF16),) * (depth - 1),
            (z, student_scale, teach, pupil_image, pupil_text, row_lse, *col_lses),
            [smem] * 2 + [vmem] * (4 + depth),
            vmem,
            (pltpu.VMEM((texts, width), F32),),
            grant,
        )
        out = shaped((own, width), F32)
        image_grad = call(sum_kernel, out, (exchange(image_parts, PLANE),), [vmem], vmem, flops=MANY)
        text_parts = [own_text_part] + [to_line(part, s + 1) for s, part in enumerate(text_parts)]
        return call(
            back_kernel,
            (out, out),
            (image_grad, student_image, student_text, *text_parts),
            [vmem] * (3 + depth),
            vmem,
        )

    return body


def solution(mesh):
    named = physical_mesh(mesh)
    split = P(EVERY, None)
    return jax.shard_map(
        make_body(named.shape["y"] * named.shape["x"], named.shape["z"]),
        mesh=named,
        in_specs=(split, split, split, split, P(), P()),
        out_specs=(split, split),
        check_vma=False,
    )
```

time: 240 us -> 58.3 us (0.24)
  blocking collectives: 97.6 us -> 0 us
  waiting for transfers between devices: 110 us -> 19.4 us
  starting transfers between devices: 0.12 us -> 27.3 us
  between operations: 15.2 us -> 2.08 us
  other arithmetic: 12.5 us -> 0 us
  Pallas kernels: 0 us -> 5.53 us
  matrix products: 4.82 us -> 0 us
  local copies, waits for them, and re-layouts: 0.02 us -> 3.55 us
    psum x2 -> x0, waiting for transfers between devices: 110 us -> none  [the longest x1 78.8 us: body(): image_whole = lax.psum(image_partial, 'col')]
    all_gather x3 -> x0, blocking collectives: 47.8 us -> none  [the longest x1 32.7 us: body(): lax.all_gather(pupil_image, 'col', axis=0, tiled=True)]
    pmax x2 -> x0, blocking collectives: 27 us -> none  [the longest x1 20.9 us: body(): row_peaks = lax.pmax((row_local[0], row_local[2]), 'col')]
    psum x2 -> x0, blocking collectives: 22.8 us -> none  [the longest x1 17.1 us: body(): lax.psum((row_local[1] * jnp.exp(row_local[0] - row_peaks[0]), row_local[...]
    ppermute x0 -> x16, starting transfers between devices: none -> 19.3 us  [the longest x9 15.1 us: to_line(): return lax.ppermute(value, LINE, [(z, z ^ step) for z in range(depth)])]
    ppermute x0 -> x16, waiting for transfers between devices: none -> 14.1 us  [the longest x9 11.8 us: to_line(): return lax.ppermute(value, LINE, [(z, z ^ step) for z in range(depth)])]
    all_to_all x0 -> x2, starting transfers between devices: none -> 7.99 us  [exchange(): return lax.all_to_all(value, axes, split_axis=0, concat_axis=0, tiled=True)]
    reduce_sum x9 -> x0, other arithmetic: 5.95 us -> none  [the longest x4 3.14 us: unit_rows(): jnp.sum(values * values, axis=-1, keepdims=True) + EPSILON]
  transfers between devices with their start and end apart: 3 -> 18, of which waited for: 2 -> 6; matrix products, arithmetic and copies ran while one was open for 3% -> 3% of each run, Pallas kernels for 0% -> 1%
where the time goes in v1:
time: 58.3 us; the launch traced here: 57.9 us
  starting transfers between devices  27.3 us (47%)
  waiting for transfers between devices  19.4 us (33%)
  Pallas kernels  5.53 us (9%)
  local copies, waits for them, and re-layouts  3.55 us (6%)
  between operations  2.08 us (4%)
    ppermute x9, starting transfers between devices, to_line(): return lax.ppermute(value, LINE, [(z, z ^ step) for z in range(depth)])  15.1 us
    ppermute x9, waiting for transfers between devices, to_line(): return lax.ppermute(value, LINE, [(z, z ^ step) for z in range(depth)])  11.8 us
    all_to_all x2, starting transfers between devices, exchange(): return lax.all_to_all(value, axes, split_axis=0, concat_axis=0, tiled=True)  7.99 us
    pallas_call x7, Pallas kernels, call(): pl.pallas_call(kernel, out_shape=outs, in_specs=specs, out_specs=jax.tree...  5.53 us
    all_to_all x2, waiting for transfers between devices, exchange(): return lax.all_to_all(value, axes, split_axis=0, concat_axis=0, tiled=True)  5.28 us
    ppermute x3, starting transfers between devices, to_square(): return lax.ppermute(value, SQUARE, [(q, q ^ step) for q in range(squares)])  3.55 us
    ppermute x3, waiting for transfers between devices, to_square(): return lax.ppermute(value, SQUARE, [(q, q ^ step) for q in range(squares)])  2.36 us
    unnamed x6, local copies, waits for them, and re-layouts  1.7 us
  transfers between devices with their start and end apart: 18, of which 6 were waited for; matrix products, arithmetic and copies ran while one was open for 3% of the time, Pallas kernels for 1%

profile of v1, /device:TPU:0, one launch (start us, length us, event | category | flops | bytes accessed | tf_op | source)
XLA Modules:
  0.0 57.9 jit_solution(1809585911156794110)
XLA Ops:
  0.6 0.8 %constant_dynamic-update-slice_fusion.1 = bf16[64,1792]{1,0:T(8,128)(2,1)S(1)} fusion(bf16[64,512]{1,0:T(8,128)(2,1)} %raw_text_ref.1), kind=kLoop, calls=%fused_computation.1 | loop fusion | bytes 131072
  1.5 0.9 %constant_dynamic-update-slice_fusion.refs_0_ = bf16[64,1792]{1,0:T(8,128)(2,1)S(1)} fusion(bf16[64,1792]{1,0:T(8,128)(2,1)S(1)} %constant_dynamic-update-slice_fusion.1, bf16[64,1280]{1,0:T(8,128)(2,1)} %param.9), kind=kLoop, calls=%fused_computation | loop fusion | bytes 327680 | tf_op jit(solution)/shard_map/concatenate | solution.py:212
  2.4 4.1 %collective-permute-start.1 = (bf16[64,1792]{1,0:T(8,128)(2,1)S(1)}, bf16[64,1792]{1,0:T(8,128)(2,1)S(1)}, u32[]{:S(2)}, u32[]{:S(2)}) collective-permute-start(bf16[64,1792]{1,0:T(8,128)(2,1)S(1)} %constant_dynamic-update-slice_fusion.refs_0_), channel_id=1, source_target_pairs={{0,4},{2,6},{4,0},{6,2},{1,5},{3,7},{5,1},{7,3},{8,12},{10,14},{12... | collective-permute-start | bytes 688136 | tf_op jit(solution)/shard_map/ppermute | solution.py:185
  6.5 0.8 %constant_dynamic-update-slice_fusion.3 = bf16[64,1792]{1,0:T(8,128)(2,1)S(1)} fusion(bf16[64,512]{1,0:T(8,128)(2,1)} %raw_image_ref.1), kind=kLoop, calls=%fused_computation.3 | loop fusion | bytes 131072
  7.4 0.9 %constant_dynamic-update-slice_fusion.2.refs_0_ = bf16[64,1792]{1,0:T(8,128)(2,1)S(1)} fusion(bf16[64,1792]{1,0:T(8,128)(2,1)S(1)} %constant_dynamic-update-slice_fusion.3, bf16[64,1280]{1,0:T(8,128)(2,1)} %param.8), kind=kLoop, calls=%fused_computation.2 | loop fusion | bytes 327680 | tf_op jit(solution)/shard_map/concatenate | solution.py:214
  8.3 1.6 %collective-permute-start.3 = (bf16[64,1792]{1,0:T(8,128)(2,1)S(1)}, bf16[64,1792]{1,0:T(8,128)(2,1)S(1)}, u32[]{:S(2)}, u32[]{:S(2)}) collective-permute-start(bf16[64,1792]{1,0:T(8,128)(2,1)S(1)} %constant_dynamic-update-slice_fusion.2.refs_0_), channel_id=1, source_target_pairs={{0,1},{1,0},{16,17},{17,16},{2,3},{3,2},{18,19},{19,18},{4,5},{5,4... | collective-permute-start | bytes 688136 | tf_op jit(solution)/shard_map/ppermute | solution.py:188
  9.8 1.5 %collective-permute-start.4 = (bf16[64,1792]{1,0:T(8,128)(2,1)S(1)}, bf16[64,1792]{1,0:T(8,128)(2,1)S(1)}, u32[]{:S(2)}, u32[]{:S(2)}) collective-permute-start(bf16[64,1792]{1,0:T(8,128)(2,1)S(1)} %constant_dynamic-update-slice_fusion.2.refs_0_), channel_id=1, source_target_pairs={{0,16},{1,17},{16,0},{17,1},{2,18},{3,19},{18,2},{19,3},{4,20},{5,... | collective-permute-start | bytes 688136 | tf_op jit(solution)/shard_map/ppermute | solution.py:188
  11.8 1.6 %collective-permute-start = (bf16[64,1792]{1,0:T(8,128)(2,1)S(1)}, bf16[64,1792]{1,0:T(8,128)(2,1)S(1)}, u32[]{:S(2)}, u32[]{:S(2)}) collective-permute-start(bf16[64,1792]{1,0:T(8,128)(2,1)S(1)} %constant_dynamic-update-slice_fusion.refs_0_), channel_id=1, source_target_pairs={{0,2},{2,0},{4,6},{6,4},{1,3},{3,1},{5,7},{7,5},{8,10},{10,8},{12,... | collective-permute-start | bytes 688136 | tf_op jit(solution)/shard_map/ppermute | solution.py:185
  13.4 3.7 %collective-permute-done.1.refs_2_ = bf16[64,1792]{1,0:T(8,128)(2,1)S(1)} collective-permute-done((bf16[64,1792]{1,0:T(8,128)(2,1)S(1)}, bf16[64,1792]{1,0:T(8,128)(2,1)S(1)}, u32[]{:S(2)}, u32[]{:S(2)}) %collective-permute-start.1) | collective-permute-done | bytes 229408 | tf_op jit(solution)/shard_map/ppermute | solution.py:185
  17.1 0.7 %collective-permute-start.2 = (bf16[64,1792]{1,0:T(8,128)(2,1)S(1)}, bf16[64,1792]{1,0:T(8,128)(2,1)S(1)}, u32[]{:S(2)}, u32[]{:S(2)}) collective-permute-start(bf16[64,1792]{1,0:T(8,128)(2,1)S(1)} %collective-permute-done.1.refs_2_), channel_id=1, source_target_pairs={{0,2},{2,0},{4,6},{6,4},{1,3},{3,1},{5,7},{7,5},{8,10},{10,8},{12,... | collective-permute-start | bytes 688136 | tf_op jit(solution)/shard_map/ppermute | solution.py:185
  19.2 2.4 %collective-permute-done.4.refs_2_ = bf16[64,1792]{1,0:T(8,128)(2,1)S(1)} collective-permute-done((bf16[64,1792]{1,0:T(8,128)(2,1)S(1)}, bf16[64,1792]{1,0:T(8,128)(2,1)S(1)}, u32[]{:S(2)}, u32[]{:S(2)}) %collective-permute-start.4) | collective-permute-done | bytes 229408 | tf_op jit(solution)/shard_map/ppermute | solution.py:188
  22.1 4.6 %collective-permute-done.2.refs_3_ = bf16[64,1792]{1,0:T(8,128)(2,1)S(1)} collective-permute-done((bf16[64,1792]{1,0:T(8,128)(2,1)S(1)}, bf16[64,1792]{1,0:T(8,128)(2,1)S(1)}, u32[]{:S(2)}, u32[]{:S(2)}) %collective-permute-start.2) | collective-permute-done | bytes 229408 | tf_op jit(solution)/shard_map/ppermute | solution.py:185
  27.0 0.6 %shard_map.78 = (bf16[512,512]{1,0:T(8,128)(2,1)S(1)}, bf16[512,1280]{1,0:T(8,128)(2,1)S(1)}) custom-call(s32[1]{0:T(128)} %bitcast.3.core_ref, s32[1]{0:T(128)} %bitcast.4.square_ref, bf16[64,1792]{1,0:T(8,128)(2,1)S(1)} %constant_dynamic-update-slice_fusion.2.refs_0_, bf16[64,1792]{1,0:T(8,128)(2,1)S(1)} %collective-permute-done.3.refs_1_, ...), custom_call_target="tpu_custom_call" | custom-call | flops 1048576 | bytes 1048576 | tf_op jit(solution)/shard_map/pallas_call | solution.py:168
  27.6 2.0 %shard_map.79 = (f32[512,256]{1,0:T(8,128)S(1)}, f32[8,2,512]{2,1,0:T(2,128)}, f32[2,256]{1,0:T(2,128)S(1)}) custom-call(f32[1]{0:T(128)} %bitcast.5.teacher_scale_ref, f32[1]{0:T(128)} %bitcast.6.student_scale_ref, bf16[256,512]{1,0:T(8,128)(2,1)S(1)} %get-tuple-element.14.pupil_text_ref.text_ref, bf16[256,1280]{1,0:T(8,128)(2,1)S(1)} %get-tuple-element.15.master_text_ref, ...), custom_call_target="tpu_custom_call" | custom-call | flops 1048576 | bytes 1048576 | tf_op jit(solution)/shard_map/pallas_call | solution.py:168
  29.6 3.8 %all-to-all-start = ((f32[8,2,512]{2,1,0:T(2,128)}), f32[8,2,512]{2,1,0:T(2,128)S(1)}, u32[]{:S(2)}, u32[]{:S(2)}) async-start(f32[8,2,512]{2,1,0:T(2,128)} %get-tuple-element.19), calls=%async_computation | async-start | bytes 65536 | tf_op jit(solution)/shard_map/all_to_all | solution.py:198
  33.4 2.9 %collective-permute-start.11 = (f32[2,256]{1,0:T(2,128)S(1)}, f32[2,256]{1,0:T(2,128)S(1)}, u32[]{:S(2)}, u32[]{:S(2)}) collective-permute-start(f32[2,256]{1,0:T(2,128)S(1)} %get-tuple-element.20.refs_0_), channel_id=1, source_target_pairs={{0,4},{2,6},{4,0},{6,2},{1,5},{3,7},{5,1},{7,3},{8,12},{10,14},{12... | collective-permute-start | bytes 6152 | tf_op jit(solution)/shard_map/ppermute | solution.py:185
  36.3 1.4 %collective-permute-start.12 = (f32[2,256]{1,0:T(2,128)S(1)}, f32[2,256]{1,0:T(2,128)S(1)}, u32[]{:S(2)}, u32[]{:S(2)}) collective-permute-start(f32[2,256]{1,0:T(2,128)S(1)} %get-tuple-element.20.refs_0_), channel_id=1, source_target_pairs={{0,6},{2,4},{4,2},{6,0},{1,7},{3,5},{5,3},{7,1},{8,14},{10,12},{12... | collective-permute-start | bytes 6152 | tf_op jit(solution)/shard_map/ppermute | solution.py:185
  38.2 3.5 %collective-permute-done.12.refs_3_ = f32[2,256]{1,0:T(2,128)S(1)} collective-permute-done((f32[2,256]{1,0:T(2,128)S(1)}, f32[2,256]{1,0:T(2,128)S(1)}, u32[]{:S(2)}, u32[]{:S(2)}) %collective-permute-start.12) | collective-permute-done | bytes 2080 | tf_op jit(solution)/shard_map/ppermute | solution.py:185
  41.7 1.7 %shard_map.81 = (bf16[8,64,512]{2,1,0:T(8,128)(2,1)}, f32[64,512]{1,0:T(8,128)S(1)}, bf16[64,512]{1,0:T(8,128)(2,1)S(1)}, bf16[64,512]{1,0:T(8,128)(2,1)S(1)}, bf16[64,512]{1,0:T(8,128)(2,1)S(1)}) custom-call(s32[1]{0:T(128)} %bitcast.z_ref, f32[1]{0:T(128)} %bitcast.7.scale_ref, f32[512,256]{1,0:T(8,128)S(1)} %get-tuple-element.18.teach_ref, ...), custom_call_target="tpu_custom_call" | custom-call | flops 1048576 | bytes 1048576 | tf_op jit(solution)/shard_map/pallas_call | solution.py:168
  43.4 4.2 %all-to-all-start.1 = ((bf16[8,64,512]{2,1,0:T(8,128)(2,1)}), bf16[8,64,512]{2,1,0:T(8,128)(2,1)S(1)}, u32[]{:S(2)}, u32[]{:S(2)}) async-start(bf16[8,64,512]{2,1,0:T(8,128)(2,1)} %get-tuple-element.21), calls=%async_computation.1 | async-start | bytes 1048576 | tf_op jit(solution)/shard_map/all_to_all | solution.py:198
  47.6 2.0 %collective-permute-start.14 = (bf16[64,512]{1,0:T(8,128)(2,1)S(1)}, bf16[64,512]{1,0:T(8,128)(2,1)S(1)}, u32[]{:S(2)}, u32[]{:S(2)}) collective-permute-start(bf16[64,512]{1,0:T(8,128)(2,1)S(1)} %get-tuple-element.24), channel_id=1, source_target_pairs={{0,4},{2,6},{4,0},{6,2},{1,5},{3,7},{5,1},{7,3},{8,12},{10,14},{12... | collective-permute-start | bytes 196616 | tf_op jit(solution)/shard_map/ppermute | solution.py:185
  49.6 2.4 %collective-permute-start.15 = (bf16[64,512]{1,0:T(8,128)(2,1)S(1)}, bf16[64,512]{1,0:T(8,128)(2,1)S(1)}, u32[]{:S(2)}, u32[]{:S(2)}) collective-permute-start(bf16[64,512]{1,0:T(8,128)(2,1)S(1)} %get-tuple-element.25), channel_id=1, source_target_pairs={{0,6},{2,4},{4,2},{6,0},{1,7},{3,5},{5,3},{7,1},{8,14},{10,12},{12... | collective-permute-start | bytes 196616 | tf_op jit(solution)/shard_map/ppermute | solution.py:185
  52.0 4.9 %all-to-all-done.1.parts_ref = bf16[8,64,512]{2,1,0:T(8,128)(2,1)S(1)} async-done(((bf16[8,64,512]{2,1,0:T(8,128)(2,1)}), bf16[8,64,512]{2,1,0:T(8,128)(2,1)S(1)}, u32[]{:S(2)}, u32[]{:S(2)}) %all-to-all-start.1) | async-done | bytes 524320 | tf_op jit(solution)/shard_map/all_to_all | solution.py:198
  57.0 0.9 %shard_map.83 = (f32[64,512]{1,0:T(8,128)}, f32[64,512]{1,0:T(8,128)}) custom-call(f32[64,512]{1,0:T(8,128)S(1)} %shard_map.82.image_ref, bf16[64,512]{1,0:T(8,128)(2,1)S(1)} %copy-done.1, bf16[64,512]{1,0:T(8,128)(2,1)S(1)} %copy-done, f32[64,512]{1,0:T(8,128)S(1)} %get-tuple-element.22.refs_0_, bf16[64,512]{1,0:T(8,128)(2,1)S(1)} %collective-permute-done.13.refs_1_, ...), custom_call_target="tpu_custom_call" | custom-call | flops 1048576 | bytes 1048576 | tf_op jit(solution)/shard_map/pallas_call | solution.py:168
  (27 shorter events, 2.0 us)
Async XLA Ops:
  2.4 14.7 %collective-permute-start.1 = (bf16[64,1792]{1,0:T(8,128)(2,1)S(1)}, bf16[64,1792]{1,0:T(8,128)(2,1)S(1)}, u32[]{:S(2)}, u32[]{:S(2)}) collective-permute-start(bf16[64,1792]{1,0:T(8,128)(2,1)S(1)} %constant_dynamic-update-slice_fusion.refs_0_), channel_id=1, source_target_pairs={{0,4},{2,6},{4,0},{6,2},{1,5},{3,7},{5,1},{7,3},{8,12},{10,14},{12... | collective-permute-start | bytes 688136 | tf_op jit(solution)/shard_map/ppermute | solution.py:185
  8.3 10.8 %collective-permute-start.3 = (bf16[64,1792]{1,0:T(8,128)(2,1)S(1)}, bf16[64,1792]{1,0:T(8,128)(2,1)S(1)}, u32[]{:S(2)}, u32[]{:S(2)}) collective-permute-start(bf16[64,1792]{1,0:T(8,128)(2,1)S(1)} %constant_dynamic-update-slice_fusion.2.refs_0_), channel_id=1, source_target_pairs={{0,1},{1,0},{16,17},{17,16},{2,3},{3,2},{18,19},{19,18},{4,5},{5,4... | collective-permute-start | bytes 688136 | tf_op jit(solution)/shard_map/ppermute | solution.py:188
  9.8 11.7 %collective-permute-start.4 = (bf16[64,1792]{1,0:T(8,128)(2,1)S(1)}, bf16[64,1792]{1,0:T(8,128)(2,1)S(1)}, u32[]{:S(2)}, u32[]{:S(2)}) collective-permute-start(bf16[64,1792]{1,0:T(8,128)(2,1)S(1)} %constant_dynamic-update-slice_fusion.2.refs_0_), channel_id=1, source_target_pairs={{0,16},{1,17},{16,0},{17,1},{2,18},{3,19},{18,2},{19,3},{4,20},{5,... | collective-permute-start | bytes 688136 | tf_op jit(solution)/shard_map/ppermute | solution.py:188
  11.4 10.2 %collective-permute-start.5 = (bf16[64,1792]{1,0:T(8,128)(2,1)S(1)}, bf16[64,1792]{1,0:T(8,128)(2,1)S(1)}, u32[]{:S(2)}, u32[]{:S(2)}) collective-permute-start(bf16[64,1792]{1,0:T(8,128)(2,1)S(1)} %constant_dynamic-update-slice_fusion.2.refs_0_), channel_id=1, source_target_pairs={{0,17},{1,16},{16,1},{17,0},{2,19},{3,18},{18,3},{19,2},{4,21},{5,... | collective-permute-start | bytes 688136 | tf_op jit(solution)/shard_map/ppermute | solution.py:188
  11.8 10.2 %collective-permute-start = (bf16[64,1792]{1,0:T(8,128)(2,1)S(1)}, bf16[64,1792]{1,0:T(8,128)(2,1)S(1)}, u32[]{:S(2)}, u32[]{:S(2)}) collective-permute-start(bf16[64,1792]{1,0:T(8,128)(2,1)S(1)} %constant_dynamic-update-slice_fusion.refs_0_), channel_id=1, source_target_pairs={{0,2},{2,0},{4,6},{6,4},{1,3},{3,1},{5,7},{7,5},{8,10},{10,8},{12,... | collective-permute-start | bytes 688136 | tf_op jit(solution)/shard_map/ppermute | solution.py:185
  17.1 9.6 %collective-permute-start.2 = (bf16[64,1792]{1,0:T(8,128)(2,1)S(1)}, bf16[64,1792]{1,0:T(8,128)(2,1)S(1)}, u32[]{:S(2)}, u32[]{:S(2)}) collective-permute-start(bf16[64,1792]{1,0:T(8,128)(2,1)S(1)} %collective-permute-done.1.refs_2_), channel_id=1, source_target_pairs={{0,2},{2,0},{4,6},{6,4},{1,3},{3,1},{5,7},{7,5},{8,10},{10,8},{12,... | collective-permute-start | bytes 688136 | tf_op jit(solution)/shard_map/ppermute | solution.py:185
  19.1 7.9 %collective-permute-start.6 = (bf16[64,1792]{1,0:T(8,128)(2,1)S(1)}, bf16[64,1792]{1,0:T(8,128)(2,1)S(1)}, u32[]{:S(2)}, u32[]{:S(2)}) collective-permute-start(bf16[64,1792]{1,0:T(8,128)(2,1)S(1)} %constant_dynamic-update-slice_fusion.2.refs_0_), channel_id=1, source_target_pairs={{0,8},{8,0},{1,9},{9,1},{2,10},{10,2},{3,11},{11,3},{4,12},{12,4},... | collective-permute-start | bytes 688136 | tf_op jit(solution)/shard_map/ppermute | solution.py:216
  21.5 5.4 %collective-permute-start.7 = (bf16[64,1792]{1,0:T(8,128)(2,1)S(1)}, bf16[64,1792]{1,0:T(8,128)(2,1)S(1)}, u32[]{:S(2)}, u32[]{:S(2)}) collective-permute-start(bf16[64,1792]{1,0:T(8,128)(2,1)S(1)} %collective-permute-done.3.refs_1_), channel_id=1, source_target_pairs={{0,8},{8,0},{1,9},{9,1},{2,10},{10,2},{3,11},{11,3},{4,12},{12,4},... | collective-permute-start | bytes 688136 | tf_op jit(solution)/shard_map/ppermute | solution.py:216
  21.5 5.5 %collective-permute-start.8 = (bf16[64,1792]{1,0:T(8,128)(2,1)S(1)}, bf16[64,1792]{1,0:T(8,128)(2,1)S(1)}, u32[]{:S(2)}, u32[]{:S(2)}) collective-permute-start(bf16[64,1792]{1,0:T(8,128)(2,1)S(1)} %collective-permute-done.4.refs_2_), channel_id=1, source_target_pairs={{0,8},{8,0},{1,9},{9,1},{2,10},{10,2},{3,11},{11,3},{4,12},{12,4},... | collective-permute-start | bytes 688136 | tf_op jit(solution)/shard_map/ppermute | solution.py:216
  22.1 5.0 %collective-permute-start.9 = (bf16[64,1792]{1,0:T(8,128)(2,1)S(1)}, bf16[64,1792]{1,0:T(8,128)(2,1)S(1)}, u32[]{:S(2)}, u32[]{:S(2)}) collective-permute-start(bf16[64,1792]{1,0:T(8,128)(2,1)S(1)} %collective-permute-done.5.refs_3_), channel_id=1, source_target_pairs={{0,8},{8,0},{1,9},{9,1},{2,10},{10,2},{3,11},{11,3},{4,12},{12,4},... | collective-permute-start | bytes 688136 | tf_op jit(solution)/shard_map/ppermute | solution.py:216
  29.6 8.6 %all-to-all-start = ((f32[8,2,512]{2,1,0:T(2,128)}), f32[8,2,512]{2,1,0:T(2,128)S(1)}, u32[]{:S(2)}, u32[]{:S(2)}) async-start(f32[8,2,512]{2,1,0:T(2,128)} %get-tuple-element.19), calls=%async_computation | async-start | bytes 65536 | tf_op jit(solution)/shard_map/all_to_all | solution.py:198
  33.4 4.8 %collective-permute-start.10 = (f32[2,256]{1,0:T(2,128)S(1)}, f32[2,256]{1,0:T(2,128)S(1)}, u32[]{:S(2)}, u32[]{:S(2)}) collective-permute-start(f32[2,256]{1,0:T(2,128)S(1)} %get-tuple-element.20.refs_0_), channel_id=1, source_target_pairs={{0,2},{2,0},{4,6},{6,4},{1,3},{3,1},{5,7},{7,5},{8,10},{10,8},{12,... | collective-permute-start | bytes 6152 | tf_op jit(solution)/shard_map/ppermute | solution.py:185
  33.4 4.8 %collective-permute-start.11 = (f32[2,256]{1,0:T(2,128)S(1)}, f32[2,256]{1,0:T(2,128)S(1)}, u32[]{:S(2)}, u32[]{:S(2)}) collective-permute-start(f32[2,256]{1,0:T(2,128)S(1)} %get-tuple-element.20.refs_0_), channel_id=1, source_target_pairs={{0,4},{2,6},{4,0},{6,2},{1,5},{3,7},{5,1},{7,3},{8,12},{10,14},{12... | collective-permute-start | bytes 6152 | tf_op jit(solution)/shard_map/ppermute | solution.py:185
  36.3 5.4 %collective-permute-start.12 = (f32[2,256]{1,0:T(2,128)S(1)}, f32[2,256]{1,0:T(2,128)S(1)}, u32[]{:S(2)}, u32[]{:S(2)}) collective-permute-start(f32[2,256]{1,0:T(2,128)S(1)} %get-tuple-element.20.refs_0_), channel_id=1, source_target_pairs={{0,6},{2,4},{4,2},{6,0},{1,7},{3,5},{5,3},{7,1},{8,14},{10,12},{12... | collective-permute-start | bytes 6152 | tf_op jit(solution)/shard_map/ppermute | solution.py:185
  43.4 13.5 %all-to-all-start.1 = ((bf16[8,64,512]{2,1,0:T(8,128)(2,1)}), bf16[8,64,512]{2,1,0:T(8,128)(2,1)S(1)}, u32[]{:S(2)}, u32[]{:S(2)}) async-start(bf16[8,64,512]{2,1,0:T(8,128)(2,1)} %get-tuple-element.21), calls=%async_computation.1 | async-start | bytes 1048576 | tf_op jit(solution)/shard_map/all_to_all | solution.py:198
  47.6 9.3 %collective-permute-start.13 = (bf16[64,512]{1,0:T(8,128)(2,1)S(1)}, bf16[64,512]{1,0:T(8,128)(2,1)S(1)}, u32[]{:S(2)}, u32[]{:S(2)}) collective-permute-start(bf16[64,512]{1,0:T(8,128)(2,1)S(1)} %get-tuple-element.23), channel_id=1, source_target_pairs={{0,2},{2,0},{4,6},{6,4},{1,3},{3,1},{5,7},{7,5},{8,10},{10,8},{12,... | collective-permute-start | bytes 196616 | tf_op jit(solution)/shard_map/ppermute | solution.py:185
  47.6 9.3 %collective-permute-start.14 = (bf16[64,512]{1,0:T(8,128)(2,1)S(1)}, bf16[64,512]{1,0:T(8,128)(2,1)S(1)}, u32[]{:S(2)}, u32[]{:S(2)}) collective-permute-start(bf16[64,512]{1,0:T(8,128)(2,1)S(1)} %get-tuple-element.24), channel_id=1, source_target_pairs={{0,4},{2,6},{4,0},{6,2},{1,5},{3,7},{5,1},{7,3},{8,12},{10,14},{12... | collective-permute-start | bytes 196616 | tf_op jit(solution)/shard_map/ppermute | solution.py:185
  49.6 7.4 %copy-start = (bf16[64,512]{1,0:T(8,128)(2,1)S(1)}, bf16[64,512]{1,0:T(8,128)(2,1)}, u32[]{:S(2)}) copy-start(bf16[64,512]{1,0:T(8,128)(2,1)} %raw_text_ref.1) | copy-start | bytes 196612
  49.6 7.4 %copy-start.1 = (bf16[64,512]{1,0:T(8,128)(2,1)S(1)}, bf16[64,512]{1,0:T(8,128)(2,1)}, u32[]{:S(2)}) copy-start(bf16[64,512]{1,0:T(8,128)(2,1)} %raw_image_ref.1) | copy-start | bytes 196612
  49.6 7.4 %collective-permute-start.15 = (bf16[64,512]{1,0:T(8,128)(2,1)S(1)}, bf16[64,512]{1,0:T(8,128)(2,1)S(1)}, u32[]{:S(2)}, u32[]{:S(2)}) collective-permute-start(bf16[64,512]{1,0:T(8,128)(2,1)S(1)} %get-tuple-element.25), channel_id=1, source_target_pairs={{0,6},{2,4},{4,2},{6,0},{1,7},{3,5},{5,3},{7,1},{8,14},{10,12},{12... | collective-permute-start | bytes 196616 | tf_op jit(solution)/shard_map/ppermute | solution.py:185

commit v2 on v1

--- a/solution.py
+++ b/solution.py
@@ -9,7 +9,6 @@
 
 EPSILON = 1e-12
 SQUARE = ("y", "x")
-PLANE = ("core", "y", "x")
 LINE = "z"
 EVERY = ("y", "core", "z", "x")
 F32 = jnp.float32
@@ -28,6 +27,15 @@
     values = raw.astype(F32)
     inverse = lax.rsqrt(jnp.sum(values * values, axis=-1, keepdims=True) + EPSILON)
     return (values * inverse, inverse)
+
+
+def side_by_side(left, right):
+    lowest = jnp.array(-jnp.inf, left.dtype)
+    left_width, right_width = left.shape[1], right.shape[1]
+    return jnp.maximum(
+        lax.pad(left, lowest, ((0, 0, 0), (0, right_width, 0))),
+        lax.pad(right, lowest, ((0, 0, 0), (left_width, 0, 0))),
+    )
 
 
 def put_units(block, pupil_ref, master_ref, at):
@@ -92,51 +100,51 @@
             if k == 0:
                 teach_ref[at : at + step, :] = logits
             columns.append(block_lse(logits))
-            row = block_lse(scale * product(text, image))
-            for i in range(rows_ref.shape[0]):
-                rows_ref[i, k : k + 1, at : at + step] = row
+            rows_ref[k : k + 1, at : at + step] = block_lse(scale * product(text, image))
         cols_ref[k : k + 1, :] = join_lse(columns)
 
 
-def join_kernel(rows_ref, out_ref):
-    joined = join_lse([rows_ref[i] for i in range(rows_ref.shape[0])])
-    for k in range(0, 8, 2):
-        out_ref[k : k + 2, :] = joined
-
-
-def weight_kernel(depth, z_ref, scale_ref, teach_ref, image_ref, text_ref, rows_ref, *refs):
-    col_refs = refs[:depth]
-    image_out_ref, own_text_ref = refs[depth : depth + 2]
-    text_out_refs = refs[depth + 2 : -1]
-    text_part_ref = refs[-1]
-    plane, own, _ = image_out_ref.shape
-    z = z_ref[0]
+def join_kernel(*refs):
+    refs[-1][...] = join_lse([ref[...] for ref in refs[:-1]])
+
+
+def weight_kernel(core_ref, z_ref, scale_ref, teach_ref, image_ref, text_ref, *refs):
+    col_ref, row_refs = refs[0], refs[1:3]
+    keep_ref, send_ref, own_text_ref = refs[3:6]
+    text_out_refs = refs[6:-2]
+    image_part_ref, text_part_ref = refs[-2:]
+    squares, own, _ = keep_ref.shape
     scale = scale_ref[0]
-    images = plane * own
+    images = 2 * squares * own
     step = min(512, images)
-    col = join_lse([ref[...] for ref in col_refs])
+    col = col_ref[...]
+    rows = join_lse([ref[...] for ref in row_refs])
+    rows = jnp.concatenate([rows] * 4, axis=0)
     text = text_ref[...]
     for at in range(0, images, step):
-        row = jnp.transpose(rows_ref[:, at : at + step])
+        row = jnp.transpose(rows[:, at : at + step])
         image = image_ref[at : at + step, :]
         teach = teach_ref[at : at + step, :]
         learn = scale * product(image, text)
         rows_part = jnp.exp(learn - row[:, 1:2]) - jnp.exp(teach - row[:, 0:1])
         cols_part = jnp.exp(learn - col[1:2, :]) - jnp.exp(teach - col[0:1, :])
         weight = (0.5 * (rows_part + cols_part)).astype(BF16)
-        image_part = scale * jnp.dot(weight, text, preferred_element_type=F32)
-        for i in range(step // own):
-            image_out_ref[at // own + i] = image_part[i * own : (i + 1) * own].astype(BF16)
+        image_part_ref[at : at + step, :] = scale * jnp.dot(weight, text, preferred_element_type=F32)
         text_part = scale * lax.dot_general(
             weight, image, (((0,), (0,)), ((), ())), preferred_element_type=F32
         )
         if at:
             text_part = text_part_ref[...] + text_part
         text_part_ref[...] = text_part
+    core, z = core_ref[0], z_ref[0]
+    for i in range(squares):
+        for out_ref, half in ((keep_ref, core), (send_ref, 1 - core)):
+            row = pl.multiple_of((half * squares + i) * own, own)
+            out_ref[i] = image_part_ref[pl.ds(row, own), :].astype(out_ref.dtype)
     own_text_ref[...] = text_part_ref[pl.ds(pl.multiple_of(z * own, own), own), :]
-    for s in range(1, depth):
-        at = pl.multiple_of(jnp.bitwise_xor(z, s) * own, own)
-        text_out_refs[s - 1][...] = text_part_ref[pl.ds(at, own), :].astype(BF16)
+    for s, ref in enumerate(text_out_refs):
+        row = pl.multiple_of(jnp.bitwise_xor(z, s + 1) * own, own)
+        ref[...] = text_part_ref[pl.ds(row, own), :].astype(BF16)
 
 
 def back_norm(grad, raw):
@@ -144,20 +152,27 @@
     return inverse * (grad - unit * jnp.sum(unit * grad, axis=-1, keepdims=True))
 
 
-def sum_kernel(parts_ref, out_ref):
-    grad = parts_ref[0].astype(F32)
-    for i in range(1, parts_ref.shape[0]):
-        grad = grad + parts_ref[i].astype(F32)
-    out_ref[...] = grad
-
-
-def back_kernel(image_ref, raw_image_ref, raw_text_ref, *refs):
+def pair_kernel(square_ref, kept_ref, received_ref, *refs):
+    for s, ref in enumerate(refs):
+        at = jnp.bitwise_xor(square_ref[0], s)
+        ref[...] = (kept_ref[at] + received_ref[at].astype(F32)).astype(ref.dtype)
+
+
+def total_of(refs):
+    total = refs[0][...]
+    for ref in refs[1:]:
+        total = total + ref[...].astype(F32)
+    return total
+
+
+def sum_kernel(*refs):
+    refs[-1][...] = total_of(refs[:-1])
+
+
+def back_kernel(raw_image_ref, raw_text_ref, text_ref, *refs):
     image_out_ref, text_out_ref = refs[-2:]
-    grad = refs[0][...]
-    for ref in refs[1:-2]:
-        grad = grad + ref[...].astype(F32)
-    text_out_ref[...] = back_norm(grad, raw_text_ref[...])
-    image_out_ref[...] = back_norm(image_ref[...], raw_image_ref[...])
+    text_out_ref[...] = back_norm(text_ref[...], raw_text_ref[...])
+    image_out_ref[...] = back_norm(total_of(refs[:-2]), raw_image_ref[...])
 
 
 def shaped(shape, dtype):
@@ -176,6 +191,10 @@
     )(*ins)
 
 
+def bits(count):
+    return [1 << i for i in reversed(range((count - 1).bit_length()))]
+
+
 def make_body(squares, depth):
     plane = 2 * squares
     vmem = pl.BlockSpec(memory_space=pltpu.VMEM)
@@ -188,14 +207,16 @@
         return lax.ppermute(value, SQUARE, [(q, q ^ step) for q in range(squares)])
 
     def gather_line(value):
-        blocks = {0: value}
-        for s in sorted(range(1, depth), key=lambda s: bin(s).count("1")):
+        first = bits(depth)
+        held = lax.optimization_barrier([value] + [to_line(value, s) for s in first])
+        blocks = dict(zip([0] + first, held))
+        for s in sorted(set(range(depth)) - set(blocks), key=lambda s: bin(s).count("1")):
             near = s & -s
             blocks[s] = to_line(blocks[s ^ near], near)
         return [blocks[s] for s in range(depth)]
 
-    def exchange(value, axes):
-        return lax.all_to_all(value, axes, split_axis=0, concat_axis=0, tiled=True)
+    def to_sibling(value):
+        return lax.ppermute(value, "core", [(0, 1), (1, 0)])
 
     def body(student_image, student_text, teacher_image, teacher_text, teacher_scale, student_scale):
         own, width = student_image.shape
@@ -209,11 +230,11 @@
         student_scale = student_scale.reshape(1)
         grant = 16 if images * texts <= 512 * 256 else 56
 
-        raw_text = jnp.concatenate([student_text, teacher_text], 1)
+        raw_text = side_by_side(student_text, teacher_text)
         raw_texts = gather_line(raw_text)
-        raw_image = jnp.concatenate([student_image, teacher_image], 1)
+        raw_image = side_by_side(student_image, teacher_image)
         same = [raw_image] + [to_square(raw_image, s) for s in range(1, squares)]
-        other = [lax.ppermute(block, "core", [(0, 1), (1, 0)]) for block in same]
+        other = [to_sibling(block) for block in same]
 
         pupil_text, master_text = call(
             text_unit_kernel,
@@ -234,34 +255,49 @@
         )
         teach, row_lse, col_lse = call(
             logits_kernel,
-            (shaped((images, texts), F32), shaped((plane, 2, images), F32), shaped((2, texts), F32)),
+            (shaped((images, texts), F32), shaped((2, images), F32), shaped((2, texts), F32)),
             (teacher_scale, student_scale, pupil_text, master_text, pupil_image, master_image),
             [smem, smem] + [vmem] * 4,
             vmem,
             grant=grant,
         )
-        row_lse = call(
-            join_kernel, shaped((8, images), F32), (exchange(row_lse, PLANE),), [vmem], vmem, flops=MANY
-        )
-        col_lses = [col_lse] + [to_line(col_lse, s) for s in range(1, depth)]
-        image_parts, own_text_part, *text_parts = call(
-            functools.partial(weight_kernel, depth),
-            (shaped((plane, own, width), BF16), shaped((own, width), F32))
-            + (shaped((own, width), BF16),) * (depth - 1),
-            (z, student_scale, teach, pupil_image, pupil_text, row_lse, *col_lses),
-            [smem] * 2 + [vmem] * (4 + depth),
-            vmem,
-            (pltpu.VMEM((texts, width), F32),),
+        def joined(parts, flops):
+            out = shaped(parts[0].shape, F32)
+            return call(join_kernel, out, parts, [vmem] * 2, vmem, flops=flops)
+
+        row_lses = [row_lse, to_sibling(row_lse)]
+        for s in reversed(bits(squares)):
+            row_lse = joined(row_lses, 1 << 10)
+            row_lses = [row_lse, to_square(row_lse, s)]
+        for s in bits(depth):
+            col_lse = joined([col_lse, to_line(col_lse, s)], MANY if s == 1 else 1 << 31)
+        block = shaped((own, width), F32)
+        sent = shaped((own, width), BF16)
+        kept, for_sibling, own_text, *for_line = call(
+            weight_kernel,
+            (shaped((squares, own, width), F32), shaped((squares, own, width), BF16), block)
+            + (sent,) * (depth - 1),
+            (core, z, student_scale, teach, pupil_image, pupil_text, col_lse, *row_lses),
+            [smem] * 3 + [vmem] * 6,
+            vmem,
+            (pltpu.VMEM((images, width), F32), pltpu.VMEM((texts, width), F32)),
             grant,
         )
-        out = shaped((own, width), F32)
-        image_grad = call(sum_kernel, out, (exchange(image_parts, PLANE),), [vmem], vmem, flops=MANY)
-        text_parts = [own_text_part] + [to_line(part, s + 1) for s, part in enumerate(text_parts)]
+        text_parts = [own_text] + [to_line(part, s + 1) for s, part in enumerate(for_line)]
+        text_grad = call(sum_kernel, block, text_parts, [vmem] * depth, vmem, flops=MANY)
+        own_image, *for_square = call(
+            pair_kernel,
+            (block,) + (sent,) * (squares - 1),
+            (square, kept, to_sibling(for_sibling)),
+            [smem] + [vmem] * 2,
+            vmem,
+        )
+        image_parts = [own_image] + [to_square(part, s + 1) for s, part in enumerate(for_square)]
         return call(
             back_kernel,
-            (out, out),
-            (image_grad, student_image, student_text, *text_parts),
-            [vmem] * (3 + depth),
+            (block, block),
+            (student_image, student_text, text_grad, *image_parts),
+            [vmem] * (3 + squares),
             vmem,
         )
 

time: 58.3 us -> 50.9 us (0.87)
  waiting for transfers between devices: 19.4 us -> 14.4 us
  local copies, waits for them, and re-layouts: 3.55 us -> 0.01 us
  other arithmetic: 0 us -> 1.87 us
  Pallas kernels: 5.53 us -> 4.34 us
  starting transfers between devices: 27.3 us -> 28 us
    all_to_all x2 -> x0, starting transfers between devices: 7.99 us -> none  [exchange(): return lax.all_to_all(value, axes, split_axis=0, concat_axis=0, tiled=True)]
    ppermute x3 -> x8, starting transfers between devices: 3.55 us -> 10.3 us  [to_square(): return lax.ppermute(value, SQUARE, [(q, q ^ step) for q in range(squares)])]
    all_to_all x2 -> x0, waiting for transfers between devices: 5.28 us -> none  [exchange(): return lax.all_to_all(value, axes, split_axis=0, concat_axis=0, tiled=True)]
    ppermute x3 -> x8, waiting for transfers between devices: 2.36 us -> 6.14 us  [to_square(): return lax.ppermute(value, SQUARE, [(q, q ^ step) for q in range(squares)])]
    ppermute x9 -> x8, waiting for transfers between devices: 11.8 us -> 8.26 us  [to_line(): return lax.ppermute(value, LINE, [(z, z ^ step) for z in range(depth)])]
    max x0 -> x2, other arithmetic: none -> 1.87 us  [side_by_side(): jnp.maximum(lax.pad(left, lowest, ((0, 0, 0), (0, right_width, 0))), lax....]
    concatenate x2 -> x0, local copies, waits for them, and re-layouts: 1.85 us -> none  [the longest x1 0.93 us: body(): raw_text = jnp.concatenate([student_text, teacher_text], 1)]
    unnamed x6 -> x4, local copies, waits for them, and re-layouts: 1.7 us -> 0.01 us
  transfers between devices with their start and end apart: 18 -> 22, of which waited for: 6 -> 9; matrix products, arithmetic and copies ran while one was open for 3% -> 2% of each run, Pallas kernels for 1% -> 1%
where the time goes in v2:
time: 50.9 us; the launch traced here: 50.7 us
  starting transfers between devices  28 us (55%)
  waiting for transfers between devices  14.4 us (28%)
  Pallas kernels  4.34 us (9%)
  between operations  2.05 us (4%)
  other arithmetic  1.87 us (4%)
    ppermute x8, starting transfers between devices, to_line(): return lax.ppermute(value, LINE, [(z, z ^ step) for z in range(depth)])  16.5 us
    ppermute x8, starting transfers between devices, to_square(): return lax.ppermute(value, SQUARE, [(q, q ^ step) for q in range(squares)])  10.3 us
    ppermute x8, waiting for transfers between devices, to_line(): return lax.ppermute(value, LINE, [(z, z ^ step) for z in range(depth)])  8.26 us
    ppermute x8, waiting for transfers between devices, to_square(): return lax.ppermute(value, SQUARE, [(q, q ^ step) for q in range(squares)])  6.14 us
    pallas_call x11, Pallas kernels, call(): pl.pallas_call(kernel, out_shape=outs, in_specs=specs, out_specs=jax.tree...  4.34 us
    max x2, other arithmetic, side_by_side(): jnp.maximum(lax.pad(left, lowest, ((0, 0, 0), (0, right_width, 0))), lax....  1.87 us
    ppermute x6, starting transfers between devices, to_sibling(): return lax.ppermute(value, 'core', [(0, 1), (1, 0)])  1.23 us
  transfers between devices with their start and end apart: 22, of which 9 were waited for; matrix products, arithmetic and copies ran while one was open for 2% of the time, Pallas kernels for 1%

profile of v2, /device:TPU:0, one launch (start us, length us, event | category | flops | bytes accessed | tf_op | source)
XLA Modules:
  0.0 50.7 jit_solution(15261980058887468738)
XLA Ops:
  0.6 0.9 %pad_maximum_fusion.1.refs_0_ = bf16[64,1792]{1,0:T(8,128)(2,1)S(1)} fusion(bf16[64,1280]{1,0:T(8,128)(2,1)} %param.9, bf16[64,512]{1,0:T(8,128)(2,1)} %raw_text_ref.1), kind=kLoop, calls=%fused_computation.1 | loop fusion | flops 458752 | bytes 458752 | tf_op jit(solution)/shard_map/max | solution.py:35
  1.6 4.1 %collective-permute-start = (bf16[64,1792]{1,0:T(8,128)(2,1)S(1)}, bf16[64,1792]{1,0:T(8,128)(2,1)S(1)}, u32[]{:S(2)}, u32[]{:S(2)}) collective-permute-start(bf16[64,1792]{1,0:T(8,128)(2,1)S(1)} %pad_maximum_fusion.1.refs_0_), channel_id=1, source_target_pairs={{0,4},{2,6},{4,0},{6,2},{1,5},{3,7},{5,1},{7,3},{8,12},{10,14},{12... | collective-permute-start | bytes 688136 | tf_op jit(solution)/shard_map/ppermute | solution.py:204
  5.7 1.6 %collective-permute-start.1 = (bf16[64,1792]{1,0:T(8,128)(2,1)S(1)}, bf16[64,1792]{1,0:T(8,128)(2,1)S(1)}, u32[]{:S(2)}, u32[]{:S(2)}) collective-permute-start(bf16[64,1792]{1,0:T(8,128)(2,1)S(1)} %pad_maximum_fusion.1.refs_0_), channel_id=1, source_target_pairs={{0,2},{2,0},{4,6},{6,4},{1,3},{3,1},{5,7},{7,5},{8,10},{10,8},{12,... | collective-permute-start | bytes 688136 | tf_op jit(solution)/shard_map/ppermute | solution.py:204
  7.2 0.9 %pad_maximum_fusion.refs_0_ = bf16[64,1792]{1,0:T(8,128)(2,1)S(1)} fusion(bf16[64,1280]{1,0:T(8,128)(2,1)} %param.8, bf16[64,512]{1,0:T(8,128)(2,1)} %raw_image_ref.1), kind=kLoop, calls=%fused_computation | loop fusion | flops 458752 | bytes 458752 | tf_op jit(solution)/shard_map/max | solution.py:35
  8.2 1.6 %collective-permute-start.3 = (bf16[64,1792]{1,0:T(8,128)(2,1)S(1)}, bf16[64,1792]{1,0:T(8,128)(2,1)S(1)}, u32[]{:S(2)}, u32[]{:S(2)}) collective-permute-start(bf16[64,1792]{1,0:T(8,128)(2,1)S(1)} %pad_maximum_fusion.refs_0_), channel_id=1, source_target_pairs={{0,1},{1,0},{16,17},{17,16},{2,3},{3,2},{18,19},{19,18},{4,5},{5,4... | collective-permute-start | bytes 688136 | tf_op jit(solution)/shard_map/ppermute | solution.py:207
  9.7 1.5 %collective-permute-start.4 = (bf16[64,1792]{1,0:T(8,128)(2,1)S(1)}, bf16[64,1792]{1,0:T(8,128)(2,1)S(1)}, u32[]{:S(2)}, u32[]{:S(2)}) collective-permute-start(bf16[64,1792]{1,0:T(8,128)(2,1)S(1)} %pad_maximum_fusion.refs_0_), channel_id=1, source_target_pairs={{0,16},{1,17},{16,0},{17,1},{2,18},{3,19},{18,2},{19,3},{4,20},{5,... | collective-permute-start | bytes 688136 | tf_op jit(solution)/shard_map/ppermute | solution.py:207
  11.7 4.6 %collective-permute-done.refs_2_ = bf16[64,1792]{1,0:T(8,128)(2,1)S(1)} collective-permute-done((bf16[64,1792]{1,0:T(8,128)(2,1)S(1)}, bf16[64,1792]{1,0:T(8,128)(2,1)S(1)}, u32[]{:S(2)}, u32[]{:S(2)}) %collective-permute-start) | collective-permute-done | bytes 229408 | tf_op jit(solution)/shard_map/ppermute | solution.py:204
  16.5 1.5 %collective-permute-start.2 = (bf16[64,1792]{1,0:T(8,128)(2,1)S(1)}, bf16[64,1792]{1,0:T(8,128)(2,1)S(1)}, u32[]{:S(2)}, u32[]{:S(2)}) collective-permute-start(bf16[64,1792]{1,0:T(8,128)(2,1)S(1)} %collective-permute-done.refs_2_), channel_id=1, source_target_pairs={{0,2},{2,0},{4,6},{6,4},{1,3},{3,1},{5,7},{7,5},{8,10},{10,8},{12,... | collective-permute-start | bytes 688136 | tf_op jit(solution)/shard_map/ppermute | solution.py:204
  19.9 1.3 %collective-permute-done.4.refs_2_ = bf16[64,1792]{1,0:T(8,128)(2,1)S(1)} collective-permute-done((bf16[64,1792]{1,0:T(8,128)(2,1)S(1)}, bf16[64,1792]{1,0:T(8,128)(2,1)S(1)}, u32[]{:S(2)}, u32[]{:S(2)}) %collective-permute-start.4) | collective-permute-done | bytes 229408 | tf_op jit(solution)/shard_map/ppermute | solution.py:207
  21.7 1.4 %collective-permute-done.2.refs_3_ = bf16[64,1792]{1,0:T(8,128)(2,1)S(1)} collective-permute-done((bf16[64,1792]{1,0:T(8,128)(2,1)S(1)}, bf16[64,1792]{1,0:T(8,128)(2,1)S(1)}, u32[]{:S(2)}, u32[]{:S(2)}) %collective-permute-start.2) | collective-permute-done | bytes 229408 | tf_op jit(solution)/shard_map/ppermute | solution.py:204
  24.0 1.4 %shard_map.79 = (f32[512,256]{1,0:T(8,128)S(1)}, f32[2,512]{1,0:T(2,128)S(1)}, f32[2,256]{1,0:T(2,128)S(1)}) custom-call(f32[1]{0:T(128)} %bitcast.5.teacher_scale_ref, f32[1]{0:T(128)} %bitcast.6.student_scale_ref, bf16[256,512]{1,0:T(8,128)(2,1)S(1)} %get-tuple-element.25.pupil_text_ref.text_ref, bf16[256,1280]{1,0:T(8,128)(2,1)S(1)} %get-tuple-element.26.master_text_ref, ...), custom_call_target="tpu_custom_call" | custom-call | flops 1048576 | bytes 1048576 | tf_op jit(solution)/shard_map/pallas_call | solution.py:183
  25.4 3.1 %collective-permute-start.10 = (f32[2,256]{1,0:T(2,128)S(1)}, f32[2,256]{1,0:T(2,128)S(1)}, u32[]{:S(2)}, u32[]{:S(2)}) collective-permute-start(f32[2,256]{1,0:T(2,128)S(1)} %get-tuple-element.30.refs_0_), channel_id=1, source_target_pairs={{0,4},{2,6},{4,0},{6,2},{1,5},{3,7},{5,1},{7,3},{8,12},{10,14},{12... | collective-permute-start | bytes 6152 | tf_op jit(solution)/shard_map/ppermute | solution.py:204
  28.6 1.6 %collective-permute-start.13 = (f32[2,512]{1,0:T(2,128)S(1)}, f32[2,512]{1,0:T(2,128)S(1)}, u32[]{:S(2)}, u32[]{:S(2)}) collective-permute-start(f32[2,512]{1,0:T(2,128)S(1)} %shard_map.82.refs_0_), channel_id=1, source_target_pairs={{0,1},{1,0},{16,17},{17,16},{2,3},{3,2},{18,19},{19,18},{4,5},{5,4... | collective-permute-start | bytes 12296 | tf_op jit(solution)/shard_map/ppermute | solution.py:207
  30.1 1.8 %collective-permute-start.11 = (f32[2,256]{1,0:T(2,128)S(1)}, f32[2,256]{1,0:T(2,128)S(1)}, u32[]{:S(2)}, u32[]{:S(2)}) collective-permute-start(f32[2,256]{1,0:T(2,128)S(1)} %shard_map.80.refs_0_), channel_id=1, source_target_pairs={{0,2},{2,0},{4,6},{6,4},{1,3},{3,1},{5,7},{7,5},{8,10},{10,8},{12,... | collective-permute-start | bytes 6152 | tf_op jit(solution)/shard_map/ppermute | solution.py:204
  32.2 1.6 %collective-permute-start.14 = (f32[2,512]{1,0:T(2,128)S(1)}, f32[2,512]{1,0:T(2,128)S(1)}, u32[]{:S(2)}, u32[]{:S(2)}) collective-permute-start(f32[2,512]{1,0:T(2,128)S(1)} %shard_map.83.refs_1_), channel_id=1, source_target_pairs={{0,16},{1,17},{16,0},{17,1},{2,18},{3,19},{18,2},{19,3},{4,20},{5,... | collective-permute-start | bytes 12296 | tf_op jit(solution)/shard_map/ppermute | solution.py:207
  33.9 2.1 %collective-permute-done.14.refs_2_ = f32[2,512]{1,0:T(2,128)S(1)} collective-permute-done((f32[2,512]{1,0:T(2,128)S(1)}, f32[2,512]{1,0:T(2,128)S(1)}, u32[]{:S(2)}, u32[]{:S(2)}) %collective-permute-start.14) | collective-permute-done | bytes 4128 | tf_op jit(solution)/shard_map/ppermute | solution.py:207
  35.9 1.1 %shard_map.84 = (f32[4,64,512]{2,1,0:T(8,128)S(1)}, bf16[4,64,512]{2,1,0:T(8,128)(2,1)S(1)}, f32[64,512]{1,0:T(8,128)S(1)}, bf16[64,512]{1,0:T(8,128)(2,1)S(1)},...) custom-call(s32[1]{0:T(128)} %bitcast.core_ref, s32[1]{0:T(128)} %bitcast.1.z_ref, f32[1]{0:T(128)} %bitcast.7.scale_ref, ...), custom_call_target="tpu_custom_call" | custom-call | flops 1048576 | bytes 1048576 | tf_op jit(solution)/shard_map/pallas_call | solution.py:183
  37.1 1.8 %collective-permute-start.15 = (bf16[64,512]{1,0:T(8,128)(2,1)S(1)}, bf16[64,512]{1,0:T(8,128)(2,1)S(1)}, u32[]{:S(2)}, u32[]{:S(2)}) collective-permute-start(bf16[64,512]{1,0:T(8,128)(2,1)S(1)} %get-tuple-element.33), channel_id=1, source_target_pairs={{0,2},{2,0},{4,6},{6,4},{1,3},{3,1},{5,7},{7,5},{8,10},{10,8},{12,... | collective-permute-start | bytes 196616 | tf_op jit(solution)/shard_map/ppermute | solution.py:204
  38.9 1.2 %collective-permute-start.16 = (bf16[64,512]{1,0:T(8,128)(2,1)S(1)}, bf16[64,512]{1,0:T(8,128)(2,1)S(1)}, u32[]{:S(2)}, u32[]{:S(2)}) collective-permute-start(bf16[64,512]{1,0:T(8,128)(2,1)S(1)} %get-tuple-element.34), channel_id=1, source_target_pairs={{0,4},{2,6},{4,0},{6,2},{1,5},{3,7},{5,1},{7,3},{8,12},{10,14},{12... | collective-permute-start | bytes 196616 | tf_op jit(solution)/shard_map/ppermute | solution.py:204
  40.0 1.5 %collective-permute-start.17 = (bf16[64,512]{1,0:T(8,128)(2,1)S(1)}, bf16[64,512]{1,0:T(8,128)(2,1)S(1)}, u32[]{:S(2)}, u32[]{:S(2)}) collective-permute-start(bf16[64,512]{1,0:T(8,128)(2,1)S(1)} %get-tuple-element.35), channel_id=1, source_target_pairs={{0,6},{2,4},{4,2},{6,0},{1,7},{3,5},{5,3},{7,1},{8,14},{10,12},{12... | collective-permute-start | bytes 196616 | tf_op jit(solution)/shard_map/ppermute | solution.py:204
  41.6 1.6 %collective-permute-start.19 = (bf16[64,512]{1,0:T(8,128)(2,1)S(1)}, bf16[64,512]{1,0:T(8,128)(2,1)S(1)}, u32[]{:S(2)}, u32[]{:S(2)}) collective-permute-start(bf16[64,512]{1,0:T(8,128)(2,1)S(1)} %get-tuple-element.39), channel_id=1, source_target_pairs={{0,1},{1,0},{16,17},{17,16},{2,3},{3,2},{18,19},{19,18},{4,5},{5,4... | collective-permute-start | bytes 196616 | tf_op jit(solution)/shard_map/ppermute | solution.py:207
  43.1 1.5 %collective-permute-start.20 = (bf16[64,512]{1,0:T(8,128)(2,1)S(1)}, bf16[64,512]{1,0:T(8,128)(2,1)S(1)}, u32[]{:S(2)}, u32[]{:S(2)}) collective-permute-start(bf16[64,512]{1,0:T(8,128)(2,1)S(1)} %get-tuple-element.40), channel_id=1, source_target_pairs={{0,16},{1,17},{16,0},{17,1},{2,18},{3,19},{18,2},{19,3},{4,20},{5,... | collective-permute-start | bytes 196616 | tf_op jit(solution)/shard_map/ppermute | solution.py:207
  45.1 2.2 %collective-permute-done.16.refs_2_ = bf16[64,512]{1,0:T(8,128)(2,1)S(1)} collective-permute-done((bf16[64,512]{1,0:T(8,128)(2,1)S(1)}, bf16[64,512]{1,0:T(8,128)(2,1)S(1)}, u32[]{:S(2)}, u32[]{:S(2)}) %collective-permute-start.16) | collective-permute-done | bytes 65568 | tf_op jit(solution)/shard_map/ppermute | solution.py:204
  48.1 1.7 %collective-permute-done.21.refs_3_ = bf16[64,512]{1,0:T(8,128)(2,1)S(1)} collective-permute-done((bf16[64,512]{1,0:T(8,128)(2,1)S(1)}, bf16[64,512]{1,0:T(8,128)(2,1)S(1)}, u32[]{:S(2)}, u32[]{:S(2)}) %collective-permute-start.21) | collective-permute-done | bytes 65568 | tf_op jit(solution)/shard_map/ppermute | solution.py:207
  (37 shorter events, 5.3 us)
Async XLA Ops:
  1.6 14.7 %collective-permute-start = (bf16[64,1792]{1,0:T(8,128)(2,1)S(1)}, bf16[64,1792]{1,0:T(8,128)(2,1)S(1)}, u32[]{:S(2)}, u32[]{:S(2)}) collective-permute-start(bf16[64,1792]{1,0:T(8,128)(2,1)S(1)} %pad_maximum_fusion.1.refs_0_), channel_id=1, source_target_pairs={{0,4},{2,6},{4,0},{6,2},{1,5},{3,7},{5,1},{7,3},{8,12},{10,14},{12... | collective-permute-start | bytes 688136 | tf_op jit(solution)/shard_map/ppermute | solution.py:204
  5.7 10.8 %collective-permute-start.1 = (bf16[64,1792]{1,0:T(8,128)(2,1)S(1)}, bf16[64,1792]{1,0:T(8,128)(2,1)S(1)}, u32[]{:S(2)}, u32[]{:S(2)}) collective-permute-start(bf16[64,1792]{1,0:T(8,128)(2,1)S(1)} %pad_maximum_fusion.1.refs_0_), channel_id=1, source_target_pairs={{0,2},{2,0},{4,6},{6,4},{1,3},{3,1},{5,7},{7,5},{8,10},{10,8},{12,... | collective-permute-start | bytes 688136 | tf_op jit(solution)/shard_map/ppermute | solution.py:204
  8.2 11.1 %collective-permute-start.3 = (bf16[64,1792]{1,0:T(8,128)(2,1)S(1)}, bf16[64,1792]{1,0:T(8,128)(2,1)S(1)}, u32[]{:S(2)}, u32[]{:S(2)}) collective-permute-start(bf16[64,1792]{1,0:T(8,128)(2,1)S(1)} %pad_maximum_fusion.refs_0_), channel_id=1, source_target_pairs={{0,1},{1,0},{16,17},{17,16},{2,3},{3,2},{18,19},{19,18},{4,5},{5,4... | collective-permute-start | bytes 688136 | tf_op jit(solution)/shard_map/ppermute | solution.py:207
  9.7 11.4 %collective-permute-start.4 = (bf16[64,1792]{1,0:T(8,128)(2,1)S(1)}, bf16[64,1792]{1,0:T(8,128)(2,1)S(1)}, u32[]{:S(2)}, u32[]{:S(2)}) collective-permute-start(bf16[64,1792]{1,0:T(8,128)(2,1)S(1)} %pad_maximum_fusion.refs_0_), channel_id=1, source_target_pairs={{0,16},{1,17},{16,0},{17,1},{2,18},{3,19},{18,2},{19,3},{4,20},{5,... | collective-permute-start | bytes 688136 | tf_op jit(solution)/shard_map/ppermute | solution.py:207
  11.3 9.9 %collective-permute-start.5 = (bf16[64,1792]{1,0:T(8,128)(2,1)S(1)}, bf16[64,1792]{1,0:T(8,128)(2,1)S(1)}, u32[]{:S(2)}, u32[]{:S(2)}) collective-permute-start(bf16[64,1792]{1,0:T(8,128)(2,1)S(1)} %pad_maximum_fusion.refs_0_), channel_id=1, source_target_pairs={{0,17},{1,16},{16,1},{17,0},{2,19},{3,18},{18,3},{19,2},{4,21},{5,... | collective-permute-start | bytes 688136 | tf_op jit(solution)/shard_map/ppermute | solution.py:207
  16.5 6.5 %collective-permute-start.2 = (bf16[64,1792]{1,0:T(8,128)(2,1)S(1)}, bf16[64,1792]{1,0:T(8,128)(2,1)S(1)}, u32[]{:S(2)}, u32[]{:S(2)}) collective-permute-start(bf16[64,1792]{1,0:T(8,128)(2,1)S(1)} %collective-permute-done.refs_2_), channel_id=1, source_target_pairs={{0,2},{2,0},{4,6},{6,4},{1,3},{3,1},{5,7},{7,5},{8,10},{10,8},{12,... | collective-permute-start | bytes 688136 | tf_op jit(solution)/shard_map/ppermute | solution.py:204
  18.0 5.3 %collective-permute-start.6 = (bf16[64,1792]{1,0:T(8,128)(2,1)S(1)}, bf16[64,1792]{1,0:T(8,128)(2,1)S(1)}, u32[]{:S(2)}, u32[]{:S(2)}) collective-permute-start(bf16[64,1792]{1,0:T(8,128)(2,1)S(1)} %pad_maximum_fusion.refs_0_), channel_id=1, source_target_pairs={{0,8},{8,0},{1,9},{9,1},{2,10},{10,2},{3,11},{11,3},{4,12},{12,4},... | collective-permute-start | bytes 688136 | tf_op jit(solution)/shard_map/ppermute | solution.py:219
  19.3 4.0 %collective-permute-start.7 = (bf16[64,1792]{1,0:T(8,128)(2,1)S(1)}, bf16[64,1792]{1,0:T(8,128)(2,1)S(1)}, u32[]{:S(2)}, u32[]{:S(2)}) collective-permute-start(bf16[64,1792]{1,0:T(8,128)(2,1)S(1)} %collective-permute-done.3.refs_1_), channel_id=1, source_target_pairs={{0,8},{8,0},{1,9},{9,1},{2,10},{10,2},{3,11},{11,3},{4,12},{12,4},... | collective-permute-start | bytes 688136 | tf_op jit(solution)/shard_map/ppermute | solution.py:219
  21.2 2.2 %collective-permute-start.8 = (bf16[64,1792]{1,0:T(8,128)(2,1)S(1)}, bf16[64,1792]{1,0:T(8,128)(2,1)S(1)}, u32[]{:S(2)}, u32[]{:S(2)}) collective-permute-start(bf16[64,1792]{1,0:T(8,128)(2,1)S(1)} %collective-permute-done.4.refs_2_), channel_id=1, source_target_pairs={{0,8},{8,0},{1,9},{9,1},{2,10},{10,2},{3,11},{11,3},{4,12},{12,4},... | collective-permute-start | bytes 688136 | tf_op jit(solution)/shard_map/ppermute | solution.py:219
  21.2 2.2 %collective-permute-start.9 = (bf16[64,1792]{1,0:T(8,128)(2,1)S(1)}, bf16[64,1792]{1,0:T(8,128)(2,1)S(1)}, u32[]{:S(2)}, u32[]{:S(2)}) collective-permute-start(bf16[64,1792]{1,0:T(8,128)(2,1)S(1)} %collective-permute-done.5.refs_3_), channel_id=1, source_target_pairs={{0,8},{8,0},{1,9},{9,1},{2,10},{10,2},{3,11},{11,3},{4,12},{12,4},... | collective-permute-start | bytes 688136 | tf_op jit(solution)/shard_map/ppermute | solution.py:219
  25.3 3.2 %collective-permute-start.12 = (f32[2,512]{1,0:T(2,128)S(1)}, f32[2,512]{1,0:T(2,128)S(1)}, u32[]{:S(2)}, u32[]{:S(2)}) collective-permute-start(f32[2,512]{1,0:T(2,128)S(1)} %get-tuple-element.31.refs_0_), channel_id=1, source_target_pairs={{0,8},{8,0},{1,9},{9,1},{2,10},{10,2},{3,11},{11,3},{4,12},{12,4},... | collective-permute-start | bytes 12296 | tf_op jit(solution)/shard_map/ppermute | solution.py:219
  25.4 4.7 %collective-permute-start.10 = (f32[2,256]{1,0:T(2,128)S(1)}, f32[2,256]{1,0:T(2,128)S(1)}, u32[]{:S(2)}, u32[]{:S(2)}) collective-permute-start(f32[2,256]{1,0:T(2,128)S(1)} %get-tuple-element.30.refs_0_), channel_id=1, source_target_pairs={{0,4},{2,6},{4,0},{6,2},{1,5},{3,7},{5,1},{7,3},{8,12},{10,14},{12... | collective-permute-start | bytes 6152 | tf_op jit(solution)/shard_map/ppermute | solution.py:204
  28.6 3.7 %collective-permute-start.13 = (f32[2,512]{1,0:T(2,128)S(1)}, f32[2,512]{1,0:T(2,128)S(1)}, u32[]{:S(2)}, u32[]{:S(2)}) collective-permute-start(f32[2,512]{1,0:T(2,128)S(1)} %shard_map.82.refs_0_), channel_id=1, source_target_pairs={{0,1},{1,0},{16,17},{17,16},{2,3},{3,2},{18,19},{19,18},{4,5},{5,4... | collective-permute-start | bytes 12296 | tf_op jit(solution)/shard_map/ppermute | solution.py:207
  30.1 3.7 %collective-permute-start.11 = (f32[2,256]{1,0:T(2,128)S(1)}, f32[2,256]{1,0:T(2,128)S(1)}, u32[]{:S(2)}, u32[]{:S(2)}) collective-permute-start(f32[2,256]{1,0:T(2,128)S(1)} %shard_map.80.refs_0_), channel_id=1, source_target_pairs={{0,2},{2,0},{4,6},{6,4},{1,3},{3,1},{5,7},{7,5},{8,10},{10,8},{12,... | collective-permute-start | bytes 6152 | tf_op jit(solution)/shard_map/ppermute | solution.py:204
  32.2 3.7 %collective-permute-start.14 = (f32[2,512]{1,0:T(2,128)S(1)}, f32[2,512]{1,0:T(2,128)S(1)}, u32[]{:S(2)}, u32[]{:S(2)}) collective-permute-start(f32[2,512]{1,0:T(2,128)S(1)} %shard_map.83.refs_1_), channel_id=1, source_target_pairs={{0,16},{1,17},{16,0},{17,1},{2,18},{3,19},{18,2},{19,3},{4,20},{5,... | collective-permute-start | bytes 12296 | tf_op jit(solution)/shard_map/ppermute | solution.py:207
  37.0 4.5 %collective-permute-start.18 = (bf16[4,64,512]{2,1,0:T(8,128)(2,1)S(1)}, bf16[4,64,512]{2,1,0:T(8,128)(2,1)S(1)}, u32[]{:S(2)}, u32[]{:S(2)}) collective-permute-start(bf16[4,64,512]{2,1,0:T(8,128)(2,1)S(1)} %get-tuple-element.37), channel_id=1, source_target_pairs={{0,8},{8,0},{1,9},{9,1},{2,10},{10,2},{3,11},{11,3},{4,12},{12,4},... | collective-permute-start | bytes 786440 | tf_op jit(solution)/shard_map/ppermute | solution.py:219
  37.1 7.6 %collective-permute-start.15 = (bf16[64,512]{1,0:T(8,128)(2,1)S(1)}, bf16[64,512]{1,0:T(8,128)(2,1)S(1)}, u32[]{:S(2)}, u32[]{:S(2)}) collective-permute-start(bf16[64,512]{1,0:T(8,128)(2,1)S(1)} %get-tuple-element.33), channel_id=1, source_target_pairs={{0,2},{2,0},{4,6},{6,4},{1,3},{3,1},{5,7},{7,5},{8,10},{10,8},{12,... | collective-permute-start | bytes 196616 | tf_op jit(solution)/shard_map/ppermute | solution.py:204
  38.9 8.4 %collective-permute-start.16 = (bf16[64,512]{1,0:T(8,128)(2,1)S(1)}, bf16[64,512]{1,0:T(8,128)(2,1)S(1)}, u32[]{:S(2)}, u32[]{:S(2)}) collective-permute-start(bf16[64,512]{1,0:T(8,128)(2,1)S(1)} %get-tuple-element.34), channel_id=1, source_target_pairs={{0,4},{2,6},{4,0},{6,2},{1,5},{3,7},{5,1},{7,3},{8,12},{10,14},{12... | collective-permute-start | bytes 196616 | tf_op jit(solution)/shard_map/ppermute | solution.py:204
  40.0 7.3 %collective-permute-start.17 = (bf16[64,512]{1,0:T(8,128)(2,1)S(1)}, bf16[64,512]{1,0:T(8,128)(2,1)S(1)}, u32[]{:S(2)}, u32[]{:S(2)}) collective-permute-start(bf16[64,512]{1,0:T(8,128)(2,1)S(1)} %get-tuple-element.35), channel_id=1, source_target_pairs={{0,6},{2,4},{4,2},{6,0},{1,7},{3,5},{5,3},{7,1},{8,14},{10,12},{12... | collective-permute-start | bytes 196616 | tf_op jit(solution)/shard_map/ppermute | solution.py:204
  41.6 5.8 %collective-permute-start.19 = (bf16[64,512]{1,0:T(8,128)(2,1)S(1)}, bf16[64,512]{1,0:T(8,128)(2,1)S(1)}, u32[]{:S(2)}, u32[]{:S(2)}) collective-permute-start(bf16[64,512]{1,0:T(8,128)(2,1)S(1)} %get-tuple-element.39), channel_id=1, source_target_pairs={{0,1},{1,0},{16,17},{17,16},{2,3},{3,2},{18,19},{19,18},{4,5},{5,4... | collective-permute-start | bytes 196616 | tf_op jit(solution)/shard_map/ppermute | solution.py:207
  43.1 5.0 %collective-permute-start.20 = (bf16[64,512]{1,0:T(8,128)(2,1)S(1)}, bf16[64,512]{1,0:T(8,128)(2,1)S(1)}, u32[]{:S(2)}, u32[]{:S(2)}) collective-permute-start(bf16[64,512]{1,0:T(8,128)(2,1)S(1)} %get-tuple-element.40), channel_id=1, source_target_pairs={{0,16},{1,17},{16,0},{17,1},{2,18},{3,19},{18,2},{19,3},{4,20},{5,... | collective-permute-start | bytes 196616 | tf_op jit(solution)/shard_map/ppermute | solution.py:207
  44.7 5.2 %collective-permute-start.21 = (bf16[64,512]{1,0:T(8,128)(2,1)S(1)}, bf16[64,512]{1,0:T(8,128)(2,1)S(1)}, u32[]{:S(2)}, u32[]{:S(2)}) collective-permute-start(bf16[64,512]{1,0:T(8,128)(2,1)S(1)} %get-tuple-element.41), channel_id=1, source_target_pairs={{0,17},{1,16},{16,1},{17,0},{2,19},{3,18},{18,3},{19,2},{4,21},{5,... | collective-permute-start | bytes 196616 | tf_op jit(solution)/shard_map/ppermute | solution.py:207
  47.3 2.5 %copy-start = (bf16[64,512]{1,0:T(8,128)(2,1)S(1)}, bf16[64,512]{1,0:T(8,128)(2,1)}, u32[]{:S(2)}) copy-start(bf16[64,512]{1,0:T(8,128)(2,1)} %raw_image_ref.1) | copy-start | bytes 196612
  47.3 2.5 %copy-start.1 = (bf16[64,512]{1,0:T(8,128)(2,1)S(1)}, bf16[64,512]{1,0:T(8,128)(2,1)}, u32[]{:S(2)}) copy-start(bf16[64,512]{1,0:T(8,128)(2,1)} %raw_text_ref.1) | copy-start | bytes 196612

commit v3 on v2

--- a/solution.py
+++ b/solution.py
@@ -51,7 +51,7 @@
     squares = len(blocks) // 2
     core = core_ref[0]
     for s in range(squares):
-        at = jnp.bitwise_xor(square_ref[0], s)
+        at = jnp.bitwise_xor(square_ref[0], squares - 1 - s)
         for ref, half in ((blocks[s], core), (blocks[squares + s], 1 - core)):
             row = pl.multiple_of((half * squares + at) * own, own)
             put_units(ref[...], pupil_ref, master_ref, row)
@@ -158,21 +158,11 @@
         ref[...] = (kept_ref[at] + received_ref[at].astype(F32)).astype(ref.dtype)
 
 
-def total_of(refs):
-    total = refs[0][...]
-    for ref in refs[1:]:
-        total = total + ref[...].astype(F32)
-    return total
-
-
-def sum_kernel(*refs):
-    refs[-1][...] = total_of(refs[:-1])
-
-
-def back_kernel(raw_image_ref, raw_text_ref, text_ref, *refs):
-    image_out_ref, text_out_ref = refs[-2:]
-    text_out_ref[...] = back_norm(text_ref[...], raw_text_ref[...])
-    image_out_ref[...] = back_norm(total_of(refs[:-2]), raw_image_ref[...])
+def back_kernel(raw_ref, own_ref, *refs):
+    grad = own_ref[...]
+    for ref in refs[:-1]:
+        grad = grad + ref[...].astype(F32)
+    refs[-1][...] = back_norm(grad, raw_ref[...])
 
 
 def shaped(shape, dtype):
@@ -233,7 +223,7 @@
         raw_text = side_by_side(student_text, teacher_text)
         raw_texts = gather_line(raw_text)
         raw_image = side_by_side(student_image, teacher_image)
-        same = [raw_image] + [to_square(raw_image, s) for s in range(1, squares)]
+        same = [to_square(raw_image, s) for s in reversed(range(1, squares))] + [raw_image]
         other = [to_sibling(block) for block in same]
 
         pupil_text, master_text = call(
@@ -270,7 +260,7 @@
             row_lse = joined(row_lses, 1 << 10)
             row_lses = [row_lse, to_square(row_lse, s)]
         for s in bits(depth):
-            col_lse = joined([col_lse, to_line(col_lse, s)], MANY if s == 1 else 1 << 31)
+            col_lse = joined([col_lse, to_line(col_lse, s)], MANY if s == 1 else 1 << 10)
         block = shaped((own, width), F32)
         sent = shaped((own, width), BF16)
         kept, for_sibling, own_text, *for_line = call(
@@ -283,8 +273,15 @@
             (pltpu.VMEM((images, width), F32), pltpu.VMEM((texts, width), F32)),
             grant,
         )
-        text_parts = [own_text] + [to_line(part, s + 1) for s, part in enumerate(for_line)]
-        text_grad = call(sum_kernel, block, text_parts, [vmem] * depth, vmem, flops=MANY)
+        text_parts = [to_line(part, s + 1) for s, part in reversed(list(enumerate(for_line)))]
+        text_grad = call(
+            back_kernel,
+            block,
+            (student_text, own_text, *text_parts),
+            [vmem] * (1 + depth),
+            vmem,
+            flops=MANY,
+        )
         own_image, *for_square = call(
             pair_kernel,
             (block,) + (sent,) * (squares - 1),
@@ -292,14 +289,15 @@
             [smem] + [vmem] * 2,
             vmem,
         )
-        image_parts = [own_image] + [to_square(part, s + 1) for s, part in enumerate(for_square)]
-        return call(
+        image_parts = [to_square(part, s + 1) for s, part in reversed(list(enumerate(for_square)))]
+        image_grad = call(
             back_kernel,
-            (block, block),
-            (student_image, student_text, text_grad, *image_parts),
-            [vmem] * (3 + squares),
-            vmem,
-        )
+            block,
+            (student_image, own_image, *image_parts),
+            [vmem] * (1 + squares),
+            vmem,
+        )
+        return (image_grad, text_grad)
 
     return body
 

time: 50.9 us -> 51.4 us (level)
  Pallas kernels: 4.34 us -> 5.1 us
    ppermute x8, waiting for transfers between devices: 6.14 us -> 2.99 us  [to_square(): return lax.ppermute(value, SQUARE, [(q, q ^ step) for q in range(squares)])]
    ppermute x8, waiting for transfers between devices: 8.26 us -> 10 us  [to_line(): return lax.ppermute(value, LINE, [(z, z ^ step) for z in range(depth)])]
    ppermute x6, waiting for transfers between devices: 0.02 us -> 1.17 us  [to_sibling(): return lax.ppermute(value, 'core', [(0, 1), (1, 0)])]
    pallas_call x11, Pallas kernels: 4.34 us -> 5.1 us  [call(): pl.pallas_call(kernel, out_shape=outs, in_specs=specs, out_specs=jax.tree...]
  transfers between devices with their start and end apart: 22 -> 22, of which waited for: 9 -> 11; matrix products, arithmetic and copies ran while one was open for 2% -> 2% of each run, Pallas kernels for 1% -> 2%
where the time goes in v3:
time: 51.4 us; the launch traced here: 51.1 us
  starting transfers between devices  27.9 us (54%)
  waiting for transfers between devices  14.2 us (28%)
  Pallas kernels  5.1 us (10%)
  between operations  2.05 us (4%)
  other arithmetic  1.87 us (4%)
    ppermute x8, starting transfers between devices, to_line(): return lax.ppermute(value, LINE, [(z, z ^ step) for z in range(depth)])  16.7 us
    ppermute x8, waiting for transfers between devices, to_line(): return lax.ppermute(value, LINE, [(z, z ^ step) for z in range(depth)])  10 us
    ppermute x8, starting transfers between devices, to_square(): return lax.ppermute(value, SQUARE, [(q, q ^ step) for q in range(squares)])  10 us
    pallas_call x11, Pallas kernels, call(): pl.pallas_call(kernel, out_shape=outs, in_specs=specs, out_specs=jax.tree...  5.1 us
    ppermute x8, waiting for transfers between devices, to_square(): return lax.ppermute(value, SQUARE, [(q, q ^ step) for q in range(squares)])  2.99 us
    max x2, other arithmetic, side_by_side(): jnp.maximum(lax.pad(left, lowest, ((0, 0, 0), (0, right_width, 0))), lax....  1.87 us
    ppermute x6, waiting for transfers between devices, to_sibling(): return lax.ppermute(value, 'core', [(0, 1), (1, 0)])  1.17 us
    ppermute x6, starting transfers between devices, to_sibling(): return lax.ppermute(value, 'core', [(0, 1), (1, 0)])  1.15 us
  transfers between devices with their start and end apart: 22, of which 11 were waited for; matrix products, arithmetic and copies ran while one was open for 2% of the time, Pallas kernels for 2%

profile of v3, /device:TPU:0, one launch (start us, length us, event | category | flops | bytes accessed | tf_op | source)
XLA Modules:
  0.0 51.1 jit_solution(5306937858941148128)
XLA Ops:
  0.6 0.9 %pad_maximum_fusion.1.refs_0_ = bf16[64,1792]{1,0:T(8,128)(2,1)S(1)} fusion(bf16[64,1280]{1,0:T(8,128)(2,1)} %param.9, bf16[64,512]{1,0:T(8,128)(2,1)} %raw_ref.3), kind=kLoop, calls=%fused_computation.1 | loop fusion | flops 458752 | bytes 458752 | tf_op jit(solution)/shard_map/max | solution.py:35
  1.6 4.1 %collective-permute-start = (bf16[64,1792]{1,0:T(8,128)(2,1)S(1)}, bf16[64,1792]{1,0:T(8,128)(2,1)S(1)}, u32[]{:S(2)}, u32[]{:S(2)}) collective-permute-start(bf16[64,1792]{1,0:T(8,128)(2,1)S(1)} %pad_maximum_fusion.1.refs_0_), channel_id=1, source_target_pairs={{0,4},{2,6},{4,0},{6,2},{1,5},{3,7},{5,1},{7,3},{8,12},{10,14},{12... | collective-permute-start | bytes 688136 | tf_op jit(solution)/shard_map/ppermute | solution.py:194
  5.7 1.6 %collective-permute-start.1 = (bf16[64,1792]{1,0:T(8,128)(2,1)S(1)}, bf16[64,1792]{1,0:T(8,128)(2,1)S(1)}, u32[]{:S(2)}, u32[]{:S(2)}) collective-permute-start(bf16[64,1792]{1,0:T(8,128)(2,1)S(1)} %pad_maximum_fusion.1.refs_0_), channel_id=1, source_target_pairs={{0,2},{2,0},{4,6},{6,4},{1,3},{3,1},{5,7},{7,5},{8,10},{10,8},{12,... | collective-permute-start | bytes 688136 | tf_op jit(solution)/shard_map/ppermute | solution.py:194
  7.2 0.9 %pad_maximum_fusion.refs_3_ = bf16[64,1792]{1,0:T(8,128)(2,1)S(1)} fusion(bf16[64,1280]{1,0:T(8,128)(2,1)} %param.8, bf16[64,512]{1,0:T(8,128)(2,1)} %raw_ref.2), kind=kLoop, calls=%fused_computation | loop fusion | flops 458752 | bytes 458752 | tf_op jit(solution)/shard_map/max | solution.py:35
  8.2 2.5 %collective-permute-start.3 = (bf16[64,1792]{1,0:T(8,128)(2,1)S(1)}, bf16[64,1792]{1,0:T(8,128)(2,1)S(1)}, u32[]{:S(2)}, u32[]{:S(2)}) collective-permute-start(bf16[64,1792]{1,0:T(8,128)(2,1)S(1)} %pad_maximum_fusion.refs_3_), channel_id=1, source_target_pairs={{0,17},{1,16},{16,1},{17,0},{2,19},{3,18},{18,3},{19,2},{4,21},{5,... | collective-permute-start | bytes 688136 | tf_op jit(solution)/shard_map/ppermute | solution.py:197
  11.7 4.6 %collective-permute-done.refs_2_ = bf16[64,1792]{1,0:T(8,128)(2,1)S(1)} collective-permute-done((bf16[64,1792]{1,0:T(8,128)(2,1)S(1)}, bf16[64,1792]{1,0:T(8,128)(2,1)S(1)}, u32[]{:S(2)}, u32[]{:S(2)}) %collective-permute-start) | collective-permute-done | bytes 229408 | tf_op jit(solution)/shard_map/ppermute | solution.py:194
  16.5 1.5 %collective-permute-start.2 = (bf16[64,1792]{1,0:T(8,128)(2,1)S(1)}, bf16[64,1792]{1,0:T(8,128)(2,1)S(1)}, u32[]{:S(2)}, u32[]{:S(2)}) collective-permute-start(bf16[64,1792]{1,0:T(8,128)(2,1)S(1)} %collective-permute-done.refs_2_), channel_id=1, source_target_pairs={{0,2},{2,0},{4,6},{6,4},{1,3},{3,1},{5,7},{7,5},{8,10},{10,8},{12,... | collective-permute-start | bytes 688136 | tf_op jit(solution)/shard_map/ppermute | solution.py:194
  19.9 1.0 %collective-permute-done.4.refs_1_ = bf16[64,1792]{1,0:T(8,128)(2,1)S(1)} collective-permute-done((bf16[64,1792]{1,0:T(8,128)(2,1)S(1)}, bf16[64,1792]{1,0:T(8,128)(2,1)S(1)}, u32[]{:S(2)}, u32[]{:S(2)}) %collective-permute-start.4) | collective-permute-done | bytes 229408 | tf_op jit(solution)/shard_map/ppermute | solution.py:197
  21.4 1.7 %collective-permute-done.2.refs_3_ = bf16[64,1792]{1,0:T(8,128)(2,1)S(1)} collective-permute-done((bf16[64,1792]{1,0:T(8,128)(2,1)S(1)}, bf16[64,1792]{1,0:T(8,128)(2,1)S(1)}, u32[]{:S(2)}, u32[]{:S(2)}) %collective-permute-start.2) | collective-permute-done | bytes 229408 | tf_op jit(solution)/shard_map/ppermute | solution.py:194
  24.0 1.4 %shard_map.79 = (f32[512,256]{1,0:T(8,128)S(1)}, f32[2,512]{1,0:T(2,128)S(1)}, f32[2,256]{1,0:T(2,128)S(1)}) custom-call(f32[1]{0:T(128)} %bitcast.5.teacher_scale_ref, f32[1]{0:T(128)} %bitcast.6.student_scale_ref, bf16[256,512]{1,0:T(8,128)(2,1)S(1)} %get-tuple-element.25.pupil_text_ref.text_ref, bf16[256,1280]{1,0:T(8,128)(2,1)S(1)} %get-tuple-element.26.master_text_ref, ...), custom_call_target="tpu_custom_call" | custom-call | flops 1048576 | bytes 1048576 | tf_op jit(solution)/shard_map/pallas_call | solution.py:173
  25.4 1.2 %collective-permute-done.12.refs_1_ = f32[2,512]{1,0:T(2,128)S(1)} collective-permute-done((f32[2,512]{1,0:T(2,128)S(1)}, f32[2,512]{1,0:T(2,128)S(1)}, u32[]{:S(2)}, u32[]{:S(2)}) %collective-permute-start.12) | collective-permute-done | bytes 4128 | tf_op jit(solution)/shard_map/ppermute | solution.py:209
  26.6 1.3 %collective-permute-start.13 = (f32[2,512]{1,0:T(2,128)S(1)}, f32[2,512]{1,0:T(2,128)S(1)}, u32[]{:S(2)}, u32[]{:S(2)}) collective-permute-start(f32[2,512]{1,0:T(2,128)S(1)} %shard_map.82.refs_0_), channel_id=1, source_target_pairs={{0,1},{1,0},{16,17},{17,16},{2,3},{3,2},{18,19},{19,18},{4,5},{5,4... | collective-permute-start | bytes 12296 | tf_op jit(solution)/shard_map/ppermute | solution.py:197
  27.9 3.3 %collective-permute-start.10 = (f32[2,256]{1,0:T(2,128)S(1)}, f32[2,256]{1,0:T(2,128)S(1)}, u32[]{:S(2)}, u32[]{:S(2)}) collective-permute-start(f32[2,256]{1,0:T(2,128)S(1)} %get-tuple-element.30.refs_0_), channel_id=1, source_target_pairs={{0,4},{2,6},{4,0},{6,2},{1,5},{3,7},{5,1},{7,3},{8,12},{10,14},{12... | collective-permute-start | bytes 6152 | tf_op jit(solution)/shard_map/ppermute | solution.py:194
  31.2 1.6 %collective-permute-done.10.refs_1_ = f32[2,256]{1,0:T(2,128)S(1)} collective-permute-done((f32[2,256]{1,0:T(2,128)S(1)}, f32[2,256]{1,0:T(2,128)S(1)}, u32[]{:S(2)}, u32[]{:S(2)}) %collective-permute-start.10) | collective-permute-done | bytes 2080 | tf_op jit(solution)/shard_map/ppermute | solution.py:194
  32.8 1.8 %collective-permute-start.11 = (f32[2,256]{1,0:T(2,128)S(1)}, f32[2,256]{1,0:T(2,128)S(1)}, u32[]{:S(2)}, u32[]{:S(2)}) collective-permute-start(f32[2,256]{1,0:T(2,128)S(1)} %shard_map.80.refs_0_), channel_id=1, source_target_pairs={{0,2},{2,0},{4,6},{6,4},{1,3},{3,1},{5,7},{7,5},{8,10},{10,8},{12,... | collective-permute-start | bytes 6152 | tf_op jit(solution)/shard_map/ppermute | solution.py:194
  34.6 1.6 %collective-permute-start.14 = (f32[2,512]{1,0:T(2,128)S(1)}, f32[2,512]{1,0:T(2,128)S(1)}, u32[]{:S(2)}, u32[]{:S(2)}) collective-permute-start(f32[2,512]{1,0:T(2,128)S(1)} %shard_map.83.refs_1_), channel_id=1, source_target_pairs={{0,16},{1,17},{16,0},{17,1},{2,18},{3,19},{18,2},{19,3},{4,20},{5,... | collective-permute-start | bytes 12296 | tf_op jit(solution)/shard_map/ppermute | solution.py:197
  36.4 1.8 %collective-permute-done.14.refs_2_ = f32[2,512]{1,0:T(2,128)S(1)} collective-permute-done((f32[2,512]{1,0:T(2,128)S(1)}, f32[2,512]{1,0:T(2,128)S(1)}, u32[]{:S(2)}, u32[]{:S(2)}) %collective-permute-start.14) | collective-permute-done | bytes 4128 | tf_op jit(solution)/shard_map/ppermute | solution.py:197
  38.3 1.1 %shard_map.84 = (f32[4,64,512]{2,1,0:T(8,128)S(1)}, bf16[4,64,512]{2,1,0:T(8,128)(2,1)S(1)}, f32[64,512]{1,0:T(8,128)S(1)}, bf16[64,512]{1,0:T(8,128)(2,1)S(1)},...) custom-call(s32[1]{0:T(128)} %bitcast.1.core_ref, s32[1]{0:T(128)} %bitcast.2.z_ref, f32[1]{0:T(128)} %bitcast.7.scale_ref, ...), custom_call_target="tpu_custom_call" | custom-call | flops 1048576 | bytes 1048576 | tf_op jit(solution)/shard_map/pallas_call | solution.py:173
  39.4 2.7 %collective-permute-start.19 = (bf16[64,512]{1,0:T(8,128)(2,1)S(1)}, bf16[64,512]{1,0:T(8,128)(2,1)S(1)}, u32[]{:S(2)}, u32[]{:S(2)}) collective-permute-start(bf16[64,512]{1,0:T(8,128)(2,1)S(1)} %get-tuple-element.39), channel_id=1, source_target_pairs={{0,6},{2,4},{4,2},{6,0},{1,7},{3,5},{5,3},{7,1},{8,14},{10,12},{12... | collective-permute-start | bytes 196616 | tf_op jit(solution)/shard_map/ppermute | solution.py:194
  42.5 1.4 %collective-permute-start.21 = (bf16[64,512]{1,0:T(8,128)(2,1)S(1)}, bf16[64,512]{1,0:T(8,128)(2,1)S(1)}, u32[]{:S(2)}, u32[]{:S(2)}) collective-permute-start(bf16[64,512]{1,0:T(8,128)(2,1)S(1)} %get-tuple-element.41), channel_id=1, source_target_pairs={{0,2},{2,0},{4,6},{6,4},{1,3},{3,1},{5,7},{7,5},{8,10},{10,8},{12,... | collective-permute-start | bytes 196616 | tf_op jit(solution)/shard_map/ppermute | solution.py:194
  43.9 1.6 %collective-permute-start.16 = (bf16[64,512]{1,0:T(8,128)(2,1)S(1)}, bf16[64,512]{1,0:T(8,128)(2,1)S(1)}, u32[]{:S(2)}, u32[]{:S(2)}) collective-permute-start(bf16[64,512]{1,0:T(8,128)(2,1)S(1)} %get-tuple-element.35), channel_id=1, source_target_pairs={{0,17},{1,16},{16,1},{17,0},{2,19},{3,18},{18,3},{19,2},{4,21},{5,... | collective-permute-start | bytes 196616 | tf_op jit(solution)/shard_map/ppermute | solution.py:197
  46.0 1.5 %collective-permute-start.18 = (bf16[64,512]{1,0:T(8,128)(2,1)S(1)}, bf16[64,512]{1,0:T(8,128)(2,1)S(1)}, u32[]{:S(2)}, u32[]{:S(2)}) collective-permute-start(bf16[64,512]{1,0:T(8,128)(2,1)S(1)} %get-tuple-element.37), channel_id=1, source_target_pairs={{0,1},{1,0},{16,17},{17,16},{2,3},{3,2},{18,19},{19,18},{4,5},{5,4... | collective-permute-start | bytes 196616 | tf_op jit(solution)/shard_map/ppermute | solution.py:197
  47.5 1.8 %collective-permute-done.20.refs_1_ = bf16[64,512]{1,0:T(8,128)(2,1)S(1)} collective-permute-done((bf16[64,512]{1,0:T(8,128)(2,1)S(1)}, bf16[64,512]{1,0:T(8,128)(2,1)S(1)}, u32[]{:S(2)}, u32[]{:S(2)}) %collective-permute-start.20) | collective-permute-done | bytes 65568 | tf_op jit(solution)/shard_map/ppermute | solution.py:194
  49.3 0.8 %shard_map.87 = f32[64,512]{1,0:T(8,128)} custom-call(bf16[64,512]{1,0:T(8,128)(2,1)S(1)} %copy-done.1, f32[64,512]{1,0:T(8,128)S(1)} %get-tuple-element.38.own_ref, bf16[64,512]{1,0:T(8,128)(2,1)S(1)} %collective-permute-done.19.refs_0_, bf16[64,512]{1,0:T(8,128)(2,1)S(1)} %collective-permute-done.20.refs_1_, ...), custom_call_target="tpu_custom_call" | custom-call | flops 34359738368 | bytes 1048576 | tf_op jit(solution)/shard_map/pallas_call | solution.py:173
  (37 shorter events, 5.5 us)
Async XLA Ops:
  1.6 14.7 %collective-permute-start = (bf16[64,1792]{1,0:T(8,128)(2,1)S(1)}, bf16[64,1792]{1,0:T(8,128)(2,1)S(1)}, u32[]{:S(2)}, u32[]{:S(2)}) collective-permute-start(bf16[64,1792]{1,0:T(8,128)(2,1)S(1)} %pad_maximum_fusion.1.refs_0_), channel_id=1, source_target_pairs={{0,4},{2,6},{4,0},{6,2},{1,5},{3,7},{5,1},{7,3},{8,12},{10,14},{12... | collective-permute-start | bytes 688136 | tf_op jit(solution)/shard_map/ppermute | solution.py:194
  5.7 10.8 %collective-permute-start.1 = (bf16[64,1792]{1,0:T(8,128)(2,1)S(1)}, bf16[64,1792]{1,0:T(8,128)(2,1)S(1)}, u32[]{:S(2)}, u32[]{:S(2)}) collective-permute-start(bf16[64,1792]{1,0:T(8,128)(2,1)S(1)} %pad_maximum_fusion.1.refs_0_), channel_id=1, source_target_pairs={{0,2},{2,0},{4,6},{6,4},{1,3},{3,1},{5,7},{7,5},{8,10},{10,8},{12,... | collective-permute-start | bytes 688136 | tf_op jit(solution)/shard_map/ppermute | solution.py:194
  8.2 11.1 %collective-permute-start.3 = (bf16[64,1792]{1,0:T(8,128)(2,1)S(1)}, bf16[64,1792]{1,0:T(8,128)(2,1)S(1)}, u32[]{:S(2)}, u32[]{:S(2)}) collective-permute-start(bf16[64,1792]{1,0:T(8,128)(2,1)S(1)} %pad_maximum_fusion.refs_3_), channel_id=1, source_target_pairs={{0,17},{1,16},{16,1},{17,0},{2,19},{3,18},{18,3},{19,2},{4,21},{5,... | collective-permute-start | bytes 688136 | tf_op jit(solution)/shard_map/ppermute | solution.py:197
  10.7 10.2 %collective-permute-start.4 = (bf16[64,1792]{1,0:T(8,128)(2,1)S(1)}, bf16[64,1792]{1,0:T(8,128)(2,1)S(1)}, u32[]{:S(2)}, u32[]{:S(2)}) collective-permute-start(bf16[64,1792]{1,0:T(8,128)(2,1)S(1)} %pad_maximum_fusion.refs_3_), channel_id=1, source_target_pairs={{0,16},{1,17},{16,0},{17,1},{2,18},{3,19},{18,2},{19,3},{4,20},{5,... | collective-permute-start | bytes 688136 | tf_op jit(solution)/shard_map/ppermute | solution.py:197
  11.2 9.7 %collective-permute-start.5 = (bf16[64,1792]{1,0:T(8,128)(2,1)S(1)}, bf16[64,1792]{1,0:T(8,128)(2,1)S(1)}, u32[]{:S(2)}, u32[]{:S(2)}) collective-permute-start(bf16[64,1792]{1,0:T(8,128)(2,1)S(1)} %pad_maximum_fusion.refs_3_), channel_id=1, source_target_pairs={{0,1},{1,0},{16,17},{17,16},{2,3},{3,2},{18,19},{19,18},{4,5},{5,4... | collective-permute-start | bytes 688136 | tf_op jit(solution)/shard_map/ppermute | solution.py:197
  16.5 6.5 %collective-permute-start.2 = (bf16[64,1792]{1,0:T(8,128)(2,1)S(1)}, bf16[64,1792]{1,0:T(8,128)(2,1)S(1)}, u32[]{:S(2)}, u32[]{:S(2)}) collective-permute-start(bf16[64,1792]{1,0:T(8,128)(2,1)S(1)} %collective-permute-done.refs_2_), channel_id=1, source_target_pairs={{0,2},{2,0},{4,6},{6,4},{1,3},{3,1},{5,7},{7,5},{8,10},{10,8},{12,... | collective-permute-start | bytes 688136 | tf_op jit(solution)/shard_map/ppermute | solution.py:194
  18.0 5.3 %collective-permute-start.9 = (bf16[64,1792]{1,0:T(8,128)(2,1)S(1)}, bf16[64,1792]{1,0:T(8,128)(2,1)S(1)}, u32[]{:S(2)}, u32[]{:S(2)}) collective-permute-start(bf16[64,1792]{1,0:T(8,128)(2,1)S(1)} %pad_maximum_fusion.refs_3_), channel_id=1, source_target_pairs={{0,8},{8,0},{1,9},{9,1},{2,10},{10,2},{3,11},{11,3},{4,12},{12,4},... | collective-permute-start | bytes 688136 | tf_op jit(solution)/shard_map/ppermute | solution.py:209
  19.3 4.0 %collective-permute-start.6 = (bf16[64,1792]{1,0:T(8,128)(2,1)S(1)}, bf16[64,1792]{1,0:T(8,128)(2,1)S(1)}, u32[]{:S(2)}, u32[]{:S(2)}) collective-permute-start(bf16[64,1792]{1,0:T(8,128)(2,1)S(1)} %collective-permute-done.3.refs_0_), channel_id=1, source_target_pairs={{0,8},{8,0},{1,9},{9,1},{2,10},{10,2},{3,11},{11,3},{4,12},{12,4},... | collective-permute-start | bytes 688136 | tf_op jit(solution)/shard_map/ppermute | solution.py:209
  20.8 2.5 %collective-permute-start.7 = (bf16[64,1792]{1,0:T(8,128)(2,1)S(1)}, bf16[64,1792]{1,0:T(8,128)(2,1)S(1)}, u32[]{:S(2)}, u32[]{:S(2)}) collective-permute-start(bf16[64,1792]{1,0:T(8,128)(2,1)S(1)} %collective-permute-done.4.refs_1_), channel_id=1, source_target_pairs={{0,8},{8,0},{1,9},{9,1},{2,10},{10,2},{3,11},{11,3},{4,12},{12,4},... | collective-permute-start | bytes 688136 | tf_op jit(solution)/shard_map/ppermute | solution.py:209
  20.9 2.4 %collective-permute-start.8 = (bf16[64,1792]{1,0:T(8,128)(2,1)S(1)}, bf16[64,1792]{1,0:T(8,128)(2,1)S(1)}, u32[]{:S(2)}, u32[]{:S(2)}) collective-permute-start(bf16[64,1792]{1,0:T(8,128)(2,1)S(1)} %collective-permute-done.5.refs_2_), channel_id=1, source_target_pairs={{0,8},{8,0},{1,9},{9,1},{2,10},{10,2},{3,11},{11,3},{4,12},{12,4},... | collective-permute-start | bytes 688136 | tf_op jit(solution)/shard_map/ppermute | solution.py:209
  25.3 1.2 %collective-permute-start.12 = (f32[2,512]{1,0:T(2,128)S(1)}, f32[2,512]{1,0:T(2,128)S(1)}, u32[]{:S(2)}, u32[]{:S(2)}) collective-permute-start(f32[2,512]{1,0:T(2,128)S(1)} %get-tuple-element.31.refs_0_), channel_id=1, source_target_pairs={{0,8},{8,0},{1,9},{9,1},{2,10},{10,2},{3,11},{11,3},{4,12},{12,4},... | collective-permute-start | bytes 12296 | tf_op jit(solution)/shard_map/ppermute | solution.py:209
  26.6 8.0 %collective-permute-start.13 = (f32[2,512]{1,0:T(2,128)S(1)}, f32[2,512]{1,0:T(2,128)S(1)}, u32[]{:S(2)}, u32[]{:S(2)}) collective-permute-start(f32[2,512]{1,0:T(2,128)S(1)} %shard_map.82.refs_0_), channel_id=1, source_target_pairs={{0,1},{1,0},{16,17},{17,16},{2,3},{3,2},{18,19},{19,18},{4,5},{5,4... | collective-permute-start | bytes 12296 | tf_op jit(solution)/shard_map/ppermute | solution.py:197
  27.9 4.9 %collective-permute-start.10 = (f32[2,256]{1,0:T(2,128)S(1)}, f32[2,256]{1,0:T(2,128)S(1)}, u32[]{:S(2)}, u32[]{:S(2)}) collective-permute-start(f32[2,256]{1,0:T(2,128)S(1)} %get-tuple-element.30.refs_0_), channel_id=1, source_target_pairs={{0,4},{2,6},{4,0},{6,2},{1,5},{3,7},{5,1},{7,3},{8,12},{10,14},{12... | collective-permute-start | bytes 6152 | tf_op jit(solution)/shard_map/ppermute | solution.py:194
  32.8 3.7 %collective-permute-start.11 = (f32[2,256]{1,0:T(2,128)S(1)}, f32[2,256]{1,0:T(2,128)S(1)}, u32[]{:S(2)}, u32[]{:S(2)}) collective-permute-start(f32[2,256]{1,0:T(2,128)S(1)} %shard_map.80.refs_0_), channel_id=1, source_target_pairs={{0,2},{2,0},{4,6},{6,4},{1,3},{3,1},{5,7},{7,5},{8,10},{10,8},{12,... | collective-permute-start | bytes 6152 | tf_op jit(solution)/shard_map/ppermute | solution.py:194
  34.6 3.7 %collective-permute-start.14 = (f32[2,512]{1,0:T(2,128)S(1)}, f32[2,512]{1,0:T(2,128)S(1)}, u32[]{:S(2)}, u32[]{:S(2)}) collective-permute-start(f32[2,512]{1,0:T(2,128)S(1)} %shard_map.83.refs_1_), channel_id=1, source_target_pairs={{0,16},{1,17},{16,0},{17,1},{2,18},{3,19},{18,2},{19,3},{4,20},{5,... | collective-permute-start | bytes 12296 | tf_op jit(solution)/shard_map/ppermute | solution.py:197
  36.4 12.9 %copy-start.1 = (bf16[64,512]{1,0:T(8,128)(2,1)S(1)}, bf16[64,512]{1,0:T(8,128)(2,1)}, u32[]{:S(2)}) copy-start(bf16[64,512]{1,0:T(8,128)(2,1)} %raw_ref.3) | copy-start | bytes 196612
  39.3 4.5 %collective-permute-start.15 = (bf16[4,64,512]{2,1,0:T(8,128)(2,1)S(1)}, bf16[4,64,512]{2,1,0:T(8,128)(2,1)S(1)}, u32[]{:S(2)}, u32[]{:S(2)}) collective-permute-start(bf16[4,64,512]{2,1,0:T(8,128)(2,1)S(1)} %get-tuple-element.33), channel_id=1, source_target_pairs={{0,8},{8,0},{1,9},{9,1},{2,10},{10,2},{3,11},{11,3},{4,12},{12,4},... | collective-permute-start | bytes 786440 | tf_op jit(solution)/shard_map/ppermute | solution.py:209
  39.4 6.6 %collective-permute-start.19 = (bf16[64,512]{1,0:T(8,128)(2,1)S(1)}, bf16[64,512]{1,0:T(8,128)(2,1)S(1)}, u32[]{:S(2)}, u32[]{:S(2)}) collective-permute-start(bf16[64,512]{1,0:T(8,128)(2,1)S(1)} %get-tuple-element.39), channel_id=1, source_target_pairs={{0,6},{2,4},{4,2},{6,0},{1,7},{3,5},{5,3},{7,1},{8,14},{10,12},{12... | collective-permute-start | bytes 196616 | tf_op jit(solution)/shard_map/ppermute | solution.py:194
  42.1 7.2 %collective-permute-start.20 = (bf16[64,512]{1,0:T(8,128)(2,1)S(1)}, bf16[64,512]{1,0:T(8,128)(2,1)S(1)}, u32[]{:S(2)}, u32[]{:S(2)}) collective-permute-start(bf16[64,512]{1,0:T(8,128)(2,1)S(1)} %get-tuple-element.40), channel_id=1, source_target_pairs={{0,4},{2,6},{4,0},{6,2},{1,5},{3,7},{5,1},{7,3},{8,12},{10,14},{12... | collective-permute-start | bytes 196616 | tf_op jit(solution)/shard_map/ppermute | solution.py:194
  42.5 6.8 %collective-permute-start.21 = (bf16[64,512]{1,0:T(8,128)(2,1)S(1)}, bf16[64,512]{1,0:T(8,128)(2,1)S(1)}, u32[]{:S(2)}, u32[]{:S(2)}) collective-permute-start(bf16[64,512]{1,0:T(8,128)(2,1)S(1)} %get-tuple-element.41), channel_id=1, source_target_pairs={{0,2},{2,0},{4,6},{6,4},{1,3},{3,1},{5,7},{7,5},{8,10},{10,8},{12,... | collective-permute-start | bytes 196616 | tf_op jit(solution)/shard_map/ppermute | solution.py:194
  43.9 6.2 %collective-permute-start.16 = (bf16[64,512]{1,0:T(8,128)(2,1)S(1)}, bf16[64,512]{1,0:T(8,128)(2,1)S(1)}, u32[]{:S(2)}, u32[]{:S(2)}) collective-permute-start(bf16[64,512]{1,0:T(8,128)(2,1)S(1)} %get-tuple-element.35), channel_id=1, source_target_pairs={{0,17},{1,16},{16,1},{17,0},{2,19},{3,18},{18,3},{19,2},{4,21},{5,... | collective-permute-start | bytes 196616 | tf_op jit(solution)/shard_map/ppermute | solution.py:197
  45.5 4.7 %collective-permute-start.17 = (bf16[64,512]{1,0:T(8,128)(2,1)S(1)}, bf16[64,512]{1,0:T(8,128)(2,1)S(1)}, u32[]{:S(2)}, u32[]{:S(2)}) collective-permute-start(bf16[64,512]{1,0:T(8,128)(2,1)S(1)} %get-tuple-element.36), channel_id=1, source_target_pairs={{0,16},{1,17},{16,0},{17,1},{2,18},{3,19},{18,2},{19,3},{4,20},{5,... | collective-permute-start | bytes 196616 | tf_op jit(solution)/shard_map/ppermute | solution.py:197
  46.0 4.3 %collective-permute-start.18 = (bf16[64,512]{1,0:T(8,128)(2,1)S(1)}, bf16[64,512]{1,0:T(8,128)(2,1)S(1)}, u32[]{:S(2)}, u32[]{:S(2)}) collective-permute-start(bf16[64,512]{1,0:T(8,128)(2,1)S(1)} %get-tuple-element.37), channel_id=1, source_target_pairs={{0,1},{1,0},{16,17},{17,16},{2,3},{3,2},{18,19},{19,18},{4,5},{5,4... | collective-permute-start | bytes 196616 | tf_op jit(solution)/shard_map/ppermute | solution.py:197
  49.3 0.9 %copy-start = (bf16[64,512]{1,0:T(8,128)(2,1)S(1)}, bf16[64,512]{1,0:T(8,128)(2,1)}, u32[]{:S(2)}) copy-start(bf16[64,512]{1,0:T(8,128)(2,1)} %raw_ref.2) | copy-start | bytes 196612

commit v4 on v2

--- a/solution.py
+++ b/solution.py
@@ -13,7 +13,7 @@
 EVERY = ("y", "core", "z", "x")
 F32 = jnp.float32
 BF16 = jnp.bfloat16
-MANY = 1 << 35
+FEW, SOME, MANY = 1 << 10, 1 << 31, 1 << 35
 
 
 def physical_mesh(mesh):
@@ -51,7 +51,7 @@
     squares = len(blocks) // 2
     core = core_ref[0]
     for s in range(squares):
-        at = jnp.bitwise_xor(square_ref[0], s)
+        at = jnp.bitwise_xor(square_ref[0], squares - 1 - s)
         for ref, half in ((blocks[s], core), (blocks[squares + s], 1 - core)):
             row = pl.multiple_of((half * squares + at) * own, own)
             put_units(ref[...], pupil_ref, master_ref, row)
@@ -109,17 +109,15 @@
 
 
 def weight_kernel(core_ref, z_ref, scale_ref, teach_ref, image_ref, text_ref, *refs):
-    col_ref, row_refs = refs[0], refs[1:3]
-    keep_ref, send_ref, own_text_ref = refs[3:6]
-    text_out_refs = refs[6:-2]
+    col_ref, row_ref, keep_ref, send_ref, own_text_ref = refs[:5]
+    text_out_refs = refs[5:-2]
     image_part_ref, text_part_ref = refs[-2:]
     squares, own, _ = keep_ref.shape
     scale = scale_ref[0]
     images = 2 * squares * own
     step = min(512, images)
     col = col_ref[...]
-    rows = join_lse([ref[...] for ref in row_refs])
-    rows = jnp.concatenate([rows] * 4, axis=0)
+    rows = jnp.concatenate([row_ref[...]] * 4, axis=0)
     text = text_ref[...]
     for at in range(0, images, step):
         row = jnp.transpose(rows[:, at : at + step])
@@ -233,7 +231,7 @@
         raw_text = side_by_side(student_text, teacher_text)
         raw_texts = gather_line(raw_text)
         raw_image = side_by_side(student_image, teacher_image)
-        same = [raw_image] + [to_square(raw_image, s) for s in range(1, squares)]
+        same = [to_square(raw_image, s) for s in reversed(range(1, squares))] + [raw_image]
         other = [to_sibling(block) for block in same]
 
         pupil_text, master_text = call(
@@ -263,28 +261,27 @@
         )
         def joined(parts, flops):
             out = shaped(parts[0].shape, F32)
-            return call(join_kernel, out, parts, [vmem] * 2, vmem, flops=flops)
-
-        row_lses = [row_lse, to_sibling(row_lse)]
-        for s in reversed(bits(squares)):
-            row_lse = joined(row_lses, 1 << 10)
-            row_lses = [row_lse, to_square(row_lse, s)]
+            return call(join_kernel, out, parts, [vmem] * len(parts), vmem, flops=flops)
+
+        row_lse = joined([row_lse, to_sibling(row_lse)], FEW)
+        row_lses = [to_square(row_lse, s) for s in reversed(range(1, squares))]
+        row_lse = joined([row_lse, *row_lses], MANY)
         for s in bits(depth):
-            col_lse = joined([col_lse, to_line(col_lse, s)], MANY if s == 1 else 1 << 31)
+            col_lse = joined([col_lse, to_line(col_lse, s)], FEW if s == 1 else SOME)
         block = shaped((own, width), F32)
         sent = shaped((own, width), BF16)
         kept, for_sibling, own_text, *for_line = call(
             weight_kernel,
             (shaped((squares, own, width), F32), shaped((squares, own, width), BF16), block)
             + (sent,) * (depth - 1),
-            (core, z, student_scale, teach, pupil_image, pupil_text, col_lse, *row_lses),
-            [smem] * 3 + [vmem] * 6,
+            (core, z, student_scale, teach, pupil_image, pupil_text, col_lse, row_lse),
+            [smem] * 3 + [vmem] * 5,
             vmem,
             (pltpu.VMEM((images, width), F32), pltpu.VMEM((texts, width), F32)),
             grant,
         )
-        text_parts = [own_text] + [to_line(part, s + 1) for s, part in enumerate(for_line)]
-        text_grad = call(sum_kernel, block, text_parts, [vmem] * depth, vmem, flops=MANY)
+        text_parts = [to_line(part, s + 1) for s, part in enumerate(for_line)]
+        text_grad = call(sum_kernel, block, (own_text, *text_parts), [vmem] * depth, vmem, flops=MANY)
         own_image, *for_square = call(
             pair_kernel,
             (block,) + (sent,) * (squares - 1),
@@ -292,11 +289,11 @@
             [smem] + [vmem] * 2,
             vmem,
         )
-        image_parts = [own_image] + [to_square(part, s + 1) for s, part in enumerate(for_square)]
+        image_parts = [to_square(part, s + 1) for s, part in reversed(list(enumerate(for_square)))]
         return call(
             back_kernel,
             (block, block),
-            (student_image, student_text, text_grad, *image_parts),
+            (student_image, student_text, text_grad, own_image, *image_parts),
             [vmem] * (3 + squares),
             vmem,
         )

time: 50.9 us -> 49.9 us (0.980)
  waiting for transfers between devices: 14.4 us -> 13 us
    ppermute x8 -> x9, waiting for transfers between devices: 6.14 us -> 3.35 us  [to_square(): return lax.ppermute(value, SQUARE, [(q, q ^ step) for q in range(squares)])]
    ppermute x8, waiting for transfers between devices: 8.26 us -> 9.69 us  [to_line(): return lax.ppermute(value, LINE, [(z, z ^ step) for z in range(depth)])]
    ppermute x8 -> x9, starting transfers between devices: 10.3 us -> 10.7 us  [to_square(): return lax.ppermute(value, SQUARE, [(q, q ^ step) for q in range(squares)])]
  transfers between devices with their start and end apart: 22 -> 23, of which waited for: 9 -> 10; matrix products, arithmetic and copies ran while one was open for 2% -> 2% of each run, Pallas kernels for 1% -> 1%
where the time goes in v4:
time: 49.9 us; the launch traced here: 49.7 us
  starting transfers between devices  28.3 us (57%)
  waiting for transfers between devices  13 us (26%)
  Pallas kernels  4.34 us (9%)
  between operations  2.07 us (4%)
  other arithmetic  1.87 us (4%)
    ppermute x8, starting transfers between devices, to_line(): return lax.ppermute(value, LINE, [(z, z ^ step) for z in range(depth)])  16.5 us
    ppermute x9, starting transfers between devices, to_square(): return lax.ppermute(value, SQUARE, [(q, q ^ step) for q in range(squares)])  10.7 us
    ppermute x8, waiting for transfers between devices, to_line(): return lax.ppermute(value, LINE, [(z, z ^ step) for z in range(depth)])  9.69 us
    pallas_call x11, Pallas kernels, call(): pl.pallas_call(kernel, out_shape=outs, in_specs=specs, out_specs=jax.tree...  4.34 us
    ppermute x9, waiting for transfers between devices, to_square(): return lax.ppermute(value, SQUARE, [(q, q ^ step) for q in range(squares)])  3.35 us
    max x2, other arithmetic, side_by_side(): jnp.maximum(lax.pad(left, lowest, ((0, 0, 0), (0, right_width, 0))), lax....  1.87 us
    ppermute x6, starting transfers between devices, to_sibling(): return lax.ppermute(value, 'core', [(0, 1), (1, 0)])  1.15 us
  transfers between devices with their start and end apart: 23, of which 10 were waited for; matrix products, arithmetic and copies ran while one was open for 2% of the time, Pallas kernels for 1%

profile of v4, /device:TPU:0, one launch (start us, length us, event | category | flops | bytes accessed | tf_op | source)
XLA Modules:
  0.0 49.7 jit_solution(663370009627422120)
XLA Ops:
  0.6 0.9 %pad_maximum_fusion.1.refs_0_ = bf16[64,1792]{1,0:T(8,128)(2,1)S(1)} fusion(bf16[64,1280]{1,0:T(8,128)(2,1)} %param.9, bf16[64,512]{1,0:T(8,128)(2,1)} %raw_text_ref.1), kind=kLoop, calls=%fused_computation.1 | loop fusion | flops 458752 | bytes 458752 | tf_op jit(solution)/shard_map/max | solution.py:35
  1.6 4.1 %collective-permute-start = (bf16[64,1792]{1,0:T(8,128)(2,1)S(1)}, bf16[64,1792]{1,0:T(8,128)(2,1)S(1)}, u32[]{:S(2)}, u32[]{:S(2)}) collective-permute-start(bf16[64,1792]{1,0:T(8,128)(2,1)S(1)} %pad_maximum_fusion.1.refs_0_), channel_id=1, source_target_pairs={{0,4},{2,6},{4,0},{6,2},{1,5},{3,7},{5,1},{7,3},{8,12},{10,14},{12... | collective-permute-start | bytes 688136 | tf_op jit(solution)/shard_map/ppermute | solution.py:202
  5.7 1.6 %collective-permute-start.1 = (bf16[64,1792]{1,0:T(8,128)(2,1)S(1)}, bf16[64,1792]{1,0:T(8,128)(2,1)S(1)}, u32[]{:S(2)}, u32[]{:S(2)}) collective-permute-start(bf16[64,1792]{1,0:T(8,128)(2,1)S(1)} %pad_maximum_fusion.1.refs_0_), channel_id=1, source_target_pairs={{0,2},{2,0},{4,6},{6,4},{1,3},{3,1},{5,7},{7,5},{8,10},{10,8},{12,... | collective-permute-start | bytes 688136 | tf_op jit(solution)/shard_map/ppermute | solution.py:202
  7.2 0.9 %pad_maximum_fusion.refs_3_ = bf16[64,1792]{1,0:T(8,128)(2,1)S(1)} fusion(bf16[64,1280]{1,0:T(8,128)(2,1)} %param.8, bf16[64,512]{1,0:T(8,128)(2,1)} %raw_image_ref.1), kind=kLoop, calls=%fused_computation | loop fusion | flops 458752 | bytes 458752 | tf_op jit(solution)/shard_map/max | solution.py:35
  8.2 2.5 %collective-permute-start.3 = (bf16[64,1792]{1,0:T(8,128)(2,1)S(1)}, bf16[64,1792]{1,0:T(8,128)(2,1)S(1)}, u32[]{:S(2)}, u32[]{:S(2)}) collective-permute-start(bf16[64,1792]{1,0:T(8,128)(2,1)S(1)} %pad_maximum_fusion.refs_3_), channel_id=1, source_target_pairs={{0,17},{1,16},{16,1},{17,0},{2,19},{3,18},{18,3},{19,2},{4,21},{5,... | collective-permute-start | bytes 688136 | tf_op jit(solution)/shard_map/ppermute | solution.py:205
  11.7 4.6 %collective-permute-done.refs_2_ = bf16[64,1792]{1,0:T(8,128)(2,1)S(1)} collective-permute-done((bf16[64,1792]{1,0:T(8,128)(2,1)S(1)}, bf16[64,1792]{1,0:T(8,128)(2,1)S(1)}, u32[]{:S(2)}, u32[]{:S(2)}) %collective-permute-start) | collective-permute-done | bytes 229408 | tf_op jit(solution)/shard_map/ppermute | solution.py:202
  16.5 1.5 %collective-permute-start.2 = (bf16[64,1792]{1,0:T(8,128)(2,1)S(1)}, bf16[64,1792]{1,0:T(8,128)(2,1)S(1)}, u32[]{:S(2)}, u32[]{:S(2)}) collective-permute-start(bf16[64,1792]{1,0:T(8,128)(2,1)S(1)} %collective-permute-done.refs_2_), channel_id=1, source_target_pairs={{0,2},{2,0},{4,6},{6,4},{1,3},{3,1},{5,7},{7,5},{8,10},{10,8},{12,... | collective-permute-start | bytes 688136 | tf_op jit(solution)/shard_map/ppermute | solution.py:202
  19.3 0.6 %collective-permute-start.6 = (bf16[64,1792]{1,0:T(8,128)(2,1)S(1)}, bf16[64,1792]{1,0:T(8,128)(2,1)S(1)}, u32[]{:S(2)}, u32[]{:S(2)}) collective-permute-start(bf16[64,1792]{1,0:T(8,128)(2,1)S(1)} %collective-permute-done.3.refs_0_), channel_id=1, source_target_pairs={{0,8},{8,0},{1,9},{9,1},{2,10},{10,2},{3,11},{11,3},{4,12},{12,4},... | collective-permute-start | bytes 688136 | tf_op jit(solution)/shard_map/ppermute | solution.py:217
  19.9 1.0 %collective-permute-done.4.refs_1_ = bf16[64,1792]{1,0:T(8,128)(2,1)S(1)} collective-permute-done((bf16[64,1792]{1,0:T(8,128)(2,1)S(1)}, bf16[64,1792]{1,0:T(8,128)(2,1)S(1)}, u32[]{:S(2)}, u32[]{:S(2)}) %collective-permute-start.4) | collective-permute-done | bytes 229408 | tf_op jit(solution)/shard_map/ppermute | solution.py:205
  21.4 1.7 %collective-permute-done.2.refs_3_ = bf16[64,1792]{1,0:T(8,128)(2,1)S(1)} collective-permute-done((bf16[64,1792]{1,0:T(8,128)(2,1)S(1)}, bf16[64,1792]{1,0:T(8,128)(2,1)S(1)}, u32[]{:S(2)}, u32[]{:S(2)}) %collective-permute-start.2) | collective-permute-done | bytes 229408 | tf_op jit(solution)/shard_map/ppermute | solution.py:202
  23.4 0.6 %shard_map.78 = (bf16[512,512]{1,0:T(8,128)(2,1)S(1)}, bf16[512,1280]{1,0:T(8,128)(2,1)S(1)}) custom-call(s32[1]{0:T(128)} %bitcast.core_ref, s32[1]{0:T(128)} %bitcast.4.square_ref, bf16[64,1792]{1,0:T(8,128)(2,1)S(1)} %collective-permute-done.3.refs_0_, bf16[64,1792]{1,0:T(8,128)(2,1)S(1)} %collective-permute-done.4.refs_1_, ...), custom_call_target="tpu_custom_call" | custom-call | flops 1048576 | bytes 1048576 | tf_op jit(solution)/shard_map/pallas_call | solution.py:181
  24.0 1.4 %shard_map.79 = (f32[512,256]{1,0:T(8,128)S(1)}, f32[2,512]{1,0:T(2,128)S(1)}, f32[2,256]{1,0:T(2,128)S(1)}) custom-call(f32[1]{0:T(128)} %bitcast.5.teacher_scale_ref, f32[1]{0:T(128)} %bitcast.6.student_scale_ref, bf16[256,512]{1,0:T(8,128)(2,1)S(1)} %get-tuple-element.25.pupil_text_ref.text_ref, bf16[256,1280]{1,0:T(8,128)(2,1)S(1)} %get-tuple-element.26.master_text_ref, ...), custom_call_target="tpu_custom_call" | custom-call | flops 1048576 | bytes 1048576 | tf_op jit(solution)/shard_map/pallas_call | solution.py:181
  25.4 3.1 %collective-permute-start.10 = (f32[2,256]{1,0:T(2,128)S(1)}, f32[2,256]{1,0:T(2,128)S(1)}, u32[]{:S(2)}, u32[]{:S(2)}) collective-permute-start(f32[2,256]{1,0:T(2,128)S(1)} %get-tuple-element.30.refs_0_), channel_id=1, source_target_pairs={{0,4},{2,6},{4,0},{6,2},{1,5},{3,7},{5,1},{7,3},{8,12},{10,14},{12... | collective-permute-start | bytes 6152 | tf_op jit(solution)/shard_map/ppermute | solution.py:202
  28.5 2.5 %collective-permute-start.13 = (f32[2,512]{1,0:T(2,128)S(1)}, f32[2,512]{1,0:T(2,128)S(1)}, u32[]{:S(2)}, u32[]{:S(2)}) collective-permute-start(f32[2,512]{1,0:T(2,128)S(1)} %shard_map.82.refs_0_), channel_id=1, source_target_pairs={{0,17},{1,16},{16,1},{17,0},{2,19},{3,18},{18,3},{19,2},{4,21},{5,... | collective-permute-start | bytes 12296 | tf_op jit(solution)/shard_map/ppermute | solution.py:205
  32.1 1.8 %collective-permute-start.11 = (f32[2,256]{1,0:T(2,128)S(1)}, f32[2,256]{1,0:T(2,128)S(1)}, u32[]{:S(2)}, u32[]{:S(2)}) collective-permute-start(f32[2,256]{1,0:T(2,128)S(1)} %shard_map.80.refs_0_), channel_id=1, source_target_pairs={{0,2},{2,0},{4,6},{6,4},{1,3},{3,1},{5,7},{7,5},{8,10},{10,8},{12,... | collective-permute-start | bytes 6152 | tf_op jit(solution)/shard_map/ppermute | solution.py:202
  33.9 1.8 %collective-permute-done.11.refs_1_ = f32[2,256]{1,0:T(2,128)S(1)} collective-permute-done((f32[2,256]{1,0:T(2,128)S(1)}, f32[2,256]{1,0:T(2,128)S(1)}, u32[]{:S(2)}, u32[]{:S(2)}) %collective-permute-start.11) | collective-permute-done | bytes 2080 | tf_op jit(solution)/shard_map/ppermute | solution.py:202
  35.8 1.1 %shard_map.84 = (f32[4,64,512]{2,1,0:T(8,128)S(1)}, bf16[4,64,512]{2,1,0:T(8,128)(2,1)S(1)}, f32[64,512]{1,0:T(8,128)S(1)}, bf16[64,512]{1,0:T(8,128)(2,1)S(1)},...) custom-call(s32[1]{0:T(128)} %bitcast.core_ref, s32[1]{0:T(128)} %bitcast.1.z_ref, f32[1]{0:T(128)} %bitcast.7.scale_ref, ...), custom_call_target="tpu_custom_call" | custom-call | flops 1048576 | bytes 1048576 | tf_op jit(solution)/shard_map/pallas_call | solution.py:181
  37.0 1.8 %collective-permute-start.16 = (bf16[64,512]{1,0:T(8,128)(2,1)S(1)}, bf16[64,512]{1,0:T(8,128)(2,1)S(1)}, u32[]{:S(2)}, u32[]{:S(2)}) collective-permute-start(bf16[64,512]{1,0:T(8,128)(2,1)S(1)} %get-tuple-element.33), channel_id=1, source_target_pairs={{0,2},{2,0},{4,6},{6,4},{1,3},{3,1},{5,7},{7,5},{8,10},{10,8},{12,... | collective-permute-start | bytes 196616 | tf_op jit(solution)/shard_map/ppermute | solution.py:202
  38.8 1.1 %collective-permute-start.17 = (bf16[64,512]{1,0:T(8,128)(2,1)S(1)}, bf16[64,512]{1,0:T(8,128)(2,1)S(1)}, u32[]{:S(2)}, u32[]{:S(2)}) collective-permute-start(bf16[64,512]{1,0:T(8,128)(2,1)S(1)} %get-tuple-element.34), channel_id=1, source_target_pairs={{0,4},{2,6},{4,0},{6,2},{1,5},{3,7},{5,1},{7,3},{8,12},{10,14},{12... | collective-permute-start | bytes 196616 | tf_op jit(solution)/shard_map/ppermute | solution.py:202
  39.9 1.6 %collective-permute-start.18 = (bf16[64,512]{1,0:T(8,128)(2,1)S(1)}, bf16[64,512]{1,0:T(8,128)(2,1)S(1)}, u32[]{:S(2)}, u32[]{:S(2)}) collective-permute-start(bf16[64,512]{1,0:T(8,128)(2,1)S(1)} %get-tuple-element.35), channel_id=1, source_target_pairs={{0,6},{2,4},{4,2},{6,0},{1,7},{3,5},{5,3},{7,1},{8,14},{10,12},{12... | collective-permute-start | bytes 196616 | tf_op jit(solution)/shard_map/ppermute | solution.py:202
  41.5 2.5 %collective-permute-start.20 = (bf16[64,512]{1,0:T(8,128)(2,1)S(1)}, bf16[64,512]{1,0:T(8,128)(2,1)S(1)}, u32[]{:S(2)}, u32[]{:S(2)}) collective-permute-start(bf16[64,512]{1,0:T(8,128)(2,1)S(1)} %get-tuple-element.39), channel_id=1, source_target_pairs={{0,17},{1,16},{16,1},{17,0},{2,19},{3,18},{18,3},{19,2},{4,21},{5,... | collective-permute-start | bytes 196616 | tf_op jit(solution)/shard_map/ppermute | solution.py:205
  45.1 1.4 %collective-permute-done.17.refs_2_ = bf16[64,512]{1,0:T(8,128)(2,1)S(1)} collective-permute-done((bf16[64,512]{1,0:T(8,128)(2,1)S(1)}, bf16[64,512]{1,0:T(8,128)(2,1)S(1)}, u32[]{:S(2)}, u32[]{:S(2)}) %collective-permute-start.17) | collective-permute-done | bytes 65568 | tf_op jit(solution)/shard_map/ppermute | solution.py:202
  46.8 1.4 %collective-permute-done.21.refs_2_ = bf16[64,512]{1,0:T(8,128)(2,1)S(1)} collective-permute-done((bf16[64,512]{1,0:T(8,128)(2,1)S(1)}, bf16[64,512]{1,0:T(8,128)(2,1)S(1)}, u32[]{:S(2)}, u32[]{:S(2)}) %collective-permute-start.21) | collective-permute-done | bytes 65568 | tf_op jit(solution)/shard_map/ppermute | solution.py:205
  48.8 0.9 %shard_map.87 = (f32[64,512]{1,0:T(8,128)}, f32[64,512]{1,0:T(8,128)}) custom-call(bf16[64,512]{1,0:T(8,128)(2,1)S(1)} %copy-done, bf16[64,512]{1,0:T(8,128)(2,1)S(1)} %copy-done.1, f32[64,512]{1,0:T(8,128)S(1)} %shard_map.85.text_ref, f32[64,512]{1,0:T(8,128)S(1)} %get-tuple-element.38.refs_0_, bf16[64,512]{1,0:T(8,128)(2,1)S(1)} %collective-permute-done.20.refs_1_, ...), custom_call_target="tpu_custom_call" | custom-call | flops 1048576 | bytes 1048576 | tf_op jit(solution)/shard_map/pallas_call | solution.py:181
  (39 shorter events, 5.3 us)
Async XLA Ops:
  1.6 14.7 %collective-permute-start = (bf16[64,1792]{1,0:T(8,128)(2,1)S(1)}, bf16[64,1792]{1,0:T(8,128)(2,1)S(1)}, u32[]{:S(2)}, u32[]{:S(2)}) collective-permute-start(bf16[64,1792]{1,0:T(8,128)(2,1)S(1)} %pad_maximum_fusion.1.refs_0_), channel_id=1, source_target_pairs={{0,4},{2,6},{4,0},{6,2},{1,5},{3,7},{5,1},{7,3},{8,12},{10,14},{12... | collective-permute-start | bytes 688136 | tf_op jit(solution)/shard_map/ppermute | solution.py:202
  5.7 10.8 %collective-permute-start.1 = (bf16[64,1792]{1,0:T(8,128)(2,1)S(1)}, bf16[64,1792]{1,0:T(8,128)(2,1)S(1)}, u32[]{:S(2)}, u32[]{:S(2)}) collective-permute-start(bf16[64,1792]{1,0:T(8,128)(2,1)S(1)} %pad_maximum_fusion.1.refs_0_), channel_id=1, source_target_pairs={{0,2},{2,0},{4,6},{6,4},{1,3},{3,1},{5,7},{7,5},{8,10},{10,8},{12,... | collective-permute-start | bytes 688136 | tf_op jit(solution)/shard_map/ppermute | solution.py:202
  8.2 11.1 %collective-permute-start.3 = (bf16[64,1792]{1,0:T(8,128)(2,1)S(1)}, bf16[64,1792]{1,0:T(8,128)(2,1)S(1)}, u32[]{:S(2)}, u32[]{:S(2)}) collective-permute-start(bf16[64,1792]{1,0:T(8,128)(2,1)S(1)} %pad_maximum_fusion.refs_3_), channel_id=1, source_target_pairs={{0,17},{1,16},{16,1},{17,0},{2,19},{3,18},{18,3},{19,2},{4,21},{5,... | collective-permute-start | bytes 688136 | tf_op jit(solution)/shard_map/ppermute | solution.py:205
  10.7 10.2 %collective-permute-start.4 = (bf16[64,1792]{1,0:T(8,128)(2,1)S(1)}, bf16[64,1792]{1,0:T(8,128)(2,1)S(1)}, u32[]{:S(2)}, u32[]{:S(2)}) collective-permute-start(bf16[64,1792]{1,0:T(8,128)(2,1)S(1)} %pad_maximum_fusion.refs_3_), channel_id=1, source_target_pairs={{0,16},{1,17},{16,0},{17,1},{2,18},{3,19},{18,2},{19,3},{4,20},{5,... | collective-permute-start | bytes 688136 | tf_op jit(solution)/shard_map/ppermute | solution.py:205
  11.2 9.7 %collective-permute-start.5 = (bf16[64,1792]{1,0:T(8,128)(2,1)S(1)}, bf16[64,1792]{1,0:T(8,128)(2,1)S(1)}, u32[]{:S(2)}, u32[]{:S(2)}) collective-permute-start(bf16[64,1792]{1,0:T(8,128)(2,1)S(1)} %pad_maximum_fusion.refs_3_), channel_id=1, source_target_pairs={{0,1},{1,0},{16,17},{17,16},{2,3},{3,2},{18,19},{19,18},{4,5},{5,4... | collective-permute-start | bytes 688136 | tf_op jit(solution)/shard_map/ppermute | solution.py:205
  16.5 6.5 %collective-permute-start.2 = (bf16[64,1792]{1,0:T(8,128)(2,1)S(1)}, bf16[64,1792]{1,0:T(8,128)(2,1)S(1)}, u32[]{:S(2)}, u32[]{:S(2)}) collective-permute-start(bf16[64,1792]{1,0:T(8,128)(2,1)S(1)} %collective-permute-done.refs_2_), channel_id=1, source_target_pairs={{0,2},{2,0},{4,6},{6,4},{1,3},{3,1},{5,7},{7,5},{8,10},{10,8},{12,... | collective-permute-start | bytes 688136 | tf_op jit(solution)/shard_map/ppermute | solution.py:202
  18.0 5.3 %collective-permute-start.9 = (bf16[64,1792]{1,0:T(8,128)(2,1)S(1)}, bf16[64,1792]{1,0:T(8,128)(2,1)S(1)}, u32[]{:S(2)}, u32[]{:S(2)}) collective-permute-start(bf16[64,1792]{1,0:T(8,128)(2,1)S(1)} %pad_maximum_fusion.refs_3_), channel_id=1, source_target_pairs={{0,8},{8,0},{1,9},{9,1},{2,10},{10,2},{3,11},{11,3},{4,12},{12,4},... | collective-permute-start | bytes 688136 | tf_op jit(solution)/shard_map/ppermute | solution.py:217
  19.3 4.0 %collective-permute-start.6 = (bf16[64,1792]{1,0:T(8,128)(2,1)S(1)}, bf16[64,1792]{1,0:T(8,128)(2,1)S(1)}, u32[]{:S(2)}, u32[]{:S(2)}) collective-permute-start(bf16[64,1792]{1,0:T(8,128)(2,1)S(1)} %collective-permute-done.3.refs_0_), channel_id=1, source_target_pairs={{0,8},{8,0},{1,9},{9,1},{2,10},{10,2},{3,11},{11,3},{4,12},{12,4},... | collective-permute-start | bytes 688136 | tf_op jit(solution)/shard_map/ppermute | solution.py:217
  20.8 2.5 %collective-permute-start.7 = (bf16[64,1792]{1,0:T(8,128)(2,1)S(1)}, bf16[64,1792]{1,0:T(8,128)(2,1)S(1)}, u32[]{:S(2)}, u32[]{:S(2)}) collective-permute-start(bf16[64,1792]{1,0:T(8,128)(2,1)S(1)} %collective-permute-done.4.refs_1_), channel_id=1, source_target_pairs={{0,8},{8,0},{1,9},{9,1},{2,10},{10,2},{3,11},{11,3},{4,12},{12,4},... | collective-permute-start | bytes 688136 | tf_op jit(solution)/shard_map/ppermute | solution.py:217
  20.9 2.4 %collective-permute-start.8 = (bf16[64,1792]{1,0:T(8,128)(2,1)S(1)}, bf16[64,1792]{1,0:T(8,128)(2,1)S(1)}, u32[]{:S(2)}, u32[]{:S(2)}) collective-permute-start(bf16[64,1792]{1,0:T(8,128)(2,1)S(1)} %collective-permute-done.5.refs_2_), channel_id=1, source_target_pairs={{0,8},{8,0},{1,9},{9,1},{2,10},{10,2},{3,11},{11,3},{4,12},{12,4},... | collective-permute-start | bytes 688136 | tf_op jit(solution)/shard_map/ppermute | solution.py:217
  25.3 3.2 %collective-permute-start.12 = (f32[2,512]{1,0:T(2,128)S(1)}, f32[2,512]{1,0:T(2,128)S(1)}, u32[]{:S(2)}, u32[]{:S(2)}) collective-permute-start(f32[2,512]{1,0:T(2,128)S(1)} %get-tuple-element.31.refs_0_), channel_id=1, source_target_pairs={{0,8},{8,0},{1,9},{9,1},{2,10},{10,2},{3,11},{11,3},{4,12},{12,4},... | collective-permute-start | bytes 12296 | tf_op jit(solution)/shard_map/ppermute | solution.py:217
  25.4 6.7 %collective-permute-start.10 = (f32[2,256]{1,0:T(2,128)S(1)}, f32[2,256]{1,0:T(2,128)S(1)}, u32[]{:S(2)}, u32[]{:S(2)}) collective-permute-start(f32[2,256]{1,0:T(2,128)S(1)} %get-tuple-element.30.refs_0_), channel_id=1, source_target_pairs={{0,4},{2,6},{4,0},{6,2},{1,5},{3,7},{5,1},{7,3},{8,12},{10,14},{12... | collective-permute-start | bytes 6152 | tf_op jit(solution)/shard_map/ppermute | solution.py:202
  28.5 7.2 %collective-permute-start.13 = (f32[2,512]{1,0:T(2,128)S(1)}, f32[2,512]{1,0:T(2,128)S(1)}, u32[]{:S(2)}, u32[]{:S(2)}) collective-permute-start(f32[2,512]{1,0:T(2,128)S(1)} %shard_map.82.refs_0_), channel_id=1, source_target_pairs={{0,17},{1,16},{16,1},{17,0},{2,19},{3,18},{18,3},{19,2},{4,21},{5,... | collective-permute-start | bytes 12296 | tf_op jit(solution)/shard_map/ppermute | solution.py:205
  31.1 4.7 %collective-permute-start.14 = (f32[2,512]{1,0:T(2,128)S(1)}, f32[2,512]{1,0:T(2,128)S(1)}, u32[]{:S(2)}, u32[]{:S(2)}) collective-permute-start(f32[2,512]{1,0:T(2,128)S(1)} %shard_map.82.refs_0_), channel_id=1, source_target_pairs={{0,16},{1,17},{16,0},{17,1},{2,18},{3,19},{18,2},{19,3},{4,20},{5,... | collective-permute-start | bytes 12296 | tf_op jit(solution)/shard_map/ppermute | solution.py:205
  31.6 4.2 %collective-permute-start.15 = (f32[2,512]{1,0:T(2,128)S(1)}, f32[2,512]{1,0:T(2,128)S(1)}, u32[]{:S(2)}, u32[]{:S(2)}) collective-permute-start(f32[2,512]{1,0:T(2,128)S(1)} %shard_map.82.refs_0_), channel_id=1, source_target_pairs={{0,1},{1,0},{16,17},{17,16},{2,3},{3,2},{18,19},{19,18},{4,5},{5,4... | collective-permute-start | bytes 12296 | tf_op jit(solution)/shard_map/ppermute | solution.py:205
  32.1 3.7 %collective-permute-start.11 = (f32[2,256]{1,0:T(2,128)S(1)}, f32[2,256]{1,0:T(2,128)S(1)}, u32[]{:S(2)}, u32[]{:S(2)}) collective-permute-start(f32[2,256]{1,0:T(2,128)S(1)} %shard_map.80.refs_0_), channel_id=1, source_target_pairs={{0,2},{2,0},{4,6},{6,4},{1,3},{3,1},{5,7},{7,5},{8,10},{10,8},{12,... | collective-permute-start | bytes 6152 | tf_op jit(solution)/shard_map/ppermute | solution.py:202
  36.9 4.5 %collective-permute-start.19 = (bf16[4,64,512]{2,1,0:T(8,128)(2,1)S(1)}, bf16[4,64,512]{2,1,0:T(8,128)(2,1)S(1)}, u32[]{:S(2)}, u32[]{:S(2)}) collective-permute-start(bf16[4,64,512]{2,1,0:T(8,128)(2,1)S(1)} %get-tuple-element.37), channel_id=1, source_target_pairs={{0,8},{8,0},{1,9},{9,1},{2,10},{10,2},{3,11},{11,3},{4,12},{12,4},... | collective-permute-start | bytes 786440 | tf_op jit(solution)/shard_map/ppermute | solution.py:217
  37.0 7.5 %collective-permute-start.16 = (bf16[64,512]{1,0:T(8,128)(2,1)S(1)}, bf16[64,512]{1,0:T(8,128)(2,1)S(1)}, u32[]{:S(2)}, u32[]{:S(2)}) collective-permute-start(bf16[64,512]{1,0:T(8,128)(2,1)S(1)} %get-tuple-element.33), channel_id=1, source_target_pairs={{0,2},{2,0},{4,6},{6,4},{1,3},{3,1},{5,7},{7,5},{8,10},{10,8},{12,... | collective-permute-start | bytes 196616 | tf_op jit(solution)/shard_map/ppermute | solution.py:202
  38.8 7.7 %collective-permute-start.17 = (bf16[64,512]{1,0:T(8,128)(2,1)S(1)}, bf16[64,512]{1,0:T(8,128)(2,1)S(1)}, u32[]{:S(2)}, u32[]{:S(2)}) collective-permute-start(bf16[64,512]{1,0:T(8,128)(2,1)S(1)} %get-tuple-element.34), channel_id=1, source_target_pairs={{0,4},{2,6},{4,0},{6,2},{1,5},{3,7},{5,1},{7,3},{8,12},{10,14},{12... | collective-permute-start | bytes 196616 | tf_op jit(solution)/shard_map/ppermute | solution.py:202
  39.9 6.6 %collective-permute-start.18 = (bf16[64,512]{1,0:T(8,128)(2,1)S(1)}, bf16[64,512]{1,0:T(8,128)(2,1)S(1)}, u32[]{:S(2)}, u32[]{:S(2)}) collective-permute-start(bf16[64,512]{1,0:T(8,128)(2,1)S(1)} %get-tuple-element.35), channel_id=1, source_target_pairs={{0,6},{2,4},{4,2},{6,0},{1,7},{3,5},{5,3},{7,1},{8,14},{10,12},{12... | collective-permute-start | bytes 196616 | tf_op jit(solution)/shard_map/ppermute | solution.py:202
  41.5 5.3 %collective-permute-start.20 = (bf16[64,512]{1,0:T(8,128)(2,1)S(1)}, bf16[64,512]{1,0:T(8,128)(2,1)S(1)}, u32[]{:S(2)}, u32[]{:S(2)}) collective-permute-start(bf16[64,512]{1,0:T(8,128)(2,1)S(1)} %get-tuple-element.39), channel_id=1, source_target_pairs={{0,17},{1,16},{16,1},{17,0},{2,19},{3,18},{18,3},{19,2},{4,21},{5,... | collective-permute-start | bytes 196616 | tf_op jit(solution)/shard_map/ppermute | solution.py:205
  44.0 4.3 %collective-permute-start.21 = (bf16[64,512]{1,0:T(8,128)(2,1)S(1)}, bf16[64,512]{1,0:T(8,128)(2,1)S(1)}, u32[]{:S(2)}, u32[]{:S(2)}) collective-permute-start(bf16[64,512]{1,0:T(8,128)(2,1)S(1)} %get-tuple-element.40), channel_id=1, source_target_pairs={{0,16},{1,17},{16,0},{17,1},{2,18},{3,19},{18,2},{19,3},{4,20},{5,... | collective-permute-start | bytes 196616 | tf_op jit(solution)/shard_map/ppermute | solution.py:205
  44.5 4.3 %collective-permute-start.22 = (bf16[64,512]{1,0:T(8,128)(2,1)S(1)}, bf16[64,512]{1,0:T(8,128)(2,1)S(1)}, u32[]{:S(2)}, u32[]{:S(2)}) collective-permute-start(bf16[64,512]{1,0:T(8,128)(2,1)S(1)} %get-tuple-element.41), channel_id=1, source_target_pairs={{0,1},{1,0},{16,17},{17,16},{2,3},{3,2},{18,19},{19,18},{4,5},{5,4... | collective-permute-start | bytes 196616 | tf_op jit(solution)/shard_map/ppermute | solution.py:205
  46.5 2.3 %copy-start.1 = (bf16[64,512]{1,0:T(8,128)(2,1)S(1)}, bf16[64,512]{1,0:T(8,128)(2,1)}, u32[]{:S(2)}) copy-start(bf16[64,512]{1,0:T(8,128)(2,1)} %raw_text_ref.1) | copy-start | bytes 196612
  (1 other events, 2.3 us)

commit v5 on v4

--- a/solution.py
+++ b/solution.py
@@ -44,17 +44,12 @@
     master_ref[pl.ds(at, own), :] = unit_rows(block[:, width:])[0].astype(BF16)
 
 
-def image_unit_kernel(core_ref, square_ref, *refs):
+def image_unit_kernel(square_ref, *refs):
     pupil_ref, master_ref = refs[-2:]
-    blocks = refs[:-2]
-    own = blocks[0].shape[0]
-    squares = len(blocks) // 2
-    core = core_ref[0]
-    for s in range(squares):
-        at = jnp.bitwise_xor(square_ref[0], squares - 1 - s)
-        for ref, half in ((blocks[s], core), (blocks[squares + s], 1 - core)):
-            row = pl.multiple_of((half * squares + at) * own, own)
-            put_units(ref[...], pupil_ref, master_ref, row)
+    own = refs[0].shape[0]
+    for s, ref in enumerate(refs[:-2]):
+        row = pl.multiple_of(jnp.bitwise_xor(square_ref[0], s) * own, own)
+        put_units(ref[...], pupil_ref, master_ref, row)
 
 
 def text_unit_kernel(z_ref, *refs):
@@ -79,28 +74,37 @@
     return top + jnp.log(sum(jnp.exp(p - top) for p in parts))
 
 
+def chunks(pairs):
+    half = pairs[0][0].shape[0]
+    step = min(512, half)
+    return [
+        (k * half + at, [pair[k] for pair in pairs], slice(at, at + step))
+        for k in range(2)
+        for at in range(0, half, step)
+    ]
+
+
 def logits_kernel(
-    teacher_scale_ref, student_scale_ref, pupil_text_ref, master_text_ref, pupil_image_ref,
-    master_image_ref, teach_ref, rows_ref, cols_ref,
+    teacher_scale_ref, student_scale_ref, pupil_text_ref, master_text_ref, pupil_same_ref,
+    pupil_other_ref, master_same_ref, master_other_ref, teach_ref, rows_ref, cols_ref,
 ):
-    images = pupil_image_ref.shape[0]
-    step = min(512, images)
-    for k, (scale_ref, image_ref, text_ref) in enumerate(
+    for k, (scale_ref, pair, text_ref) in enumerate(
         (
-            (teacher_scale_ref, master_image_ref, master_text_ref),
-            (student_scale_ref, pupil_image_ref, pupil_text_ref),
+            (teacher_scale_ref, (master_same_ref, master_other_ref), master_text_ref),
+            (student_scale_ref, (pupil_same_ref, pupil_other_ref), pupil_text_ref),
         )
     ):
         scale = scale_ref[0]
         text = text_ref[...]
         columns = []
-        for at in range(0, images, step):
-            image = image_ref[at : at + step, :]
+        for at, (ref,), part in chunks([pair]):
+            image = ref[part, :]
+            rows = slice(at, at + image.shape[0])
             logits = scale * product(image, text)
             if k == 0:
-                teach_ref[at : at + step, :] = logits
+                teach_ref[rows, :] = logits
             columns.append(block_lse(logits))
-            rows_ref[k : k + 1, at : at + step] = block_lse(scale * product(text, image))
+            rows_ref[k : k + 1, rows] = block_lse(scale * product(text, image))
         cols_ref[k : k + 1, :] = join_lse(columns)
 
 
@@ -108,37 +112,41 @@
     refs[-1][...] = join_lse([ref[...] for ref in refs[:-1]])
 
 
-def weight_kernel(core_ref, z_ref, scale_ref, teach_ref, image_ref, text_ref, *refs):
-    col_ref, row_ref, keep_ref, send_ref, own_text_ref = refs[:5]
-    text_out_refs = refs[5:-2]
-    image_part_ref, text_part_ref = refs[-2:]
-    squares, own, _ = keep_ref.shape
+def join_sibling_kernel(own_ref, other_ref, out_ref):
+    half = own_ref.shape[1] // 2
+    for here, there in ((slice(0, half), slice(half, None)), (slice(half, None), slice(0, half))):
+        out_ref[:, here] = join_lse([own_ref[:, here], other_ref[:, there]])
+
+
+def weight_kernel(z_ref, scale_ref, teach_ref, same_ref, other_ref, text_ref, col_ref, row_ref, *refs):
+    keep_ref, send_ref, own_text_ref = refs[:3]
+    text_out_refs = refs[3:-1]
+    text_part_ref = refs[-1]
+    squares, own, width = keep_ref.shape
     scale = scale_ref[0]
-    images = 2 * squares * own
-    step = min(512, images)
     col = col_ref[...]
     rows = jnp.concatenate([row_ref[...]] * 4, axis=0)
     text = text_ref[...]
-    for at in range(0, images, step):
-        row = jnp.transpose(rows[:, at : at + step])
-        image = image_ref[at : at + step, :]
-        teach = teach_ref[at : at + step, :]
+    pairs = [(same_ref, other_ref), (keep_ref, send_ref)]
+    pairs[1] = tuple(ref.reshape(squares * own, width) for ref in pairs[1])
+    text_part = None
+    for at, (image_ref, out_ref), part in chunks(pairs):
+        image = image_ref[part, :]
+        here = slice(at, at + image.shape[0])
+        row = jnp.transpose(rows[:, here])
+        teach = teach_ref[here, :]
         learn = scale * product(image, text)
         rows_part = jnp.exp(learn - row[:, 1:2]) - jnp.exp(teach - row[:, 0:1])
         cols_part = jnp.exp(learn - col[1:2, :]) - jnp.exp(teach - col[0:1, :])
         weight = (0.5 * (rows_part + cols_part)).astype(BF16)
-        image_part_ref[at : at + step, :] = scale * jnp.dot(weight, text, preferred_element_type=F32)
-        text_part = scale * lax.dot_general(
+        image_part = scale * jnp.dot(weight, text, preferred_element_type=F32)
+        out_ref[part, :] = image_part.astype(out_ref.dtype)
+        piece = scale * lax.dot_general(
             weight, image, (((0,), (0,)), ((), ())), preferred_element_type=F32
         )
-        if at:
-            text_part = text_part_ref[...] + text_part
-        text_part_ref[...] = text_part
-    core, z = core_ref[0], z_ref[0]
-    for i in range(squares):
-        for out_ref, half in ((keep_ref, core), (send_ref, 1 - core)):
-            row = pl.multiple_of((half * squares + i) * own, own)
-            out_ref[i] = image_part_ref[pl.ds(row, own), :].astype(out_ref.dtype)
+        text_part = piece if text_part is None else text_part + piece
+    text_part_ref[...] = text_part
+    z = z_ref[0]
     own_text_ref[...] = text_part_ref[pl.ds(pl.multiple_of(z * own, own), own), :]
     for s, ref in enumerate(text_out_refs):
         row = pl.multiple_of(jnp.bitwise_xor(z, s + 1) * own, own)
@@ -205,7 +213,7 @@
         return lax.ppermute(value, SQUARE, [(q, q ^ step) for q in range(squares)])
 
     def gather_line(value):
-        first = bits(depth)
+        first = bits(depth)[::-1]
         held = lax.optimization_barrier([value] + [to_line(value, s) for s in first])
         blocks = dict(zip([0] + first, held))
         for s in sorted(set(range(depth)) - set(blocks), key=lambda s: bin(s).count("1")):
@@ -220,7 +228,6 @@
         own, width = student_image.shape
         both = width + teacher_image.shape[1]
         images, texts = plane * own, depth * own
-        core = lax.axis_index("core").astype(jnp.int32).reshape(1)
         square = lax.axis_index("y") * lax.axis_size("x") + lax.axis_index("x")
         square = square.astype(jnp.int32).reshape(1)
         z = lax.axis_index("z").astype(jnp.int32).reshape(1)
@@ -231,8 +238,7 @@
         raw_text = side_by_side(student_text, teacher_text)
         raw_texts = gather_line(raw_text)
         raw_image = side_by_side(student_image, teacher_image)
-        same = [to_square(raw_image, s) for s in reversed(range(1, squares))] + [raw_image]
-        other = [to_sibling(block) for block in same]
+        blocks = [raw_image] + [to_square(raw_image, s) for s in range(1, squares)]
 
         pupil_text, master_text = call(
             text_unit_kernel,
@@ -243,28 +249,38 @@
             grant=grant,
             flops=MANY,
         )
-        pupil_image, master_image = call(
+        half = squares * own
+        pupil, master = call(
             image_unit_kernel,
-            (shaped((images, width), BF16), shaped((images, both - width), BF16)),
-            (core, square, *same, *other),
-            [smem] * 2 + [vmem] * plane,
+            (shaped((half, width), BF16), shaped((half, both - width), BF16)),
+            (square, *blocks),
+            [smem] + [vmem] * squares,
             vmem,
             grant=grant,
-        )
+            flops=MANY,
+        )
+        pupils, masters = (pupil, to_sibling(pupil)), (master, to_sibling(master))
         teach, row_lse, col_lse = call(
             logits_kernel,
             (shaped((images, texts), F32), shaped((2, images), F32), shaped((2, texts), F32)),
-            (teacher_scale, student_scale, pupil_text, master_text, pupil_image, master_image),
-            [smem, smem] + [vmem] * 4,
+            (teacher_scale, student_scale, pupil_text, master_text, *pupils, *masters),
+            [smem, smem] + [vmem] * 6,
             vmem,
             grant=grant,
         )
+
         def joined(parts, flops):
             out = shaped(parts[0].shape, F32)
             return call(join_kernel, out, parts, [vmem] * len(parts), vmem, flops=flops)
 
-        row_lse = joined([row_lse, to_sibling(row_lse)], FEW)
-        row_lses = [to_square(row_lse, s) for s in reversed(range(1, squares))]
+        row_lse = call(
+            join_sibling_kernel,
+            shaped(row_lse.shape, F32),
+            (row_lse, to_sibling(row_lse)),
+            [vmem] * 2,
+            vmem,
+        )
+        row_lses = [to_square(row_lse, s) for s in range(1, squares)]
         row_lse = joined([row_lse, *row_lses], MANY)
         for s in bits(depth):
             col_lse = joined([col_lse, to_line(col_lse, s)], FEW if s == 1 else SOME)
@@ -274,10 +290,10 @@
             weight_kernel,
             (shaped((squares, own, width), F32), shaped((squares, own, width), BF16), block)
             + (sent,) * (depth - 1),
-            (core, z, student_scale, teach, pupil_image, pupil_text, col_lse, row_lse),
-            [smem] * 3 + [vmem] * 5,
-            vmem,
-            (pltpu.VMEM((images, width), F32), pltpu.VMEM((texts, width), F32)),
+            (z, student_scale, teach, *pupils, pupil_text, col_lse, row_lse),
+            [smem] * 2 + [vmem] * 6,
+            vmem,
+            (pltpu.VMEM((texts, width), F32),),
             grant,
         )
         text_parts = [to_line(part, s + 1) for s, part in enumerate(for_line)]

time: 49.9 us -> 49.4 us (0.990)
  waiting for transfers between devices: 13 us -> 14.1 us
  other arithmetic: 1.87 us -> 0.99 us
    ppermute x9, waiting for transfers between devices: 3.35 us -> 4.31 us  [to_square(): return lax.ppermute(value, SQUARE, [(q, q ^ step) for q in range(squares)])]
    max x2, other arithmetic: 1.87 us -> 0.99 us  [side_by_side(): jnp.maximum(lax.pad(left, lowest, ((0, 0, 0), (0, right_width, 0))), lax....]
    ppermute x6 -> x4, starting transfers between devices: 1.15 us -> 0.71 us  [to_sibling(): return lax.ppermute(value, 'core', [(0, 1), (1, 0)])]
  transfers between devices with their start and end apart: 23 -> 21, of which waited for: 10 -> 10; matrix products, arithmetic and copies ran while one was open for 2% -> 0% of each run, Pallas kernels for 1% -> 1%
where the time goes in v5:
time: 49.4 us; the launch traced here: 49.2 us
  starting transfers between devices  27.9 us (56%)
  waiting for transfers between devices  14.1 us (29%)
  Pallas kernels  4.13 us (8%)
  between operations  2.08 us (4%)
  other arithmetic  0.99 us (2%)
    ppermute x8, starting transfers between devices, to_line(): return lax.ppermute(value, LINE, [(z, z ^ step) for z in range(depth)])  16.5 us
    ppermute x9, starting transfers between devices, to_square(): return lax.ppermute(value, SQUARE, [(q, q ^ step) for q in range(squares)])  10.7 us
    ppermute x8, waiting for transfers between devices, to_line(): return lax.ppermute(value, LINE, [(z, z ^ step) for z in range(depth)])  9.76 us
    ppermute x9, waiting for transfers between devices, to_square(): return lax.ppermute(value, SQUARE, [(q, q ^ step) for q in range(squares)])  4.31 us
    pallas_call x11, Pallas kernels, call(): pl.pallas_call(kernel, out_shape=outs, in_specs=specs, out_specs=jax.tree...  4.13 us
    max x2, other arithmetic, side_by_side(): jnp.maximum(lax.pad(left, lowest, ((0, 0, 0), (0, right_width, 0))), lax....  0.99 us
  transfers between devices with their start and end apart: 21, of which 10 were waited for; matrix products, arithmetic and copies ran while one was open for 0% of the time, Pallas kernels for 1%

profile of v5, /device:TPU:0, one launch (start us, length us, event | category | flops | bytes accessed | tf_op | source)
XLA Modules:
  0.0 49.2 jit_solution(2889234793018030206)
XLA Ops:
  0.6 1.0 %pad_maximum_fusion.1.refs_0_ = bf16[64,1792]{1,0:T(8,128)(2,1)S(1)} fusion(bf16[64,1280]{1,0:T(8,128)(2,1)} %param.9, bf16[64,512]{1,0:T(8,128)(2,1)} %raw_text_ref.1), kind=kLoop, calls=%fused_computation.1 | loop fusion | flops 458752 | bytes 458752 | tf_op jit(solution)/shard_map/max | solution.py:35
  1.6 4.1 %collective-permute-start.1 = (bf16[64,1792]{1,0:T(8,128)(2,1)S(1)}, bf16[64,1792]{1,0:T(8,128)(2,1)S(1)}, u32[]{:S(2)}, u32[]{:S(2)}) collective-permute-start(bf16[64,1792]{1,0:T(8,128)(2,1)S(1)} %pad_maximum_fusion.1.refs_0_), channel_id=1, source_target_pairs={{0,4},{2,6},{4,0},{6,2},{1,5},{3,7},{5,1},{7,3},{8,12},{10,14},{12... | collective-permute-start | bytes 688136 | tf_op jit(solution)/shard_map/ppermute | solution.py:210
  5.7 1.6 %collective-permute-start = (bf16[64,1792]{1,0:T(8,128)(2,1)S(1)}, bf16[64,1792]{1,0:T(8,128)(2,1)S(1)}, u32[]{:S(2)}, u32[]{:S(2)}) collective-permute-start(bf16[64,1792]{1,0:T(8,128)(2,1)S(1)} %pad_maximum_fusion.1.refs_0_), channel_id=1, source_target_pairs={{0,2},{2,0},{4,6},{6,4},{1,3},{3,1},{5,7},{7,5},{8,10},{10,8},{12,... | collective-permute-start | bytes 688136 | tf_op jit(solution)/shard_map/ppermute | solution.py:210
  7.3 2.5 %collective-permute-start.5 = (bf16[64,1792]{1,0:T(8,128)(2,1)S(1)}, bf16[64,1792]{1,0:T(8,128)(2,1)S(1)}, u32[]{:S(2)}, u32[]{:S(2)}) collective-permute-start(bf16[64,1792]{1,0:T(8,128)(2,1)S(1)} %pad_maximum_fusion.refs_0_), channel_id=1, source_target_pairs={{0,17},{1,16},{16,1},{17,0},{2,19},{3,18},{18,3},{19,2},{4,21},{5,... | collective-permute-start | bytes 688136 | tf_op jit(solution)/shard_map/ppermute | solution.py:213
  10.4 0.5 %collective-permute-start.3 = (bf16[64,1792]{1,0:T(8,128)(2,1)S(1)}, bf16[64,1792]{1,0:T(8,128)(2,1)S(1)}, u32[]{:S(2)}, u32[]{:S(2)}) collective-permute-start(bf16[64,1792]{1,0:T(8,128)(2,1)S(1)} %pad_maximum_fusion.refs_0_), channel_id=1, source_target_pairs={{0,1},{1,0},{16,17},{17,16},{2,3},{3,2},{18,19},{19,18},{4,5},{5,4... | collective-permute-start | bytes 688136 | tf_op jit(solution)/shard_map/ppermute | solution.py:213
  12.2 4.2 %collective-permute-done.1.refs_2_ = bf16[64,1792]{1,0:T(8,128)(2,1)S(1)} collective-permute-done((bf16[64,1792]{1,0:T(8,128)(2,1)S(1)}, bf16[64,1792]{1,0:T(8,128)(2,1)S(1)}, u32[]{:S(2)}, u32[]{:S(2)}) %collective-permute-start.1) | collective-permute-done | bytes 229408 | tf_op jit(solution)/shard_map/ppermute | solution.py:210
  16.5 1.5 %collective-permute-start.2 = (bf16[64,1792]{1,0:T(8,128)(2,1)S(1)}, bf16[64,1792]{1,0:T(8,128)(2,1)S(1)}, u32[]{:S(2)}, u32[]{:S(2)}) collective-permute-start(bf16[64,1792]{1,0:T(8,128)(2,1)S(1)} %collective-permute-done.1.refs_2_), channel_id=1, source_target_pairs={{0,2},{2,0},{4,6},{6,4},{1,3},{3,1},{5,7},{7,5},{8,10},{10,8},{12,... | collective-permute-start | bytes 688136 | tf_op jit(solution)/shard_map/ppermute | solution.py:210
  18.0 2.0 %collective-permute-done.4.refs_2_ = bf16[64,1792]{1,0:T(8,128)(2,1)S(1)} collective-permute-done((bf16[64,1792]{1,0:T(8,128)(2,1)S(1)}, bf16[64,1792]{1,0:T(8,128)(2,1)S(1)}, u32[]{:S(2)}, u32[]{:S(2)}) %collective-permute-start.4) | collective-permute-done | bytes 229408 | tf_op jit(solution)/shard_map/ppermute | solution.py:213
  21.0 2.1 %collective-permute-done.2.refs_3_ = bf16[64,1792]{1,0:T(8,128)(2,1)S(1)} collective-permute-done((bf16[64,1792]{1,0:T(8,128)(2,1)S(1)}, bf16[64,1792]{1,0:T(8,128)(2,1)S(1)}, u32[]{:S(2)}, u32[]{:S(2)}) %collective-permute-start.2) | collective-permute-done | bytes 229408 | tf_op jit(solution)/shard_map/ppermute | solution.py:210
  23.4 1.3 %shard_map.79 = (f32[512,256]{1,0:T(8,128)S(1)}, f32[2,512]{1,0:T(2,128)S(1)}, f32[2,256]{1,0:T(2,128)S(1)}) custom-call(f32[1]{0:T(128)} %bitcast.4.teacher_scale_ref, f32[1]{0:T(128)} %bitcast.5.student_scale_ref, bf16[256,512]{1,0:T(8,128)(2,1)S(1)} %get-tuple-element.25.pupil_text_ref.text_ref, bf16[256,1280]{1,0:T(8,128)(2,1)S(1)} %get-tuple-element.26.master_text_ref, ...), custom_call_target="tpu_custom_call" | custom-call | flops 1048576 | bytes 1048576 | tf_op jit(solution)/shard_map/pallas_call | solution.py:189
  24.8 3.1 %collective-permute-start.8 = (f32[2,256]{1,0:T(2,128)S(1)}, f32[2,256]{1,0:T(2,128)S(1)}, u32[]{:S(2)}, u32[]{:S(2)}) collective-permute-start(f32[2,256]{1,0:T(2,128)S(1)} %get-tuple-element.30.refs_0_), channel_id=1, source_target_pairs={{0,4},{2,6},{4,0},{6,2},{1,5},{3,7},{5,1},{7,3},{8,12},{10,14},{12... | collective-permute-start | bytes 6152 | tf_op jit(solution)/shard_map/ppermute | solution.py:210
  27.9 2.5 %collective-permute-start.13 = (f32[2,512]{1,0:T(2,128)S(1)}, f32[2,512]{1,0:T(2,128)S(1)}, u32[]{:S(2)}, u32[]{:S(2)}) collective-permute-start(f32[2,512]{1,0:T(2,128)S(1)} %shard_map.82.refs_0_), channel_id=1, source_target_pairs={{0,17},{1,16},{16,1},{17,0},{2,19},{3,18},{18,3},{19,2},{4,21},{5,... | collective-permute-start | bytes 12296 | tf_op jit(solution)/shard_map/ppermute | solution.py:213
  30.9 0.5 %collective-permute-start.11 = (f32[2,512]{1,0:T(2,128)S(1)}, f32[2,512]{1,0:T(2,128)S(1)}, u32[]{:S(2)}, u32[]{:S(2)}) collective-permute-start(f32[2,512]{1,0:T(2,128)S(1)} %shard_map.82.refs_0_), channel_id=1, source_target_pairs={{0,1},{1,0},{16,17},{17,16},{2,3},{3,2},{18,19},{19,18},{4,5},{5,4... | collective-permute-start | bytes 12296 | tf_op jit(solution)/shard_map/ppermute | solution.py:213
  31.5 1.8 %collective-permute-start.9 = (f32[2,256]{1,0:T(2,128)S(1)}, f32[2,256]{1,0:T(2,128)S(1)}, u32[]{:S(2)}, u32[]{:S(2)}) collective-permute-start(f32[2,256]{1,0:T(2,128)S(1)} %shard_map.80.refs_0_), channel_id=1, source_target_pairs={{0,2},{2,0},{4,6},{6,4},{1,3},{3,1},{5,7},{7,5},{8,10},{10,8},{12,... | collective-permute-start | bytes 6152 | tf_op jit(solution)/shard_map/ppermute | solution.py:210
  33.3 1.8 %collective-permute-done.9.refs_1_ = f32[2,256]{1,0:T(2,128)S(1)} collective-permute-done((f32[2,256]{1,0:T(2,128)S(1)}, f32[2,256]{1,0:T(2,128)S(1)}, u32[]{:S(2)}, u32[]{:S(2)}) %collective-permute-start.9) | collective-permute-done | bytes 2080 | tf_op jit(solution)/shard_map/ppermute | solution.py:210
  35.2 1.2 %shard_map.84 = (f32[4,64,512]{2,1,0:T(8,128)S(1)}, bf16[4,64,512]{2,1,0:T(8,128)(2,1)S(1)}, f32[64,512]{1,0:T(8,128)S(1)}, bf16[64,512]{1,0:T(8,128)(2,1)S(1)},...) custom-call(s32[1]{0:T(128)} %bitcast.z_ref, f32[1]{0:T(128)} %bitcast.6.scale_ref, ...), custom_call_target="tpu_custom_call" | custom-call | flops 1048576 | bytes 1048576 | tf_op jit(solution)/shard_map/pallas_call | solution.py:189
  36.5 1.8 %collective-permute-start.14 = (bf16[64,512]{1,0:T(8,128)(2,1)S(1)}, bf16[64,512]{1,0:T(8,128)(2,1)S(1)}, u32[]{:S(2)}, u32[]{:S(2)}) collective-permute-start(bf16[64,512]{1,0:T(8,128)(2,1)S(1)} %get-tuple-element.33), channel_id=1, source_target_pairs={{0,2},{2,0},{4,6},{6,4},{1,3},{3,1},{5,7},{7,5},{8,10},{10,8},{12,... | collective-permute-start | bytes 196616 | tf_op jit(solution)/shard_map/ppermute | solution.py:210
  38.3 1.1 %collective-permute-start.15 = (bf16[64,512]{1,0:T(8,128)(2,1)S(1)}, bf16[64,512]{1,0:T(8,128)(2,1)S(1)}, u32[]{:S(2)}, u32[]{:S(2)}) collective-permute-start(bf16[64,512]{1,0:T(8,128)(2,1)S(1)} %get-tuple-element.34), channel_id=1, source_target_pairs={{0,4},{2,6},{4,0},{6,2},{1,5},{3,7},{5,1},{7,3},{8,12},{10,14},{12... | collective-permute-start | bytes 196616 | tf_op jit(solution)/shard_map/ppermute | solution.py:210
  39.4 1.6 %collective-permute-start.16 = (bf16[64,512]{1,0:T(8,128)(2,1)S(1)}, bf16[64,512]{1,0:T(8,128)(2,1)S(1)}, u32[]{:S(2)}, u32[]{:S(2)}) collective-permute-start(bf16[64,512]{1,0:T(8,128)(2,1)S(1)} %get-tuple-element.35), channel_id=1, source_target_pairs={{0,6},{2,4},{4,2},{6,0},{1,7},{3,5},{5,3},{7,1},{8,14},{10,12},{12... | collective-permute-start | bytes 196616 | tf_op jit(solution)/shard_map/ppermute | solution.py:210
  41.0 2.5 %collective-permute-start.18 = (bf16[64,512]{1,0:T(8,128)(2,1)S(1)}, bf16[64,512]{1,0:T(8,128)(2,1)S(1)}, u32[]{:S(2)}, u32[]{:S(2)}) collective-permute-start(bf16[64,512]{1,0:T(8,128)(2,1)S(1)} %get-tuple-element.39), channel_id=1, source_target_pairs={{0,17},{1,16},{16,1},{17,0},{2,19},{3,18},{18,3},{19,2},{4,21},{5,... | collective-permute-start | bytes 196616 | tf_op jit(solution)/shard_map/ppermute | solution.py:213
  44.1 0.5 %collective-permute-start.20 = (bf16[64,512]{1,0:T(8,128)(2,1)S(1)}, bf16[64,512]{1,0:T(8,128)(2,1)S(1)}, u32[]{:S(2)}, u32[]{:S(2)}) collective-permute-start(bf16[64,512]{1,0:T(8,128)(2,1)S(1)} %get-tuple-element.41), channel_id=1, source_target_pairs={{0,1},{1,0},{16,17},{17,16},{2,3},{3,2},{18,19},{19,18},{4,5},{5,4... | collective-permute-start | bytes 196616 | tf_op jit(solution)/shard_map/ppermute | solution.py:213
  44.6 1.4 %collective-permute-done.15.refs_2_ = bf16[64,512]{1,0:T(8,128)(2,1)S(1)} collective-permute-done((bf16[64,512]{1,0:T(8,128)(2,1)S(1)}, bf16[64,512]{1,0:T(8,128)(2,1)S(1)}, u32[]{:S(2)}, u32[]{:S(2)}) %collective-permute-start.15) | collective-permute-done | bytes 65568 | tf_op jit(solution)/shard_map/ppermute | solution.py:210
  46.4 1.4 %collective-permute-done.19.refs_2_ = bf16[64,512]{1,0:T(8,128)(2,1)S(1)} collective-permute-done((bf16[64,512]{1,0:T(8,128)(2,1)S(1)}, bf16[64,512]{1,0:T(8,128)(2,1)S(1)}, u32[]{:S(2)}, u32[]{:S(2)}) %collective-permute-start.19) | collective-permute-done | bytes 65568 | tf_op jit(solution)/shard_map/ppermute | solution.py:213
  48.3 0.9 %shard_map.87 = (f32[64,512]{1,0:T(8,128)}, f32[64,512]{1,0:T(8,128)}) custom-call(bf16[64,512]{1,0:T(8,128)(2,1)S(1)} %copy-done, bf16[64,512]{1,0:T(8,128)(2,1)S(1)} %copy-done.1, f32[64,512]{1,0:T(8,128)S(1)} %shard_map.85.text_ref, f32[64,512]{1,0:T(8,128)S(1)} %get-tuple-element.38.refs_0_, bf16[64,512]{1,0:T(8,128)(2,1)S(1)} %collective-permute-done.18.refs_1_, ...), custom_call_target="tpu_custom_call" | custom-call | flops 1048576 | bytes 1048576 | tf_op jit(solution)/shard_map/pallas_call | solution.py:189
  (37 shorter events, 4.1 us)
Async XLA Ops:
  0.6 6.7 %copy-start = (bf16[64,512]{1,0:T(8,128)(2,1)S(1)}, bf16[64,512]{1,0:T(8,128)(2,1)}, u32[]{:S(2)}) copy-start(bf16[64,512]{1,0:T(8,128)(2,1)} %raw_image_ref.1) | copy-start | bytes 196612
  0.6 6.7 %copy-start.2 = (bf16[64,1280]{1,0:T(8,128)(2,1)S(1)}, bf16[64,1280]{1,0:T(8,128)(2,1)}, u32[]{:S(2)}) copy-start(bf16[64,1280]{1,0:T(8,128)(2,1)} %param.8) | copy-start | bytes 491524
  1.6 14.7 %collective-permute-start.1 = (bf16[64,1792]{1,0:T(8,128)(2,1)S(1)}, bf16[64,1792]{1,0:T(8,128)(2,1)S(1)}, u32[]{:S(2)}, u32[]{:S(2)}) collective-permute-start(bf16[64,1792]{1,0:T(8,128)(2,1)S(1)} %pad_maximum_fusion.1.refs_0_), channel_id=1, source_target_pairs={{0,4},{2,6},{4,0},{6,2},{1,5},{3,7},{5,1},{7,3},{8,12},{10,14},{12... | collective-permute-start | bytes 688136 | tf_op jit(solution)/shard_map/ppermute | solution.py:210
  5.7 10.8 %collective-permute-start = (bf16[64,1792]{1,0:T(8,128)(2,1)S(1)}, bf16[64,1792]{1,0:T(8,128)(2,1)S(1)}, u32[]{:S(2)}, u32[]{:S(2)}) collective-permute-start(bf16[64,1792]{1,0:T(8,128)(2,1)S(1)} %pad_maximum_fusion.1.refs_0_), channel_id=1, source_target_pairs={{0,2},{2,0},{4,6},{6,4},{1,3},{3,1},{5,7},{7,5},{8,10},{10,8},{12,... | collective-permute-start | bytes 688136 | tf_op jit(solution)/shard_map/ppermute | solution.py:210
  7.3 10.7 %collective-permute-start.5 = (bf16[64,1792]{1,0:T(8,128)(2,1)S(1)}, bf16[64,1792]{1,0:T(8,128)(2,1)S(1)}, u32[]{:S(2)}, u32[]{:S(2)}) collective-permute-start(bf16[64,1792]{1,0:T(8,128)(2,1)S(1)} %pad_maximum_fusion.refs_0_), channel_id=1, source_target_pairs={{0,17},{1,16},{16,1},{17,0},{2,19},{3,18},{18,3},{19,2},{4,21},{5,... | collective-permute-start | bytes 688136 | tf_op jit(solution)/shard_map/ppermute | solution.py:213
  9.8 10.2 %collective-permute-start.4 = (bf16[64,1792]{1,0:T(8,128)(2,1)S(1)}, bf16[64,1792]{1,0:T(8,128)(2,1)S(1)}, u32[]{:S(2)}, u32[]{:S(2)}) collective-permute-start(bf16[64,1792]{1,0:T(8,128)(2,1)S(1)} %pad_maximum_fusion.refs_0_), channel_id=1, source_target_pairs={{0,16},{1,17},{16,0},{17,1},{2,18},{3,19},{18,2},{19,3},{4,20},{5,... | collective-permute-start | bytes 688136 | tf_op jit(solution)/shard_map/ppermute | solution.py:213
  10.4 9.7 %collective-permute-start.3 = (bf16[64,1792]{1,0:T(8,128)(2,1)S(1)}, bf16[64,1792]{1,0:T(8,128)(2,1)S(1)}, u32[]{:S(2)}, u32[]{:S(2)}) collective-permute-start(bf16[64,1792]{1,0:T(8,128)(2,1)S(1)} %pad_maximum_fusion.refs_0_), channel_id=1, source_target_pairs={{0,1},{1,0},{16,17},{17,16},{2,3},{3,2},{18,19},{19,18},{4,5},{5,4... | collective-permute-start | bytes 688136 | tf_op jit(solution)/shard_map/ppermute | solution.py:213
  16.5 6.5 %collective-permute-start.2 = (bf16[64,1792]{1,0:T(8,128)(2,1)S(1)}, bf16[64,1792]{1,0:T(8,128)(2,1)S(1)}, u32[]{:S(2)}, u32[]{:S(2)}) collective-permute-start(bf16[64,1792]{1,0:T(8,128)(2,1)S(1)} %collective-permute-done.1.refs_2_), channel_id=1, source_target_pairs={{0,2},{2,0},{4,6},{6,4},{1,3},{3,1},{5,7},{7,5},{8,10},{10,8},{12,... | collective-permute-start | bytes 688136 | tf_op jit(solution)/shard_map/ppermute | solution.py:210
  20.4 3.0 %collective-permute-start.6 = (bf16[256,512]{1,0:T(8,128)(2,1)S(1)}, bf16[256,512]{1,0:T(8,128)(2,1)S(1)}, u32[]{:S(2)}, u32[]{:S(2)}) collective-permute-start(bf16[256,512]{1,0:T(8,128)(2,1)S(1)} %get-tuple-element.27.pupil_same_ref.same_ref), channel_id=1, source_target_pairs={{0,8},{8,0},{1,9},{9,1},{2,10},{10,2},{3,11},{11,3},{4,12},{12,4},... | collective-permute-start | bytes 786440 | tf_op jit(solution)/shard_map/ppermute | solution.py:225
  20.5 2.9 %collective-permute-start.7 = (bf16[256,1280]{1,0:T(8,128)(2,1)S(1)}, bf16[256,1280]{1,0:T(8,128)(2,1)S(1)}, u32[]{:S(2)}, u32[]{:S(2)}) collective-permute-start(bf16[256,1280]{1,0:T(8,128)(2,1)S(1)} %get-tuple-element.28.master_same_ref), channel_id=1, source_target_pairs={{0,8},{8,0},{1,9},{9,1},{2,10},{10,2},{3,11},{11,3},{4,12},{12,4},... | collective-permute-start | bytes 1966088 | tf_op jit(solution)/shard_map/ppermute | solution.py:225
  24.7 3.2 %collective-permute-start.10 = (f32[2,512]{1,0:T(2,128)S(1)}, f32[2,512]{1,0:T(2,128)S(1)}, u32[]{:S(2)}, u32[]{:S(2)}) collective-permute-start(f32[2,512]{1,0:T(2,128)S(1)} %get-tuple-element.31.own_ref), channel_id=1, source_target_pairs={{0,8},{8,0},{1,9},{9,1},{2,10},{10,2},{3,11},{11,3},{4,12},{12,4},... | collective-permute-start | bytes 12296 | tf_op jit(solution)/shard_map/ppermute | solution.py:225
  24.8 6.7 %collective-permute-start.8 = (f32[2,256]{1,0:T(2,128)S(1)}, f32[2,256]{1,0:T(2,128)S(1)}, u32[]{:S(2)}, u32[]{:S(2)}) collective-permute-start(f32[2,256]{1,0:T(2,128)S(1)} %get-tuple-element.30.refs_0_), channel_id=1, source_target_pairs={{0,4},{2,6},{4,0},{6,2},{1,5},{3,7},{5,1},{7,3},{8,12},{10,14},{12... | collective-permute-start | bytes 6152 | tf_op jit(solution)/shard_map/ppermute | solution.py:210
  27.9 7.2 %collective-permute-start.13 = (f32[2,512]{1,0:T(2,128)S(1)}, f32[2,512]{1,0:T(2,128)S(1)}, u32[]{:S(2)}, u32[]{:S(2)}) collective-permute-start(f32[2,512]{1,0:T(2,128)S(1)} %shard_map.82.refs_0_), channel_id=1, source_target_pairs={{0,17},{1,16},{16,1},{17,0},{2,19},{3,18},{18,3},{19,2},{4,21},{5,... | collective-permute-start | bytes 12296 | tf_op jit(solution)/shard_map/ppermute | solution.py:213
  30.4 4.7 %collective-permute-start.12 = (f32[2,512]{1,0:T(2,128)S(1)}, f32[2,512]{1,0:T(2,128)S(1)}, u32[]{:S(2)}, u32[]{:S(2)}) collective-permute-start(f32[2,512]{1,0:T(2,128)S(1)} %shard_map.82.refs_0_), channel_id=1, source_target_pairs={{0,16},{1,17},{16,0},{17,1},{2,18},{3,19},{18,2},{19,3},{4,20},{5,... | collective-permute-start | bytes 12296 | tf_op jit(solution)/shard_map/ppermute | solution.py:213
  30.9 4.2 %collective-permute-start.11 = (f32[2,512]{1,0:T(2,128)S(1)}, f32[2,512]{1,0:T(2,128)S(1)}, u32[]{:S(2)}, u32[]{:S(2)}) collective-permute-start(f32[2,512]{1,0:T(2,128)S(1)} %shard_map.82.refs_0_), channel_id=1, source_target_pairs={{0,1},{1,0},{16,17},{17,16},{2,3},{3,2},{18,19},{19,18},{4,5},{5,4... | collective-permute-start | bytes 12296 | tf_op jit(solution)/shard_map/ppermute | solution.py:213
  31.5 3.7 %collective-permute-start.9 = (f32[2,256]{1,0:T(2,128)S(1)}, f32[2,256]{1,0:T(2,128)S(1)}, u32[]{:S(2)}, u32[]{:S(2)}) collective-permute-start(f32[2,256]{1,0:T(2,128)S(1)} %shard_map.80.refs_0_), channel_id=1, source_target_pairs={{0,2},{2,0},{4,6},{6,4},{1,3},{3,1},{5,7},{7,5},{8,10},{10,8},{12,... | collective-permute-start | bytes 6152 | tf_op jit(solution)/shard_map/ppermute | solution.py:210
  36.5 4.5 %collective-permute-start.17 = (bf16[4,64,512]{2,1,0:T(8,128)(2,1)S(1)}, bf16[4,64,512]{2,1,0:T(8,128)(2,1)S(1)}, u32[]{:S(2)}, u32[]{:S(2)}) collective-permute-start(bf16[4,64,512]{2,1,0:T(8,128)(2,1)S(1)} %get-tuple-element.37), channel_id=1, source_target_pairs={{0,8},{8,0},{1,9},{9,1},{2,10},{10,2},{3,11},{11,3},{4,12},{12,4},... | collective-permute-start | bytes 786440 | tf_op jit(solution)/shard_map/ppermute | solution.py:225
  36.5 7.5 %collective-permute-start.14 = (bf16[64,512]{1,0:T(8,128)(2,1)S(1)}, bf16[64,512]{1,0:T(8,128)(2,1)S(1)}, u32[]{:S(2)}, u32[]{:S(2)}) collective-permute-start(bf16[64,512]{1,0:T(8,128)(2,1)S(1)} %get-tuple-element.33), channel_id=1, source_target_pairs={{0,2},{2,0},{4,6},{6,4},{1,3},{3,1},{5,7},{7,5},{8,10},{10,8},{12,... | collective-permute-start | bytes 196616 | tf_op jit(solution)/shard_map/ppermute | solution.py:210
  38.3 7.7 %collective-permute-start.15 = (bf16[64,512]{1,0:T(8,128)(2,1)S(1)}, bf16[64,512]{1,0:T(8,128)(2,1)S(1)}, u32[]{:S(2)}, u32[]{:S(2)}) collective-permute-start(bf16[64,512]{1,0:T(8,128)(2,1)S(1)} %get-tuple-element.34), channel_id=1, source_target_pairs={{0,4},{2,6},{4,0},{6,2},{1,5},{3,7},{5,1},{7,3},{8,12},{10,14},{12... | collective-permute-start | bytes 196616 | tf_op jit(solution)/shard_map/ppermute | solution.py:210
  39.4 6.6 %collective-permute-start.16 = (bf16[64,512]{1,0:T(8,128)(2,1)S(1)}, bf16[64,512]{1,0:T(8,128)(2,1)S(1)}, u32[]{:S(2)}, u32[]{:S(2)}) collective-permute-start(bf16[64,512]{1,0:T(8,128)(2,1)S(1)} %get-tuple-element.35), channel_id=1, source_target_pairs={{0,6},{2,4},{4,2},{6,0},{1,7},{3,5},{5,3},{7,1},{8,14},{10,12},{12... | collective-permute-start | bytes 196616 | tf_op jit(solution)/shard_map/ppermute | solution.py:210
  41.0 5.3 %collective-permute-start.18 = (bf16[64,512]{1,0:T(8,128)(2,1)S(1)}, bf16[64,512]{1,0:T(8,128)(2,1)S(1)}, u32[]{:S(2)}, u32[]{:S(2)}) collective-permute-start(bf16[64,512]{1,0:T(8,128)(2,1)S(1)} %get-tuple-element.39), channel_id=1, source_target_pairs={{0,17},{1,16},{16,1},{17,0},{2,19},{3,18},{18,3},{19,2},{4,21},{5,... | collective-permute-start | bytes 196616 | tf_op jit(solution)/shard_map/ppermute | solution.py:213
  43.5 4.3 %collective-permute-start.19 = (bf16[64,512]{1,0:T(8,128)(2,1)S(1)}, bf16[64,512]{1,0:T(8,128)(2,1)S(1)}, u32[]{:S(2)}, u32[]{:S(2)}) collective-permute-start(bf16[64,512]{1,0:T(8,128)(2,1)S(1)} %get-tuple-element.40), channel_id=1, source_target_pairs={{0,16},{1,17},{16,0},{17,1},{2,18},{3,19},{18,2},{19,3},{4,20},{5,... | collective-permute-start | bytes 196616 | tf_op jit(solution)/shard_map/ppermute | solution.py:213
  44.1 4.3 %collective-permute-start.20 = (bf16[64,512]{1,0:T(8,128)(2,1)S(1)}, bf16[64,512]{1,0:T(8,128)(2,1)S(1)}, u32[]{:S(2)}, u32[]{:S(2)}) collective-permute-start(bf16[64,512]{1,0:T(8,128)(2,1)S(1)} %get-tuple-element.41), channel_id=1, source_target_pairs={{0,1},{1,0},{16,17},{17,16},{2,3},{3,2},{18,19},{19,18},{4,5},{5,4... | collective-permute-start | bytes 196616 | tf_op jit(solution)/shard_map/ppermute | solution.py:213
  46.0 2.3 %copy-start.1 = (bf16[64,512]{1,0:T(8,128)(2,1)S(1)}, bf16[64,512]{1,0:T(8,128)(2,1)}, u32[]{:S(2)}) copy-start(bf16[64,512]{1,0:T(8,128)(2,1)} %raw_text_ref.1) | copy-start | bytes 196612

commit v6 on v5

--- a/solution.py
+++ b/solution.py
@@ -39,6 +39,7 @@
 
 
 def put_units(block, pupil_ref, master_ref, at):
+    at = pl.multiple_of(at, block.shape[0])
     own, width = block.shape[0], pupil_ref.shape[1]
     pupil_ref[pl.ds(at, own), :] = unit_rows(block[:, :width])[0].astype(BF16)
     master_ref[pl.ds(at, own), :] = unit_rows(block[:, width:])[0].astype(BF16)
@@ -52,12 +53,23 @@
         put_units(ref[...], pupil_ref, master_ref, row)
 
 
-def text_unit_kernel(z_ref, *refs):
+def unit_kernel(raw_ref, out_ref):
+    out_ref[...] = unit_rows(raw_ref[...])[0].astype(BF16)
+
+
+def text_unit_kernel(distances, z_ref, student_ref, teacher_ref, near_ref, *refs):
     pupil_ref, master_ref = refs[-2:]
-    own = refs[0].shape[0]
-    for s, ref in enumerate(refs[:-2]):
-        row = pl.multiple_of(jnp.bitwise_xor(z_ref[0], s) * own, own)
-        put_units(ref[...], pupil_ref, master_ref, row)
+    own = near_ref.shape[0]
+
+    def place(s):
+        return pl.ds(pl.multiple_of(jnp.bitwise_xor(z_ref[0], s) * own, own), own)
+
+    put_units(near_ref[...], pupil_ref, master_ref, jnp.bitwise_xor(z_ref[0], 1) * own)
+    unit_kernel(student_ref, pupil_ref.at[place(0)])
+    unit_kernel(teacher_ref, master_ref.at[place(0)])
+    for k, s in enumerate(distances):
+        pupil_ref[place(s), :] = refs[2 * k][...]
+        master_ref[place(s), :] = refs[2 * k + 1][...]
 
 
 def product(left, right):
@@ -212,14 +224,30 @@
     def to_square(value, step):
         return lax.ppermute(value, SQUARE, [(q, q ^ step) for q in range(squares)])
 
-    def gather_line(value):
-        first = bits(depth)[::-1]
-        held = lax.optimization_barrier([value] + [to_line(value, s) for s in first])
-        blocks = dict(zip([0] + first, held))
-        for s in sorted(set(range(depth)) - set(blocks), key=lambda s: bin(s).count("1")):
-            near = s & -s
-            blocks[s] = to_line(blocks[s ^ near], near)
-        return [blocks[s] for s in range(depth)]
+    def gather_square(value):
+        first = bits(squares)
+        blocks = dict(zip([0] + first, [value] + [to_square(value, s) for s in first]))
+        for s in sorted(set(range(squares)) - set(blocks), key=lambda s: bin(s).count("1")):
+            hop = s & -s
+            blocks[s] = to_square(blocks[s ^ hop], hop)
+        return [blocks[s] for s in range(squares)]
+
+    def gather_line(student, teacher):
+        far = bits(depth)[:-1]
+        parts = [student, teacher]
+        units = {s: [to_line(part, s) for part in parts] for s in far}
+        near = to_line(side_by_side(student, teacher), 1)
+        for s in far:
+            units[s][0], near = lax.optimization_barrier((units[s][0], near))
+            for k, raw in enumerate(units[s]):
+                units[s][k] = call(
+                    unit_kernel, shaped(raw.shape, BF16), (raw,), [vmem], vmem, flops=SOME
+                )
+        rest = set(range(2, depth)) - set(far)
+        for s in sorted(rest, key=lambda s: bin(s).count("1")):
+            hop = s & -s
+            units[s] = [to_line(part, hop) for part in units[s ^ hop]]
+        return near, units
 
     def to_sibling(value):
         return lax.ppermute(value, "core", [(0, 1), (1, 0)])
@@ -235,16 +263,16 @@
         student_scale = student_scale.reshape(1)
         grant = 16 if images * texts <= 512 * 256 else 56
 
-        raw_text = side_by_side(student_text, teacher_text)
-        raw_texts = gather_line(raw_text)
         raw_image = side_by_side(student_image, teacher_image)
-        blocks = [raw_image] + [to_square(raw_image, s) for s in range(1, squares)]
+        blocks = gather_square(raw_image)
+        near, units = gather_line(student_text, teacher_text)
+        raw_texts = [student_text, teacher_text, near] + sum(units.values(), [])
 
         pupil_text, master_text = call(
-            text_unit_kernel,
+            functools.partial(text_unit_kernel, tuple(units)),
             (shaped((texts, width), BF16), shaped((texts, both - width), BF16)),
             (z, *raw_texts),
-            [smem] + [vmem] * depth,
+            [smem] + [vmem] * len(raw_texts),
             vmem,
             grant=grant,
             flops=MANY,

time: 49.4 us -> 48.8 us (0.988)
  waiting for transfers between devices: 14.1 us -> 13.5 us
    ppermute x8 -> x10, starting transfers between devices: 16.5 us -> 15.5 us  [to_line(): return lax.ppermute(value, LINE, [(z, z ^ step) for z in range(depth)])]
    ppermute x9, starting transfers between devices: 10.7 us -> 11.7 us  [to_square(): return lax.ppermute(value, SQUARE, [(q, q ^ step) for q in range(squares)])]
    ppermute x8 -> x10, waiting for transfers between devices: 9.76 us -> 8.91 us  [to_line(): return lax.ppermute(value, LINE, [(z, z ^ step) for z in range(depth)])]
    pallas_call x11 -> x13, Pallas kernels: 4.13 us -> 4.27 us  [call(): pl.pallas_call(kernel, out_shape=outs, in_specs=specs, out_specs=jax.tree...]
  transfers between devices with their start and end apart: 21 -> 23, of which waited for: 10 -> 9; matrix products, arithmetic and copies ran while one was open for 0% -> 2% of each run, Pallas kernels for 1% -> 2%
where the time goes in v6:
time: 48.8 us; the launch traced here: 48.7 us
  starting transfers between devices  27.9 us (57%)
  waiting for transfers between devices  13.5 us (28%)
  Pallas kernels  4.27 us (9%)
  between operations  2.11 us (4%)
  other arithmetic  0.95 us (2%)
    ppermute x10, starting transfers between devices, to_line(): return lax.ppermute(value, LINE, [(z, z ^ step) for z in range(depth)])  15.5 us
    ppermute x9, starting transfers between devices, to_square(): return lax.ppermute(value, SQUARE, [(q, q ^ step) for q in range(squares)])  11.7 us
    ppermute x10, waiting for transfers between devices, to_line(): return lax.ppermute(value, LINE, [(z, z ^ step) for z in range(depth)])  8.91 us
    ppermute x9, waiting for transfers between devices, to_square(): return lax.ppermute(value, SQUARE, [(q, q ^ step) for q in range(squares)])  4.55 us
    pallas_call x13, Pallas kernels, call(): pl.pallas_call(kernel, out_shape=outs, in_specs=specs, out_specs=jax.tree...  4.27 us
  transfers between devices with their start and end apart: 23, of which 9 were waited for; matrix products, arithmetic and copies ran while one was open for 2% of the time, Pallas kernels for 2%

profile of v6, /device:TPU:0, one launch (start us, length us, event | category | flops | bytes accessed | tf_op | source)
XLA Modules:
  0.0 48.7 jit_solution(3180706540405925298)
XLA Ops:
  0.7 4.1 %collective-permute-start.2 = (bf16[64,1280]{1,0:T(8,128)(2,1)}, bf16[64,1280]{1,0:T(8,128)(2,1)S(1)}, u32[]{:S(2)}, u32[]{:S(2)}) collective-permute-start(bf16[64,1280]{1,0:T(8,128)(2,1)} %teacher_ref.1), channel_id=1, source_target_pairs={{0,4},{2,6},{4,0},{6,2},{1,5},{3,7},{5,1},{7,3},{8,12},{10,14},{12... | collective-permute-start | bytes 491528 | tf_op jit(solution)/shard_map/ppermute | solution.py:222
  4.8 0.9 %pad_maximum_fusion.refs_0_ = bf16[64,1792]{1,0:T(8,128)(2,1)S(1)} fusion(bf16[64,1280]{1,0:T(8,128)(2,1)} %param.8, bf16[64,512]{1,0:T(8,128)(2,1)} %raw_image_ref.1), kind=kLoop, calls=%fused_computation | loop fusion | flops 458752 | bytes 458752 | tf_op jit(solution)/shard_map/max | solution.py:35
  5.7 1.6 %collective-permute-start.6 = (bf16[64,1792]{1,0:T(8,128)(2,1)S(1)}, bf16[64,1792]{1,0:T(8,128)(2,1)S(1)}, u32[]{:S(2)}, u32[]{:S(2)}) collective-permute-start(bf16[64,1792]{1,0:T(8,128)(2,1)S(1)} %pad_maximum_fusion.refs_0_), channel_id=1, source_target_pairs={{0,16},{1,17},{16,0},{17,1},{2,18},{3,19},{18,2},{19,3},{4,20},{5,... | collective-permute-start | bytes 688136 | tf_op jit(solution)/shard_map/ppermute | solution.py:225
  7.3 1.6 %collective-permute-start.1 = (bf16[64,1792]{1,0:T(8,128)(2,1)S(1)}, bf16[64,1792]{1,0:T(8,128)(2,1)S(1)}, u32[]{:S(2)}, u32[]{:S(2)}) collective-permute-start(bf16[64,1792]{1,0:T(8,128)(2,1)S(1)} %pad_maximum_fusion.1), channel_id=1, source_target_pairs={{0,2},{2,0},{4,6},{6,4},{1,3},{3,1},{5,7},{7,5},{8,10},{10,8},{12,... | collective-permute-start | bytes 688136 | tf_op jit(solution)/shard_map/ppermute | solution.py:222
  9.3 1.5 %collective-permute-start.5 = (bf16[64,1792]{1,0:T(8,128)(2,1)S(1)}, bf16[64,1792]{1,0:T(8,128)(2,1)S(1)}, u32[]{:S(2)}, u32[]{:S(2)}) collective-permute-start(bf16[64,1792]{1,0:T(8,128)(2,1)S(1)} %pad_maximum_fusion.refs_0_), channel_id=1, source_target_pairs={{0,1},{1,0},{16,17},{17,16},{2,3},{3,2},{18,19},{19,18},{4,5},{5,4... | collective-permute-start | bytes 688136 | tf_op jit(solution)/shard_map/ppermute | solution.py:225
  12.8 1.5 %collective-permute-start.7 = (bf16[64,1792]{1,0:T(8,128)(2,1)S(1)}, bf16[64,1792]{1,0:T(8,128)(2,1)S(1)}, u32[]{:S(2)}, u32[]{:S(2)}) collective-permute-start(bf16[64,1792]{1,0:T(8,128)(2,1)S(1)} %collective-permute-done.6.refs_2_), channel_id=1, source_target_pairs={{0,1},{1,0},{16,17},{17,16},{2,3},{3,2},{18,19},{19,18},{4,5},{5,4... | collective-permute-start | bytes 688136 | tf_op jit(solution)/shard_map/ppermute | solution.py:225
  14.4 1.6 %collective-permute-start.4 = (bf16[64,1280]{1,0:T(8,128)(2,1)S(1)}, bf16[64,1280]{1,0:T(8,128)(2,1)S(1)}, u32[]{:S(2)}, u32[]{:S(2)}) collective-permute-start(bf16[64,1280]{1,0:T(8,128)(2,1)S(1)} %shard_map.78.refs_1_), channel_id=1, source_target_pairs={{0,2},{2,0},{4,6},{6,4},{1,3},{3,1},{5,7},{7,5},{8,10},{10,8},{12,... | collective-permute-start | bytes 491528 | tf_op jit(solution)/shard_map/ppermute | solution.py:222
  16.1 2.7 %collective-permute-done.1.near_ref = bf16[64,1792]{1,0:T(8,128)(2,1)S(1)} collective-permute-done((bf16[64,1792]{1,0:T(8,128)(2,1)S(1)}, bf16[64,1792]{1,0:T(8,128)(2,1)S(1)}, u32[]{:S(2)}, u32[]{:S(2)}) %collective-permute-start.1) | collective-permute-done | bytes 229408 | tf_op jit(solution)/shard_map/ppermute | solution.py:222
  19.0 1.4 %collective-permute-done.7.refs_3_ = bf16[64,1792]{1,0:T(8,128)(2,1)S(1)} collective-permute-done((bf16[64,1792]{1,0:T(8,128)(2,1)S(1)}, bf16[64,1792]{1,0:T(8,128)(2,1)S(1)}, u32[]{:S(2)}, u32[]{:S(2)}) %collective-permute-start.7) | collective-permute-done | bytes 229408 | tf_op jit(solution)/shard_map/ppermute | solution.py:225
  21.3 2.0 %collective-permute-done.3.refs_2_ = bf16[64,512]{1,0:T(8,128)(2,1)S(1)} collective-permute-done((bf16[64,512]{1,0:T(8,128)(2,1)S(1)}, bf16[64,512]{1,0:T(8,128)(2,1)S(1)}, u32[]{:S(2)}, u32[]{:S(2)}) %collective-permute-start.3) | collective-permute-done | bytes 65568 | tf_op jit(solution)/shard_map/ppermute | solution.py:222
  23.5 1.3 %shard_map.81 = (f32[512,256]{1,0:T(8,128)S(1)}, f32[2,512]{1,0:T(2,128)S(1)}, f32[2,256]{1,0:T(2,128)S(1)}) custom-call(f32[1]{0:T(128)} %bitcast.4.teacher_scale_ref, f32[1]{0:T(128)} %bitcast.5.student_scale_ref, bf16[256,512]{1,0:T(8,128)(2,1)S(1)} %get-tuple-element.23.pupil_text_ref.text_ref, bf16[256,1280]{1,0:T(8,128)(2,1)S(1)} %get-tuple-element.24.master_text_ref, ...), custom_call_target="tpu_custom_call" | custom-call | flops 1048576 | bytes 1048576 | tf_op jit(solution)/shard_map/pallas_call | solution.py:201
  24.9 2.5 %collective-permute-start.10 = (f32[2,256]{1,0:T(2,128)S(1)}, f32[2,256]{1,0:T(2,128)S(1)}, u32[]{:S(2)}, u32[]{:S(2)}) collective-permute-start(f32[2,256]{1,0:T(2,128)S(1)} %get-tuple-element.28.refs_0_), channel_id=1, source_target_pairs={{0,4},{2,6},{4,0},{6,2},{1,5},{3,7},{5,1},{7,3},{8,12},{10,14},{12... | collective-permute-start | bytes 6152 | tf_op jit(solution)/shard_map/ppermute | solution.py:222
  27.4 1.5 %collective-permute-start.15 = (f32[2,512]{1,0:T(2,128)S(1)}, f32[2,512]{1,0:T(2,128)S(1)}, u32[]{:S(2)}, u32[]{:S(2)}) collective-permute-start(f32[2,512]{1,0:T(2,128)S(1)} %shard_map.84.refs_0_), channel_id=1, source_target_pairs={{0,17},{1,16},{16,1},{17,0},{2,19},{3,18},{18,3},{19,2},{4,21},{5,... | collective-permute-start | bytes 12296 | tf_op jit(solution)/shard_map/ppermute | solution.py:225
  28.9 1.5 %collective-permute-start.14 = (f32[2,512]{1,0:T(2,128)S(1)}, f32[2,512]{1,0:T(2,128)S(1)}, u32[]{:S(2)}, u32[]{:S(2)}) collective-permute-start(f32[2,512]{1,0:T(2,128)S(1)} %shard_map.84.refs_0_), channel_id=1, source_target_pairs={{0,16},{1,17},{16,0},{17,1},{2,18},{3,19},{18,2},{19,3},{4,20},{5,... | collective-permute-start | bytes 12296 | tf_op jit(solution)/shard_map/ppermute | solution.py:225
  31.7 2.9 %collective-permute-done.11.refs_1_ = f32[2,256]{1,0:T(2,128)S(1)} collective-permute-done((f32[2,256]{1,0:T(2,128)S(1)}, f32[2,256]{1,0:T(2,128)S(1)}, u32[]{:S(2)}, u32[]{:S(2)}) %collective-permute-start.11) | collective-permute-done | bytes 2080 | tf_op jit(solution)/shard_map/ppermute | solution.py:222
  34.7 1.2 %shard_map.86 = (f32[4,64,512]{2,1,0:T(8,128)S(1)}, bf16[4,64,512]{2,1,0:T(8,128)(2,1)S(1)}, f32[64,512]{1,0:T(8,128)S(1)}, bf16[64,512]{1,0:T(8,128)(2,1)S(1)},...) custom-call(s32[1]{0:T(128)} %bitcast.z_ref, f32[1]{0:T(128)} %bitcast.6.scale_ref, ...), custom_call_target="tpu_custom_call" | custom-call | flops 1048576 | bytes 1048576 | tf_op jit(solution)/shard_map/pallas_call | solution.py:201
  36.8 1.1 %collective-permute-start.17 = (bf16[64,512]{1,0:T(8,128)(2,1)S(1)}, bf16[64,512]{1,0:T(8,128)(2,1)S(1)}, u32[]{:S(2)}, u32[]{:S(2)}) collective-permute-start(bf16[64,512]{1,0:T(8,128)(2,1)S(1)} %get-tuple-element.32), channel_id=1, source_target_pairs={{0,4},{2,6},{4,0},{6,2},{1,5},{3,7},{5,1},{7,3},{8,12},{10,14},{12... | collective-permute-start | bytes 196616 | tf_op jit(solution)/shard_map/ppermute | solution.py:222
  37.8 2.6 %collective-permute-start.18 = (bf16[64,512]{1,0:T(8,128)(2,1)S(1)}, bf16[64,512]{1,0:T(8,128)(2,1)S(1)}, u32[]{:S(2)}, u32[]{:S(2)}) collective-permute-start(bf16[64,512]{1,0:T(8,128)(2,1)S(1)} %get-tuple-element.33), channel_id=1, source_target_pairs={{0,6},{2,4},{4,2},{6,0},{1,7},{3,5},{5,3},{7,1},{8,14},{10,12},{12... | collective-permute-start | bytes 196616 | tf_op jit(solution)/shard_map/ppermute | solution.py:222
  40.5 1.5 %collective-permute-start.20 = (bf16[64,512]{1,0:T(8,128)(2,1)S(1)}, bf16[64,512]{1,0:T(8,128)(2,1)S(1)}, u32[]{:S(2)}, u32[]{:S(2)}) collective-permute-start(bf16[64,512]{1,0:T(8,128)(2,1)S(1)} %get-tuple-element.37), channel_id=1, source_target_pairs={{0,17},{1,16},{16,1},{17,0},{2,19},{3,18},{18,3},{19,2},{4,21},{5,... | collective-permute-start | bytes 196616 | tf_op jit(solution)/shard_map/ppermute | solution.py:225
  42.0 1.5 %collective-permute-start.21 = (bf16[64,512]{1,0:T(8,128)(2,1)S(1)}, bf16[64,512]{1,0:T(8,128)(2,1)S(1)}, u32[]{:S(2)}, u32[]{:S(2)}) collective-permute-start(bf16[64,512]{1,0:T(8,128)(2,1)S(1)} %get-tuple-element.38), channel_id=1, source_target_pairs={{0,16},{1,17},{16,0},{17,1},{2,18},{3,19},{18,2},{19,3},{4,20},{5,... | collective-permute-start | bytes 196616 | tf_op jit(solution)/shard_map/ppermute | solution.py:225
  44.1 1.3 %collective-permute-done.17.refs_2_ = bf16[64,512]{1,0:T(8,128)(2,1)S(1)} collective-permute-done((bf16[64,512]{1,0:T(8,128)(2,1)S(1)}, bf16[64,512]{1,0:T(8,128)(2,1)S(1)}, u32[]{:S(2)}, u32[]{:S(2)}) %collective-permute-start.17) | collective-permute-done | bytes 65568 | tf_op jit(solution)/shard_map/ppermute | solution.py:222
  45.4 1.0 %collective-permute-done.20.refs_1_ = bf16[64,512]{1,0:T(8,128)(2,1)S(1)} collective-permute-done((bf16[64,512]{1,0:T(8,128)(2,1)S(1)}, bf16[64,512]{1,0:T(8,128)(2,1)S(1)}, u32[]{:S(2)}, u32[]{:S(2)}) %collective-permute-start.20) | collective-permute-done | bytes 65568 | tf_op jit(solution)/shard_map/ppermute | solution.py:225
  46.7 1.1 %collective-permute-done.22.refs_3_ = bf16[64,512]{1,0:T(8,128)(2,1)S(1)} collective-permute-done((bf16[64,512]{1,0:T(8,128)(2,1)S(1)}, bf16[64,512]{1,0:T(8,128)(2,1)S(1)}, u32[]{:S(2)}, u32[]{:S(2)}) %collective-permute-start.22) | collective-permute-done | bytes 65568 | tf_op jit(solution)/shard_map/ppermute | solution.py:225
  47.8 0.9 %shard_map.89 = (f32[64,512]{1,0:T(8,128)}, f32[64,512]{1,0:T(8,128)}) custom-call(bf16[64,512]{1,0:T(8,128)(2,1)S(1)} %copy-done, bf16[64,512]{1,0:T(8,128)(2,1)S(1)} %copy-done.1, f32[64,512]{1,0:T(8,128)S(1)} %shard_map.87.text_ref, f32[64,512]{1,0:T(8,128)S(1)} %get-tuple-element.36.refs_0_, bf16[64,512]{1,0:T(8,128)(2,1)S(1)} %collective-permute-done.20.refs_1_, ...), custom_call_target="tpu_custom_call" | custom-call | flops 1048576 | bytes 1048576 | tf_op jit(solution)/shard_map/pallas_call | solution.py:201
  (43 shorter events, 5.7 us)
Async XLA Ops:
  0.6 6.6 %copy-start.2 = (bf16[64,1280]{1,0:T(8,128)(2,1)S(1)}, bf16[64,1280]{1,0:T(8,128)(2,1)}, u32[]{:S(2)}) copy-start(bf16[64,1280]{1,0:T(8,128)(2,1)} %teacher_ref.1) | copy-start | bytes 491524
  0.7 13.7 %collective-permute-start.2 = (bf16[64,1280]{1,0:T(8,128)(2,1)}, bf16[64,1280]{1,0:T(8,128)(2,1)S(1)}, u32[]{:S(2)}, u32[]{:S(2)}) collective-permute-start(bf16[64,1280]{1,0:T(8,128)(2,1)} %teacher_ref.1), channel_id=1, source_target_pairs={{0,4},{2,6},{4,0},{6,2},{1,5},{3,7},{5,1},{7,3},{8,12},{10,14},{12... | collective-permute-start | bytes 491528 | tf_op jit(solution)/shard_map/ppermute | solution.py:222
  5.7 7.1 %collective-permute-start.6 = (bf16[64,1792]{1,0:T(8,128)(2,1)S(1)}, bf16[64,1792]{1,0:T(8,128)(2,1)S(1)}, u32[]{:S(2)}, u32[]{:S(2)}) collective-permute-start(bf16[64,1792]{1,0:T(8,128)(2,1)S(1)} %pad_maximum_fusion.refs_0_), channel_id=1, source_target_pairs={{0,16},{1,17},{16,0},{17,1},{2,18},{3,19},{18,2},{19,3},{4,20},{5,... | collective-permute-start | bytes 688136 | tf_op jit(solution)/shard_map/ppermute | solution.py:225
  7.3 11.5 %collective-permute-start.1 = (bf16[64,1792]{1,0:T(8,128)(2,1)S(1)}, bf16[64,1792]{1,0:T(8,128)(2,1)S(1)}, u32[]{:S(2)}, u32[]{:S(2)}) collective-permute-start(bf16[64,1792]{1,0:T(8,128)(2,1)S(1)} %pad_maximum_fusion.1), channel_id=1, source_target_pairs={{0,2},{2,0},{4,6},{6,4},{1,3},{3,1},{5,7},{7,5},{8,10},{10,8},{12,... | collective-permute-start | bytes 688136 | tf_op jit(solution)/shard_map/ppermute | solution.py:222
  8.9 7.1 %collective-permute-start = (bf16[64,512]{1,0:T(8,128)(2,1)S(1)}, bf16[64,512]{1,0:T(8,128)(2,1)S(1)}, u32[]{:S(2)}, u32[]{:S(2)}) collective-permute-start(bf16[64,512]{1,0:T(8,128)(2,1)S(1)} %copy-done.1), channel_id=1, source_target_pairs={{0,4},{2,6},{4,0},{6,2},{1,5},{3,7},{5,1},{7,3},{8,12},{10,14},{12... | collective-permute-start | bytes 196616 | tf_op jit(solution)/shard_map/ppermute | solution.py:222
  9.3 9.7 %collective-permute-start.5 = (bf16[64,1792]{1,0:T(8,128)(2,1)S(1)}, bf16[64,1792]{1,0:T(8,128)(2,1)S(1)}, u32[]{:S(2)}, u32[]{:S(2)}) collective-permute-start(bf16[64,1792]{1,0:T(8,128)(2,1)S(1)} %pad_maximum_fusion.refs_0_), channel_id=1, source_target_pairs={{0,1},{1,0},{16,17},{17,16},{2,3},{3,2},{18,19},{19,18},{4,5},{5,4... | collective-permute-start | bytes 688136 | tf_op jit(solution)/shard_map/ppermute | solution.py:225
  12.8 7.6 %collective-permute-start.7 = (bf16[64,1792]{1,0:T(8,128)(2,1)S(1)}, bf16[64,1792]{1,0:T(8,128)(2,1)S(1)}, u32[]{:S(2)}, u32[]{:S(2)}) collective-permute-start(bf16[64,1792]{1,0:T(8,128)(2,1)S(1)} %collective-permute-done.6.refs_2_), channel_id=1, source_target_pairs={{0,1},{1,0},{16,17},{17,16},{2,3},{3,2},{18,19},{19,18},{4,5},{5,4... | collective-permute-start | bytes 688136 | tf_op jit(solution)/shard_map/ppermute | solution.py:225
  14.4 8.8 %collective-permute-start.4 = (bf16[64,1280]{1,0:T(8,128)(2,1)S(1)}, bf16[64,1280]{1,0:T(8,128)(2,1)S(1)}, u32[]{:S(2)}, u32[]{:S(2)}) collective-permute-start(bf16[64,1280]{1,0:T(8,128)(2,1)S(1)} %shard_map.78.refs_1_), channel_id=1, source_target_pairs={{0,2},{2,0},{4,6},{6,4},{1,3},{3,1},{5,7},{7,5},{8,10},{10,8},{12,... | collective-permute-start | bytes 491528 | tf_op jit(solution)/shard_map/ppermute | solution.py:222
  18.9 4.3 %collective-permute-start.3 = (bf16[64,512]{1,0:T(8,128)(2,1)S(1)}, bf16[64,512]{1,0:T(8,128)(2,1)S(1)}, u32[]{:S(2)}, u32[]{:S(2)}) collective-permute-start(bf16[64,512]{1,0:T(8,128)(2,1)S(1)} %shard_map.77.refs_0_), channel_id=1, source_target_pairs={{0,2},{2,0},{4,6},{6,4},{1,3},{3,1},{5,7},{7,5},{8,10},{10,8},{12,... | collective-permute-start | bytes 196616 | tf_op jit(solution)/shard_map/ppermute | solution.py:222
  20.7 2.8 %collective-permute-start.8 = (bf16[256,512]{1,0:T(8,128)(2,1)S(1)}, bf16[256,512]{1,0:T(8,128)(2,1)S(1)}, u32[]{:S(2)}, u32[]{:S(2)}) collective-permute-start(bf16[256,512]{1,0:T(8,128)(2,1)S(1)} %get-tuple-element.25.pupil_same_ref.same_ref), channel_id=1, source_target_pairs={{0,8},{8,0},{1,9},{9,1},{2,10},{10,2},{3,11},{11,3},{4,12},{12,4},... | collective-permute-start | bytes 786440 | tf_op jit(solution)/shard_map/ppermute | solution.py:253
  20.8 2.7 %collective-permute-start.9 = (bf16[256,1280]{1,0:T(8,128)(2,1)S(1)}, bf16[256,1280]{1,0:T(8,128)(2,1)S(1)}, u32[]{:S(2)}, u32[]{:S(2)}) collective-permute-start(bf16[256,1280]{1,0:T(8,128)(2,1)S(1)} %get-tuple-element.26.master_same_ref), channel_id=1, source_target_pairs={{0,8},{8,0},{1,9},{9,1},{2,10},{10,2},{3,11},{11,3},{4,12},{12,4},... | collective-permute-start | bytes 1966088 | tf_op jit(solution)/shard_map/ppermute | solution.py:253
  24.8 2.6 %collective-permute-start.12 = (f32[2,512]{1,0:T(2,128)S(1)}, f32[2,512]{1,0:T(2,128)S(1)}, u32[]{:S(2)}, u32[]{:S(2)}) collective-permute-start(f32[2,512]{1,0:T(2,128)S(1)} %get-tuple-element.29.own_ref), channel_id=1, source_target_pairs={{0,8},{8,0},{1,9},{9,1},{2,10},{10,2},{3,11},{11,3},{4,12},{12,4},... | collective-permute-start | bytes 12296 | tf_op jit(solution)/shard_map/ppermute | solution.py:253
  24.9 6.1 %collective-permute-start.10 = (f32[2,256]{1,0:T(2,128)S(1)}, f32[2,256]{1,0:T(2,128)S(1)}, u32[]{:S(2)}, u32[]{:S(2)}) collective-permute-start(f32[2,256]{1,0:T(2,128)S(1)} %get-tuple-element.28.refs_0_), channel_id=1, source_target_pairs={{0,4},{2,6},{4,0},{6,2},{1,5},{3,7},{5,1},{7,3},{8,12},{10,14},{12... | collective-permute-start | bytes 6152 | tf_op jit(solution)/shard_map/ppermute | solution.py:222
  27.4 7.2 %collective-permute-start.15 = (f32[2,512]{1,0:T(2,128)S(1)}, f32[2,512]{1,0:T(2,128)S(1)}, u32[]{:S(2)}, u32[]{:S(2)}) collective-permute-start(f32[2,512]{1,0:T(2,128)S(1)} %shard_map.84.refs_0_), channel_id=1, source_target_pairs={{0,17},{1,16},{16,1},{17,0},{2,19},{3,18},{18,3},{19,2},{4,21},{5,... | collective-permute-start | bytes 12296 | tf_op jit(solution)/shard_map/ppermute | solution.py:225
  28.9 5.8 %collective-permute-start.14 = (f32[2,512]{1,0:T(2,128)S(1)}, f32[2,512]{1,0:T(2,128)S(1)}, u32[]{:S(2)}, u32[]{:S(2)}) collective-permute-start(f32[2,512]{1,0:T(2,128)S(1)} %shard_map.84.refs_0_), channel_id=1, source_target_pairs={{0,16},{1,17},{16,0},{17,1},{2,18},{3,19},{18,2},{19,3},{4,20},{5,... | collective-permute-start | bytes 12296 | tf_op jit(solution)/shard_map/ppermute | solution.py:225
  30.4 4.2 %collective-permute-start.13 = (f32[2,512]{1,0:T(2,128)S(1)}, f32[2,512]{1,0:T(2,128)S(1)}, u32[]{:S(2)}, u32[]{:S(2)}) collective-permute-start(f32[2,512]{1,0:T(2,128)S(1)} %shard_map.84.refs_0_), channel_id=1, source_target_pairs={{0,1},{1,0},{16,17},{17,16},{2,3},{3,2},{18,19},{19,18},{4,5},{5,4... | collective-permute-start | bytes 12296 | tf_op jit(solution)/shard_map/ppermute | solution.py:225
  30.9 3.7 %collective-permute-start.11 = (f32[2,256]{1,0:T(2,128)S(1)}, f32[2,256]{1,0:T(2,128)S(1)}, u32[]{:S(2)}, u32[]{:S(2)}) collective-permute-start(f32[2,256]{1,0:T(2,128)S(1)} %shard_map.82.refs_0_), channel_id=1, source_target_pairs={{0,2},{2,0},{4,6},{6,4},{1,3},{3,1},{5,7},{7,5},{8,10},{10,8},{12,... | collective-permute-start | bytes 6152 | tf_op jit(solution)/shard_map/ppermute | solution.py:222
  35.9 4.5 %collective-permute-start.19 = (bf16[4,64,512]{2,1,0:T(8,128)(2,1)S(1)}, bf16[4,64,512]{2,1,0:T(8,128)(2,1)S(1)}, u32[]{:S(2)}, u32[]{:S(2)}) collective-permute-start(bf16[4,64,512]{2,1,0:T(8,128)(2,1)S(1)} %get-tuple-element.35), channel_id=1, source_target_pairs={{0,8},{8,0},{1,9},{9,1},{2,10},{10,2},{3,11},{11,3},{4,12},{12,4},... | collective-permute-start | bytes 786440 | tf_op jit(solution)/shard_map/ppermute | solution.py:253
  36.0 7.5 %collective-permute-start.16 = (bf16[64,512]{1,0:T(8,128)(2,1)S(1)}, bf16[64,512]{1,0:T(8,128)(2,1)S(1)}, u32[]{:S(2)}, u32[]{:S(2)}) collective-permute-start(bf16[64,512]{1,0:T(8,128)(2,1)S(1)} %get-tuple-element.31), channel_id=1, source_target_pairs={{0,2},{2,0},{4,6},{6,4},{1,3},{3,1},{5,7},{7,5},{8,10},{10,8},{12,... | collective-permute-start | bytes 196616 | tf_op jit(solution)/shard_map/ppermute | solution.py:222
  36.8 8.6 %collective-permute-start.17 = (bf16[64,512]{1,0:T(8,128)(2,1)S(1)}, bf16[64,512]{1,0:T(8,128)(2,1)S(1)}, u32[]{:S(2)}, u32[]{:S(2)}) collective-permute-start(bf16[64,512]{1,0:T(8,128)(2,1)S(1)} %get-tuple-element.32), channel_id=1, source_target_pairs={{0,4},{2,6},{4,0},{6,2},{1,5},{3,7},{5,1},{7,3},{8,12},{10,14},{12... | collective-permute-start | bytes 196616 | tf_op jit(solution)/shard_map/ppermute | solution.py:222
  37.8 7.5 %collective-permute-start.18 = (bf16[64,512]{1,0:T(8,128)(2,1)S(1)}, bf16[64,512]{1,0:T(8,128)(2,1)S(1)}, u32[]{:S(2)}, u32[]{:S(2)}) collective-permute-start(bf16[64,512]{1,0:T(8,128)(2,1)S(1)} %get-tuple-element.33), channel_id=1, source_target_pairs={{0,6},{2,4},{4,2},{6,0},{1,7},{3,5},{5,3},{7,1},{8,14},{10,12},{12... | collective-permute-start | bytes 196616 | tf_op jit(solution)/shard_map/ppermute | solution.py:222
  40.5 5.9 %collective-permute-start.20 = (bf16[64,512]{1,0:T(8,128)(2,1)S(1)}, bf16[64,512]{1,0:T(8,128)(2,1)S(1)}, u32[]{:S(2)}, u32[]{:S(2)}) collective-permute-start(bf16[64,512]{1,0:T(8,128)(2,1)S(1)} %get-tuple-element.37), channel_id=1, source_target_pairs={{0,17},{1,16},{16,1},{17,0},{2,19},{3,18},{18,3},{19,2},{4,21},{5,... | collective-permute-start | bytes 196616 | tf_op jit(solution)/shard_map/ppermute | solution.py:225
  42.0 4.7 %collective-permute-start.21 = (bf16[64,512]{1,0:T(8,128)(2,1)S(1)}, bf16[64,512]{1,0:T(8,128)(2,1)S(1)}, u32[]{:S(2)}, u32[]{:S(2)}) collective-permute-start(bf16[64,512]{1,0:T(8,128)(2,1)S(1)} %get-tuple-element.38), channel_id=1, source_target_pairs={{0,16},{1,17},{16,0},{17,1},{2,18},{3,19},{18,2},{19,3},{4,20},{5,... | collective-permute-start | bytes 196616 | tf_op jit(solution)/shard_map/ppermute | solution.py:225
  43.5 4.3 %collective-permute-start.22 = (bf16[64,512]{1,0:T(8,128)(2,1)S(1)}, bf16[64,512]{1,0:T(8,128)(2,1)S(1)}, u32[]{:S(2)}, u32[]{:S(2)}) collective-permute-start(bf16[64,512]{1,0:T(8,128)(2,1)S(1)} %get-tuple-element.39), channel_id=1, source_target_pairs={{0,1},{1,0},{16,17},{17,16},{2,3},{3,2},{18,19},{19,18},{4,5},{5,4... | collective-permute-start | bytes 196616 | tf_op jit(solution)/shard_map/ppermute | solution.py:225
  (2 other events, 9.1 us)

commit v7 on v6

--- a/solution.py
+++ b/solution.py
@@ -226,7 +226,8 @@
 
     def gather_square(value):
         first = bits(squares)
-        blocks = dict(zip([0] + first, [value] + [to_square(value, s) for s in first]))
+        held = lax.optimization_barrier([value] + [to_square(value, s) for s in first])
+        blocks = dict(zip([0] + first, held))
         for s in sorted(set(range(squares)) - set(blocks), key=lambda s: bin(s).count("1")):
             hop = s & -s
             blocks[s] = to_square(blocks[s ^ hop], hop)

time: 48.8 us -> 49 us (level)
  waiting for transfers between devices: 13.5 us -> 15.8 us
  starting transfers between devices: 27.9 us -> 25.7 us
    ppermute x10, waiting for transfers between devices: 8.91 us -> 14.5 us  [to_line(): return lax.ppermute(value, LINE, [(z, z ^ step) for z in range(depth)])]
    ppermute x9, waiting for transfers between devices: 4.55 us -> 1.31 us  [to_square(): return lax.ppermute(value, SQUARE, [(q, q ^ step) for q in range(squares)])]
    ppermute x10, starting transfers between devices: 15.5 us -> 12.7 us  [to_line(): return lax.ppermute(value, LINE, [(z, z ^ step) for z in range(depth)])]
    ppermute x9, starting transfers between devices: 11.7 us -> 12.2 us  [to_square(): return lax.ppermute(value, SQUARE, [(q, q ^ step) for q in range(squares)])]
  transfers between devices with their start and end apart: 23 -> 23, of which waited for: 9 -> 9; matrix products, arithmetic and copies ran while one was open for 2% -> 0% of each run, Pallas kernels for 2% -> 2%
where the time goes in v7:
time: 49 us; the launch traced here: 48.8 us
  starting transfers between devices  25.7 us (52%)
  waiting for transfers between devices  15.8 us (32%)
  Pallas kernels  4.27 us (9%)
  between operations  2.1 us (4%)
  other arithmetic  0.99 us (2%)
    ppermute x10, waiting for transfers between devices, to_line(): return lax.ppermute(value, LINE, [(z, z ^ step) for z in range(depth)])  14.5 us
    ppermute x10, starting transfers between devices, to_line(): return lax.ppermute(value, LINE, [(z, z ^ step) for z in range(depth)])  12.7 us
    ppermute x9, starting transfers between devices, to_square(): return lax.ppermute(value, SQUARE, [(q, q ^ step) for q in range(squares)])  12.2 us
    pallas_call x13, Pallas kernels, call(): pl.pallas_call(kernel, out_shape=outs, in_specs=specs, out_specs=jax.tree...  4.27 us
    ppermute x9, waiting for transfers between devices, to_square(): return lax.ppermute(value, SQUARE, [(q, q ^ step) for q in range(squares)])  1.31 us
    max x2, other arithmetic, side_by_side(): jnp.maximum(lax.pad(left, lowest, ((0, 0, 0), (0, right_width, 0))), lax....  0.99 us
  transfers between devices with their start and end apart: 23, of which 9 were waited for; matrix products, arithmetic and copies ran while one was open for 0% of the time, Pallas kernels for 2%

profile of v7, /device:TPU:0, one launch (start us, length us, event | category | flops | bytes accessed | tf_op | source)
XLA Modules:
  0.0 48.8 jit_solution(12255108104631155991)
XLA Ops:
  0.7 1.0 %pad_maximum_fusion.refs_0_ = bf16[64,1792]{1,0:T(8,128)(2,1)S(1)} fusion(bf16[64,1280]{1,0:T(8,128)(2,1)} %param.8, bf16[64,512]{1,0:T(8,128)(2,1)} %raw_image_ref.1), kind=kLoop, calls=%fused_computation | loop fusion | flops 458752 | bytes 458752 | tf_op jit(solution)/shard_map/max | solution.py:35
  1.6 3.0 %collective-permute-start.6 = (bf16[64,1792]{1,0:T(8,128)(2,1)S(1)}, bf16[64,1792]{1,0:T(8,128)(2,1)S(1)}, u32[]{:S(2)}, u32[]{:S(2)}) collective-permute-start(bf16[64,1792]{1,0:T(8,128)(2,1)S(1)} %pad_maximum_fusion.refs_0_), channel_id=1, source_target_pairs={{0,1},{1,0},{16,17},{17,16},{2,3},{3,2},{18,19},{19,18},{4,5},{5,4... | collective-permute-start | bytes 688136 | tf_op jit(solution)/shard_map/ppermute | solution.py:225
  4.6 1.5 %collective-permute-start.5 = (bf16[64,1792]{1,0:T(8,128)(2,1)S(1)}, bf16[64,1792]{1,0:T(8,128)(2,1)S(1)}, u32[]{:S(2)}, u32[]{:S(2)}) collective-permute-start(bf16[64,1792]{1,0:T(8,128)(2,1)S(1)} %pad_maximum_fusion.refs_0_), channel_id=1, source_target_pairs={{0,16},{1,17},{16,0},{17,1},{2,18},{3,19},{18,2},{19,3},{4,20},{5,... | collective-permute-start | bytes 688136 | tf_op jit(solution)/shard_map/ppermute | solution.py:225
  6.2 2.6 %collective-permute-start.2 = (bf16[64,1280]{1,0:T(8,128)(2,1)S(1)}, bf16[64,1280]{1,0:T(8,128)(2,1)S(1)}, u32[]{:S(2)}, u32[]{:S(2)}) collective-permute-start(bf16[64,1280]{1,0:T(8,128)(2,1)S(1)} %copy-done.2), channel_id=1, source_target_pairs={{0,4},{2,6},{4,0},{6,2},{1,5},{3,7},{5,1},{7,3},{8,12},{10,14},{12... | collective-permute-start | bytes 491528 | tf_op jit(solution)/shard_map/ppermute | solution.py:222
  8.8 1.6 %collective-permute-start.1 = (bf16[64,1792]{1,0:T(8,128)(2,1)S(1)}, bf16[64,1792]{1,0:T(8,128)(2,1)S(1)}, u32[]{:S(2)}, u32[]{:S(2)}) collective-permute-start(bf16[64,1792]{1,0:T(8,128)(2,1)S(1)} %pad_maximum_fusion.1), channel_id=1, source_target_pairs={{0,2},{2,0},{4,6},{6,4},{1,3},{3,1},{5,7},{7,5},{8,10},{10,8},{12,... | collective-permute-start | bytes 688136 | tf_op jit(solution)/shard_map/ppermute | solution.py:222
  12.7 4.1 %collective-permute-done.2.raw_ref = bf16[64,1280]{1,0:T(8,128)(2,1)S(1)} collective-permute-done((bf16[64,1280]{1,0:T(8,128)(2,1)S(1)}, bf16[64,1280]{1,0:T(8,128)(2,1)S(1)}, u32[]{:S(2)}, u32[]{:S(2)}) %collective-permute-start.2) | collective-permute-done | bytes 163872 | tf_op jit(solution)/shard_map/ppermute | solution.py:222
  17.1 1.9 %collective-permute-done.raw_ref = bf16[64,512]{1,0:T(8,128)(2,1)S(1)} collective-permute-done((bf16[64,512]{1,0:T(8,128)(2,1)S(1)}, bf16[64,512]{1,0:T(8,128)(2,1)S(1)}, u32[]{:S(2)}, u32[]{:S(2)}) %collective-permute-start) | collective-permute-done | bytes 65568 | tf_op jit(solution)/shard_map/ppermute | solution.py:222
  19.0 1.4 %collective-permute-done.1.near_ref = bf16[64,1792]{1,0:T(8,128)(2,1)S(1)} collective-permute-done((bf16[64,1792]{1,0:T(8,128)(2,1)S(1)}, bf16[64,1792]{1,0:T(8,128)(2,1)S(1)}, u32[]{:S(2)}, u32[]{:S(2)}) %collective-permute-start.1) | collective-permute-done | bytes 229408 | tf_op jit(solution)/shard_map/ppermute | solution.py:222
  21.4 3.4 %collective-permute-done.3.refs_2_ = bf16[64,512]{1,0:T(8,128)(2,1)S(1)} collective-permute-done((bf16[64,512]{1,0:T(8,128)(2,1)S(1)}, bf16[64,512]{1,0:T(8,128)(2,1)S(1)}, u32[]{:S(2)}, u32[]{:S(2)}) %collective-permute-start.3) | collective-permute-done | bytes 65568 | tf_op jit(solution)/shard_map/ppermute | solution.py:222
  25.0 1.3 %shard_map.81 = (f32[512,256]{1,0:T(8,128)S(1)}, f32[2,512]{1,0:T(2,128)S(1)}, f32[2,256]{1,0:T(2,128)S(1)}) custom-call(f32[1]{0:T(128)} %bitcast.4.teacher_scale_ref, f32[1]{0:T(128)} %bitcast.5.student_scale_ref, bf16[256,512]{1,0:T(8,128)(2,1)S(1)} %get-tuple-element.26.pupil_text_ref.text_ref, bf16[256,1280]{1,0:T(8,128)(2,1)S(1)} %get-tuple-element.27.master_text_ref, ...), custom_call_target="tpu_custom_call" | custom-call | flops 1048576 | bytes 1048576 | tf_op jit(solution)/shard_map/pallas_call | solution.py:201
  26.4 2.1 %collective-permute-start.10 = (f32[2,256]{1,0:T(2,128)S(1)}, f32[2,256]{1,0:T(2,128)S(1)}, u32[]{:S(2)}, u32[]{:S(2)}) collective-permute-start(f32[2,256]{1,0:T(2,128)S(1)} %get-tuple-element.34.refs_0_), channel_id=1, source_target_pairs={{0,4},{2,6},{4,0},{6,2},{1,5},{3,7},{5,1},{7,3},{8,12},{10,14},{12... | collective-permute-start | bytes 6152 | tf_op jit(solution)/shard_map/ppermute | solution.py:222
  29.0 1.5 %collective-permute-start.14 = (f32[2,512]{1,0:T(2,128)S(1)}, f32[2,512]{1,0:T(2,128)S(1)}, u32[]{:S(2)}, u32[]{:S(2)}) collective-permute-start(f32[2,512]{1,0:T(2,128)S(1)} %shard_map.84.refs_0_), channel_id=1, source_target_pairs={{0,16},{1,17},{16,0},{17,1},{2,18},{3,19},{18,2},{19,3},{4,20},{5,... | collective-permute-start | bytes 12296 | tf_op jit(solution)/shard_map/ppermute | solution.py:225
  30.6 1.5 %collective-permute-start.13 = (f32[2,512]{1,0:T(2,128)S(1)}, f32[2,512]{1,0:T(2,128)S(1)}, u32[]{:S(2)}, u32[]{:S(2)}) collective-permute-start(f32[2,512]{1,0:T(2,128)S(1)} %shard_map.84.refs_0_), channel_id=1, source_target_pairs={{0,1},{1,0},{16,17},{17,16},{2,3},{3,2},{18,19},{19,18},{4,5},{5,4... | collective-permute-start | bytes 12296 | tf_op jit(solution)/shard_map/ppermute | solution.py:225
  32.1 1.3 %collective-permute-start.11 = (f32[2,256]{1,0:T(2,128)S(1)}, f32[2,256]{1,0:T(2,128)S(1)}, u32[]{:S(2)}, u32[]{:S(2)}) collective-permute-start(f32[2,256]{1,0:T(2,128)S(1)} %shard_map.82.refs_0_), channel_id=1, source_target_pairs={{0,2},{2,0},{4,6},{6,4},{1,3},{3,1},{5,7},{7,5},{8,10},{10,8},{12,... | collective-permute-start | bytes 6152 | tf_op jit(solution)/shard_map/ppermute | solution.py:222
  33.4 2.3 %collective-permute-done.11.refs_1_ = f32[2,256]{1,0:T(2,128)S(1)} collective-permute-done((f32[2,256]{1,0:T(2,128)S(1)}, f32[2,256]{1,0:T(2,128)S(1)}, u32[]{:S(2)}, u32[]{:S(2)}) %collective-permute-start.11) | collective-permute-done | bytes 2080 | tf_op jit(solution)/shard_map/ppermute | solution.py:222
  35.8 1.2 %shard_map.86 = (f32[4,64,512]{2,1,0:T(8,128)S(1)}, bf16[4,64,512]{2,1,0:T(8,128)(2,1)S(1)}, f32[64,512]{1,0:T(8,128)S(1)}, bf16[64,512]{1,0:T(8,128)(2,1)S(1)},...) custom-call(s32[1]{0:T(128)} %bitcast.z_ref, f32[1]{0:T(128)} %bitcast.6.scale_ref, ...), custom_call_target="tpu_custom_call" | custom-call | flops 1048576 | bytes 1048576 | tf_op jit(solution)/shard_map/pallas_call | solution.py:201
  37.1 1.3 %collective-permute-start.16 = (bf16[64,512]{1,0:T(8,128)(2,1)S(1)}, bf16[64,512]{1,0:T(8,128)(2,1)S(1)}, u32[]{:S(2)}, u32[]{:S(2)}) collective-permute-start(bf16[64,512]{1,0:T(8,128)(2,1)S(1)} %get-tuple-element.37), channel_id=1, source_target_pairs={{0,2},{2,0},{4,6},{6,4},{1,3},{3,1},{5,7},{7,5},{8,10},{10,8},{12,... | collective-permute-start | bytes 196616 | tf_op jit(solution)/shard_map/ppermute | solution.py:222
  38.4 1.1 %collective-permute-start.17 = (bf16[64,512]{1,0:T(8,128)(2,1)S(1)}, bf16[64,512]{1,0:T(8,128)(2,1)S(1)}, u32[]{:S(2)}, u32[]{:S(2)}) collective-permute-start(bf16[64,512]{1,0:T(8,128)(2,1)S(1)} %get-tuple-element.38), channel_id=1, source_target_pairs={{0,4},{2,6},{4,0},{6,2},{1,5},{3,7},{5,1},{7,3},{8,12},{10,14},{12... | collective-permute-start | bytes 196616 | tf_op jit(solution)/shard_map/ppermute | solution.py:222
  39.5 2.1 %collective-permute-start.18 = (bf16[64,512]{1,0:T(8,128)(2,1)S(1)}, bf16[64,512]{1,0:T(8,128)(2,1)S(1)}, u32[]{:S(2)}, u32[]{:S(2)}) collective-permute-start(bf16[64,512]{1,0:T(8,128)(2,1)S(1)} %get-tuple-element.39), channel_id=1, source_target_pairs={{0,6},{2,4},{4,2},{6,0},{1,7},{3,5},{5,3},{7,1},{8,14},{10,12},{12... | collective-permute-start | bytes 196616 | tf_op jit(solution)/shard_map/ppermute | solution.py:222
  42.2 1.5 %collective-permute-start.21 = (bf16[64,512]{1,0:T(8,128)(2,1)S(1)}, bf16[64,512]{1,0:T(8,128)(2,1)S(1)}, u32[]{:S(2)}, u32[]{:S(2)}) collective-permute-start(bf16[64,512]{1,0:T(8,128)(2,1)S(1)} %get-tuple-element.44), channel_id=1, source_target_pairs={{0,16},{1,17},{16,0},{17,1},{2,18},{3,19},{18,2},{19,3},{4,20},{5,... | collective-permute-start | bytes 196616 | tf_op jit(solution)/shard_map/ppermute | solution.py:225
  43.7 1.5 %collective-permute-start.22 = (bf16[64,512]{1,0:T(8,128)(2,1)S(1)}, bf16[64,512]{1,0:T(8,128)(2,1)S(1)}, u32[]{:S(2)}, u32[]{:S(2)}) collective-permute-start(bf16[64,512]{1,0:T(8,128)(2,1)S(1)} %get-tuple-element.45), channel_id=1, source_target_pairs={{0,1},{1,0},{16,17},{17,16},{2,3},{3,2},{18,19},{19,18},{4,5},{5,4... | collective-permute-start | bytes 196616 | tf_op jit(solution)/shard_map/ppermute | solution.py:225
  45.2 1.4 %collective-permute-done.17.refs_2_ = bf16[64,512]{1,0:T(8,128)(2,1)S(1)} collective-permute-done((bf16[64,512]{1,0:T(8,128)(2,1)S(1)}, bf16[64,512]{1,0:T(8,128)(2,1)S(1)}, u32[]{:S(2)}, u32[]{:S(2)}) %collective-permute-start.17) | collective-permute-done | bytes 65568 | tf_op jit(solution)/shard_map/ppermute | solution.py:222
  47.1 0.8 %collective-permute-done.22.refs_3_ = bf16[64,512]{1,0:T(8,128)(2,1)S(1)} collective-permute-done((bf16[64,512]{1,0:T(8,128)(2,1)S(1)}, bf16[64,512]{1,0:T(8,128)(2,1)S(1)}, u32[]{:S(2)}, u32[]{:S(2)}) %collective-permute-start.22) | collective-permute-done | bytes 65568 | tf_op jit(solution)/shard_map/ppermute | solution.py:225
  48.0 0.9 %shard_map.89 = (f32[64,512]{1,0:T(8,128)}, f32[64,512]{1,0:T(8,128)}) custom-call(bf16[64,512]{1,0:T(8,128)(2,1)S(1)} %copy-done, bf16[64,512]{1,0:T(8,128)(2,1)S(1)} %copy-done.1, f32[64,512]{1,0:T(8,128)S(1)} %shard_map.87.text_ref, f32[64,512]{1,0:T(8,128)S(1)} %get-tuple-element.42.refs_0_, bf16[64,512]{1,0:T(8,128)(2,1)S(1)} %collective-permute-done.20.refs_1_, ...), custom_call_target="tpu_custom_call" | custom-call | flops 1048576 | bytes 1048576 | tf_op jit(solution)/shard_map/pallas_call | solution.py:201
  (43 shorter events, 4.4 us)
Async XLA Ops:
  0.6 8.1 %copy-start.1 = (bf16[64,512]{1,0:T(8,128)(2,1)S(1)}, bf16[64,512]{1,0:T(8,128)(2,1)}, u32[]{:S(2)}) copy-start(bf16[64,512]{1,0:T(8,128)(2,1)} %raw_text_ref.1) | copy-start | bytes 196612
  1.6 10.4 %collective-permute-start.6 = (bf16[64,1792]{1,0:T(8,128)(2,1)S(1)}, bf16[64,1792]{1,0:T(8,128)(2,1)S(1)}, u32[]{:S(2)}, u32[]{:S(2)}) collective-permute-start(bf16[64,1792]{1,0:T(8,128)(2,1)S(1)} %pad_maximum_fusion.refs_0_), channel_id=1, source_target_pairs={{0,1},{1,0},{16,17},{17,16},{2,3},{3,2},{18,19},{19,18},{4,5},{5,4... | collective-permute-start | bytes 688136 | tf_op jit(solution)/shard_map/ppermute | solution.py:225
  4.6 7.4 %collective-permute-start.5 = (bf16[64,1792]{1,0:T(8,128)(2,1)S(1)}, bf16[64,1792]{1,0:T(8,128)(2,1)S(1)}, u32[]{:S(2)}, u32[]{:S(2)}) collective-permute-start(bf16[64,1792]{1,0:T(8,128)(2,1)S(1)} %pad_maximum_fusion.refs_0_), channel_id=1, source_target_pairs={{0,16},{1,17},{16,0},{17,1},{2,18},{3,19},{18,2},{19,3},{4,20},{5,... | collective-permute-start | bytes 688136 | tf_op jit(solution)/shard_map/ppermute | solution.py:225
  6.2 10.6 %collective-permute-start.2 = (bf16[64,1280]{1,0:T(8,128)(2,1)S(1)}, bf16[64,1280]{1,0:T(8,128)(2,1)S(1)}, u32[]{:S(2)}, u32[]{:S(2)}) collective-permute-start(bf16[64,1280]{1,0:T(8,128)(2,1)S(1)} %copy-done.2), channel_id=1, source_target_pairs={{0,4},{2,6},{4,0},{6,2},{1,5},{3,7},{5,1},{7,3},{8,12},{10,14},{12... | collective-permute-start | bytes 491528 | tf_op jit(solution)/shard_map/ppermute | solution.py:222
  8.8 11.6 %collective-permute-start.1 = (bf16[64,1792]{1,0:T(8,128)(2,1)S(1)}, bf16[64,1792]{1,0:T(8,128)(2,1)S(1)}, u32[]{:S(2)}, u32[]{:S(2)}) collective-permute-start(bf16[64,1792]{1,0:T(8,128)(2,1)S(1)} %pad_maximum_fusion.1), channel_id=1, source_target_pairs={{0,2},{2,0},{4,6},{6,4},{1,3},{3,1},{5,7},{7,5},{8,10},{10,8},{12,... | collective-permute-start | bytes 688136 | tf_op jit(solution)/shard_map/ppermute | solution.py:222
  10.4 8.6 %collective-permute-start = (bf16[64,512]{1,0:T(8,128)(2,1)S(1)}, bf16[64,512]{1,0:T(8,128)(2,1)S(1)}, u32[]{:S(2)}, u32[]{:S(2)}) collective-permute-start(bf16[64,512]{1,0:T(8,128)(2,1)S(1)} %copy-done.1), channel_id=1, source_target_pairs={{0,4},{2,6},{4,0},{6,2},{1,5},{3,7},{5,1},{7,3},{8,12},{10,14},{12... | collective-permute-start | bytes 196616 | tf_op jit(solution)/shard_map/ppermute | solution.py:222
  12.1 8.5 %collective-permute-start.7 = (bf16[64,1792]{1,0:T(8,128)(2,1)S(1)}, bf16[64,1792]{1,0:T(8,128)(2,1)S(1)}, u32[]{:S(2)}, u32[]{:S(2)}) collective-permute-start(bf16[64,1792]{1,0:T(8,128)(2,1)S(1)} %collective-permute-done.5.refs_2_), channel_id=1, source_target_pairs={{0,1},{1,0},{16,17},{17,16},{2,3},{3,2},{18,19},{19,18},{4,5},{5,4... | collective-permute-start | bytes 688136 | tf_op jit(solution)/shard_map/ppermute | solution.py:225
  16.9 7.9 %collective-permute-start.4 = (bf16[64,1280]{1,0:T(8,128)(2,1)S(1)}, bf16[64,1280]{1,0:T(8,128)(2,1)S(1)}, u32[]{:S(2)}, u32[]{:S(2)}) collective-permute-start(bf16[64,1280]{1,0:T(8,128)(2,1)S(1)} %shard_map.78.refs_1_), channel_id=1, source_target_pairs={{0,2},{2,0},{4,6},{6,4},{1,3},{3,1},{5,7},{7,5},{8,10},{10,8},{12,... | collective-permute-start | bytes 491528 | tf_op jit(solution)/shard_map/ppermute | solution.py:222
  20.4 4.3 %collective-permute-start.3 = (bf16[64,512]{1,0:T(8,128)(2,1)S(1)}, bf16[64,512]{1,0:T(8,128)(2,1)S(1)}, u32[]{:S(2)}, u32[]{:S(2)}) collective-permute-start(bf16[64,512]{1,0:T(8,128)(2,1)S(1)} %shard_map.77.refs_0_), channel_id=1, source_target_pairs={{0,2},{2,0},{4,6},{6,4},{1,3},{3,1},{5,7},{7,5},{8,10},{10,8},{12,... | collective-permute-start | bytes 196616 | tf_op jit(solution)/shard_map/ppermute | solution.py:222
  20.8 4.1 %collective-permute-start.8 = (bf16[256,512]{1,0:T(8,128)(2,1)S(1)}, bf16[256,512]{1,0:T(8,128)(2,1)S(1)}, u32[]{:S(2)}, u32[]{:S(2)}) collective-permute-start(bf16[256,512]{1,0:T(8,128)(2,1)S(1)} %get-tuple-element.31.pupil_same_ref.same_ref), channel_id=1, source_target_pairs={{0,8},{8,0},{1,9},{9,1},{2,10},{10,2},{3,11},{11,3},{4,12},{12,4},... | collective-permute-start | bytes 786440 | tf_op jit(solution)/shard_map/ppermute | solution.py:254
  20.9 4.1 %collective-permute-start.9 = (bf16[256,1280]{1,0:T(8,128)(2,1)S(1)}, bf16[256,1280]{1,0:T(8,128)(2,1)S(1)}, u32[]{:S(2)}, u32[]{:S(2)}) collective-permute-start(bf16[256,1280]{1,0:T(8,128)(2,1)S(1)} %get-tuple-element.32.master_same_ref), channel_id=1, source_target_pairs={{0,8},{8,0},{1,9},{9,1},{2,10},{10,2},{3,11},{11,3},{4,12},{12,4},... | collective-permute-start | bytes 1966088 | tf_op jit(solution)/shard_map/ppermute | solution.py:254
  26.3 2.2 %collective-permute-start.12 = (f32[2,512]{1,0:T(2,128)S(1)}, f32[2,512]{1,0:T(2,128)S(1)}, u32[]{:S(2)}, u32[]{:S(2)}) collective-permute-start(f32[2,512]{1,0:T(2,128)S(1)} %get-tuple-element.35.own_ref), channel_id=1, source_target_pairs={{0,8},{8,0},{1,9},{9,1},{2,10},{10,2},{3,11},{11,3},{4,12},{12,4},... | collective-permute-start | bytes 12296 | tf_op jit(solution)/shard_map/ppermute | solution.py:254
  26.4 5.7 %collective-permute-start.10 = (f32[2,256]{1,0:T(2,128)S(1)}, f32[2,256]{1,0:T(2,128)S(1)}, u32[]{:S(2)}, u32[]{:S(2)}) collective-permute-start(f32[2,256]{1,0:T(2,128)S(1)} %get-tuple-element.34.refs_0_), channel_id=1, source_target_pairs={{0,4},{2,6},{4,0},{6,2},{1,5},{3,7},{5,1},{7,3},{8,12},{10,14},{12... | collective-permute-start | bytes 6152 | tf_op jit(solution)/shard_map/ppermute | solution.py:222
  28.5 7.2 %collective-permute-start.15 = (f32[2,512]{1,0:T(2,128)S(1)}, f32[2,512]{1,0:T(2,128)S(1)}, u32[]{:S(2)}, u32[]{:S(2)}) collective-permute-start(f32[2,512]{1,0:T(2,128)S(1)} %shard_map.84.refs_0_), channel_id=1, source_target_pairs={{0,17},{1,16},{16,1},{17,0},{2,19},{3,18},{18,3},{19,2},{4,21},{5,... | collective-permute-start | bytes 12296 | tf_op jit(solution)/shard_map/ppermute | solution.py:225
  29.0 6.7 %collective-permute-start.14 = (f32[2,512]{1,0:T(2,128)S(1)}, f32[2,512]{1,0:T(2,128)S(1)}, u32[]{:S(2)}, u32[]{:S(2)}) collective-permute-start(f32[2,512]{1,0:T(2,128)S(1)} %shard_map.84.refs_0_), channel_id=1, source_target_pairs={{0,16},{1,17},{16,0},{17,1},{2,18},{3,19},{18,2},{19,3},{4,20},{5,... | collective-permute-start | bytes 12296 | tf_op jit(solution)/shard_map/ppermute | solution.py:225
  30.6 5.2 %collective-permute-start.13 = (f32[2,512]{1,0:T(2,128)S(1)}, f32[2,512]{1,0:T(2,128)S(1)}, u32[]{:S(2)}, u32[]{:S(2)}) collective-permute-start(f32[2,512]{1,0:T(2,128)S(1)} %shard_map.84.refs_0_), channel_id=1, source_target_pairs={{0,1},{1,0},{16,17},{17,16},{2,3},{3,2},{18,19},{19,18},{4,5},{5,4... | collective-permute-start | bytes 12296 | tf_op jit(solution)/shard_map/ppermute | solution.py:225
  32.1 3.7 %collective-permute-start.11 = (f32[2,256]{1,0:T(2,128)S(1)}, f32[2,256]{1,0:T(2,128)S(1)}, u32[]{:S(2)}, u32[]{:S(2)}) collective-permute-start(f32[2,256]{1,0:T(2,128)S(1)} %shard_map.82.refs_0_), channel_id=1, source_target_pairs={{0,2},{2,0},{4,6},{6,4},{1,3},{3,1},{5,7},{7,5},{8,10},{10,8},{12,... | collective-permute-start | bytes 6152 | tf_op jit(solution)/shard_map/ppermute | solution.py:222
  37.0 4.5 %collective-permute-start.19 = (bf16[4,64,512]{2,1,0:T(8,128)(2,1)S(1)}, bf16[4,64,512]{2,1,0:T(8,128)(2,1)S(1)}, u32[]{:S(2)}, u32[]{:S(2)}) collective-permute-start(bf16[4,64,512]{2,1,0:T(8,128)(2,1)S(1)} %get-tuple-element.41), channel_id=1, source_target_pairs={{0,8},{8,0},{1,9},{9,1},{2,10},{10,2},{3,11},{11,3},{4,12},{12,4},... | collective-permute-start | bytes 786440 | tf_op jit(solution)/shard_map/ppermute | solution.py:254
  37.1 6.6 %collective-permute-start.16 = (bf16[64,512]{1,0:T(8,128)(2,1)S(1)}, bf16[64,512]{1,0:T(8,128)(2,1)S(1)}, u32[]{:S(2)}, u32[]{:S(2)}) collective-permute-start(bf16[64,512]{1,0:T(8,128)(2,1)S(1)} %get-tuple-element.37), channel_id=1, source_target_pairs={{0,2},{2,0},{4,6},{6,4},{1,3},{3,1},{5,7},{7,5},{8,10},{10,8},{12,... | collective-permute-start | bytes 196616 | tf_op jit(solution)/shard_map/ppermute | solution.py:222
  38.4 8.2 %collective-permute-start.17 = (bf16[64,512]{1,0:T(8,128)(2,1)S(1)}, bf16[64,512]{1,0:T(8,128)(2,1)S(1)}, u32[]{:S(2)}, u32[]{:S(2)}) collective-permute-start(bf16[64,512]{1,0:T(8,128)(2,1)S(1)} %get-tuple-element.38), channel_id=1, source_target_pairs={{0,4},{2,6},{4,0},{6,2},{1,5},{3,7},{5,1},{7,3},{8,12},{10,14},{12... | collective-permute-start | bytes 196616 | tf_op jit(solution)/shard_map/ppermute | solution.py:222
  39.5 7.1 %collective-permute-start.18 = (bf16[64,512]{1,0:T(8,128)(2,1)S(1)}, bf16[64,512]{1,0:T(8,128)(2,1)S(1)}, u32[]{:S(2)}, u32[]{:S(2)}) collective-permute-start(bf16[64,512]{1,0:T(8,128)(2,1)S(1)} %get-tuple-element.39), channel_id=1, source_target_pairs={{0,6},{2,4},{4,2},{6,0},{1,7},{3,5},{5,3},{7,1},{8,14},{10,12},{12... | collective-permute-start | bytes 196616 | tf_op jit(solution)/shard_map/ppermute | solution.py:222
  41.6 5.4 %collective-permute-start.20 = (bf16[64,512]{1,0:T(8,128)(2,1)S(1)}, bf16[64,512]{1,0:T(8,128)(2,1)S(1)}, u32[]{:S(2)}, u32[]{:S(2)}) collective-permute-start(bf16[64,512]{1,0:T(8,128)(2,1)S(1)} %get-tuple-element.43), channel_id=1, source_target_pairs={{0,17},{1,16},{16,1},{17,0},{2,19},{3,18},{18,3},{19,2},{4,21},{5,... | collective-permute-start | bytes 196616 | tf_op jit(solution)/shard_map/ppermute | solution.py:225
  42.2 5.0 %collective-permute-start.21 = (bf16[64,512]{1,0:T(8,128)(2,1)S(1)}, bf16[64,512]{1,0:T(8,128)(2,1)S(1)}, u32[]{:S(2)}, u32[]{:S(2)}) collective-permute-start(bf16[64,512]{1,0:T(8,128)(2,1)S(1)} %get-tuple-element.44), channel_id=1, source_target_pairs={{0,16},{1,17},{16,0},{17,1},{2,18},{3,19},{18,2},{19,3},{4,20},{5,... | collective-permute-start | bytes 196616 | tf_op jit(solution)/shard_map/ppermute | solution.py:225
  43.7 4.3 %collective-permute-start.22 = (bf16[64,512]{1,0:T(8,128)(2,1)S(1)}, bf16[64,512]{1,0:T(8,128)(2,1)S(1)}, u32[]{:S(2)}, u32[]{:S(2)}) collective-permute-start(bf16[64,512]{1,0:T(8,128)(2,1)S(1)} %get-tuple-element.45), channel_id=1, source_target_pairs={{0,1},{1,0},{16,17},{17,16},{2,3},{3,2},{18,19},{19,18},{4,5},{5,4... | collective-permute-start | bytes 196616 | tf_op jit(solution)/shard_map/ppermute | solution.py:225
  (2 other events, 6.9 us)

commit v8 on v6

--- a/solution.py
+++ b/solution.py
@@ -232,13 +232,13 @@
             blocks[s] = to_square(blocks[s ^ hop], hop)
         return [blocks[s] for s in range(squares)]
 
-    def gather_line(student, teacher):
+    def gather_line(student, teacher, plane_block):
         far = bits(depth)[:-1]
         parts = [student, teacher]
         units = {s: [to_line(part, s) for part in parts] for s in far}
         near = to_line(side_by_side(student, teacher), 1)
         for s in far:
-            units[s][0], near = lax.optimization_barrier((units[s][0], near))
+            units[s][0], near, plane_block = lax.optimization_barrier((units[s][0], near, plane_block))
             for k, raw in enumerate(units[s]):
                 units[s][k] = call(
                     unit_kernel, shaped(raw.shape, BF16), (raw,), [vmem], vmem, flops=SOME
@@ -247,7 +247,7 @@
         for s in sorted(rest, key=lambda s: bin(s).count("1")):
             hop = s & -s
             units[s] = [to_line(part, hop) for part in units[s ^ hop]]
-        return near, units
+        return near, units, plane_block
 
     def to_sibling(value):
         return lax.ppermute(value, "core", [(0, 1), (1, 0)])
@@ -265,7 +265,7 @@
 
         raw_image = side_by_side(student_image, teacher_image)
         blocks = gather_square(raw_image)
-        near, units = gather_line(student_text, teacher_text)
+        near, units, blocks[1] = gather_line(student_text, teacher_text, blocks[1])
         raw_texts = [student_text, teacher_text, near] + sum(units.values(), [])
 
         pupil_text, master_text = call(

time: 48.8 us -> 48 us (0.984)
  waiting for transfers between devices: 13.5 us -> 12.6 us
    ppermute x10, waiting for transfers between devices: 8.91 us -> 8.4 us  [to_line(): return lax.ppermute(value, LINE, [(z, z ^ step) for z in range(depth)])]
where the time goes in v8:
time: 48 us; the launch traced here: 47.8 us
  starting transfers between devices  27.9 us (58%)
  waiting for transfers between devices  12.6 us (26%)
  Pallas kernels  4.27 us (9%)
  between operations  2.1 us (4%)
  other arithmetic  0.95 us (2%)
    ppermute x10, starting transfers between devices, to_line(): return lax.ppermute(value, LINE, [(z, z ^ step) for z in range(depth)])  15.5 us
    ppermute x9, starting transfers between devices, to_square(): return lax.ppermute(value, SQUARE, [(q, q ^ step) for q in range(squares)])  11.7 us
    ppermute x10, waiting for transfers between devices, to_line(): return lax.ppermute(value, LINE, [(z, z ^ step) for z in range(depth)])  8.4 us
    pallas_call x13, Pallas kernels, call(): pl.pallas_call(kernel, out_shape=outs, in_specs=specs, out_specs=jax.tree...  4.27 us
    ppermute x9, waiting for transfers between devices, to_square(): return lax.ppermute(value, SQUARE, [(q, q ^ step) for q in range(squares)])  4.18 us
  transfers between devices with their start and end apart: 23, of which 9 were waited for; matrix products, arithmetic and copies ran while one was open for 2% of the time, Pallas kernels for 2%

profile of v8, /device:TPU:0, one launch (start us, length us, event | category | flops | bytes accessed | tf_op | source)
XLA Modules:
  0.0 47.8 jit_solution(6613142983825483339)
XLA Ops:
  0.7 4.1 %collective-permute-start.3 = (bf16[64,1280]{1,0:T(8,128)(2,1)}, bf16[64,1280]{1,0:T(8,128)(2,1)S(1)}, u32[]{:S(2)}, u32[]{:S(2)}) collective-permute-start(bf16[64,1280]{1,0:T(8,128)(2,1)} %teacher_ref.1), channel_id=1, source_target_pairs={{0,4},{2,6},{4,0},{6,2},{1,5},{3,7},{5,1},{7,3},{8,12},{10,14},{12... | collective-permute-start | bytes 491528 | tf_op jit(solution)/shard_map/ppermute | solution.py:222
  4.8 0.9 %pad_maximum_fusion.refs_0_ = bf16[64,1792]{1,0:T(8,128)(2,1)S(1)} fusion(bf16[64,1280]{1,0:T(8,128)(2,1)} %param.8, bf16[64,512]{1,0:T(8,128)(2,1)} %raw_image_ref.1), kind=kLoop, calls=%fused_computation | loop fusion | flops 458752 | bytes 458752 | tf_op jit(solution)/shard_map/max | solution.py:35
  5.7 1.6 %collective-permute-start.6 = (bf16[64,1792]{1,0:T(8,128)(2,1)S(1)}, bf16[64,1792]{1,0:T(8,128)(2,1)S(1)}, u32[]{:S(2)}, u32[]{:S(2)}) collective-permute-start(bf16[64,1792]{1,0:T(8,128)(2,1)S(1)} %pad_maximum_fusion.refs_0_), channel_id=1, source_target_pairs={{0,16},{1,17},{16,0},{17,1},{2,18},{3,19},{18,2},{19,3},{4,20},{5,... | collective-permute-start | bytes 688136 | tf_op jit(solution)/shard_map/ppermute | solution.py:225
  7.3 1.6 %collective-permute-start.1 = (bf16[64,1792]{1,0:T(8,128)(2,1)S(1)}, bf16[64,1792]{1,0:T(8,128)(2,1)S(1)}, u32[]{:S(2)}, u32[]{:S(2)}) collective-permute-start(bf16[64,1792]{1,0:T(8,128)(2,1)S(1)} %pad_maximum_fusion.1), channel_id=1, source_target_pairs={{0,2},{2,0},{4,6},{6,4},{1,3},{3,1},{5,7},{7,5},{8,10},{10,8},{12,... | collective-permute-start | bytes 688136 | tf_op jit(solution)/shard_map/ppermute | solution.py:222
  8.9 1.5 %collective-permute-start.2 = (bf16[64,1792]{1,0:T(8,128)(2,1)S(1)}, bf16[64,1792]{1,0:T(8,128)(2,1)S(1)}, u32[]{:S(2)}, u32[]{:S(2)}) collective-permute-start(bf16[64,1792]{1,0:T(8,128)(2,1)S(1)} %pad_maximum_fusion.refs_0_), channel_id=1, source_target_pairs={{0,1},{1,0},{16,17},{17,16},{2,3},{3,2},{18,19},{19,18},{4,5},{5,4... | collective-permute-start | bytes 688136 | tf_op jit(solution)/shard_map/ppermute | solution.py:225
  12.8 1.5 %collective-permute-start.7 = (bf16[64,1792]{1,0:T(8,128)(2,1)S(1)}, bf16[64,1792]{1,0:T(8,128)(2,1)S(1)}, u32[]{:S(2)}, u32[]{:S(2)}) collective-permute-start(bf16[64,1792]{1,0:T(8,128)(2,1)S(1)} %collective-permute-done.6.refs_2_), channel_id=1, source_target_pairs={{0,1},{1,0},{16,17},{17,16},{2,3},{3,2},{18,19},{19,18},{4,5},{5,4... | collective-permute-start | bytes 688136 | tf_op jit(solution)/shard_map/ppermute | solution.py:225
  14.4 1.6 %collective-permute-start.5 = (bf16[64,1280]{1,0:T(8,128)(2,1)S(1)}, bf16[64,1280]{1,0:T(8,128)(2,1)S(1)}, u32[]{:S(2)}, u32[]{:S(2)}) collective-permute-start(bf16[64,1280]{1,0:T(8,128)(2,1)S(1)} %shard_map.78.refs_1_), channel_id=1, source_target_pairs={{0,2},{2,0},{4,6},{6,4},{1,3},{3,1},{5,7},{7,5},{8,10},{10,8},{12,... | collective-permute-start | bytes 491528 | tf_op jit(solution)/shard_map/ppermute | solution.py:222
  16.1 2.7 %collective-permute-done.1.near_ref = bf16[64,1792]{1,0:T(8,128)(2,1)S(1)} collective-permute-done((bf16[64,1792]{1,0:T(8,128)(2,1)S(1)}, bf16[64,1792]{1,0:T(8,128)(2,1)S(1)}, u32[]{:S(2)}, u32[]{:S(2)}) %collective-permute-start.1) | collective-permute-done | bytes 229408 | tf_op jit(solution)/shard_map/ppermute | solution.py:222
  19.0 1.3 %collective-permute-done.7.refs_3_ = bf16[64,1792]{1,0:T(8,128)(2,1)S(1)} collective-permute-done((bf16[64,1792]{1,0:T(8,128)(2,1)S(1)}, bf16[64,1792]{1,0:T(8,128)(2,1)S(1)}, u32[]{:S(2)}, u32[]{:S(2)}) %collective-permute-start.7) | collective-permute-done | bytes 229408 | tf_op jit(solution)/shard_map/ppermute | solution.py:225
  21.2 2.0 %collective-permute-done.4.refs_2_ = bf16[64,512]{1,0:T(8,128)(2,1)S(1)} collective-permute-done((bf16[64,512]{1,0:T(8,128)(2,1)S(1)}, bf16[64,512]{1,0:T(8,128)(2,1)S(1)}, u32[]{:S(2)}, u32[]{:S(2)}) %collective-permute-start.4) | collective-permute-done | bytes 65568 | tf_op jit(solution)/shard_map/ppermute | solution.py:222
  23.5 1.3 %shard_map.81 = (f32[512,256]{1,0:T(8,128)S(1)}, f32[2,512]{1,0:T(2,128)S(1)}, f32[2,256]{1,0:T(2,128)S(1)}) custom-call(f32[1]{0:T(128)} %bitcast.4.teacher_scale_ref, f32[1]{0:T(128)} %bitcast.5.student_scale_ref, bf16[256,512]{1,0:T(8,128)(2,1)S(1)} %get-tuple-element.24.pupil_text_ref.text_ref, bf16[256,1280]{1,0:T(8,128)(2,1)S(1)} %get-tuple-element.25.master_text_ref, ...), custom_call_target="tpu_custom_call" | custom-call | flops 1048576 | bytes 1048576 | tf_op jit(solution)/shard_map/pallas_call | solution.py:201
  24.9 1.6 %collective-permute-start.10 = (f32[2,256]{1,0:T(2,128)S(1)}, f32[2,256]{1,0:T(2,128)S(1)}, u32[]{:S(2)}, u32[]{:S(2)}) collective-permute-start(f32[2,256]{1,0:T(2,128)S(1)} %get-tuple-element.30.refs_0_), channel_id=1, source_target_pairs={{0,4},{2,6},{4,0},{6,2},{1,5},{3,7},{5,1},{7,3},{8,12},{10,14},{12... | collective-permute-start | bytes 6152 | tf_op jit(solution)/shard_map/ppermute | solution.py:222
  26.5 1.6 %collective-permute-start.15 = (f32[2,512]{1,0:T(2,128)S(1)}, f32[2,512]{1,0:T(2,128)S(1)}, u32[]{:S(2)}, u32[]{:S(2)}) collective-permute-start(f32[2,512]{1,0:T(2,128)S(1)} %shard_map.84.refs_0_), channel_id=1, source_target_pairs={{0,17},{1,16},{16,1},{17,0},{2,19},{3,18},{18,3},{19,2},{4,21},{5,... | collective-permute-start | bytes 12296 | tf_op jit(solution)/shard_map/ppermute | solution.py:225
  28.1 1.4 %collective-permute-start.14 = (f32[2,512]{1,0:T(2,128)S(1)}, f32[2,512]{1,0:T(2,128)S(1)}, u32[]{:S(2)}, u32[]{:S(2)}) collective-permute-start(f32[2,512]{1,0:T(2,128)S(1)} %shard_map.84.refs_0_), channel_id=1, source_target_pairs={{0,16},{1,17},{16,0},{17,1},{2,18},{3,19},{18,2},{19,3},{4,20},{5,... | collective-permute-start | bytes 12296 | tf_op jit(solution)/shard_map/ppermute | solution.py:225
  30.1 1.7 %collective-permute-start.11 = (f32[2,256]{1,0:T(2,128)S(1)}, f32[2,256]{1,0:T(2,128)S(1)}, u32[]{:S(2)}, u32[]{:S(2)}) collective-permute-start(f32[2,256]{1,0:T(2,128)S(1)} %shard_map.82.refs_0_), channel_id=1, source_target_pairs={{0,2},{2,0},{4,6},{6,4},{1,3},{3,1},{5,7},{7,5},{8,10},{10,8},{12,... | collective-permute-start | bytes 6152 | tf_op jit(solution)/shard_map/ppermute | solution.py:222
  31.7 2.0 %collective-permute-done.11.refs_1_ = f32[2,256]{1,0:T(2,128)S(1)} collective-permute-done((f32[2,256]{1,0:T(2,128)S(1)}, f32[2,256]{1,0:T(2,128)S(1)}, u32[]{:S(2)}, u32[]{:S(2)}) %collective-permute-start.11) | collective-permute-done | bytes 2080 | tf_op jit(solution)/shard_map/ppermute | solution.py:222
  33.8 1.2 %shard_map.86 = (f32[4,64,512]{2,1,0:T(8,128)S(1)}, bf16[4,64,512]{2,1,0:T(8,128)(2,1)S(1)}, f32[64,512]{1,0:T(8,128)S(1)}, bf16[64,512]{1,0:T(8,128)(2,1)S(1)},...) custom-call(s32[1]{0:T(128)} %bitcast.z_ref, f32[1]{0:T(128)} %bitcast.6.scale_ref, ...), custom_call_target="tpu_custom_call" | custom-call | flops 1048576 | bytes 1048576 | tf_op jit(solution)/shard_map/pallas_call | solution.py:201
  35.1 1.7 %collective-permute-start.16 = (bf16[64,512]{1,0:T(8,128)(2,1)S(1)}, bf16[64,512]{1,0:T(8,128)(2,1)S(1)}, u32[]{:S(2)}, u32[]{:S(2)}) collective-permute-start(bf16[64,512]{1,0:T(8,128)(2,1)S(1)} %get-tuple-element.33), channel_id=1, source_target_pairs={{0,2},{2,0},{4,6},{6,4},{1,3},{3,1},{5,7},{7,5},{8,10},{10,8},{12,... | collective-permute-start | bytes 196616 | tf_op jit(solution)/shard_map/ppermute | solution.py:222
  36.8 1.1 %collective-permute-start.17 = (bf16[64,512]{1,0:T(8,128)(2,1)S(1)}, bf16[64,512]{1,0:T(8,128)(2,1)S(1)}, u32[]{:S(2)}, u32[]{:S(2)}) collective-permute-start(bf16[64,512]{1,0:T(8,128)(2,1)S(1)} %get-tuple-element.34), channel_id=1, source_target_pairs={{0,4},{2,6},{4,0},{6,2},{1,5},{3,7},{5,1},{7,3},{8,12},{10,14},{12... | collective-permute-start | bytes 196616 | tf_op jit(solution)/shard_map/ppermute | solution.py:222
  37.9 1.7 %collective-permute-start.18 = (bf16[64,512]{1,0:T(8,128)(2,1)S(1)}, bf16[64,512]{1,0:T(8,128)(2,1)S(1)}, u32[]{:S(2)}, u32[]{:S(2)}) collective-permute-start(bf16[64,512]{1,0:T(8,128)(2,1)S(1)} %get-tuple-element.35), channel_id=1, source_target_pairs={{0,6},{2,4},{4,2},{6,0},{1,7},{3,5},{5,3},{7,1},{8,14},{10,12},{12... | collective-permute-start | bytes 196616 | tf_op jit(solution)/shard_map/ppermute | solution.py:222
  39.6 1.6 %collective-permute-start.20 = (bf16[64,512]{1,0:T(8,128)(2,1)S(1)}, bf16[64,512]{1,0:T(8,128)(2,1)S(1)}, u32[]{:S(2)}, u32[]{:S(2)}) collective-permute-start(bf16[64,512]{1,0:T(8,128)(2,1)S(1)} %get-tuple-element.39), channel_id=1, source_target_pairs={{0,17},{1,16},{16,1},{17,0},{2,19},{3,18},{18,3},{19,2},{4,21},{5,... | collective-permute-start | bytes 196616 | tf_op jit(solution)/shard_map/ppermute | solution.py:225
  41.2 1.4 %collective-permute-start.21 = (bf16[64,512]{1,0:T(8,128)(2,1)S(1)}, bf16[64,512]{1,0:T(8,128)(2,1)S(1)}, u32[]{:S(2)}, u32[]{:S(2)}) collective-permute-start(bf16[64,512]{1,0:T(8,128)(2,1)S(1)} %get-tuple-element.40), channel_id=1, source_target_pairs={{0,16},{1,17},{16,0},{17,1},{2,18},{3,19},{18,2},{19,3},{4,20},{5,... | collective-permute-start | bytes 196616 | tf_op jit(solution)/shard_map/ppermute | solution.py:225
  43.2 1.6 %collective-permute-done.17.refs_2_ = bf16[64,512]{1,0:T(8,128)(2,1)S(1)} collective-permute-done((bf16[64,512]{1,0:T(8,128)(2,1)S(1)}, bf16[64,512]{1,0:T(8,128)(2,1)S(1)}, u32[]{:S(2)}, u32[]{:S(2)}) %collective-permute-start.17) | collective-permute-done | bytes 65568 | tf_op jit(solution)/shard_map/ppermute | solution.py:222
  45.8 1.1 %collective-permute-done.22.refs_3_ = bf16[64,512]{1,0:T(8,128)(2,1)S(1)} collective-permute-done((bf16[64,512]{1,0:T(8,128)(2,1)S(1)}, bf16[64,512]{1,0:T(8,128)(2,1)S(1)}, u32[]{:S(2)}, u32[]{:S(2)}) %collective-permute-start.22) | collective-permute-done | bytes 65568 | tf_op jit(solution)/shard_map/ppermute | solution.py:225
  (43 shorter events, 5.7 us)
Async XLA Ops:
  0.6 6.6 %copy-start.2 = (bf16[64,1280]{1,0:T(8,128)(2,1)S(1)}, bf16[64,1280]{1,0:T(8,128)(2,1)}, u32[]{:S(2)}) copy-start(bf16[64,1280]{1,0:T(8,128)(2,1)} %teacher_ref.1) | copy-start | bytes 491524
  0.7 13.7 %collective-permute-start.3 = (bf16[64,1280]{1,0:T(8,128)(2,1)}, bf16[64,1280]{1,0:T(8,128)(2,1)S(1)}, u32[]{:S(2)}, u32[]{:S(2)}) collective-permute-start(bf16[64,1280]{1,0:T(8,128)(2,1)} %teacher_ref.1), channel_id=1, source_target_pairs={{0,4},{2,6},{4,0},{6,2},{1,5},{3,7},{5,1},{7,3},{8,12},{10,14},{12... | collective-permute-start | bytes 491528 | tf_op jit(solution)/shard_map/ppermute | solution.py:222
  5.7 7.1 %collective-permute-start.6 = (bf16[64,1792]{1,0:T(8,128)(2,1)S(1)}, bf16[64,1792]{1,0:T(8,128)(2,1)S(1)}, u32[]{:S(2)}, u32[]{:S(2)}) collective-permute-start(bf16[64,1792]{1,0:T(8,128)(2,1)S(1)} %pad_maximum_fusion.refs_0_), channel_id=1, source_target_pairs={{0,16},{1,17},{16,0},{17,1},{2,18},{3,19},{18,2},{19,3},{4,20},{5,... | collective-permute-start | bytes 688136 | tf_op jit(solution)/shard_map/ppermute | solution.py:225
  7.3 11.5 %collective-permute-start.1 = (bf16[64,1792]{1,0:T(8,128)(2,1)S(1)}, bf16[64,1792]{1,0:T(8,128)(2,1)S(1)}, u32[]{:S(2)}, u32[]{:S(2)}) collective-permute-start(bf16[64,1792]{1,0:T(8,128)(2,1)S(1)} %pad_maximum_fusion.1), channel_id=1, source_target_pairs={{0,2},{2,0},{4,6},{6,4},{1,3},{3,1},{5,7},{7,5},{8,10},{10,8},{12,... | collective-permute-start | bytes 688136 | tf_op jit(solution)/shard_map/ppermute | solution.py:222
  8.9 9.9 %collective-permute-start.2 = (bf16[64,1792]{1,0:T(8,128)(2,1)S(1)}, bf16[64,1792]{1,0:T(8,128)(2,1)S(1)}, u32[]{:S(2)}, u32[]{:S(2)}) collective-permute-start(bf16[64,1792]{1,0:T(8,128)(2,1)S(1)} %pad_maximum_fusion.refs_0_), channel_id=1, source_target_pairs={{0,1},{1,0},{16,17},{17,16},{2,3},{3,2},{18,19},{19,18},{4,5},{5,4... | collective-permute-start | bytes 688136 | tf_op jit(solution)/shard_map/ppermute | solution.py:225
  10.4 5.7 %collective-permute-start = (bf16[64,512]{1,0:T(8,128)(2,1)S(1)}, bf16[64,512]{1,0:T(8,128)(2,1)S(1)}, u32[]{:S(2)}, u32[]{:S(2)}) collective-permute-start(bf16[64,512]{1,0:T(8,128)(2,1)S(1)} %copy-done.1), channel_id=1, source_target_pairs={{0,4},{2,6},{4,0},{6,2},{1,5},{3,7},{5,1},{7,3},{8,12},{10,14},{12... | collective-permute-start | bytes 196616 | tf_op jit(solution)/shard_map/ppermute | solution.py:222
  12.8 7.5 %collective-permute-start.7 = (bf16[64,1792]{1,0:T(8,128)(2,1)S(1)}, bf16[64,1792]{1,0:T(8,128)(2,1)S(1)}, u32[]{:S(2)}, u32[]{:S(2)}) collective-permute-start(bf16[64,1792]{1,0:T(8,128)(2,1)S(1)} %collective-permute-done.6.refs_2_), channel_id=1, source_target_pairs={{0,1},{1,0},{16,17},{17,16},{2,3},{3,2},{18,19},{19,18},{4,5},{5,4... | collective-permute-start | bytes 688136 | tf_op jit(solution)/shard_map/ppermute | solution.py:225
  14.4 8.8 %collective-permute-start.5 = (bf16[64,1280]{1,0:T(8,128)(2,1)S(1)}, bf16[64,1280]{1,0:T(8,128)(2,1)S(1)}, u32[]{:S(2)}, u32[]{:S(2)}) collective-permute-start(bf16[64,1280]{1,0:T(8,128)(2,1)S(1)} %shard_map.78.refs_1_), channel_id=1, source_target_pairs={{0,2},{2,0},{4,6},{6,4},{1,3},{3,1},{5,7},{7,5},{8,10},{10,8},{12,... | collective-permute-start | bytes 491528 | tf_op jit(solution)/shard_map/ppermute | solution.py:222
  18.9 4.3 %collective-permute-start.4 = (bf16[64,512]{1,0:T(8,128)(2,1)S(1)}, bf16[64,512]{1,0:T(8,128)(2,1)S(1)}, u32[]{:S(2)}, u32[]{:S(2)}) collective-permute-start(bf16[64,512]{1,0:T(8,128)(2,1)S(1)} %shard_map.77.refs_0_), channel_id=1, source_target_pairs={{0,2},{2,0},{4,6},{6,4},{1,3},{3,1},{5,7},{7,5},{8,10},{10,8},{12,... | collective-permute-start | bytes 196616 | tf_op jit(solution)/shard_map/ppermute | solution.py:222
  20.6 2.8 %collective-permute-start.8 = (bf16[256,512]{1,0:T(8,128)(2,1)S(1)}, bf16[256,512]{1,0:T(8,128)(2,1)S(1)}, u32[]{:S(2)}, u32[]{:S(2)}) collective-permute-start(bf16[256,512]{1,0:T(8,128)(2,1)S(1)} %get-tuple-element.27.pupil_same_ref.same_ref), channel_id=1, source_target_pairs={{0,8},{8,0},{1,9},{9,1},{2,10},{10,2},{3,11},{11,3},{4,12},{12,4},... | collective-permute-start | bytes 786440 | tf_op jit(solution)/shard_map/ppermute | solution.py:253
  20.7 2.8 %collective-permute-start.9 = (bf16[256,1280]{1,0:T(8,128)(2,1)S(1)}, bf16[256,1280]{1,0:T(8,128)(2,1)S(1)}, u32[]{:S(2)}, u32[]{:S(2)}) collective-permute-start(bf16[256,1280]{1,0:T(8,128)(2,1)S(1)} %get-tuple-element.28.master_same_ref), channel_id=1, source_target_pairs={{0,8},{8,0},{1,9},{9,1},{2,10},{10,2},{3,11},{11,3},{4,12},{12,4},... | collective-permute-start | bytes 1966088 | tf_op jit(solution)/shard_map/ppermute | solution.py:253
  24.8 1.7 %collective-permute-start.12 = (f32[2,512]{1,0:T(2,128)S(1)}, f32[2,512]{1,0:T(2,128)S(1)}, u32[]{:S(2)}, u32[]{:S(2)}) collective-permute-start(f32[2,512]{1,0:T(2,128)S(1)} %get-tuple-element.31.own_ref), channel_id=1, source_target_pairs={{0,8},{8,0},{1,9},{9,1},{2,10},{10,2},{3,11},{11,3},{4,12},{12,4},... | collective-permute-start | bytes 12296 | tf_op jit(solution)/shard_map/ppermute | solution.py:253
  24.9 5.1 %collective-permute-start.10 = (f32[2,256]{1,0:T(2,128)S(1)}, f32[2,256]{1,0:T(2,128)S(1)}, u32[]{:S(2)}, u32[]{:S(2)}) collective-permute-start(f32[2,256]{1,0:T(2,128)S(1)} %get-tuple-element.30.refs_0_), channel_id=1, source_target_pairs={{0,4},{2,6},{4,0},{6,2},{1,5},{3,7},{5,1},{7,3},{8,12},{10,14},{12... | collective-permute-start | bytes 6152 | tf_op jit(solution)/shard_map/ppermute | solution.py:222
  26.5 7.2 %collective-permute-start.15 = (f32[2,512]{1,0:T(2,128)S(1)}, f32[2,512]{1,0:T(2,128)S(1)}, u32[]{:S(2)}, u32[]{:S(2)}) collective-permute-start(f32[2,512]{1,0:T(2,128)S(1)} %shard_map.84.refs_0_), channel_id=1, source_target_pairs={{0,17},{1,16},{16,1},{17,0},{2,19},{3,18},{18,3},{19,2},{4,21},{5,... | collective-permute-start | bytes 12296 | tf_op jit(solution)/shard_map/ppermute | solution.py:225
  28.1 5.6 %collective-permute-start.14 = (f32[2,512]{1,0:T(2,128)S(1)}, f32[2,512]{1,0:T(2,128)S(1)}, u32[]{:S(2)}, u32[]{:S(2)}) collective-permute-start(f32[2,512]{1,0:T(2,128)S(1)} %shard_map.84.refs_0_), channel_id=1, source_target_pairs={{0,16},{1,17},{16,0},{17,1},{2,18},{3,19},{18,2},{19,3},{4,20},{5,... | collective-permute-start | bytes 12296 | tf_op jit(solution)/shard_map/ppermute | solution.py:225
  29.5 4.2 %collective-permute-start.13 = (f32[2,512]{1,0:T(2,128)S(1)}, f32[2,512]{1,0:T(2,128)S(1)}, u32[]{:S(2)}, u32[]{:S(2)}) collective-permute-start(f32[2,512]{1,0:T(2,128)S(1)} %shard_map.84.refs_0_), channel_id=1, source_target_pairs={{0,1},{1,0},{16,17},{17,16},{2,3},{3,2},{18,19},{19,18},{4,5},{5,4... | collective-permute-start | bytes 12296 | tf_op jit(solution)/shard_map/ppermute | solution.py:225
  30.1 3.7 %collective-permute-start.11 = (f32[2,256]{1,0:T(2,128)S(1)}, f32[2,256]{1,0:T(2,128)S(1)}, u32[]{:S(2)}, u32[]{:S(2)}) collective-permute-start(f32[2,256]{1,0:T(2,128)S(1)} %shard_map.82.refs_0_), channel_id=1, source_target_pairs={{0,2},{2,0},{4,6},{6,4},{1,3},{3,1},{5,7},{7,5},{8,10},{10,8},{12,... | collective-permute-start | bytes 6152 | tf_op jit(solution)/shard_map/ppermute | solution.py:222
  35.0 4.5 %collective-permute-start.19 = (bf16[4,64,512]{2,1,0:T(8,128)(2,1)S(1)}, bf16[4,64,512]{2,1,0:T(8,128)(2,1)S(1)}, u32[]{:S(2)}, u32[]{:S(2)}) collective-permute-start(bf16[4,64,512]{2,1,0:T(8,128)(2,1)S(1)} %get-tuple-element.37), channel_id=1, source_target_pairs={{0,8},{8,0},{1,9},{9,1},{2,10},{10,2},{3,11},{11,3},{4,12},{12,4},... | collective-permute-start | bytes 786440 | tf_op jit(solution)/shard_map/ppermute | solution.py:253
  35.1 7.5 %collective-permute-start.16 = (bf16[64,512]{1,0:T(8,128)(2,1)S(1)}, bf16[64,512]{1,0:T(8,128)(2,1)S(1)}, u32[]{:S(2)}, u32[]{:S(2)}) collective-permute-start(bf16[64,512]{1,0:T(8,128)(2,1)S(1)} %get-tuple-element.33), channel_id=1, source_target_pairs={{0,2},{2,0},{4,6},{6,4},{1,3},{3,1},{5,7},{7,5},{8,10},{10,8},{12,... | collective-permute-start | bytes 196616 | tf_op jit(solution)/shard_map/ppermute | solution.py:222
  36.8 8.0 %collective-permute-start.17 = (bf16[64,512]{1,0:T(8,128)(2,1)S(1)}, bf16[64,512]{1,0:T(8,128)(2,1)S(1)}, u32[]{:S(2)}, u32[]{:S(2)}) collective-permute-start(bf16[64,512]{1,0:T(8,128)(2,1)S(1)} %get-tuple-element.34), channel_id=1, source_target_pairs={{0,4},{2,6},{4,0},{6,2},{1,5},{3,7},{5,1},{7,3},{8,12},{10,14},{12... | collective-permute-start | bytes 196616 | tf_op jit(solution)/shard_map/ppermute | solution.py:222
  37.9 6.9 %collective-permute-start.18 = (bf16[64,512]{1,0:T(8,128)(2,1)S(1)}, bf16[64,512]{1,0:T(8,128)(2,1)S(1)}, u32[]{:S(2)}, u32[]{:S(2)}) collective-permute-start(bf16[64,512]{1,0:T(8,128)(2,1)S(1)} %get-tuple-element.35), channel_id=1, source_target_pairs={{0,6},{2,4},{4,2},{6,0},{1,7},{3,5},{5,3},{7,1},{8,14},{10,12},{12... | collective-permute-start | bytes 196616 | tf_op jit(solution)/shard_map/ppermute | solution.py:222
  39.6 5.7 %collective-permute-start.20 = (bf16[64,512]{1,0:T(8,128)(2,1)S(1)}, bf16[64,512]{1,0:T(8,128)(2,1)S(1)}, u32[]{:S(2)}, u32[]{:S(2)}) collective-permute-start(bf16[64,512]{1,0:T(8,128)(2,1)S(1)} %get-tuple-element.39), channel_id=1, source_target_pairs={{0,17},{1,16},{16,1},{17,0},{2,19},{3,18},{18,3},{19,2},{4,21},{5,... | collective-permute-start | bytes 196616 | tf_op jit(solution)/shard_map/ppermute | solution.py:225
  41.2 4.5 %collective-permute-start.21 = (bf16[64,512]{1,0:T(8,128)(2,1)S(1)}, bf16[64,512]{1,0:T(8,128)(2,1)S(1)}, u32[]{:S(2)}, u32[]{:S(2)}) collective-permute-start(bf16[64,512]{1,0:T(8,128)(2,1)S(1)} %get-tuple-element.40), channel_id=1, source_target_pairs={{0,16},{1,17},{16,0},{17,1},{2,18},{3,19},{18,2},{19,3},{4,20},{5,... | collective-permute-start | bytes 196616 | tf_op jit(solution)/shard_map/ppermute | solution.py:225
  42.6 4.3 %collective-permute-start.22 = (bf16[64,512]{1,0:T(8,128)(2,1)S(1)}, bf16[64,512]{1,0:T(8,128)(2,1)S(1)}, u32[]{:S(2)}, u32[]{:S(2)}) collective-permute-start(bf16[64,512]{1,0:T(8,128)(2,1)S(1)} %get-tuple-element.41), channel_id=1, source_target_pairs={{0,1},{1,0},{16,17},{17,16},{2,3},{3,2},{18,19},{19,18},{4,5},{5,4... | collective-permute-start | bytes 196616 | tf_op jit(solution)/shard_map/ppermute | solution.py:225
  (2 other events, 8.8 us)

commit v9 on v6

--- a/solution.py
+++ b/solution.py
@@ -241,7 +241,7 @@
             units[s][0], near = lax.optimization_barrier((units[s][0], near))
             for k, raw in enumerate(units[s]):
                 units[s][k] = call(
-                    unit_kernel, shaped(raw.shape, BF16), (raw,), [vmem], vmem, flops=SOME
+                    unit_kernel, shaped(raw.shape, BF16), (raw,), [vmem], vmem, flops=(FEW, SOME)[k]
                 )
         rest = set(range(2, depth)) - set(far)
         for s in sorted(rest, key=lambda s: bin(s).count("1")):

time: 48.8 us -> 47.8 us (0.980)
  waiting for transfers between devices: 13.5 us -> 11.2 us
  starting transfers between devices: 27.9 us -> 29.1 us
    ppermute x10, waiting for transfers between devices: 8.91 us -> 7.07 us  [to_line(): return lax.ppermute(value, LINE, [(z, z ^ step) for z in range(depth)])]
    ppermute x9, waiting for transfers between devices: 4.55 us -> 3.21 us  [to_square(): return lax.ppermute(value, SQUARE, [(q, q ^ step) for q in range(squares)])]
    ppermute x10, starting transfers between devices: 15.5 us -> 16.6 us  [to_line(): return lax.ppermute(value, LINE, [(z, z ^ step) for z in range(depth)])]
    ppermute x4, waiting for transfers between devices: 0.01 us -> 0.93 us  [to_sibling(): return lax.ppermute(value, 'core', [(0, 1), (1, 0)])]
  transfers between devices with their start and end apart: 23 -> 23, of which waited for: 9 -> 10; matrix products, arithmetic and copies ran while one was open for 2% -> 2% of each run, Pallas kernels for 2% -> 2%
where the time goes in v9:
time: 47.8 us; the launch traced here: 47.6 us
  starting transfers between devices  29.1 us (61%)
  waiting for transfers between devices  11.2 us (23%)
  Pallas kernels  4.27 us (9%)
  between operations  2.08 us (4%)
  other arithmetic  0.95 us (2%)
    ppermute x10, starting transfers between devices, to_line(): return lax.ppermute(value, LINE, [(z, z ^ step) for z in range(depth)])  16.6 us
    ppermute x9, starting transfers between devices, to_square(): return lax.ppermute(value, SQUARE, [(q, q ^ step) for q in range(squares)])  11.7 us
    ppermute x10, waiting for transfers between devices, to_line(): return lax.ppermute(value, LINE, [(z, z ^ step) for z in range(depth)])  7.07 us
    pallas_call x13, Pallas kernels, call(): pl.pallas_call(kernel, out_shape=outs, in_specs=specs, out_specs=jax.tree...  4.27 us
    ppermute x9, waiting for transfers between devices, to_square(): return lax.ppermute(value, SQUARE, [(q, q ^ step) for q in range(squares)])  3.21 us
  transfers between devices with their start and end apart: 23, of which 10 were waited for; matrix products, arithmetic and copies ran while one was open for 2% of the time, Pallas kernels for 2%

profile of v9, /device:TPU:0, one launch (start us, length us, event | category | flops | bytes accessed | tf_op | source)
XLA Modules:
  0.0 47.6 jit_solution(13944425452368357063)
XLA Ops:
  0.7 4.1 %collective-permute-start.2 = (bf16[64,1280]{1,0:T(8,128)(2,1)}, bf16[64,1280]{1,0:T(8,128)(2,1)S(1)}, u32[]{:S(2)}, u32[]{:S(2)}) collective-permute-start(bf16[64,1280]{1,0:T(8,128)(2,1)} %teacher_ref.1), channel_id=1, source_target_pairs={{0,4},{2,6},{4,0},{6,2},{1,5},{3,7},{5,1},{7,3},{8,12},{10,14},{12... | collective-permute-start | bytes 491528 | tf_op jit(solution)/shard_map/ppermute | solution.py:222
  4.8 0.9 %pad_maximum_fusion.refs_0_ = bf16[64,1792]{1,0:T(8,128)(2,1)S(1)} fusion(bf16[64,1280]{1,0:T(8,128)(2,1)} %param.8, bf16[64,512]{1,0:T(8,128)(2,1)} %raw_image_ref.1), kind=kLoop, calls=%fused_computation | loop fusion | flops 458752 | bytes 458752 | tf_op jit(solution)/shard_map/max | solution.py:35
  5.7 1.6 %collective-permute-start.6 = (bf16[64,1792]{1,0:T(8,128)(2,1)S(1)}, bf16[64,1792]{1,0:T(8,128)(2,1)S(1)}, u32[]{:S(2)}, u32[]{:S(2)}) collective-permute-start(bf16[64,1792]{1,0:T(8,128)(2,1)S(1)} %pad_maximum_fusion.refs_0_), channel_id=1, source_target_pairs={{0,16},{1,17},{16,0},{17,1},{2,18},{3,19},{18,2},{19,3},{4,20},{5,... | collective-permute-start | bytes 688136 | tf_op jit(solution)/shard_map/ppermute | solution.py:225
  7.3 1.6 %collective-permute-start.1 = (bf16[64,1792]{1,0:T(8,128)(2,1)S(1)}, bf16[64,1792]{1,0:T(8,128)(2,1)S(1)}, u32[]{:S(2)}, u32[]{:S(2)}) collective-permute-start(bf16[64,1792]{1,0:T(8,128)(2,1)S(1)} %pad_maximum_fusion.1), channel_id=1, source_target_pairs={{0,2},{2,0},{4,6},{6,4},{1,3},{3,1},{5,7},{7,5},{8,10},{10,8},{12,... | collective-permute-start | bytes 688136 | tf_op jit(solution)/shard_map/ppermute | solution.py:222
  8.9 1.5 %collective-permute-start.5 = (bf16[64,1792]{1,0:T(8,128)(2,1)S(1)}, bf16[64,1792]{1,0:T(8,128)(2,1)S(1)}, u32[]{:S(2)}, u32[]{:S(2)}) collective-permute-start(bf16[64,1792]{1,0:T(8,128)(2,1)S(1)} %pad_maximum_fusion.refs_0_), channel_id=1, source_target_pairs={{0,1},{1,0},{16,17},{17,16},{2,3},{3,2},{18,19},{19,18},{4,5},{5,4... | collective-permute-start | bytes 688136 | tf_op jit(solution)/shard_map/ppermute | solution.py:225
  10.4 2.4 %collective-permute-done.6.refs_2_ = bf16[64,1792]{1,0:T(8,128)(2,1)S(1)} collective-permute-done((bf16[64,1792]{1,0:T(8,128)(2,1)S(1)}, bf16[64,1792]{1,0:T(8,128)(2,1)S(1)}, u32[]{:S(2)}, u32[]{:S(2)}) %collective-permute-start.6) | collective-permute-done | bytes 229408 | tf_op jit(solution)/shard_map/ppermute | solution.py:225
  12.8 1.5 %collective-permute-start.7 = (bf16[64,1792]{1,0:T(8,128)(2,1)S(1)}, bf16[64,1792]{1,0:T(8,128)(2,1)S(1)}, u32[]{:S(2)}, u32[]{:S(2)}) collective-permute-start(bf16[64,1792]{1,0:T(8,128)(2,1)S(1)} %collective-permute-done.6.refs_2_), channel_id=1, source_target_pairs={{0,1},{1,0},{16,17},{17,16},{2,3},{3,2},{18,19},{19,18},{4,5},{5,4... | collective-permute-start | bytes 688136 | tf_op jit(solution)/shard_map/ppermute | solution.py:225
  16.1 1.6 %collective-permute-start.4 = (bf16[64,1280]{1,0:T(8,128)(2,1)S(1)}, bf16[64,1280]{1,0:T(8,128)(2,1)S(1)}, u32[]{:S(2)}, u32[]{:S(2)}) collective-permute-start(bf16[64,1280]{1,0:T(8,128)(2,1)S(1)} %shard_map.78.refs_1_), channel_id=1, source_target_pairs={{0,2},{2,0},{4,6},{6,4},{1,3},{3,1},{5,7},{7,5},{8,10},{10,8},{12,... | collective-permute-start | bytes 491528 | tf_op jit(solution)/shard_map/ppermute | solution.py:222
  17.7 1.9 %collective-permute-done.raw_ref = bf16[64,512]{1,0:T(8,128)(2,1)S(1)} collective-permute-done((bf16[64,512]{1,0:T(8,128)(2,1)S(1)}, bf16[64,512]{1,0:T(8,128)(2,1)S(1)}, u32[]{:S(2)}, u32[]{:S(2)}) %collective-permute-start) | collective-permute-done | bytes 65568 | tf_op jit(solution)/shard_map/ppermute | solution.py:222
  19.7 2.2 %collective-permute-start.3 = (bf16[64,512]{1,0:T(8,128)(2,1)S(1)}, bf16[64,512]{1,0:T(8,128)(2,1)S(1)}, u32[]{:S(2)}, u32[]{:S(2)}) collective-permute-start(bf16[64,512]{1,0:T(8,128)(2,1)S(1)} %shard_map.77.refs_0_), channel_id=1, source_target_pairs={{0,2},{2,0},{4,6},{6,4},{1,3},{3,1},{5,7},{7,5},{8,10},{10,8},{12,... | collective-permute-start | bytes 196616 | tf_op jit(solution)/shard_map/ppermute | solution.py:222
  22.8 1.4 %collective-permute-done.3.refs_2_ = bf16[64,512]{1,0:T(8,128)(2,1)S(1)} collective-permute-done((bf16[64,512]{1,0:T(8,128)(2,1)S(1)}, bf16[64,512]{1,0:T(8,128)(2,1)S(1)}, u32[]{:S(2)}, u32[]{:S(2)}) %collective-permute-start.3) | collective-permute-done | bytes 65568 | tf_op jit(solution)/shard_map/ppermute | solution.py:222
  24.7 1.3 %shard_map.81 = (f32[512,256]{1,0:T(8,128)S(1)}, f32[2,512]{1,0:T(2,128)S(1)}, f32[2,256]{1,0:T(2,128)S(1)}) custom-call(f32[1]{0:T(128)} %bitcast.4.teacher_scale_ref, f32[1]{0:T(128)} %bitcast.5.student_scale_ref, bf16[256,512]{1,0:T(8,128)(2,1)S(1)} %get-tuple-element.23.pupil_text_ref.text_ref, bf16[256,1280]{1,0:T(8,128)(2,1)S(1)} %get-tuple-element.24.master_text_ref, ...), custom_call_target="tpu_custom_call" | custom-call | flops 1048576 | bytes 1048576 | tf_op jit(solution)/shard_map/pallas_call | solution.py:201
  27.3 1.6 %collective-permute-start.15 = (f32[2,512]{1,0:T(2,128)S(1)}, f32[2,512]{1,0:T(2,128)S(1)}, u32[]{:S(2)}, u32[]{:S(2)}) collective-permute-start(f32[2,512]{1,0:T(2,128)S(1)} %shard_map.84.refs_0_), channel_id=1, source_target_pairs={{0,17},{1,16},{16,1},{17,0},{2,19},{3,18},{18,3},{19,2},{4,21},{5,... | collective-permute-start | bytes 12296 | tf_op jit(solution)/shard_map/ppermute | solution.py:225
  29.4 1.5 %collective-permute-start.13 = (f32[2,512]{1,0:T(2,128)S(1)}, f32[2,512]{1,0:T(2,128)S(1)}, u32[]{:S(2)}, u32[]{:S(2)}) collective-permute-start(f32[2,512]{1,0:T(2,128)S(1)} %shard_map.84.refs_0_), channel_id=1, source_target_pairs={{0,1},{1,0},{16,17},{17,16},{2,3},{3,2},{18,19},{19,18},{4,5},{5,4... | collective-permute-start | bytes 12296 | tf_op jit(solution)/shard_map/ppermute | solution.py:225
  30.9 1.7 %collective-permute-start.11 = (f32[2,256]{1,0:T(2,128)S(1)}, f32[2,256]{1,0:T(2,128)S(1)}, u32[]{:S(2)}, u32[]{:S(2)}) collective-permute-start(f32[2,256]{1,0:T(2,128)S(1)} %shard_map.82.refs_0_), channel_id=1, source_target_pairs={{0,2},{2,0},{4,6},{6,4},{1,3},{3,1},{5,7},{7,5},{8,10},{10,8},{12,... | collective-permute-start | bytes 6152 | tf_op jit(solution)/shard_map/ppermute | solution.py:222
  32.6 1.9 %collective-permute-done.11.refs_1_ = f32[2,256]{1,0:T(2,128)S(1)} collective-permute-done((f32[2,256]{1,0:T(2,128)S(1)}, f32[2,256]{1,0:T(2,128)S(1)}, u32[]{:S(2)}, u32[]{:S(2)}) %collective-permute-start.11) | collective-permute-done | bytes 2080 | tf_op jit(solution)/shard_map/ppermute | solution.py:222
  34.6 1.2 %shard_map.86 = (f32[4,64,512]{2,1,0:T(8,128)S(1)}, bf16[4,64,512]{2,1,0:T(8,128)(2,1)S(1)}, f32[64,512]{1,0:T(8,128)S(1)}, bf16[64,512]{1,0:T(8,128)(2,1)S(1)},...) custom-call(s32[1]{0:T(128)} %bitcast.z_ref, f32[1]{0:T(128)} %bitcast.6.scale_ref, ...), custom_call_target="tpu_custom_call" | custom-call | flops 1048576 | bytes 1048576 | tf_op jit(solution)/shard_map/pallas_call | solution.py:201
  35.9 1.7 %collective-permute-start.16 = (bf16[64,512]{1,0:T(8,128)(2,1)S(1)}, bf16[64,512]{1,0:T(8,128)(2,1)S(1)}, u32[]{:S(2)}, u32[]{:S(2)}) collective-permute-start(bf16[64,512]{1,0:T(8,128)(2,1)S(1)} %get-tuple-element.31), channel_id=1, source_target_pairs={{0,2},{2,0},{4,6},{6,4},{1,3},{3,1},{5,7},{7,5},{8,10},{10,8},{12,... | collective-permute-start | bytes 196616 | tf_op jit(solution)/shard_map/ppermute | solution.py:222
  37.6 1.8 %collective-permute-start.17 = (bf16[64,512]{1,0:T(8,128)(2,1)S(1)}, bf16[64,512]{1,0:T(8,128)(2,1)S(1)}, u32[]{:S(2)}, u32[]{:S(2)}) collective-permute-start(bf16[64,512]{1,0:T(8,128)(2,1)S(1)} %get-tuple-element.32), channel_id=1, source_target_pairs={{0,4},{2,6},{4,0},{6,2},{1,5},{3,7},{5,1},{7,3},{8,12},{10,14},{12... | collective-permute-start | bytes 196616 | tf_op jit(solution)/shard_map/ppermute | solution.py:222
  39.5 0.9 %collective-permute-start.18 = (bf16[64,512]{1,0:T(8,128)(2,1)S(1)}, bf16[64,512]{1,0:T(8,128)(2,1)S(1)}, u32[]{:S(2)}, u32[]{:S(2)}) collective-permute-start(bf16[64,512]{1,0:T(8,128)(2,1)S(1)} %get-tuple-element.33), channel_id=1, source_target_pairs={{0,6},{2,4},{4,2},{6,0},{1,7},{3,5},{5,3},{7,1},{8,14},{10,12},{12... | collective-permute-start | bytes 196616 | tf_op jit(solution)/shard_map/ppermute | solution.py:222
  40.4 1.6 %collective-permute-start.20 = (bf16[64,512]{1,0:T(8,128)(2,1)S(1)}, bf16[64,512]{1,0:T(8,128)(2,1)S(1)}, u32[]{:S(2)}, u32[]{:S(2)}) collective-permute-start(bf16[64,512]{1,0:T(8,128)(2,1)S(1)} %get-tuple-element.37), channel_id=1, source_target_pairs={{0,17},{1,16},{16,1},{17,0},{2,19},{3,18},{18,3},{19,2},{4,21},{5,... | collective-permute-start | bytes 196616 | tf_op jit(solution)/shard_map/ppermute | solution.py:225
  42.5 1.5 %collective-permute-start.22 = (bf16[64,512]{1,0:T(8,128)(2,1)S(1)}, bf16[64,512]{1,0:T(8,128)(2,1)S(1)}, u32[]{:S(2)}, u32[]{:S(2)}) collective-permute-start(bf16[64,512]{1,0:T(8,128)(2,1)S(1)} %get-tuple-element.39), channel_id=1, source_target_pairs={{0,1},{1,0},{16,17},{17,16},{2,3},{3,2},{18,19},{19,18},{4,5},{5,4... | collective-permute-start | bytes 196616 | tf_op jit(solution)/shard_map/ppermute | solution.py:225
  44.0 1.9 %collective-permute-done.17.refs_2_ = bf16[64,512]{1,0:T(8,128)(2,1)S(1)} collective-permute-done((bf16[64,512]{1,0:T(8,128)(2,1)S(1)}, bf16[64,512]{1,0:T(8,128)(2,1)S(1)}, u32[]{:S(2)}, u32[]{:S(2)}) %collective-permute-start.17) | collective-permute-done | bytes 65568 | tf_op jit(solution)/shard_map/ppermute | solution.py:222
  46.8 0.9 %shard_map.89 = (f32[64,512]{1,0:T(8,128)}, f32[64,512]{1,0:T(8,128)}) custom-call(bf16[64,512]{1,0:T(8,128)(2,1)S(1)} %copy-done, bf16[64,512]{1,0:T(8,128)(2,1)S(1)} %copy-done.1, f32[64,512]{1,0:T(8,128)S(1)} %shard_map.87.text_ref, f32[64,512]{1,0:T(8,128)S(1)} %get-tuple-element.36.refs_0_, bf16[64,512]{1,0:T(8,128)(2,1)S(1)} %collective-permute-done.20.refs_1_, ...), custom_call_target="tpu_custom_call" | custom-call | flops 1048576 | bytes 1048576 | tf_op jit(solution)/shard_map/pallas_call | solution.py:201
  (43 shorter events, 5.3 us)
Async XLA Ops:
  0.6 6.6 %copy-start.2 = (bf16[64,1280]{1,0:T(8,128)(2,1)S(1)}, bf16[64,1280]{1,0:T(8,128)(2,1)}, u32[]{:S(2)}) copy-start(bf16[64,1280]{1,0:T(8,128)(2,1)} %teacher_ref.1) | copy-start | bytes 491524
  0.7 15.3 %collective-permute-start.2 = (bf16[64,1280]{1,0:T(8,128)(2,1)}, bf16[64,1280]{1,0:T(8,128)(2,1)S(1)}, u32[]{:S(2)}, u32[]{:S(2)}) collective-permute-start(bf16[64,1280]{1,0:T(8,128)(2,1)} %teacher_ref.1), channel_id=1, source_target_pairs={{0,4},{2,6},{4,0},{6,2},{1,5},{3,7},{5,1},{7,3},{8,12},{10,14},{12... | collective-permute-start | bytes 491528 | tf_op jit(solution)/shard_map/ppermute | solution.py:222
  5.7 7.1 %collective-permute-start.6 = (bf16[64,1792]{1,0:T(8,128)(2,1)S(1)}, bf16[64,1792]{1,0:T(8,128)(2,1)S(1)}, u32[]{:S(2)}, u32[]{:S(2)}) collective-permute-start(bf16[64,1792]{1,0:T(8,128)(2,1)S(1)} %pad_maximum_fusion.refs_0_), channel_id=1, source_target_pairs={{0,16},{1,17},{16,0},{17,1},{2,18},{3,19},{18,2},{19,3},{4,20},{5,... | collective-permute-start | bytes 688136 | tf_op jit(solution)/shard_map/ppermute | solution.py:225
  7.3 12.3 %collective-permute-start.1 = (bf16[64,1792]{1,0:T(8,128)(2,1)S(1)}, bf16[64,1792]{1,0:T(8,128)(2,1)S(1)}, u32[]{:S(2)}, u32[]{:S(2)}) collective-permute-start(bf16[64,1792]{1,0:T(8,128)(2,1)S(1)} %pad_maximum_fusion.1), channel_id=1, source_target_pairs={{0,2},{2,0},{4,6},{6,4},{1,3},{3,1},{5,7},{7,5},{8,10},{10,8},{12,... | collective-permute-start | bytes 688136 | tf_op jit(solution)/shard_map/ppermute | solution.py:222
  8.9 13.0 %collective-permute-start.5 = (bf16[64,1792]{1,0:T(8,128)(2,1)S(1)}, bf16[64,1792]{1,0:T(8,128)(2,1)S(1)}, u32[]{:S(2)}, u32[]{:S(2)}) collective-permute-start(bf16[64,1792]{1,0:T(8,128)(2,1)S(1)} %pad_maximum_fusion.refs_0_), channel_id=1, source_target_pairs={{0,1},{1,0},{16,17},{17,16},{2,3},{3,2},{18,19},{19,18},{4,5},{5,4... | collective-permute-start | bytes 688136 | tf_op jit(solution)/shard_map/ppermute | solution.py:225
  12.8 9.1 %collective-permute-start.7 = (bf16[64,1792]{1,0:T(8,128)(2,1)S(1)}, bf16[64,1792]{1,0:T(8,128)(2,1)S(1)}, u32[]{:S(2)}, u32[]{:S(2)}) collective-permute-start(bf16[64,1792]{1,0:T(8,128)(2,1)S(1)} %collective-permute-done.6.refs_2_), channel_id=1, source_target_pairs={{0,1},{1,0},{16,17},{17,16},{2,3},{3,2},{18,19},{19,18},{4,5},{5,4... | collective-permute-start | bytes 688136 | tf_op jit(solution)/shard_map/ppermute | solution.py:225
  14.3 5.3 %collective-permute-start = (bf16[64,512]{1,0:T(8,128)(2,1)S(1)}, bf16[64,512]{1,0:T(8,128)(2,1)S(1)}, u32[]{:S(2)}, u32[]{:S(2)}) collective-permute-start(bf16[64,512]{1,0:T(8,128)(2,1)S(1)} %copy-done.1), channel_id=1, source_target_pairs={{0,4},{2,6},{4,0},{6,2},{1,5},{3,7},{5,1},{7,3},{8,12},{10,14},{12... | collective-permute-start | bytes 196616 | tf_op jit(solution)/shard_map/ppermute | solution.py:222
  16.1 8.1 %collective-permute-start.4 = (bf16[64,1280]{1,0:T(8,128)(2,1)S(1)}, bf16[64,1280]{1,0:T(8,128)(2,1)S(1)}, u32[]{:S(2)}, u32[]{:S(2)}) collective-permute-start(bf16[64,1280]{1,0:T(8,128)(2,1)S(1)} %shard_map.78.refs_1_), channel_id=1, source_target_pairs={{0,2},{2,0},{4,6},{6,4},{1,3},{3,1},{5,7},{7,5},{8,10},{10,8},{12,... | collective-permute-start | bytes 491528 | tf_op jit(solution)/shard_map/ppermute | solution.py:222
  19.7 4.5 %collective-permute-start.3 = (bf16[64,512]{1,0:T(8,128)(2,1)S(1)}, bf16[64,512]{1,0:T(8,128)(2,1)S(1)}, u32[]{:S(2)}, u32[]{:S(2)}) collective-permute-start(bf16[64,512]{1,0:T(8,128)(2,1)S(1)} %shard_map.77.refs_0_), channel_id=1, source_target_pairs={{0,2},{2,0},{4,6},{6,4},{1,3},{3,1},{5,7},{7,5},{8,10},{10,8},{12,... | collective-permute-start | bytes 196616 | tf_op jit(solution)/shard_map/ppermute | solution.py:222
  22.2 2.2 %collective-permute-start.8 = (bf16[256,512]{1,0:T(8,128)(2,1)S(1)}, bf16[256,512]{1,0:T(8,128)(2,1)S(1)}, u32[]{:S(2)}, u32[]{:S(2)}) collective-permute-start(bf16[256,512]{1,0:T(8,128)(2,1)S(1)} %get-tuple-element.25.pupil_same_ref.same_ref), channel_id=1, source_target_pairs={{0,8},{8,0},{1,9},{9,1},{2,10},{10,2},{3,11},{11,3},{4,12},{12,4},... | collective-permute-start | bytes 786440 | tf_op jit(solution)/shard_map/ppermute | solution.py:253
  22.3 2.5 %collective-permute-start.9 = (bf16[256,1280]{1,0:T(8,128)(2,1)S(1)}, bf16[256,1280]{1,0:T(8,128)(2,1)S(1)}, u32[]{:S(2)}, u32[]{:S(2)}) collective-permute-start(bf16[256,1280]{1,0:T(8,128)(2,1)S(1)} %get-tuple-element.26.master_same_ref), channel_id=1, source_target_pairs={{0,8},{8,0},{1,9},{9,1},{2,10},{10,2},{3,11},{11,3},{4,12},{12,4},... | collective-permute-start | bytes 1966088 | tf_op jit(solution)/shard_map/ppermute | solution.py:253
  26.0 1.2 %collective-permute-start.12 = (f32[2,512]{1,0:T(2,128)S(1)}, f32[2,512]{1,0:T(2,128)S(1)}, u32[]{:S(2)}, u32[]{:S(2)}) collective-permute-start(f32[2,512]{1,0:T(2,128)S(1)} %get-tuple-element.29.own_ref), channel_id=1, source_target_pairs={{0,8},{8,0},{1,9},{9,1},{2,10},{10,2},{3,11},{11,3},{4,12},{12,4},... | collective-permute-start | bytes 12296 | tf_op jit(solution)/shard_map/ppermute | solution.py:253
  26.3 4.6 %collective-permute-start.10 = (f32[2,256]{1,0:T(2,128)S(1)}, f32[2,256]{1,0:T(2,128)S(1)}, u32[]{:S(2)}, u32[]{:S(2)}) collective-permute-start(f32[2,256]{1,0:T(2,128)S(1)} %get-tuple-element.28.refs_0_), channel_id=1, source_target_pairs={{0,4},{2,6},{4,0},{6,2},{1,5},{3,7},{5,1},{7,3},{8,12},{10,14},{12... | collective-permute-start | bytes 6152 | tf_op jit(solution)/shard_map/ppermute | solution.py:222
  27.3 7.2 %collective-permute-start.15 = (f32[2,512]{1,0:T(2,128)S(1)}, f32[2,512]{1,0:T(2,128)S(1)}, u32[]{:S(2)}, u32[]{:S(2)}) collective-permute-start(f32[2,512]{1,0:T(2,128)S(1)} %shard_map.84.refs_0_), channel_id=1, source_target_pairs={{0,17},{1,16},{16,1},{17,0},{2,19},{3,18},{18,3},{19,2},{4,21},{5,... | collective-permute-start | bytes 12296 | tf_op jit(solution)/shard_map/ppermute | solution.py:225
  28.8 5.7 %collective-permute-start.14 = (f32[2,512]{1,0:T(2,128)S(1)}, f32[2,512]{1,0:T(2,128)S(1)}, u32[]{:S(2)}, u32[]{:S(2)}) collective-permute-start(f32[2,512]{1,0:T(2,128)S(1)} %shard_map.84.refs_0_), channel_id=1, source_target_pairs={{0,16},{1,17},{16,0},{17,1},{2,18},{3,19},{18,2},{19,3},{4,20},{5,... | collective-permute-start | bytes 12296 | tf_op jit(solution)/shard_map/ppermute | solution.py:225
  29.4 5.2 %collective-permute-start.13 = (f32[2,512]{1,0:T(2,128)S(1)}, f32[2,512]{1,0:T(2,128)S(1)}, u32[]{:S(2)}, u32[]{:S(2)}) collective-permute-start(f32[2,512]{1,0:T(2,128)S(1)} %shard_map.84.refs_0_), channel_id=1, source_target_pairs={{0,1},{1,0},{16,17},{17,16},{2,3},{3,2},{18,19},{19,18},{4,5},{5,4... | collective-permute-start | bytes 12296 | tf_op jit(solution)/shard_map/ppermute | solution.py:225
  30.9 3.7 %collective-permute-start.11 = (f32[2,256]{1,0:T(2,128)S(1)}, f32[2,256]{1,0:T(2,128)S(1)}, u32[]{:S(2)}, u32[]{:S(2)}) collective-permute-start(f32[2,256]{1,0:T(2,128)S(1)} %shard_map.82.refs_0_), channel_id=1, source_target_pairs={{0,2},{2,0},{4,6},{6,4},{1,3},{3,1},{5,7},{7,5},{8,10},{10,8},{12,... | collective-permute-start | bytes 6152 | tf_op jit(solution)/shard_map/ppermute | solution.py:222
  35.8 4.5 %collective-permute-start.19 = (bf16[4,64,512]{2,1,0:T(8,128)(2,1)S(1)}, bf16[4,64,512]{2,1,0:T(8,128)(2,1)S(1)}, u32[]{:S(2)}, u32[]{:S(2)}) collective-permute-start(bf16[4,64,512]{2,1,0:T(8,128)(2,1)S(1)} %get-tuple-element.35), channel_id=1, source_target_pairs={{0,8},{8,0},{1,9},{9,1},{2,10},{10,2},{3,11},{11,3},{4,12},{12,4},... | collective-permute-start | bytes 786440 | tf_op jit(solution)/shard_map/ppermute | solution.py:253
  35.9 6.6 %collective-permute-start.16 = (bf16[64,512]{1,0:T(8,128)(2,1)S(1)}, bf16[64,512]{1,0:T(8,128)(2,1)S(1)}, u32[]{:S(2)}, u32[]{:S(2)}) collective-permute-start(bf16[64,512]{1,0:T(8,128)(2,1)S(1)} %get-tuple-element.31), channel_id=1, source_target_pairs={{0,2},{2,0},{4,6},{6,4},{1,3},{3,1},{5,7},{7,5},{8,10},{10,8},{12,... | collective-permute-start | bytes 196616 | tf_op jit(solution)/shard_map/ppermute | solution.py:222
  37.6 8.2 %collective-permute-start.17 = (bf16[64,512]{1,0:T(8,128)(2,1)S(1)}, bf16[64,512]{1,0:T(8,128)(2,1)S(1)}, u32[]{:S(2)}, u32[]{:S(2)}) collective-permute-start(bf16[64,512]{1,0:T(8,128)(2,1)S(1)} %get-tuple-element.32), channel_id=1, source_target_pairs={{0,4},{2,6},{4,0},{6,2},{1,5},{3,7},{5,1},{7,3},{8,12},{10,14},{12... | collective-permute-start | bytes 196616 | tf_op jit(solution)/shard_map/ppermute | solution.py:222
  39.5 6.4 %collective-permute-start.18 = (bf16[64,512]{1,0:T(8,128)(2,1)S(1)}, bf16[64,512]{1,0:T(8,128)(2,1)S(1)}, u32[]{:S(2)}, u32[]{:S(2)}) collective-permute-start(bf16[64,512]{1,0:T(8,128)(2,1)S(1)} %get-tuple-element.33), channel_id=1, source_target_pairs={{0,6},{2,4},{4,2},{6,0},{1,7},{3,5},{5,3},{7,1},{8,14},{10,12},{12... | collective-permute-start | bytes 196616 | tf_op jit(solution)/shard_map/ppermute | solution.py:222
  40.4 5.8 %collective-permute-start.20 = (bf16[64,512]{1,0:T(8,128)(2,1)S(1)}, bf16[64,512]{1,0:T(8,128)(2,1)S(1)}, u32[]{:S(2)}, u32[]{:S(2)}) collective-permute-start(bf16[64,512]{1,0:T(8,128)(2,1)S(1)} %get-tuple-element.37), channel_id=1, source_target_pairs={{0,17},{1,16},{16,1},{17,0},{2,19},{3,18},{18,3},{19,2},{4,21},{5,... | collective-permute-start | bytes 196616 | tf_op jit(solution)/shard_map/ppermute | solution.py:225
  42.0 4.6 %collective-permute-start.21 = (bf16[64,512]{1,0:T(8,128)(2,1)S(1)}, bf16[64,512]{1,0:T(8,128)(2,1)S(1)}, u32[]{:S(2)}, u32[]{:S(2)}) collective-permute-start(bf16[64,512]{1,0:T(8,128)(2,1)S(1)} %get-tuple-element.38), channel_id=1, source_target_pairs={{0,16},{1,17},{16,0},{17,1},{2,18},{3,19},{18,2},{19,3},{4,20},{5,... | collective-permute-start | bytes 196616 | tf_op jit(solution)/shard_map/ppermute | solution.py:225
  42.5 4.3 %collective-permute-start.22 = (bf16[64,512]{1,0:T(8,128)(2,1)S(1)}, bf16[64,512]{1,0:T(8,128)(2,1)S(1)}, u32[]{:S(2)}, u32[]{:S(2)}) collective-permute-start(bf16[64,512]{1,0:T(8,128)(2,1)S(1)} %get-tuple-element.39), channel_id=1, source_target_pairs={{0,1},{1,0},{16,17},{17,16},{2,3},{3,2},{18,19},{19,18},{4,5},{5,4... | collective-permute-start | bytes 196616 | tf_op jit(solution)/shard_map/ppermute | solution.py:225
  (2 other events, 7.5 us)

commit v10 on v9

--- a/solution.py
+++ b/solution.py
@@ -308,8 +308,10 @@
             [vmem] * 2,
             vmem,
         )
-        row_lses = [to_square(row_lse, s) for s in range(1, squares)]
-        row_lse = joined([row_lse, *row_lses], MANY)
+        row_lses = {s: to_square(row_lse, s) for s in range(1, squares)}
+        near = [row_lses.pop(s) for s in bits(squares)[::-1]]
+        row_lse = joined([row_lse, *row_lses.values()], SOME)
+        row_lse = joined([row_lse, *near], MANY)
         for s in bits(depth):
             col_lse = joined([col_lse, to_line(col_lse, s)], FEW if s == 1 else SOME)
         block = shaped((own, width), F32)

time: 47.8 us -> 50.8 us (1.063)
  waiting for transfers between devices: 11.2 us -> 14.2 us
    ppermute x9, waiting for transfers between devices: 3.21 us -> 7.15 us  [to_square(): return lax.ppermute(value, SQUARE, [(q, q ^ step) for q in range(squares)])]
    ppermute x10, waiting for transfers between devices: 7.07 us -> 6.14 us  [to_line(): return lax.ppermute(value, LINE, [(z, z ^ step) for z in range(depth)])]
    pallas_call x13 -> x14, Pallas kernels: 4.27 us -> 4.28 us  [call(): pl.pallas_call(kernel, out_shape=outs, in_specs=specs, out_specs=jax.tree...]
  transfers between devices with their start and end apart: 23 -> 23, of which waited for: 10 -> 12; matrix products, arithmetic and copies ran while one was open for 2% -> 2% of each run, Pallas kernels for 2% -> 2%
where the time goes in v10:
time: 50.8 us; the launch traced here: 50.6 us
  starting transfers between devices  29.1 us (57%)
  waiting for transfers between devices  14.2 us (28%)
  Pallas kernels  4.28 us (8%)
  between operations  2.07 us (4%)
  other arithmetic  0.95 us (2%)
    ppermute x10, starting transfers between devices, to_line(): return lax.ppermute(value, LINE, [(z, z ^ step) for z in range(depth)])  16.5 us
    ppermute x9, starting transfers between devices, to_square(): return lax.ppermute(value, SQUARE, [(q, q ^ step) for q in range(squares)])  11.7 us
    ppermute x9, waiting for transfers between devices, to_square(): return lax.ppermute(value, SQUARE, [(q, q ^ step) for q in range(squares)])  7.15 us
    ppermute x10, waiting for transfers between devices, to_line(): return lax.ppermute(value, LINE, [(z, z ^ step) for z in range(depth)])  6.14 us
    pallas_call x14, Pallas kernels, call(): pl.pallas_call(kernel, out_shape=outs, in_specs=specs, out_specs=jax.tree...  4.28 us
  transfers between devices with their start and end apart: 23, of which 12 were waited for; matrix products, arithmetic and copies ran while one was open for 2% of the time, Pallas kernels for 2%

profile of v10, /device:TPU:0, one launch (start us, length us, event | category | flops | bytes accessed | tf_op | source)
XLA Modules:
  0.0 50.6 jit_solution(8284343547033177086)
XLA Ops:
  0.7 4.1 %collective-permute-start.2 = (bf16[64,1280]{1,0:T(8,128)(2,1)}, bf16[64,1280]{1,0:T(8,128)(2,1)S(1)}, u32[]{:S(2)}, u32[]{:S(2)}) collective-permute-start(bf16[64,1280]{1,0:T(8,128)(2,1)} %teacher_ref.1), channel_id=1, source_target_pairs={{0,4},{2,6},{4,0},{6,2},{1,5},{3,7},{5,1},{7,3},{8,12},{10,14},{12... | collective-permute-start | bytes 491528 | tf_op jit(solution)/shard_map/ppermute | solution.py:222
  4.8 0.9 %pad_maximum_fusion.refs_0_ = bf16[64,1792]{1,0:T(8,128)(2,1)S(1)} fusion(bf16[64,1280]{1,0:T(8,128)(2,1)} %param.8, bf16[64,512]{1,0:T(8,128)(2,1)} %raw_image_ref.1), kind=kLoop, calls=%fused_computation | loop fusion | flops 458752 | bytes 458752 | tf_op jit(solution)/shard_map/max | solution.py:35
  5.7 1.6 %collective-permute-start.6 = (bf16[64,1792]{1,0:T(8,128)(2,1)S(1)}, bf16[64,1792]{1,0:T(8,128)(2,1)S(1)}, u32[]{:S(2)}, u32[]{:S(2)}) collective-permute-start(bf16[64,1792]{1,0:T(8,128)(2,1)S(1)} %pad_maximum_fusion.refs_0_), channel_id=1, source_target_pairs={{0,16},{1,17},{16,0},{17,1},{2,18},{3,19},{18,2},{19,3},{4,20},{5,... | collective-permute-start | bytes 688136 | tf_op jit(solution)/shard_map/ppermute | solution.py:225
  7.3 1.6 %collective-permute-start.1 = (bf16[64,1792]{1,0:T(8,128)(2,1)S(1)}, bf16[64,1792]{1,0:T(8,128)(2,1)S(1)}, u32[]{:S(2)}, u32[]{:S(2)}) collective-permute-start(bf16[64,1792]{1,0:T(8,128)(2,1)S(1)} %pad_maximum_fusion.1), channel_id=1, source_target_pairs={{0,2},{2,0},{4,6},{6,4},{1,3},{3,1},{5,7},{7,5},{8,10},{10,8},{12,... | collective-permute-start | bytes 688136 | tf_op jit(solution)/shard_map/ppermute | solution.py:222
  8.9 1.5 %collective-permute-start.5 = (bf16[64,1792]{1,0:T(8,128)(2,1)S(1)}, bf16[64,1792]{1,0:T(8,128)(2,1)S(1)}, u32[]{:S(2)}, u32[]{:S(2)}) collective-permute-start(bf16[64,1792]{1,0:T(8,128)(2,1)S(1)} %pad_maximum_fusion.refs_0_), channel_id=1, source_target_pairs={{0,1},{1,0},{16,17},{17,16},{2,3},{3,2},{18,19},{19,18},{4,5},{5,4... | collective-permute-start | bytes 688136 | tf_op jit(solution)/shard_map/ppermute | solution.py:225
  10.4 2.4 %collective-permute-done.6.refs_2_ = bf16[64,1792]{1,0:T(8,128)(2,1)S(1)} collective-permute-done((bf16[64,1792]{1,0:T(8,128)(2,1)S(1)}, bf16[64,1792]{1,0:T(8,128)(2,1)S(1)}, u32[]{:S(2)}, u32[]{:S(2)}) %collective-permute-start.6) | collective-permute-done | bytes 229408 | tf_op jit(solution)/shard_map/ppermute | solution.py:225
  12.8 1.5 %collective-permute-start.7 = (bf16[64,1792]{1,0:T(8,128)(2,1)S(1)}, bf16[64,1792]{1,0:T(8,128)(2,1)S(1)}, u32[]{:S(2)}, u32[]{:S(2)}) collective-permute-start(bf16[64,1792]{1,0:T(8,128)(2,1)S(1)} %collective-permute-done.6.refs_2_), channel_id=1, source_target_pairs={{0,1},{1,0},{16,17},{17,16},{2,3},{3,2},{18,19},{19,18},{4,5},{5,4... | collective-permute-start | bytes 688136 | tf_op jit(solution)/shard_map/ppermute | solution.py:225
  16.1 1.6 %collective-permute-start.4 = (bf16[64,1280]{1,0:T(8,128)(2,1)S(1)}, bf16[64,1280]{1,0:T(8,128)(2,1)S(1)}, u32[]{:S(2)}, u32[]{:S(2)}) collective-permute-start(bf16[64,1280]{1,0:T(8,128)(2,1)S(1)} %shard_map.78.refs_1_), channel_id=1, source_target_pairs={{0,2},{2,0},{4,6},{6,4},{1,3},{3,1},{5,7},{7,5},{8,10},{10,8},{12,... | collective-permute-start | bytes 491528 | tf_op jit(solution)/shard_map/ppermute | solution.py:222
  17.7 1.9 %collective-permute-done.raw_ref = bf16[64,512]{1,0:T(8,128)(2,1)S(1)} collective-permute-done((bf16[64,512]{1,0:T(8,128)(2,1)S(1)}, bf16[64,512]{1,0:T(8,128)(2,1)S(1)}, u32[]{:S(2)}, u32[]{:S(2)}) %collective-permute-start) | collective-permute-done | bytes 65568 | tf_op jit(solution)/shard_map/ppermute | solution.py:222
  19.7 2.2 %collective-permute-start.3 = (bf16[64,512]{1,0:T(8,128)(2,1)S(1)}, bf16[64,512]{1,0:T(8,128)(2,1)S(1)}, u32[]{:S(2)}, u32[]{:S(2)}) collective-permute-start(bf16[64,512]{1,0:T(8,128)(2,1)S(1)} %shard_map.77.refs_0_), channel_id=1, source_target_pairs={{0,2},{2,0},{4,6},{6,4},{1,3},{3,1},{5,7},{7,5},{8,10},{10,8},{12,... | collective-permute-start | bytes 196616 | tf_op jit(solution)/shard_map/ppermute | solution.py:222
  22.8 1.4 %collective-permute-done.3.refs_2_ = bf16[64,512]{1,0:T(8,128)(2,1)S(1)} collective-permute-done((bf16[64,512]{1,0:T(8,128)(2,1)S(1)}, bf16[64,512]{1,0:T(8,128)(2,1)S(1)}, u32[]{:S(2)}, u32[]{:S(2)}) %collective-permute-start.3) | collective-permute-done | bytes 65568 | tf_op jit(solution)/shard_map/ppermute | solution.py:222
  24.7 1.3 %shard_map.81 = (f32[512,256]{1,0:T(8,128)S(1)}, f32[2,512]{1,0:T(2,128)S(1)}, f32[2,256]{1,0:T(2,128)S(1)}) custom-call(f32[1]{0:T(128)} %bitcast.4.teacher_scale_ref, f32[1]{0:T(128)} %bitcast.5.student_scale_ref, bf16[256,512]{1,0:T(8,128)(2,1)S(1)} %get-tuple-element.23.pupil_text_ref.text_ref, bf16[256,1280]{1,0:T(8,128)(2,1)S(1)} %get-tuple-element.24.master_text_ref, ...), custom_call_target="tpu_custom_call" | custom-call | flops 1048576 | bytes 1048576 | tf_op jit(solution)/shard_map/pallas_call | solution.py:201
  27.3 1.6 %collective-permute-start.13 = (f32[2,512]{1,0:T(2,128)S(1)}, f32[2,512]{1,0:T(2,128)S(1)}, u32[]{:S(2)}, u32[]{:S(2)}) collective-permute-start(f32[2,512]{1,0:T(2,128)S(1)} %shard_map.84.refs_0_), channel_id=1, source_target_pairs={{0,17},{1,16},{16,1},{17,0},{2,19},{3,18},{18,3},{19,2},{4,21},{5,... | collective-permute-start | bytes 12296 | tf_op jit(solution)/shard_map/ppermute | solution.py:225
  28.8 1.9 %collective-permute-done.10.refs_1_ = f32[2,256]{1,0:T(2,128)S(1)} collective-permute-done((f32[2,256]{1,0:T(2,128)S(1)}, f32[2,256]{1,0:T(2,128)S(1)}, u32[]{:S(2)}, u32[]{:S(2)}) %collective-permute-start.10) | collective-permute-done | bytes 2080 | tf_op jit(solution)/shard_map/ppermute | solution.py:222
  30.8 1.7 %collective-permute-start.11 = (f32[2,256]{1,0:T(2,128)S(1)}, f32[2,256]{1,0:T(2,128)S(1)}, u32[]{:S(2)}, u32[]{:S(2)}) collective-permute-start(f32[2,256]{1,0:T(2,128)S(1)} %shard_map.82.refs_0_), channel_id=1, source_target_pairs={{0,2},{2,0},{4,6},{6,4},{1,3},{3,1},{5,7},{7,5},{8,10},{10,8},{12,... | collective-permute-start | bytes 6152 | tf_op jit(solution)/shard_map/ppermute | solution.py:222
  32.4 1.5 %collective-permute-start.15 = (f32[2,512]{1,0:T(2,128)S(1)}, f32[2,512]{1,0:T(2,128)S(1)}, u32[]{:S(2)}, u32[]{:S(2)}) collective-permute-start(f32[2,512]{1,0:T(2,128)S(1)} %shard_map.84.refs_0_), channel_id=1, source_target_pairs={{0,16},{1,17},{16,0},{17,1},{2,18},{3,19},{18,2},{19,3},{4,20},{5,... | collective-permute-start | bytes 12296 | tf_op jit(solution)/shard_map/ppermute | solution.py:225
  34.5 1.5 %collective-permute-done.15.refs_2_ = f32[2,512]{1,0:T(2,128)S(1)} collective-permute-done((f32[2,512]{1,0:T(2,128)S(1)}, f32[2,512]{1,0:T(2,128)S(1)}, u32[]{:S(2)}, u32[]{:S(2)}) %collective-permute-start.15) | collective-permute-done | bytes 4128 | tf_op jit(solution)/shard_map/ppermute | solution.py:225
  36.0 1.5 %collective-permute-done.14.refs_1_ = f32[2,512]{1,0:T(2,128)S(1)} collective-permute-done((f32[2,512]{1,0:T(2,128)S(1)}, f32[2,512]{1,0:T(2,128)S(1)}, u32[]{:S(2)}, u32[]{:S(2)}) %collective-permute-start.14) | collective-permute-done | bytes 4128 | tf_op jit(solution)/shard_map/ppermute | solution.py:225
  37.6 1.2 %shard_map.87 = (f32[4,64,512]{2,1,0:T(8,128)S(1)}, bf16[4,64,512]{2,1,0:T(8,128)(2,1)S(1)}, f32[64,512]{1,0:T(8,128)S(1)}, bf16[64,512]{1,0:T(8,128)(2,1)S(1)},...) custom-call(s32[1]{0:T(128)} %bitcast.z_ref, f32[1]{0:T(128)} %bitcast.6.scale_ref, ...), custom_call_target="tpu_custom_call" | custom-call | flops 1048576 | bytes 1048576 | tf_op jit(solution)/shard_map/pallas_call | solution.py:201
  39.8 3.5 %collective-permute-start.18 = (bf16[64,512]{1,0:T(8,128)(2,1)S(1)}, bf16[64,512]{1,0:T(8,128)(2,1)S(1)}, u32[]{:S(2)}, u32[]{:S(2)}) collective-permute-start(bf16[64,512]{1,0:T(8,128)(2,1)S(1)} %get-tuple-element.33), channel_id=1, source_target_pairs={{0,6},{2,4},{4,2},{6,0},{1,7},{3,5},{5,3},{7,1},{8,14},{10,12},{12... | collective-permute-start | bytes 196616 | tf_op jit(solution)/shard_map/ppermute | solution.py:222
  43.9 1.5 %collective-permute-start.21 = (bf16[64,512]{1,0:T(8,128)(2,1)S(1)}, bf16[64,512]{1,0:T(8,128)(2,1)S(1)}, u32[]{:S(2)}, u32[]{:S(2)}) collective-permute-start(bf16[64,512]{1,0:T(8,128)(2,1)S(1)} %get-tuple-element.38), channel_id=1, source_target_pairs={{0,16},{1,17},{16,0},{17,1},{2,18},{3,19},{18,2},{19,3},{4,20},{5,... | collective-permute-start | bytes 196616 | tf_op jit(solution)/shard_map/ppermute | solution.py:225
  45.5 1.5 %collective-permute-start.22 = (bf16[64,512]{1,0:T(8,128)(2,1)S(1)}, bf16[64,512]{1,0:T(8,128)(2,1)S(1)}, u32[]{:S(2)}, u32[]{:S(2)}) collective-permute-start(bf16[64,512]{1,0:T(8,128)(2,1)S(1)} %get-tuple-element.39), channel_id=1, source_target_pairs={{0,1},{1,0},{16,17},{17,16},{2,3},{3,2},{18,19},{19,18},{4,5},{5,4... | collective-permute-start | bytes 196616 | tf_op jit(solution)/shard_map/ppermute | solution.py:225
  47.0 1.0 %collective-permute-done.17.refs_2_ = bf16[64,512]{1,0:T(8,128)(2,1)S(1)} collective-permute-done((bf16[64,512]{1,0:T(8,128)(2,1)S(1)}, bf16[64,512]{1,0:T(8,128)(2,1)S(1)}, u32[]{:S(2)}, u32[]{:S(2)}) %collective-permute-start.17) | collective-permute-done | bytes 65568 | tf_op jit(solution)/shard_map/ppermute | solution.py:222
  49.7 0.9 %shard_map.90 = (f32[64,512]{1,0:T(8,128)}, f32[64,512]{1,0:T(8,128)}) custom-call(bf16[64,512]{1,0:T(8,128)(2,1)S(1)} %copy-done, bf16[64,512]{1,0:T(8,128)(2,1)S(1)} %copy-done.1, f32[64,512]{1,0:T(8,128)S(1)} %shard_map.88.text_ref, f32[64,512]{1,0:T(8,128)S(1)} %get-tuple-element.36.refs_0_, bf16[64,512]{1,0:T(8,128)(2,1)S(1)} %collective-permute-done.20.refs_1_, ...), custom_call_target="tpu_custom_call" | custom-call | flops 1048576 | bytes 1048576 | tf_op jit(solution)/shard_map/pallas_call | solution.py:201
  (44 shorter events, 7.2 us)
Async XLA Ops:
  0.6 6.6 %copy-start.2 = (bf16[64,1280]{1,0:T(8,128)(2,1)S(1)}, bf16[64,1280]{1,0:T(8,128)(2,1)}, u32[]{:S(2)}) copy-start(bf16[64,1280]{1,0:T(8,128)(2,1)} %teacher_ref.1) | copy-start | bytes 491524
  0.7 15.3 %collective-permute-start.2 = (bf16[64,1280]{1,0:T(8,128)(2,1)}, bf16[64,1280]{1,0:T(8,128)(2,1)S(1)}, u32[]{:S(2)}, u32[]{:S(2)}) collective-permute-start(bf16[64,1280]{1,0:T(8,128)(2,1)} %teacher_ref.1), channel_id=1, source_target_pairs={{0,4},{2,6},{4,0},{6,2},{1,5},{3,7},{5,1},{7,3},{8,12},{10,14},{12... | collective-permute-start | bytes 491528 | tf_op jit(solution)/shard_map/ppermute | solution.py:222
  5.7 7.1 %collective-permute-start.6 = (bf16[64,1792]{1,0:T(8,128)(2,1)S(1)}, bf16[64,1792]{1,0:T(8,128)(2,1)S(1)}, u32[]{:S(2)}, u32[]{:S(2)}) collective-permute-start(bf16[64,1792]{1,0:T(8,128)(2,1)S(1)} %pad_maximum_fusion.refs_0_), channel_id=1, source_target_pairs={{0,16},{1,17},{16,0},{17,1},{2,18},{3,19},{18,2},{19,3},{4,20},{5,... | collective-permute-start | bytes 688136 | tf_op jit(solution)/shard_map/ppermute | solution.py:225
  7.3 12.3 %collective-permute-start.1 = (bf16[64,1792]{1,0:T(8,128)(2,1)S(1)}, bf16[64,1792]{1,0:T(8,128)(2,1)S(1)}, u32[]{:S(2)}, u32[]{:S(2)}) collective-permute-start(bf16[64,1792]{1,0:T(8,128)(2,1)S(1)} %pad_maximum_fusion.1), channel_id=1, source_target_pairs={{0,2},{2,0},{4,6},{6,4},{1,3},{3,1},{5,7},{7,5},{8,10},{10,8},{12,... | collective-permute-start | bytes 688136 | tf_op jit(solution)/shard_map/ppermute | solution.py:222
  8.9 13.0 %collective-permute-start.5 = (bf16[64,1792]{1,0:T(8,128)(2,1)S(1)}, bf16[64,1792]{1,0:T(8,128)(2,1)S(1)}, u32[]{:S(2)}, u32[]{:S(2)}) collective-permute-start(bf16[64,1792]{1,0:T(8,128)(2,1)S(1)} %pad_maximum_fusion.refs_0_), channel_id=1, source_target_pairs={{0,1},{1,0},{16,17},{17,16},{2,3},{3,2},{18,19},{19,18},{4,5},{5,4... | collective-permute-start | bytes 688136 | tf_op jit(solution)/shard_map/ppermute | solution.py:225
  12.8 9.1 %collective-permute-start.7 = (bf16[64,1792]{1,0:T(8,128)(2,1)S(1)}, bf16[64,1792]{1,0:T(8,128)(2,1)S(1)}, u32[]{:S(2)}, u32[]{:S(2)}) collective-permute-start(bf16[64,1792]{1,0:T(8,128)(2,1)S(1)} %collective-permute-done.6.refs_2_), channel_id=1, source_target_pairs={{0,1},{1,0},{16,17},{17,16},{2,3},{3,2},{18,19},{19,18},{4,5},{5,4... | collective-permute-start | bytes 688136 | tf_op jit(solution)/shard_map/ppermute | solution.py:225
  14.3 5.3 %collective-permute-start = (bf16[64,512]{1,0:T(8,128)(2,1)S(1)}, bf16[64,512]{1,0:T(8,128)(2,1)S(1)}, u32[]{:S(2)}, u32[]{:S(2)}) collective-permute-start(bf16[64,512]{1,0:T(8,128)(2,1)S(1)} %copy-done.1), channel_id=1, source_target_pairs={{0,4},{2,6},{4,0},{6,2},{1,5},{3,7},{5,1},{7,3},{8,12},{10,14},{12... | collective-permute-start | bytes 196616 | tf_op jit(solution)/shard_map/ppermute | solution.py:222
  16.1 8.1 %collective-permute-start.4 = (bf16[64,1280]{1,0:T(8,128)(2,1)S(1)}, bf16[64,1280]{1,0:T(8,128)(2,1)S(1)}, u32[]{:S(2)}, u32[]{:S(2)}) collective-permute-start(bf16[64,1280]{1,0:T(8,128)(2,1)S(1)} %shard_map.78.refs_1_), channel_id=1, source_target_pairs={{0,2},{2,0},{4,6},{6,4},{1,3},{3,1},{5,7},{7,5},{8,10},{10,8},{12,... | collective-permute-start | bytes 491528 | tf_op jit(solution)/shard_map/ppermute | solution.py:222
  19.7 4.5 %collective-permute-start.3 = (bf16[64,512]{1,0:T(8,128)(2,1)S(1)}, bf16[64,512]{1,0:T(8,128)(2,1)S(1)}, u32[]{:S(2)}, u32[]{:S(2)}) collective-permute-start(bf16[64,512]{1,0:T(8,128)(2,1)S(1)} %shard_map.77.refs_0_), channel_id=1, source_target_pairs={{0,2},{2,0},{4,6},{6,4},{1,3},{3,1},{5,7},{7,5},{8,10},{10,8},{12,... | collective-permute-start | bytes 196616 | tf_op jit(solution)/shard_map/ppermute | solution.py:222
  22.2 2.2 %collective-permute-start.8 = (bf16[256,512]{1,0:T(8,128)(2,1)S(1)}, bf16[256,512]{1,0:T(8,128)(2,1)S(1)}, u32[]{:S(2)}, u32[]{:S(2)}) collective-permute-start(bf16[256,512]{1,0:T(8,128)(2,1)S(1)} %get-tuple-element.25.pupil_same_ref.same_ref), channel_id=1, source_target_pairs={{0,8},{8,0},{1,9},{9,1},{2,10},{10,2},{3,11},{11,3},{4,12},{12,4},... | collective-permute-start | bytes 786440 | tf_op jit(solution)/shard_map/ppermute | solution.py:253
  22.3 2.5 %collective-permute-start.9 = (bf16[256,1280]{1,0:T(8,128)(2,1)S(1)}, bf16[256,1280]{1,0:T(8,128)(2,1)S(1)}, u32[]{:S(2)}, u32[]{:S(2)}) collective-permute-start(bf16[256,1280]{1,0:T(8,128)(2,1)S(1)} %get-tuple-element.26.master_same_ref), channel_id=1, source_target_pairs={{0,8},{8,0},{1,9},{9,1},{2,10},{10,2},{3,11},{11,3},{4,12},{12,4},... | collective-permute-start | bytes 1966088 | tf_op jit(solution)/shard_map/ppermute | solution.py:253
  26.0 1.2 %collective-permute-start.12 = (f32[2,512]{1,0:T(2,128)S(1)}, f32[2,512]{1,0:T(2,128)S(1)}, u32[]{:S(2)}, u32[]{:S(2)}) collective-permute-start(f32[2,512]{1,0:T(2,128)S(1)} %get-tuple-element.29.own_ref), channel_id=1, source_target_pairs={{0,8},{8,0},{1,9},{9,1},{2,10},{10,2},{3,11},{11,3},{4,12},{12,4},... | collective-permute-start | bytes 12296 | tf_op jit(solution)/shard_map/ppermute | solution.py:253
  26.3 4.5 %collective-permute-start.10 = (f32[2,256]{1,0:T(2,128)S(1)}, f32[2,256]{1,0:T(2,128)S(1)}, u32[]{:S(2)}, u32[]{:S(2)}) collective-permute-start(f32[2,256]{1,0:T(2,128)S(1)} %get-tuple-element.28.refs_0_), channel_id=1, source_target_pairs={{0,4},{2,6},{4,0},{6,2},{1,5},{3,7},{5,1},{7,3},{8,12},{10,14},{12... | collective-permute-start | bytes 6152 | tf_op jit(solution)/shard_map/ppermute | solution.py:222
  27.3 7.2 %collective-permute-start.13 = (f32[2,512]{1,0:T(2,128)S(1)}, f32[2,512]{1,0:T(2,128)S(1)}, u32[]{:S(2)}, u32[]{:S(2)}) collective-permute-start(f32[2,512]{1,0:T(2,128)S(1)} %shard_map.84.refs_0_), channel_id=1, source_target_pairs={{0,17},{1,16},{16,1},{17,0},{2,19},{3,18},{18,3},{19,2},{4,21},{5,... | collective-permute-start | bytes 12296 | tf_op jit(solution)/shard_map/ppermute | solution.py:225
  30.8 3.7 %collective-permute-start.11 = (f32[2,256]{1,0:T(2,128)S(1)}, f32[2,256]{1,0:T(2,128)S(1)}, u32[]{:S(2)}, u32[]{:S(2)}) collective-permute-start(f32[2,256]{1,0:T(2,128)S(1)} %shard_map.82.refs_0_), channel_id=1, source_target_pairs={{0,2},{2,0},{4,6},{6,4},{1,3},{3,1},{5,7},{7,5},{8,10},{10,8},{12,... | collective-permute-start | bytes 6152 | tf_op jit(solution)/shard_map/ppermute | solution.py:222
  32.4 3.6 %collective-permute-start.15 = (f32[2,512]{1,0:T(2,128)S(1)}, f32[2,512]{1,0:T(2,128)S(1)}, u32[]{:S(2)}, u32[]{:S(2)}) collective-permute-start(f32[2,512]{1,0:T(2,128)S(1)} %shard_map.84.refs_0_), channel_id=1, source_target_pairs={{0,16},{1,17},{16,0},{17,1},{2,18},{3,19},{18,2},{19,3},{4,20},{5,... | collective-permute-start | bytes 12296 | tf_op jit(solution)/shard_map/ppermute | solution.py:225
  34.0 3.6 %collective-permute-start.14 = (f32[2,512]{1,0:T(2,128)S(1)}, f32[2,512]{1,0:T(2,128)S(1)}, u32[]{:S(2)}, u32[]{:S(2)}) collective-permute-start(f32[2,512]{1,0:T(2,128)S(1)} %shard_map.84.refs_0_), channel_id=1, source_target_pairs={{0,1},{1,0},{16,17},{17,16},{2,3},{3,2},{18,19},{19,18},{4,5},{5,4... | collective-permute-start | bytes 12296 | tf_op jit(solution)/shard_map/ppermute | solution.py:225
  38.8 4.5 %collective-permute-start.19 = (bf16[4,64,512]{2,1,0:T(8,128)(2,1)S(1)}, bf16[4,64,512]{2,1,0:T(8,128)(2,1)S(1)}, u32[]{:S(2)}, u32[]{:S(2)}) collective-permute-start(bf16[4,64,512]{2,1,0:T(8,128)(2,1)S(1)} %get-tuple-element.35), channel_id=1, source_target_pairs={{0,8},{8,0},{1,9},{9,1},{2,10},{10,2},{3,11},{11,3},{4,12},{12,4},... | collective-permute-start | bytes 786440 | tf_op jit(solution)/shard_map/ppermute | solution.py:253
  38.9 6.6 %collective-permute-start.16 = (bf16[64,512]{1,0:T(8,128)(2,1)S(1)}, bf16[64,512]{1,0:T(8,128)(2,1)S(1)}, u32[]{:S(2)}, u32[]{:S(2)}) collective-permute-start(bf16[64,512]{1,0:T(8,128)(2,1)S(1)} %get-tuple-element.31), channel_id=1, source_target_pairs={{0,2},{2,0},{4,6},{6,4},{1,3},{3,1},{5,7},{7,5},{8,10},{10,8},{12,... | collective-permute-start | bytes 196616 | tf_op jit(solution)/shard_map/ppermute | solution.py:222
  39.4 8.6 %collective-permute-start.17 = (bf16[64,512]{1,0:T(8,128)(2,1)S(1)}, bf16[64,512]{1,0:T(8,128)(2,1)S(1)}, u32[]{:S(2)}, u32[]{:S(2)}) collective-permute-start(bf16[64,512]{1,0:T(8,128)(2,1)S(1)} %get-tuple-element.32), channel_id=1, source_target_pairs={{0,4},{2,6},{4,0},{6,2},{1,5},{3,7},{5,1},{7,3},{8,12},{10,14},{12... | collective-permute-start | bytes 196616 | tf_op jit(solution)/shard_map/ppermute | solution.py:222
  39.8 8.1 %collective-permute-start.18 = (bf16[64,512]{1,0:T(8,128)(2,1)S(1)}, bf16[64,512]{1,0:T(8,128)(2,1)S(1)}, u32[]{:S(2)}, u32[]{:S(2)}) collective-permute-start(bf16[64,512]{1,0:T(8,128)(2,1)S(1)} %get-tuple-element.33), channel_id=1, source_target_pairs={{0,6},{2,4},{4,2},{6,0},{1,7},{3,5},{5,3},{7,1},{8,14},{10,12},{12... | collective-permute-start | bytes 196616 | tf_op jit(solution)/shard_map/ppermute | solution.py:222
  43.4 5.4 %collective-permute-start.20 = (bf16[64,512]{1,0:T(8,128)(2,1)S(1)}, bf16[64,512]{1,0:T(8,128)(2,1)S(1)}, u32[]{:S(2)}, u32[]{:S(2)}) collective-permute-start(bf16[64,512]{1,0:T(8,128)(2,1)S(1)} %get-tuple-element.37), channel_id=1, source_target_pairs={{0,17},{1,16},{16,1},{17,0},{2,19},{3,18},{18,3},{19,2},{4,21},{5,... | collective-permute-start | bytes 196616 | tf_op jit(solution)/shard_map/ppermute | solution.py:225
  43.9 5.0 %collective-permute-start.21 = (bf16[64,512]{1,0:T(8,128)(2,1)S(1)}, bf16[64,512]{1,0:T(8,128)(2,1)S(1)}, u32[]{:S(2)}, u32[]{:S(2)}) collective-permute-start(bf16[64,512]{1,0:T(8,128)(2,1)S(1)} %get-tuple-element.38), channel_id=1, source_target_pairs={{0,16},{1,17},{16,0},{17,1},{2,18},{3,19},{18,2},{19,3},{4,20},{5,... | collective-permute-start | bytes 196616 | tf_op jit(solution)/shard_map/ppermute | solution.py:225
  45.5 4.3 %collective-permute-start.22 = (bf16[64,512]{1,0:T(8,128)(2,1)S(1)}, bf16[64,512]{1,0:T(8,128)(2,1)S(1)}, u32[]{:S(2)}, u32[]{:S(2)}) collective-permute-start(bf16[64,512]{1,0:T(8,128)(2,1)S(1)} %get-tuple-element.39), channel_id=1, source_target_pairs={{0,1},{1,0},{16,17},{17,16},{2,3},{3,2},{18,19},{19,18},{4,5},{5,4... | collective-permute-start | bytes 196616 | tf_op jit(solution)/shard_map/ppermute | solution.py:225
  (2 other events, 8.4 us)

commit v11 on v9

--- a/solution.py
+++ b/solution.py
@@ -139,20 +139,25 @@
     col = col_ref[...]
     rows = jnp.concatenate([row_ref[...]] * 4, axis=0)
     text = text_ref[...]
-    pairs = [(same_ref, other_ref), (keep_ref, send_ref)]
-    pairs[1] = tuple(ref.reshape(squares * own, width) for ref in pairs[1])
+    half = squares * own
+    pupils = jnp.concatenate([same_ref[...], other_ref[...]], axis=0)
+    step = min(512, 2 * half)
+    parts = [ref.reshape(half, width) for ref in (keep_ref, send_ref)]
     text_part = None
-    for at, (image_ref, out_ref), part in chunks(pairs):
-        image = image_ref[part, :]
-        here = slice(at, at + image.shape[0])
-        row = jnp.transpose(rows[:, here])
-        teach = teach_ref[here, :]
+    for at in range(0, 2 * half, step):
+        image = pupils[at : at + step]
+        row = jnp.transpose(rows[:, at : at + step])
+        teach = teach_ref[at : at + step, :]
         learn = scale * product(image, text)
         rows_part = jnp.exp(learn - row[:, 1:2]) - jnp.exp(teach - row[:, 0:1])
         cols_part = jnp.exp(learn - col[1:2, :]) - jnp.exp(teach - col[0:1, :])
         weight = (0.5 * (rows_part + cols_part)).astype(BF16)
         image_part = scale * jnp.dot(weight, text, preferred_element_type=F32)
-        out_ref[part, :] = image_part.astype(out_ref.dtype)
+        for here in range(at, at + step, min(half, step)):
+            ref = parts[here // half]
+            first = here % half
+            piece = image_part[here - at : here - at + min(half, step)]
+            ref[first : first + piece.shape[0], :] = piece.astype(ref.dtype)
         piece = scale * lax.dot_general(
             weight, image, (((0,), (0,)), ((), ())), preferred_element_type=F32
         )

time: 47.8 us -> 47.7 us (level)
  no operation moved by 1% of the time
where the time goes in v11:
time: 47.7 us; the launch traced here: 47.5 us
  starting transfers between devices  29.1 us (61%)
  waiting for transfers between devices  11.2 us (23%)
  Pallas kernels  4.1 us (9%)
  between operations  2.08 us (4%)
  other arithmetic  0.95 us (2%)
    ppermute x10, starting transfers between devices, to_line(): return lax.ppermute(value, LINE, [(z, z ^ step) for z in range(depth)])  16.6 us
    ppermute x9, starting transfers between devices, to_square(): return lax.ppermute(value, SQUARE, [(q, q ^ step) for q in range(squares)])  11.7 us
    ppermute x10, waiting for transfers between devices, to_line(): return lax.ppermute(value, LINE, [(z, z ^ step) for z in range(depth)])  7.07 us
    pallas_call x13, Pallas kernels, call(): pl.pallas_call(kernel, out_shape=outs, in_specs=specs, out_specs=jax.tree...  4.1 us
    ppermute x9, waiting for transfers between devices, to_square(): return lax.ppermute(value, SQUARE, [(q, q ^ step) for q in range(squares)])  3.2 us
  transfers between devices with their start and end apart: 23, of which 10 were waited for; matrix products, arithmetic and copies ran while one was open for 2% of the time, Pallas kernels for 2%

profile of v11, /device:TPU:0, one launch (start us, length us, event | category | flops | bytes accessed | tf_op | source)
XLA Modules:
  0.0 47.5 jit_solution(7995431986426744436)
XLA Ops:
  0.7 4.1 %collective-permute-start.2 = (bf16[64,1280]{1,0:T(8,128)(2,1)}, bf16[64,1280]{1,0:T(8,128)(2,1)S(1)}, u32[]{:S(2)}, u32[]{:S(2)}) collective-permute-start(bf16[64,1280]{1,0:T(8,128)(2,1)} %teacher_ref.1), channel_id=1, source_target_pairs={{0,4},{2,6},{4,0},{6,2},{1,5},{3,7},{5,1},{7,3},{8,12},{10,14},{12... | collective-permute-start | bytes 491528 | tf_op jit(solution)/shard_map/ppermute | solution.py:227
  4.8 0.9 %pad_maximum_fusion.refs_0_ = bf16[64,1792]{1,0:T(8,128)(2,1)S(1)} fusion(bf16[64,1280]{1,0:T(8,128)(2,1)} %param.8, bf16[64,512]{1,0:T(8,128)(2,1)} %raw_image_ref.1), kind=kLoop, calls=%fused_computation | loop fusion | flops 458752 | bytes 458752 | tf_op jit(solution)/shard_map/max | solution.py:35
  5.7 1.6 %collective-permute-start.6 = (bf16[64,1792]{1,0:T(8,128)(2,1)S(1)}, bf16[64,1792]{1,0:T(8,128)(2,1)S(1)}, u32[]{:S(2)}, u32[]{:S(2)}) collective-permute-start(bf16[64,1792]{1,0:T(8,128)(2,1)S(1)} %pad_maximum_fusion.refs_0_), channel_id=1, source_target_pairs={{0,16},{1,17},{16,0},{17,1},{2,18},{3,19},{18,2},{19,3},{4,20},{5,... | collective-permute-start | bytes 688136 | tf_op jit(solution)/shard_map/ppermute | solution.py:230
  7.3 1.6 %collective-permute-start.1 = (bf16[64,1792]{1,0:T(8,128)(2,1)S(1)}, bf16[64,1792]{1,0:T(8,128)(2,1)S(1)}, u32[]{:S(2)}, u32[]{:S(2)}) collective-permute-start(bf16[64,1792]{1,0:T(8,128)(2,1)S(1)} %pad_maximum_fusion.1), channel_id=1, source_target_pairs={{0,2},{2,0},{4,6},{6,4},{1,3},{3,1},{5,7},{7,5},{8,10},{10,8},{12,... | collective-permute-start | bytes 688136 | tf_op jit(solution)/shard_map/ppermute | solution.py:227
  8.9 1.5 %collective-permute-start.5 = (bf16[64,1792]{1,0:T(8,128)(2,1)S(1)}, bf16[64,1792]{1,0:T(8,128)(2,1)S(1)}, u32[]{:S(2)}, u32[]{:S(2)}) collective-permute-start(bf16[64,1792]{1,0:T(8,128)(2,1)S(1)} %pad_maximum_fusion.refs_0_), channel_id=1, source_target_pairs={{0,1},{1,0},{16,17},{17,16},{2,3},{3,2},{18,19},{19,18},{4,5},{5,4... | collective-permute-start | bytes 688136 | tf_op jit(solution)/shard_map/ppermute | solution.py:230
  10.4 2.4 %collective-permute-done.6.refs_2_ = bf16[64,1792]{1,0:T(8,128)(2,1)S(1)} collective-permute-done((bf16[64,1792]{1,0:T(8,128)(2,1)S(1)}, bf16[64,1792]{1,0:T(8,128)(2,1)S(1)}, u32[]{:S(2)}, u32[]{:S(2)}) %collective-permute-start.6) | collective-permute-done | bytes 229408 | tf_op jit(solution)/shard_map/ppermute | solution.py:230
  12.8 1.5 %collective-permute-start.7 = (bf16[64,1792]{1,0:T(8,128)(2,1)S(1)}, bf16[64,1792]{1,0:T(8,128)(2,1)S(1)}, u32[]{:S(2)}, u32[]{:S(2)}) collective-permute-start(bf16[64,1792]{1,0:T(8,128)(2,1)S(1)} %collective-permute-done.6.refs_2_), channel_id=1, source_target_pairs={{0,1},{1,0},{16,17},{17,16},{2,3},{3,2},{18,19},{19,18},{4,5},{5,4... | collective-permute-start | bytes 688136 | tf_op jit(solution)/shard_map/ppermute | solution.py:230
  16.1 1.6 %collective-permute-start.4 = (bf16[64,1280]{1,0:T(8,128)(2,1)S(1)}, bf16[64,1280]{1,0:T(8,128)(2,1)S(1)}, u32[]{:S(2)}, u32[]{:S(2)}) collective-permute-start(bf16[64,1280]{1,0:T(8,128)(2,1)S(1)} %shard_map.78.refs_1_), channel_id=1, source_target_pairs={{0,2},{2,0},{4,6},{6,4},{1,3},{3,1},{5,7},{7,5},{8,10},{10,8},{12,... | collective-permute-start | bytes 491528 | tf_op jit(solution)/shard_map/ppermute | solution.py:227
  17.7 1.9 %collective-permute-done.raw_ref = bf16[64,512]{1,0:T(8,128)(2,1)S(1)} collective-permute-done((bf16[64,512]{1,0:T(8,128)(2,1)S(1)}, bf16[64,512]{1,0:T(8,128)(2,1)S(1)}, u32[]{:S(2)}, u32[]{:S(2)}) %collective-permute-start) | collective-permute-done | bytes 65568 | tf_op jit(solution)/shard_map/ppermute | solution.py:227
  19.7 2.2 %collective-permute-start.3 = (bf16[64,512]{1,0:T(8,128)(2,1)S(1)}, bf16[64,512]{1,0:T(8,128)(2,1)S(1)}, u32[]{:S(2)}, u32[]{:S(2)}) collective-permute-start(bf16[64,512]{1,0:T(8,128)(2,1)S(1)} %shard_map.77.refs_0_), channel_id=1, source_target_pairs={{0,2},{2,0},{4,6},{6,4},{1,3},{3,1},{5,7},{7,5},{8,10},{10,8},{12,... | collective-permute-start | bytes 196616 | tf_op jit(solution)/shard_map/ppermute | solution.py:227
  22.8 1.4 %collective-permute-done.3.refs_2_ = bf16[64,512]{1,0:T(8,128)(2,1)S(1)} collective-permute-done((bf16[64,512]{1,0:T(8,128)(2,1)S(1)}, bf16[64,512]{1,0:T(8,128)(2,1)S(1)}, u32[]{:S(2)}, u32[]{:S(2)}) %collective-permute-start.3) | collective-permute-done | bytes 65568 | tf_op jit(solution)/shard_map/ppermute | solution.py:227
  24.7 1.3 %shard_map.81 = (f32[512,256]{1,0:T(8,128)S(1)}, f32[2,512]{1,0:T(2,128)S(1)}, f32[2,256]{1,0:T(2,128)S(1)}) custom-call(f32[1]{0:T(128)} %bitcast.4.teacher_scale_ref, f32[1]{0:T(128)} %bitcast.5.student_scale_ref, bf16[256,512]{1,0:T(8,128)(2,1)S(1)} %get-tuple-element.23.pupil_text_ref.text_ref, bf16[256,1280]{1,0:T(8,128)(2,1)S(1)} %get-tuple-element.24.master_text_ref, ...), custom_call_target="tpu_custom_call" | custom-call | flops 1048576 | bytes 1048576 | tf_op jit(solution)/shard_map/pallas_call | solution.py:206
  27.3 1.6 %collective-permute-start.15 = (f32[2,512]{1,0:T(2,128)S(1)}, f32[2,512]{1,0:T(2,128)S(1)}, u32[]{:S(2)}, u32[]{:S(2)}) collective-permute-start(f32[2,512]{1,0:T(2,128)S(1)} %shard_map.84.refs_0_), channel_id=1, source_target_pairs={{0,17},{1,16},{16,1},{17,0},{2,19},{3,18},{18,3},{19,2},{4,21},{5,... | collective-permute-start | bytes 12296 | tf_op jit(solution)/shard_map/ppermute | solution.py:230
  29.4 1.5 %collective-permute-start.13 = (f32[2,512]{1,0:T(2,128)S(1)}, f32[2,512]{1,0:T(2,128)S(1)}, u32[]{:S(2)}, u32[]{:S(2)}) collective-permute-start(f32[2,512]{1,0:T(2,128)S(1)} %shard_map.84.refs_0_), channel_id=1, source_target_pairs={{0,1},{1,0},{16,17},{17,16},{2,3},{3,2},{18,19},{19,18},{4,5},{5,4... | collective-permute-start | bytes 12296 | tf_op jit(solution)/shard_map/ppermute | solution.py:230
  30.9 1.7 %collective-permute-start.11 = (f32[2,256]{1,0:T(2,128)S(1)}, f32[2,256]{1,0:T(2,128)S(1)}, u32[]{:S(2)}, u32[]{:S(2)}) collective-permute-start(f32[2,256]{1,0:T(2,128)S(1)} %shard_map.82.refs_0_), channel_id=1, source_target_pairs={{0,2},{2,0},{4,6},{6,4},{1,3},{3,1},{5,7},{7,5},{8,10},{10,8},{12,... | collective-permute-start | bytes 6152 | tf_op jit(solution)/shard_map/ppermute | solution.py:227
  32.6 1.9 %collective-permute-done.11.refs_1_ = f32[2,256]{1,0:T(2,128)S(1)} collective-permute-done((f32[2,256]{1,0:T(2,128)S(1)}, f32[2,256]{1,0:T(2,128)S(1)}, u32[]{:S(2)}, u32[]{:S(2)}) %collective-permute-start.11) | collective-permute-done | bytes 2080 | tf_op jit(solution)/shard_map/ppermute | solution.py:227
  34.6 1.1 %shard_map.86 = (f32[4,64,512]{2,1,0:T(8,128)S(1)}, bf16[4,64,512]{2,1,0:T(8,128)(2,1)S(1)}, f32[64,512]{1,0:T(8,128)S(1)}, bf16[64,512]{1,0:T(8,128)(2,1)S(1)},...) custom-call(s32[1]{0:T(128)} %bitcast.z_ref, f32[1]{0:T(128)} %bitcast.6.scale_ref, ...), custom_call_target="tpu_custom_call" | custom-call | flops 1048576 | bytes 1048576 | tf_op jit(solution)/shard_map/pallas_call | solution.py:206
  35.7 1.7 %collective-permute-start.16 = (bf16[64,512]{1,0:T(8,128)(2,1)S(1)}, bf16[64,512]{1,0:T(8,128)(2,1)S(1)}, u32[]{:S(2)}, u32[]{:S(2)}) collective-permute-start(bf16[64,512]{1,0:T(8,128)(2,1)S(1)} %get-tuple-element.31), channel_id=1, source_target_pairs={{0,2},{2,0},{4,6},{6,4},{1,3},{3,1},{5,7},{7,5},{8,10},{10,8},{12,... | collective-permute-start | bytes 196616 | tf_op jit(solution)/shard_map/ppermute | solution.py:227
  37.5 1.8 %collective-permute-start.17 = (bf16[64,512]{1,0:T(8,128)(2,1)S(1)}, bf16[64,512]{1,0:T(8,128)(2,1)S(1)}, u32[]{:S(2)}, u32[]{:S(2)}) collective-permute-start(bf16[64,512]{1,0:T(8,128)(2,1)S(1)} %get-tuple-element.32), channel_id=1, source_target_pairs={{0,4},{2,6},{4,0},{6,2},{1,5},{3,7},{5,1},{7,3},{8,12},{10,14},{12... | collective-permute-start | bytes 196616 | tf_op jit(solution)/shard_map/ppermute | solution.py:227
  39.3 0.9 %collective-permute-start.18 = (bf16[64,512]{1,0:T(8,128)(2,1)S(1)}, bf16[64,512]{1,0:T(8,128)(2,1)S(1)}, u32[]{:S(2)}, u32[]{:S(2)}) collective-permute-start(bf16[64,512]{1,0:T(8,128)(2,1)S(1)} %get-tuple-element.33), channel_id=1, source_target_pairs={{0,6},{2,4},{4,2},{6,0},{1,7},{3,5},{5,3},{7,1},{8,14},{10,12},{12... | collective-permute-start | bytes 196616 | tf_op jit(solution)/shard_map/ppermute | solution.py:227
  40.2 1.5 %collective-permute-start.20 = (bf16[64,512]{1,0:T(8,128)(2,1)S(1)}, bf16[64,512]{1,0:T(8,128)(2,1)S(1)}, u32[]{:S(2)}, u32[]{:S(2)}) collective-permute-start(bf16[64,512]{1,0:T(8,128)(2,1)S(1)} %get-tuple-element.37), channel_id=1, source_target_pairs={{0,17},{1,16},{16,1},{17,0},{2,19},{3,18},{18,3},{19,2},{4,21},{5,... | collective-permute-start | bytes 196616 | tf_op jit(solution)/shard_map/ppermute | solution.py:230
  42.3 1.5 %collective-permute-start.22 = (bf16[64,512]{1,0:T(8,128)(2,1)S(1)}, bf16[64,512]{1,0:T(8,128)(2,1)S(1)}, u32[]{:S(2)}, u32[]{:S(2)}) collective-permute-start(bf16[64,512]{1,0:T(8,128)(2,1)S(1)} %get-tuple-element.39), channel_id=1, source_target_pairs={{0,1},{1,0},{16,17},{17,16},{2,3},{3,2},{18,19},{19,18},{4,5},{5,4... | collective-permute-start | bytes 196616 | tf_op jit(solution)/shard_map/ppermute | solution.py:230
  43.8 1.9 %collective-permute-done.17.refs_2_ = bf16[64,512]{1,0:T(8,128)(2,1)S(1)} collective-permute-done((bf16[64,512]{1,0:T(8,128)(2,1)S(1)}, bf16[64,512]{1,0:T(8,128)(2,1)S(1)}, u32[]{:S(2)}, u32[]{:S(2)}) %collective-permute-start.17) | collective-permute-done | bytes 65568 | tf_op jit(solution)/shard_map/ppermute | solution.py:227
  46.6 0.9 %shard_map.89 = (f32[64,512]{1,0:T(8,128)}, f32[64,512]{1,0:T(8,128)}) custom-call(bf16[64,512]{1,0:T(8,128)(2,1)S(1)} %copy-done, bf16[64,512]{1,0:T(8,128)(2,1)S(1)} %copy-done.1, f32[64,512]{1,0:T(8,128)S(1)} %shard_map.87.text_ref, f32[64,512]{1,0:T(8,128)S(1)} %get-tuple-element.36.refs_0_, bf16[64,512]{1,0:T(8,128)(2,1)S(1)} %collective-permute-done.20.refs_1_, ...), custom_call_target="tpu_custom_call" | custom-call | flops 1048576 | bytes 1048576 | tf_op jit(solution)/shard_map/pallas_call | solution.py:206
  (43 shorter events, 5.3 us)
Async XLA Ops:
  0.6 6.6 %copy-start.2 = (bf16[64,1280]{1,0:T(8,128)(2,1)S(1)}, bf16[64,1280]{1,0:T(8,128)(2,1)}, u32[]{:S(2)}) copy-start(bf16[64,1280]{1,0:T(8,128)(2,1)} %teacher_ref.1) | copy-start | bytes 491524
  0.7 15.3 %collective-permute-start.2 = (bf16[64,1280]{1,0:T(8,128)(2,1)}, bf16[64,1280]{1,0:T(8,128)(2,1)S(1)}, u32[]{:S(2)}, u32[]{:S(2)}) collective-permute-start(bf16[64,1280]{1,0:T(8,128)(2,1)} %teacher_ref.1), channel_id=1, source_target_pairs={{0,4},{2,6},{4,0},{6,2},{1,5},{3,7},{5,1},{7,3},{8,12},{10,14},{12... | collective-permute-start | bytes 491528 | tf_op jit(solution)/shard_map/ppermute | solution.py:227
  5.7 7.1 %collective-permute-start.6 = (bf16[64,1792]{1,0:T(8,128)(2,1)S(1)}, bf16[64,1792]{1,0:T(8,128)(2,1)S(1)}, u32[]{:S(2)}, u32[]{:S(2)}) collective-permute-start(bf16[64,1792]{1,0:T(8,128)(2,1)S(1)} %pad_maximum_fusion.refs_0_), channel_id=1, source_target_pairs={{0,16},{1,17},{16,0},{17,1},{2,18},{3,19},{18,2},{19,3},{4,20},{5,... | collective-permute-start | bytes 688136 | tf_op jit(solution)/shard_map/ppermute | solution.py:230
  7.3 12.3 %collective-permute-start.1 = (bf16[64,1792]{1,0:T(8,128)(2,1)S(1)}, bf16[64,1792]{1,0:T(8,128)(2,1)S(1)}, u32[]{:S(2)}, u32[]{:S(2)}) collective-permute-start(bf16[64,1792]{1,0:T(8,128)(2,1)S(1)} %pad_maximum_fusion.1), channel_id=1, source_target_pairs={{0,2},{2,0},{4,6},{6,4},{1,3},{3,1},{5,7},{7,5},{8,10},{10,8},{12,... | collective-permute-start | bytes 688136 | tf_op jit(solution)/shard_map/ppermute | solution.py:227
  8.9 13.0 %collective-permute-start.5 = (bf16[64,1792]{1,0:T(8,128)(2,1)S(1)}, bf16[64,1792]{1,0:T(8,128)(2,1)S(1)}, u32[]{:S(2)}, u32[]{:S(2)}) collective-permute-start(bf16[64,1792]{1,0:T(8,128)(2,1)S(1)} %pad_maximum_fusion.refs_0_), channel_id=1, source_target_pairs={{0,1},{1,0},{16,17},{17,16},{2,3},{3,2},{18,19},{19,18},{4,5},{5,4... | collective-permute-start | bytes 688136 | tf_op jit(solution)/shard_map/ppermute | solution.py:230
  12.8 9.1 %collective-permute-start.7 = (bf16[64,1792]{1,0:T(8,128)(2,1)S(1)}, bf16[64,1792]{1,0:T(8,128)(2,1)S(1)}, u32[]{:S(2)}, u32[]{:S(2)}) collective-permute-start(bf16[64,1792]{1,0:T(8,128)(2,1)S(1)} %collective-permute-done.6.refs_2_), channel_id=1, source_target_pairs={{0,1},{1,0},{16,17},{17,16},{2,3},{3,2},{18,19},{19,18},{4,5},{5,4... | collective-permute-start | bytes 688136 | tf_op jit(solution)/shard_map/ppermute | solution.py:230
  14.3 5.3 %collective-permute-start = (bf16[64,512]{1,0:T(8,128)(2,1)S(1)}, bf16[64,512]{1,0:T(8,128)(2,1)S(1)}, u32[]{:S(2)}, u32[]{:S(2)}) collective-permute-start(bf16[64,512]{1,0:T(8,128)(2,1)S(1)} %copy-done.1), channel_id=1, source_target_pairs={{0,4},{2,6},{4,0},{6,2},{1,5},{3,7},{5,1},{7,3},{8,12},{10,14},{12... | collective-permute-start | bytes 196616 | tf_op jit(solution)/shard_map/ppermute | solution.py:227
  16.1 8.1 %collective-permute-start.4 = (bf16[64,1280]{1,0:T(8,128)(2,1)S(1)}, bf16[64,1280]{1,0:T(8,128)(2,1)S(1)}, u32[]{:S(2)}, u32[]{:S(2)}) collective-permute-start(bf16[64,1280]{1,0:T(8,128)(2,1)S(1)} %shard_map.78.refs_1_), channel_id=1, source_target_pairs={{0,2},{2,0},{4,6},{6,4},{1,3},{3,1},{5,7},{7,5},{8,10},{10,8},{12,... | collective-permute-start | bytes 491528 | tf_op jit(solution)/shard_map/ppermute | solution.py:227
  19.7 4.5 %collective-permute-start.3 = (bf16[64,512]{1,0:T(8,128)(2,1)S(1)}, bf16[64,512]{1,0:T(8,128)(2,1)S(1)}, u32[]{:S(2)}, u32[]{:S(2)}) collective-permute-start(bf16[64,512]{1,0:T(8,128)(2,1)S(1)} %shard_map.77.refs_0_), channel_id=1, source_target_pairs={{0,2},{2,0},{4,6},{6,4},{1,3},{3,1},{5,7},{7,5},{8,10},{10,8},{12,... | collective-permute-start | bytes 196616 | tf_op jit(solution)/shard_map/ppermute | solution.py:227
  22.2 2.2 %collective-permute-start.8 = (bf16[256,512]{1,0:T(8,128)(2,1)S(1)}, bf16[256,512]{1,0:T(8,128)(2,1)S(1)}, u32[]{:S(2)}, u32[]{:S(2)}) collective-permute-start(bf16[256,512]{1,0:T(8,128)(2,1)S(1)} %get-tuple-element.25.pupil_same_ref.same_ref), channel_id=1, source_target_pairs={{0,8},{8,0},{1,9},{9,1},{2,10},{10,2},{3,11},{11,3},{4,12},{12,4},... | collective-permute-start | bytes 786440 | tf_op jit(solution)/shard_map/ppermute | solution.py:258
  22.3 2.5 %collective-permute-start.9 = (bf16[256,1280]{1,0:T(8,128)(2,1)S(1)}, bf16[256,1280]{1,0:T(8,128)(2,1)S(1)}, u32[]{:S(2)}, u32[]{:S(2)}) collective-permute-start(bf16[256,1280]{1,0:T(8,128)(2,1)S(1)} %get-tuple-element.26.master_same_ref), channel_id=1, source_target_pairs={{0,8},{8,0},{1,9},{9,1},{2,10},{10,2},{3,11},{11,3},{4,12},{12,4},... | collective-permute-start | bytes 1966088 | tf_op jit(solution)/shard_map/ppermute | solution.py:258
  26.0 1.2 %collective-permute-start.12 = (f32[2,512]{1,0:T(2,128)S(1)}, f32[2,512]{1,0:T(2,128)S(1)}, u32[]{:S(2)}, u32[]{:S(2)}) collective-permute-start(f32[2,512]{1,0:T(2,128)S(1)} %get-tuple-element.29.own_ref), channel_id=1, source_target_pairs={{0,8},{8,0},{1,9},{9,1},{2,10},{10,2},{3,11},{11,3},{4,12},{12,4},... | collective-permute-start | bytes 12296 | tf_op jit(solution)/shard_map/ppermute | solution.py:258
  26.3 4.6 %collective-permute-start.10 = (f32[2,256]{1,0:T(2,128)S(1)}, f32[2,256]{1,0:T(2,128)S(1)}, u32[]{:S(2)}, u32[]{:S(2)}) collective-permute-start(f32[2,256]{1,0:T(2,128)S(1)} %get-tuple-element.28.refs_0_), channel_id=1, source_target_pairs={{0,4},{2,6},{4,0},{6,2},{1,5},{3,7},{5,1},{7,3},{8,12},{10,14},{12... | collective-permute-start | bytes 6152 | tf_op jit(solution)/shard_map/ppermute | solution.py:227
  27.3 7.2 %collective-permute-start.15 = (f32[2,512]{1,0:T(2,128)S(1)}, f32[2,512]{1,0:T(2,128)S(1)}, u32[]{:S(2)}, u32[]{:S(2)}) collective-permute-start(f32[2,512]{1,0:T(2,128)S(1)} %shard_map.84.refs_0_), channel_id=1, source_target_pairs={{0,17},{1,16},{16,1},{17,0},{2,19},{3,18},{18,3},{19,2},{4,21},{5,... | collective-permute-start | bytes 12296 | tf_op jit(solution)/shard_map/ppermute | solution.py:230
  28.8 5.7 %collective-permute-start.14 = (f32[2,512]{1,0:T(2,128)S(1)}, f32[2,512]{1,0:T(2,128)S(1)}, u32[]{:S(2)}, u32[]{:S(2)}) collective-permute-start(f32[2,512]{1,0:T(2,128)S(1)} %shard_map.84.refs_0_), channel_id=1, source_target_pairs={{0,16},{1,17},{16,0},{17,1},{2,18},{3,19},{18,2},{19,3},{4,20},{5,... | collective-permute-start | bytes 12296 | tf_op jit(solution)/shard_map/ppermute | solution.py:230
  29.4 5.2 %collective-permute-start.13 = (f32[2,512]{1,0:T(2,128)S(1)}, f32[2,512]{1,0:T(2,128)S(1)}, u32[]{:S(2)}, u32[]{:S(2)}) collective-permute-start(f32[2,512]{1,0:T(2,128)S(1)} %shard_map.84.refs_0_), channel_id=1, source_target_pairs={{0,1},{1,0},{16,17},{17,16},{2,3},{3,2},{18,19},{19,18},{4,5},{5,4... | collective-permute-start | bytes 12296 | tf_op jit(solution)/shard_map/ppermute | solution.py:230
  30.9 3.7 %collective-permute-start.11 = (f32[2,256]{1,0:T(2,128)S(1)}, f32[2,256]{1,0:T(2,128)S(1)}, u32[]{:S(2)}, u32[]{:S(2)}) collective-permute-start(f32[2,256]{1,0:T(2,128)S(1)} %shard_map.82.refs_0_), channel_id=1, source_target_pairs={{0,2},{2,0},{4,6},{6,4},{1,3},{3,1},{5,7},{7,5},{8,10},{10,8},{12,... | collective-permute-start | bytes 6152 | tf_op jit(solution)/shard_map/ppermute | solution.py:227
  35.7 4.5 %collective-permute-start.19 = (bf16[4,64,512]{2,1,0:T(8,128)(2,1)S(1)}, bf16[4,64,512]{2,1,0:T(8,128)(2,1)S(1)}, u32[]{:S(2)}, u32[]{:S(2)}) collective-permute-start(bf16[4,64,512]{2,1,0:T(8,128)(2,1)S(1)} %get-tuple-element.35), channel_id=1, source_target_pairs={{0,8},{8,0},{1,9},{9,1},{2,10},{10,2},{3,11},{11,3},{4,12},{12,4},... | collective-permute-start | bytes 786440 | tf_op jit(solution)/shard_map/ppermute | solution.py:258
  35.7 6.6 %collective-permute-start.16 = (bf16[64,512]{1,0:T(8,128)(2,1)S(1)}, bf16[64,512]{1,0:T(8,128)(2,1)S(1)}, u32[]{:S(2)}, u32[]{:S(2)}) collective-permute-start(bf16[64,512]{1,0:T(8,128)(2,1)S(1)} %get-tuple-element.31), channel_id=1, source_target_pairs={{0,2},{2,0},{4,6},{6,4},{1,3},{3,1},{5,7},{7,5},{8,10},{10,8},{12,... | collective-permute-start | bytes 196616 | tf_op jit(solution)/shard_map/ppermute | solution.py:227
  37.5 8.2 %collective-permute-start.17 = (bf16[64,512]{1,0:T(8,128)(2,1)S(1)}, bf16[64,512]{1,0:T(8,128)(2,1)S(1)}, u32[]{:S(2)}, u32[]{:S(2)}) collective-permute-start(bf16[64,512]{1,0:T(8,128)(2,1)S(1)} %get-tuple-element.32), channel_id=1, source_target_pairs={{0,4},{2,6},{4,0},{6,2},{1,5},{3,7},{5,1},{7,3},{8,12},{10,14},{12... | collective-permute-start | bytes 196616 | tf_op jit(solution)/shard_map/ppermute | solution.py:227
  39.3 6.4 %collective-permute-start.18 = (bf16[64,512]{1,0:T(8,128)(2,1)S(1)}, bf16[64,512]{1,0:T(8,128)(2,1)S(1)}, u32[]{:S(2)}, u32[]{:S(2)}) collective-permute-start(bf16[64,512]{1,0:T(8,128)(2,1)S(1)} %get-tuple-element.33), channel_id=1, source_target_pairs={{0,6},{2,4},{4,2},{6,0},{1,7},{3,5},{5,3},{7,1},{8,14},{10,12},{12... | collective-permute-start | bytes 196616 | tf_op jit(solution)/shard_map/ppermute | solution.py:227
  40.2 5.8 %collective-permute-start.20 = (bf16[64,512]{1,0:T(8,128)(2,1)S(1)}, bf16[64,512]{1,0:T(8,128)(2,1)S(1)}, u32[]{:S(2)}, u32[]{:S(2)}) collective-permute-start(bf16[64,512]{1,0:T(8,128)(2,1)S(1)} %get-tuple-element.37), channel_id=1, source_target_pairs={{0,17},{1,16},{16,1},{17,0},{2,19},{3,18},{18,3},{19,2},{4,21},{5,... | collective-permute-start | bytes 196616 | tf_op jit(solution)/shard_map/ppermute | solution.py:230
  41.8 4.6 %collective-permute-start.21 = (bf16[64,512]{1,0:T(8,128)(2,1)S(1)}, bf16[64,512]{1,0:T(8,128)(2,1)S(1)}, u32[]{:S(2)}, u32[]{:S(2)}) collective-permute-start(bf16[64,512]{1,0:T(8,128)(2,1)S(1)} %get-tuple-element.38), channel_id=1, source_target_pairs={{0,16},{1,17},{16,0},{17,1},{2,18},{3,19},{18,2},{19,3},{4,20},{5,... | collective-permute-start | bytes 196616 | tf_op jit(solution)/shard_map/ppermute | solution.py:230
  42.3 4.3 %collective-permute-start.22 = (bf16[64,512]{1,0:T(8,128)(2,1)S(1)}, bf16[64,512]{1,0:T(8,128)(2,1)S(1)}, u32[]{:S(2)}, u32[]{:S(2)}) collective-permute-start(bf16[64,512]{1,0:T(8,128)(2,1)S(1)} %get-tuple-element.39), channel_id=1, source_target_pairs={{0,1},{1,0},{16,17},{17,16},{2,3},{3,2},{18,19},{19,18},{4,5},{5,4... | collective-permute-start | bytes 196616 | tf_op jit(solution)/shard_map/ppermute | solution.py:230
  (2 other events, 7.5 us)

commit v12 on v11

--- a/solution.py
+++ b/solution.py
@@ -329,7 +329,8 @@
             (pltpu.VMEM((texts, width), F32),),
             grant,
         )
-        text_parts = [to_line(part, s + 1) for s, part in enumerate(for_line)]
+        order = sorted(range(1, depth), key=lambda s: (s != 2, s))
+        text_parts = [to_line(for_line[s - 1], s) for s in order]
         text_grad = call(sum_kernel, block, (own_text, *text_parts), [vmem] * depth, vmem, flops=MANY)
         own_image, *for_square = call(
             pair_kernel,

time: 47.7 us -> 48 us (level)
  waiting for transfers between devices: 11.2 us -> 11.9 us
    ppermute x9, waiting for transfers between devices: 3.2 us -> 3.89 us  [to_square(): return lax.ppermute(value, SQUARE, [(q, q ^ step) for q in range(squares)])]
  transfers between devices with their start and end apart: 23 -> 23, of which waited for: 10 -> 11; matrix products, arithmetic and copies ran while one was open for 2% -> 2% of each run, Pallas kernels for 2% -> 2%
where the time goes in v12:
time: 48 us; the launch traced here: 47.8 us
  starting transfers between devices  28.8 us (60%)
  waiting for transfers between devices  11.9 us (25%)
  Pallas kernels  4.1 us (9%)
  between operations  2.08 us (4%)
  other arithmetic  0.95 us (2%)
    ppermute x10, starting transfers between devices, to_line(): return lax.ppermute(value, LINE, [(z, z ^ step) for z in range(depth)])  16.6 us
    ppermute x9, starting transfers between devices, to_square(): return lax.ppermute(value, SQUARE, [(q, q ^ step) for q in range(squares)])  11.3 us
    ppermute x10, waiting for transfers between devices, to_line(): return lax.ppermute(value, LINE, [(z, z ^ step) for z in range(depth)])  7.07 us
    pallas_call x13, Pallas kernels, call(): pl.pallas_call(kernel, out_shape=outs, in_specs=specs, out_specs=jax.tree...  4.1 us
    ppermute x9, waiting for transfers between devices, to_square(): return lax.ppermute(value, SQUARE, [(q, q ^ step) for q in range(squares)])  3.89 us
  transfers between devices with their start and end apart: 23, of which 11 were waited for; matrix products, arithmetic and copies ran while one was open for 2% of the time, Pallas kernels for 2%

profile of v12, /device:TPU:0, one launch (start us, length us, event | category | flops | bytes accessed | tf_op | source)
XLA Modules:
  0.0 47.8 jit_solution(12765096764808065718)
XLA Ops:
  0.7 4.1 %collective-permute-start.2 = (bf16[64,1280]{1,0:T(8,128)(2,1)}, bf16[64,1280]{1,0:T(8,128)(2,1)S(1)}, u32[]{:S(2)}, u32[]{:S(2)}) collective-permute-start(bf16[64,1280]{1,0:T(8,128)(2,1)} %teacher_ref.1), channel_id=1, source_target_pairs={{0,4},{2,6},{4,0},{6,2},{1,5},{3,7},{5,1},{7,3},{8,12},{10,14},{12... | collective-permute-start | bytes 491528 | tf_op jit(solution)/shard_map/ppermute | solution.py:227
  4.8 0.9 %pad_maximum_fusion.refs_0_ = bf16[64,1792]{1,0:T(8,128)(2,1)S(1)} fusion(bf16[64,1280]{1,0:T(8,128)(2,1)} %param.8, bf16[64,512]{1,0:T(8,128)(2,1)} %raw_image_ref.1), kind=kLoop, calls=%fused_computation | loop fusion | flops 458752 | bytes 458752 | tf_op jit(solution)/shard_map/max | solution.py:35
  5.7 1.6 %collective-permute-start.6 = (bf16[64,1792]{1,0:T(8,128)(2,1)S(1)}, bf16[64,1792]{1,0:T(8,128)(2,1)S(1)}, u32[]{:S(2)}, u32[]{:S(2)}) collective-permute-start(bf16[64,1792]{1,0:T(8,128)(2,1)S(1)} %pad_maximum_fusion.refs_0_), channel_id=1, source_target_pairs={{0,16},{1,17},{16,0},{17,1},{2,18},{3,19},{18,2},{19,3},{4,20},{5,... | collective-permute-start | bytes 688136 | tf_op jit(solution)/shard_map/ppermute | solution.py:230
  7.3 1.6 %collective-permute-start.1 = (bf16[64,1792]{1,0:T(8,128)(2,1)S(1)}, bf16[64,1792]{1,0:T(8,128)(2,1)S(1)}, u32[]{:S(2)}, u32[]{:S(2)}) collective-permute-start(bf16[64,1792]{1,0:T(8,128)(2,1)S(1)} %pad_maximum_fusion.1), channel_id=1, source_target_pairs={{0,2},{2,0},{4,6},{6,4},{1,3},{3,1},{5,7},{7,5},{8,10},{10,8},{12,... | collective-permute-start | bytes 688136 | tf_op jit(solution)/shard_map/ppermute | solution.py:227
  8.9 1.5 %collective-permute-start.5 = (bf16[64,1792]{1,0:T(8,128)(2,1)S(1)}, bf16[64,1792]{1,0:T(8,128)(2,1)S(1)}, u32[]{:S(2)}, u32[]{:S(2)}) collective-permute-start(bf16[64,1792]{1,0:T(8,128)(2,1)S(1)} %pad_maximum_fusion.refs_0_), channel_id=1, source_target_pairs={{0,1},{1,0},{16,17},{17,16},{2,3},{3,2},{18,19},{19,18},{4,5},{5,4... | collective-permute-start | bytes 688136 | tf_op jit(solution)/shard_map/ppermute | solution.py:230
  10.4 2.4 %collective-permute-done.6.refs_2_ = bf16[64,1792]{1,0:T(8,128)(2,1)S(1)} collective-permute-done((bf16[64,1792]{1,0:T(8,128)(2,1)S(1)}, bf16[64,1792]{1,0:T(8,128)(2,1)S(1)}, u32[]{:S(2)}, u32[]{:S(2)}) %collective-permute-start.6) | collective-permute-done | bytes 229408 | tf_op jit(solution)/shard_map/ppermute | solution.py:230
  12.8 1.5 %collective-permute-start.7 = (bf16[64,1792]{1,0:T(8,128)(2,1)S(1)}, bf16[64,1792]{1,0:T(8,128)(2,1)S(1)}, u32[]{:S(2)}, u32[]{:S(2)}) collective-permute-start(bf16[64,1792]{1,0:T(8,128)(2,1)S(1)} %collective-permute-done.6.refs_2_), channel_id=1, source_target_pairs={{0,1},{1,0},{16,17},{17,16},{2,3},{3,2},{18,19},{19,18},{4,5},{5,4... | collective-permute-start | bytes 688136 | tf_op jit(solution)/shard_map/ppermute | solution.py:230
  16.1 1.6 %collective-permute-start.4 = (bf16[64,1280]{1,0:T(8,128)(2,1)S(1)}, bf16[64,1280]{1,0:T(8,128)(2,1)S(1)}, u32[]{:S(2)}, u32[]{:S(2)}) collective-permute-start(bf16[64,1280]{1,0:T(8,128)(2,1)S(1)} %shard_map.78.refs_1_), channel_id=1, source_target_pairs={{0,2},{2,0},{4,6},{6,4},{1,3},{3,1},{5,7},{7,5},{8,10},{10,8},{12,... | collective-permute-start | bytes 491528 | tf_op jit(solution)/shard_map/ppermute | solution.py:227
  17.7 1.9 %collective-permute-done.raw_ref = bf16[64,512]{1,0:T(8,128)(2,1)S(1)} collective-permute-done((bf16[64,512]{1,0:T(8,128)(2,1)S(1)}, bf16[64,512]{1,0:T(8,128)(2,1)S(1)}, u32[]{:S(2)}, u32[]{:S(2)}) %collective-permute-start) | collective-permute-done | bytes 65568 | tf_op jit(solution)/shard_map/ppermute | solution.py:227
  19.7 2.2 %collective-permute-start.3 = (bf16[64,512]{1,0:T(8,128)(2,1)S(1)}, bf16[64,512]{1,0:T(8,128)(2,1)S(1)}, u32[]{:S(2)}, u32[]{:S(2)}) collective-permute-start(bf16[64,512]{1,0:T(8,128)(2,1)S(1)} %shard_map.77.refs_0_), channel_id=1, source_target_pairs={{0,2},{2,0},{4,6},{6,4},{1,3},{3,1},{5,7},{7,5},{8,10},{10,8},{12,... | collective-permute-start | bytes 196616 | tf_op jit(solution)/shard_map/ppermute | solution.py:227
  22.8 1.4 %collective-permute-done.3.refs_2_ = bf16[64,512]{1,0:T(8,128)(2,1)S(1)} collective-permute-done((bf16[64,512]{1,0:T(8,128)(2,1)S(1)}, bf16[64,512]{1,0:T(8,128)(2,1)S(1)}, u32[]{:S(2)}, u32[]{:S(2)}) %collective-permute-start.3) | collective-permute-done | bytes 65568 | tf_op jit(solution)/shard_map/ppermute | solution.py:227
  24.7 1.3 %shard_map.81 = (f32[512,256]{1,0:T(8,128)S(1)}, f32[2,512]{1,0:T(2,128)S(1)}, f32[2,256]{1,0:T(2,128)S(1)}) custom-call(f32[1]{0:T(128)} %bitcast.4.teacher_scale_ref, f32[1]{0:T(128)} %bitcast.5.student_scale_ref, bf16[256,512]{1,0:T(8,128)(2,1)S(1)} %get-tuple-element.23.pupil_text_ref.text_ref, bf16[256,1280]{1,0:T(8,128)(2,1)S(1)} %get-tuple-element.24.master_text_ref, ...), custom_call_target="tpu_custom_call" | custom-call | flops 1048576 | bytes 1048576 | tf_op jit(solution)/shard_map/pallas_call | solution.py:206
  27.3 1.6 %collective-permute-start.15 = (f32[2,512]{1,0:T(2,128)S(1)}, f32[2,512]{1,0:T(2,128)S(1)}, u32[]{:S(2)}, u32[]{:S(2)}) collective-permute-start(f32[2,512]{1,0:T(2,128)S(1)} %shard_map.84.refs_0_), channel_id=1, source_target_pairs={{0,17},{1,16},{16,1},{17,0},{2,19},{3,18},{18,3},{19,2},{4,21},{5,... | collective-permute-start | bytes 12296 | tf_op jit(solution)/shard_map/ppermute | solution.py:230
  29.4 1.5 %collective-permute-start.13 = (f32[2,512]{1,0:T(2,128)S(1)}, f32[2,512]{1,0:T(2,128)S(1)}, u32[]{:S(2)}, u32[]{:S(2)}) collective-permute-start(f32[2,512]{1,0:T(2,128)S(1)} %shard_map.84.refs_0_), channel_id=1, source_target_pairs={{0,1},{1,0},{16,17},{17,16},{2,3},{3,2},{18,19},{19,18},{4,5},{5,4... | collective-permute-start | bytes 12296 | tf_op jit(solution)/shard_map/ppermute | solution.py:230
  30.9 1.7 %collective-permute-start.11 = (f32[2,256]{1,0:T(2,128)S(1)}, f32[2,256]{1,0:T(2,128)S(1)}, u32[]{:S(2)}, u32[]{:S(2)}) collective-permute-start(f32[2,256]{1,0:T(2,128)S(1)} %shard_map.82.refs_0_), channel_id=1, source_target_pairs={{0,2},{2,0},{4,6},{6,4},{1,3},{3,1},{5,7},{7,5},{8,10},{10,8},{12,... | collective-permute-start | bytes 6152 | tf_op jit(solution)/shard_map/ppermute | solution.py:227
  32.6 1.9 %collective-permute-done.11.refs_1_ = f32[2,256]{1,0:T(2,128)S(1)} collective-permute-done((f32[2,256]{1,0:T(2,128)S(1)}, f32[2,256]{1,0:T(2,128)S(1)}, u32[]{:S(2)}, u32[]{:S(2)}) %collective-permute-start.11) | collective-permute-done | bytes 2080 | tf_op jit(solution)/shard_map/ppermute | solution.py:227
  34.6 1.1 %shard_map.86 = (f32[4,64,512]{2,1,0:T(8,128)S(1)}, bf16[4,64,512]{2,1,0:T(8,128)(2,1)S(1)}, f32[64,512]{1,0:T(8,128)S(1)}, bf16[64,512]{1,0:T(8,128)(2,1)S(1)},...) custom-call(s32[1]{0:T(128)} %bitcast.z_ref, f32[1]{0:T(128)} %bitcast.6.scale_ref, ...), custom_call_target="tpu_custom_call" | custom-call | flops 1048576 | bytes 1048576 | tf_op jit(solution)/shard_map/pallas_call | solution.py:206
  35.7 2.0 %collective-permute-start.16 = (bf16[64,512]{1,0:T(8,128)(2,1)S(1)}, bf16[64,512]{1,0:T(8,128)(2,1)S(1)}, u32[]{:S(2)}, u32[]{:S(2)}) collective-permute-start(bf16[64,512]{1,0:T(8,128)(2,1)S(1)} %get-tuple-element.31), channel_id=1, source_target_pairs={{0,4},{2,6},{4,0},{6,2},{1,5},{3,7},{5,1},{7,3},{8,12},{10,14},{12... | collective-permute-start | bytes 196616 | tf_op jit(solution)/shard_map/ppermute | solution.py:227
  37.7 1.6 %collective-permute-start.17 = (bf16[64,512]{1,0:T(8,128)(2,1)S(1)}, bf16[64,512]{1,0:T(8,128)(2,1)S(1)}, u32[]{:S(2)}, u32[]{:S(2)}) collective-permute-start(bf16[64,512]{1,0:T(8,128)(2,1)S(1)} %get-tuple-element.32), channel_id=1, source_target_pairs={{0,2},{2,0},{4,6},{6,4},{1,3},{3,1},{5,7},{7,5},{8,10},{10,8},{12,... | collective-permute-start | bytes 196616 | tf_op jit(solution)/shard_map/ppermute | solution.py:227
  39.3 0.9 %collective-permute-start.18 = (bf16[64,512]{1,0:T(8,128)(2,1)S(1)}, bf16[64,512]{1,0:T(8,128)(2,1)S(1)}, u32[]{:S(2)}, u32[]{:S(2)}) collective-permute-start(bf16[64,512]{1,0:T(8,128)(2,1)S(1)} %get-tuple-element.33), channel_id=1, source_target_pairs={{0,6},{2,4},{4,2},{6,0},{1,7},{3,5},{5,3},{7,1},{8,14},{10,12},{12... | collective-permute-start | bytes 196616 | tf_op jit(solution)/shard_map/ppermute | solution.py:227
  40.2 1.5 %collective-permute-start.20 = (bf16[64,512]{1,0:T(8,128)(2,1)S(1)}, bf16[64,512]{1,0:T(8,128)(2,1)S(1)}, u32[]{:S(2)}, u32[]{:S(2)}) collective-permute-start(bf16[64,512]{1,0:T(8,128)(2,1)S(1)} %get-tuple-element.37), channel_id=1, source_target_pairs={{0,17},{1,16},{16,1},{17,0},{2,19},{3,18},{18,3},{19,2},{4,21},{5,... | collective-permute-start | bytes 196616 | tf_op jit(solution)/shard_map/ppermute | solution.py:230
  42.7 1.2 %collective-permute-start.22 = (bf16[64,512]{1,0:T(8,128)(2,1)S(1)}, bf16[64,512]{1,0:T(8,128)(2,1)S(1)}, u32[]{:S(2)}, u32[]{:S(2)}) collective-permute-start(bf16[64,512]{1,0:T(8,128)(2,1)S(1)} %get-tuple-element.39), channel_id=1, source_target_pairs={{0,1},{1,0},{16,17},{17,16},{2,3},{3,2},{18,19},{19,18},{4,5},{5,4... | collective-permute-start | bytes 196616 | tf_op jit(solution)/shard_map/ppermute | solution.py:230
  43.8 1.6 %collective-permute-done.18.refs_3_ = bf16[64,512]{1,0:T(8,128)(2,1)S(1)} collective-permute-done((bf16[64,512]{1,0:T(8,128)(2,1)S(1)}, bf16[64,512]{1,0:T(8,128)(2,1)S(1)}, u32[]{:S(2)}, u32[]{:S(2)}) %collective-permute-start.18) | collective-permute-done | bytes 65568 | tf_op jit(solution)/shard_map/ppermute | solution.py:227
  46.9 0.9 %shard_map.89 = (f32[64,512]{1,0:T(8,128)}, f32[64,512]{1,0:T(8,128)}) custom-call(bf16[64,512]{1,0:T(8,128)(2,1)S(1)} %copy-done, bf16[64,512]{1,0:T(8,128)(2,1)S(1)} %copy-done.1, f32[64,512]{1,0:T(8,128)S(1)} %shard_map.87.text_ref, f32[64,512]{1,0:T(8,128)S(1)} %get-tuple-element.36.refs_0_, bf16[64,512]{1,0:T(8,128)(2,1)S(1)} %collective-permute-done.20.refs_1_, ...), custom_call_target="tpu_custom_call" | custom-call | flops 1048576 | bytes 1048576 | tf_op jit(solution)/shard_map/pallas_call | solution.py:206
  (43 shorter events, 6.3 us)
Async XLA Ops:
  0.6 6.6 %copy-start.2 = (bf16[64,1280]{1,0:T(8,128)(2,1)S(1)}, bf16[64,1280]{1,0:T(8,128)(2,1)}, u32[]{:S(2)}) copy-start(bf16[64,1280]{1,0:T(8,128)(2,1)} %teacher_ref.1) | copy-start | bytes 491524
  0.7 15.3 %collective-permute-start.2 = (bf16[64,1280]{1,0:T(8,128)(2,1)}, bf16[64,1280]{1,0:T(8,128)(2,1)S(1)}, u32[]{:S(2)}, u32[]{:S(2)}) collective-permute-start(bf16[64,1280]{1,0:T(8,128)(2,1)} %teacher_ref.1), channel_id=1, source_target_pairs={{0,4},{2,6},{4,0},{6,2},{1,5},{3,7},{5,1},{7,3},{8,12},{10,14},{12... | collective-permute-start | bytes 491528 | tf_op jit(solution)/shard_map/ppermute | solution.py:227
  5.7 7.1 %collective-permute-start.6 = (bf16[64,1792]{1,0:T(8,128)(2,1)S(1)}, bf16[64,1792]{1,0:T(8,128)(2,1)S(1)}, u32[]{:S(2)}, u32[]{:S(2)}) collective-permute-start(bf16[64,1792]{1,0:T(8,128)(2,1)S(1)} %pad_maximum_fusion.refs_0_), channel_id=1, source_target_pairs={{0,16},{1,17},{16,0},{17,1},{2,18},{3,19},{18,2},{19,3},{4,20},{5,... | collective-permute-start | bytes 688136 | tf_op jit(solution)/shard_map/ppermute | solution.py:230
  7.3 12.3 %collective-permute-start.1 = (bf16[64,1792]{1,0:T(8,128)(2,1)S(1)}, bf16[64,1792]{1,0:T(8,128)(2,1)S(1)}, u32[]{:S(2)}, u32[]{:S(2)}) collective-permute-start(bf16[64,1792]{1,0:T(8,128)(2,1)S(1)} %pad_maximum_fusion.1), channel_id=1, source_target_pairs={{0,2},{2,0},{4,6},{6,4},{1,3},{3,1},{5,7},{7,5},{8,10},{10,8},{12,... | collective-permute-start | bytes 688136 | tf_op jit(solution)/shard_map/ppermute | solution.py:227
  8.9 13.0 %collective-permute-start.5 = (bf16[64,1792]{1,0:T(8,128)(2,1)S(1)}, bf16[64,1792]{1,0:T(8,128)(2,1)S(1)}, u32[]{:S(2)}, u32[]{:S(2)}) collective-permute-start(bf16[64,1792]{1,0:T(8,128)(2,1)S(1)} %pad_maximum_fusion.refs_0_), channel_id=1, source_target_pairs={{0,1},{1,0},{16,17},{17,16},{2,3},{3,2},{18,19},{19,18},{4,5},{5,4... | collective-permute-start | bytes 688136 | tf_op jit(solution)/shard_map/ppermute | solution.py:230
  12.8 9.1 %collective-permute-start.7 = (bf16[64,1792]{1,0:T(8,128)(2,1)S(1)}, bf16[64,1792]{1,0:T(8,128)(2,1)S(1)}, u32[]{:S(2)}, u32[]{:S(2)}) collective-permute-start(bf16[64,1792]{1,0:T(8,128)(2,1)S(1)} %collective-permute-done.6.refs_2_), channel_id=1, source_target_pairs={{0,1},{1,0},{16,17},{17,16},{2,3},{3,2},{18,19},{19,18},{4,5},{5,4... | collective-permute-start | bytes 688136 | tf_op jit(solution)/shard_map/ppermute | solution.py:230
  14.3 5.3 %collective-permute-start = (bf16[64,512]{1,0:T(8,128)(2,1)S(1)}, bf16[64,512]{1,0:T(8,128)(2,1)S(1)}, u32[]{:S(2)}, u32[]{:S(2)}) collective-permute-start(bf16[64,512]{1,0:T(8,128)(2,1)S(1)} %copy-done.1), channel_id=1, source_target_pairs={{0,4},{2,6},{4,0},{6,2},{1,5},{3,7},{5,1},{7,3},{8,12},{10,14},{12... | collective-permute-start | bytes 196616 | tf_op jit(solution)/shard_map/ppermute | solution.py:227
  16.1 8.1 %collective-permute-start.4 = (bf16[64,1280]{1,0:T(8,128)(2,1)S(1)}, bf16[64,1280]{1,0:T(8,128)(2,1)S(1)}, u32[]{:S(2)}, u32[]{:S(2)}) collective-permute-start(bf16[64,1280]{1,0:T(8,128)(2,1)S(1)} %shard_map.78.refs_1_), channel_id=1, source_target_pairs={{0,2},{2,0},{4,6},{6,4},{1,3},{3,1},{5,7},{7,5},{8,10},{10,8},{12,... | collective-permute-start | bytes 491528 | tf_op jit(solution)/shard_map/ppermute | solution.py:227
  19.7 4.5 %collective-permute-start.3 = (bf16[64,512]{1,0:T(8,128)(2,1)S(1)}, bf16[64,512]{1,0:T(8,128)(2,1)S(1)}, u32[]{:S(2)}, u32[]{:S(2)}) collective-permute-start(bf16[64,512]{1,0:T(8,128)(2,1)S(1)} %shard_map.77.refs_0_), channel_id=1, source_target_pairs={{0,2},{2,0},{4,6},{6,4},{1,3},{3,1},{5,7},{7,5},{8,10},{10,8},{12,... | collective-permute-start | bytes 196616 | tf_op jit(solution)/shard_map/ppermute | solution.py:227
  22.2 2.2 %collective-permute-start.8 = (bf16[256,512]{1,0:T(8,128)(2,1)S(1)}, bf16[256,512]{1,0:T(8,128)(2,1)S(1)}, u32[]{:S(2)}, u32[]{:S(2)}) collective-permute-start(bf16[256,512]{1,0:T(8,128)(2,1)S(1)} %get-tuple-element.25.pupil_same_ref.same_ref), channel_id=1, source_target_pairs={{0,8},{8,0},{1,9},{9,1},{2,10},{10,2},{3,11},{11,3},{4,12},{12,4},... | collective-permute-start | bytes 786440 | tf_op jit(solution)/shard_map/ppermute | solution.py:258
  22.3 2.5 %collective-permute-start.9 = (bf16[256,1280]{1,0:T(8,128)(2,1)S(1)}, bf16[256,1280]{1,0:T(8,128)(2,1)S(1)}, u32[]{:S(2)}, u32[]{:S(2)}) collective-permute-start(bf16[256,1280]{1,0:T(8,128)(2,1)S(1)} %get-tuple-element.26.master_same_ref), channel_id=1, source_target_pairs={{0,8},{8,0},{1,9},{9,1},{2,10},{10,2},{3,11},{11,3},{4,12},{12,4},... | collective-permute-start | bytes 1966088 | tf_op jit(solution)/shard_map/ppermute | solution.py:258
  26.0 1.2 %collective-permute-start.12 = (f32[2,512]{1,0:T(2,128)S(1)}, f32[2,512]{1,0:T(2,128)S(1)}, u32[]{:S(2)}, u32[]{:S(2)}) collective-permute-start(f32[2,512]{1,0:T(2,128)S(1)} %get-tuple-element.29.own_ref), channel_id=1, source_target_pairs={{0,8},{8,0},{1,9},{9,1},{2,10},{10,2},{3,11},{11,3},{4,12},{12,4},... | collective-permute-start | bytes 12296 | tf_op jit(solution)/shard_map/ppermute | solution.py:258
  26.3 4.6 %collective-permute-start.10 = (f32[2,256]{1,0:T(2,128)S(1)}, f32[2,256]{1,0:T(2,128)S(1)}, u32[]{:S(2)}, u32[]{:S(2)}) collective-permute-start(f32[2,256]{1,0:T(2,128)S(1)} %get-tuple-element.28.refs_0_), channel_id=1, source_target_pairs={{0,4},{2,6},{4,0},{6,2},{1,5},{3,7},{5,1},{7,3},{8,12},{10,14},{12... | collective-permute-start | bytes 6152 | tf_op jit(solution)/shard_map/ppermute | solution.py:227
  27.3 7.2 %collective-permute-start.15 = (f32[2,512]{1,0:T(2,128)S(1)}, f32[2,512]{1,0:T(2,128)S(1)}, u32[]{:S(2)}, u32[]{:S(2)}) collective-permute-start(f32[2,512]{1,0:T(2,128)S(1)} %shard_map.84.refs_0_), channel_id=1, source_target_pairs={{0,17},{1,16},{16,1},{17,0},{2,19},{3,18},{18,3},{19,2},{4,21},{5,... | collective-permute-start | bytes 12296 | tf_op jit(solution)/shard_map/ppermute | solution.py:230
  28.8 5.7 %collective-permute-start.14 = (f32[2,512]{1,0:T(2,128)S(1)}, f32[2,512]{1,0:T(2,128)S(1)}, u32[]{:S(2)}, u32[]{:S(2)}) collective-permute-start(f32[2,512]{1,0:T(2,128)S(1)} %shard_map.84.refs_0_), channel_id=1, source_target_pairs={{0,16},{1,17},{16,0},{17,1},{2,18},{3,19},{18,2},{19,3},{4,20},{5,... | collective-permute-start | bytes 12296 | tf_op jit(solution)/shard_map/ppermute | solution.py:230
  29.4 5.2 %collective-permute-start.13 = (f32[2,512]{1,0:T(2,128)S(1)}, f32[2,512]{1,0:T(2,128)S(1)}, u32[]{:S(2)}, u32[]{:S(2)}) collective-permute-start(f32[2,512]{1,0:T(2,128)S(1)} %shard_map.84.refs_0_), channel_id=1, source_target_pairs={{0,1},{1,0},{16,17},{17,16},{2,3},{3,2},{18,19},{19,18},{4,5},{5,4... | collective-permute-start | bytes 12296 | tf_op jit(solution)/shard_map/ppermute | solution.py:230
  30.9 3.7 %collective-permute-start.11 = (f32[2,256]{1,0:T(2,128)S(1)}, f32[2,256]{1,0:T(2,128)S(1)}, u32[]{:S(2)}, u32[]{:S(2)}) collective-permute-start(f32[2,256]{1,0:T(2,128)S(1)} %shard_map.82.refs_0_), channel_id=1, source_target_pairs={{0,2},{2,0},{4,6},{6,4},{1,3},{3,1},{5,7},{7,5},{8,10},{10,8},{12,... | collective-permute-start | bytes 6152 | tf_op jit(solution)/shard_map/ppermute | solution.py:227
  35.7 4.5 %collective-permute-start.19 = (bf16[4,64,512]{2,1,0:T(8,128)(2,1)S(1)}, bf16[4,64,512]{2,1,0:T(8,128)(2,1)S(1)}, u32[]{:S(2)}, u32[]{:S(2)}) collective-permute-start(bf16[4,64,512]{2,1,0:T(8,128)(2,1)S(1)} %get-tuple-element.35), channel_id=1, source_target_pairs={{0,8},{8,0},{1,9},{9,1},{2,10},{10,2},{3,11},{11,3},{4,12},{12,4},... | collective-permute-start | bytes 786440 | tf_op jit(solution)/shard_map/ppermute | solution.py:258
  35.7 6.9 %collective-permute-start.16 = (bf16[64,512]{1,0:T(8,128)(2,1)S(1)}, bf16[64,512]{1,0:T(8,128)(2,1)S(1)}, u32[]{:S(2)}, u32[]{:S(2)}) collective-permute-start(bf16[64,512]{1,0:T(8,128)(2,1)S(1)} %get-tuple-element.31), channel_id=1, source_target_pairs={{0,4},{2,6},{4,0},{6,2},{1,5},{3,7},{5,1},{7,3},{8,12},{10,14},{12... | collective-permute-start | bytes 196616 | tf_op jit(solution)/shard_map/ppermute | solution.py:227
  37.7 6.1 %collective-permute-start.17 = (bf16[64,512]{1,0:T(8,128)(2,1)S(1)}, bf16[64,512]{1,0:T(8,128)(2,1)S(1)}, u32[]{:S(2)}, u32[]{:S(2)}) collective-permute-start(bf16[64,512]{1,0:T(8,128)(2,1)S(1)} %get-tuple-element.32), channel_id=1, source_target_pairs={{0,2},{2,0},{4,6},{6,4},{1,3},{3,1},{5,7},{7,5},{8,10},{10,8},{12,... | collective-permute-start | bytes 196616 | tf_op jit(solution)/shard_map/ppermute | solution.py:227
  39.3 6.1 %collective-permute-start.18 = (bf16[64,512]{1,0:T(8,128)(2,1)S(1)}, bf16[64,512]{1,0:T(8,128)(2,1)S(1)}, u32[]{:S(2)}, u32[]{:S(2)}) collective-permute-start(bf16[64,512]{1,0:T(8,128)(2,1)S(1)} %get-tuple-element.33), channel_id=1, source_target_pairs={{0,6},{2,4},{4,2},{6,0},{1,7},{3,5},{5,3},{7,1},{8,14},{10,12},{12... | collective-permute-start | bytes 196616 | tf_op jit(solution)/shard_map/ppermute | solution.py:227
  40.2 5.8 %collective-permute-start.20 = (bf16[64,512]{1,0:T(8,128)(2,1)S(1)}, bf16[64,512]{1,0:T(8,128)(2,1)S(1)}, u32[]{:S(2)}, u32[]{:S(2)}) collective-permute-start(bf16[64,512]{1,0:T(8,128)(2,1)S(1)} %get-tuple-element.37), channel_id=1, source_target_pairs={{0,17},{1,16},{16,1},{17,0},{2,19},{3,18},{18,3},{19,2},{4,21},{5,... | collective-permute-start | bytes 196616 | tf_op jit(solution)/shard_map/ppermute | solution.py:230
  41.8 4.6 %collective-permute-start.21 = (bf16[64,512]{1,0:T(8,128)(2,1)S(1)}, bf16[64,512]{1,0:T(8,128)(2,1)S(1)}, u32[]{:S(2)}, u32[]{:S(2)}) collective-permute-start(bf16[64,512]{1,0:T(8,128)(2,1)S(1)} %get-tuple-element.38), channel_id=1, source_target_pairs={{0,16},{1,17},{16,0},{17,1},{2,18},{3,19},{18,2},{19,3},{4,20},{5,... | collective-permute-start | bytes 196616 | tf_op jit(solution)/shard_map/ppermute | solution.py:230
  42.7 4.3 %collective-permute-start.22 = (bf16[64,512]{1,0:T(8,128)(2,1)S(1)}, bf16[64,512]{1,0:T(8,128)(2,1)S(1)}, u32[]{:S(2)}, u32[]{:S(2)}) collective-permute-start(bf16[64,512]{1,0:T(8,128)(2,1)S(1)} %get-tuple-element.39), channel_id=1, source_target_pairs={{0,1},{1,0},{16,17},{17,16},{2,3},{3,2},{18,19},{19,18},{4,5},{5,4... | collective-permute-start | bytes 196616 | tf_op jit(solution)/shard_map/ppermute | solution.py:230
  (2 other events, 8.2 us)
